TPU v7x, 256 devices: a whole 4x4x8 slice. The times are simulated.
256 devices in a mesh: seq: 64 (over z, x, core), head: 4 (over y).
Axes of the slice: x: 4, y: 4, z: 8, core: 2. Of those that a mesh axis runs over, the one named last changes fastest.
Arguments:
- layer_input: bfloat16 [32768, 4096], P('seq', 'head'), may hold values from -6 to 6
- gate_weight: bfloat16 [4096, 128], P('head'), may hold values from -0.09375 to 0.09375
- queries: bfloat16 [32768, 2048], P('seq', 'head'), may hold values from -3 to 3
- key_vectors: bfloat16 [32768, 2048], P('seq', 'head'), may hold values from -3 to 3
- value_vectors: bfloat16 [32768, 2048], P('seq', 'head'), may hold values from -3 to 3
- grad_output: bfloat16 [32768, 2048], P('seq', 'head'), may hold values from -6 to 6
- reach_level: int32 [512], P('seq'), may hold values from 1 to 7
Outputs:
- grad_queries: bfloat16 [32768, 2048], P('seq', 'head')
- grad_keys: bfloat16 [32768, 2048], P('seq', 'head')
- grad_values: bfloat16 [32768, 2048], P('seq', 'head')
- grad_gate_weight: float32 [4096, 128], P('head')
All inputs are finite; a program needn't handle non-finite values.
Results may differ from a plain program's by a relative error of at most 0.0057.
Values may be sent and summed in bfloat16 or wider, within the bound.
No kernel may reach another device: no remote copies, remote signals or barrier semaphores. Data moves between devices by JAX's collectives and lax.ppermute only.
A program may use at most 64 MiB of HBM per device.

v0:
```python
import math

import jax
import jax.numpy as jnp
from jax import lax
from jax.sharding import PartitionSpec as P

HEAD_DIM = 128
SPAN = 64
LEVELS = 8


def from_partner(value, axis, stride):
    mask = 2**stride
    pairs = [(source, source ^ mask) for source in range(lax.axis_size(axis))]
    return lax.ppermute(value, axis, pairs)


def span_level(first, second):
    xored = jnp.bitwise_xor(first, second)
    total = jnp.zeros(xored.shape, jnp.int32)
    for power_idx in range(LEVELS - 1):
        total = total + (xored >= 1 << power_idx).astype(jnp.int32)
    return total


def contract_rows(left, right):
    return lax.dot_general(
        left, right, (((0,), (0,)), ((), ())), preferred_element_type=jnp.float32
    )


def shards(layer_input, gate_weight, queries, key_vectors, value_vectors, grad_output, reach_level):
    seq_count = lax.axis_size("seq")
    seq_bits = seq_count.bit_length() - 1
    tok_count = queries.shape[0]
    spans_here = reach_level.shape[0]
    span_bits = spans_here.bit_length() - 1
    heads_here = queries.shape[1] // HEAD_DIM
    inv_dim = 1.0 / HEAD_DIM
    seq_place = lax.axis_index("seq")
    partial_logits = jnp.dot(layer_input, gate_weight, preferred_element_type=jnp.float32)
    logits = lax.psum_scatter(partial_logits, "head", scatter_dimension=1, tiled=True)
    gates = jax.nn.sigmoid(logits).reshape(tok_count, heads_here, LEVELS)
    allowed = (jnp.arange(LEVELS)[None, :] <= reach_level[:, None]).astype(jnp.float32)
    allowed_tok = jnp.repeat(allowed, SPAN, axis=0)
    weight = gates * allowed_tok[:, None, :]
    query_rows = queries.reshape(tok_count, heads_here, HEAD_DIM)
    key_rows = key_vectors.reshape(tok_count, heads_here, HEAD_DIM)
    value_rows = value_vectors.reshape(tok_count, heads_here, HEAD_DIM)
    grad_rows = grad_output.reshape(tok_count, heads_here, HEAD_DIM)

    def level_of_bit(bit_index):
        return min(bit_index + 1 + span_bits, LEVELS - 1)

    cross_levels = sorted(set((level_of_bit(bit_index) for bit_index in range(seq_bits))))
    block_state = (
        jnp.einsum("shp,shq->hpq", key_rows, value_rows, preferred_element_type=jnp.float32)
        * inv_dim
    )
    level_grads = {}
    for level in cross_levels:
        gated = (weight[:, :, level, None] * query_rows).astype(jnp.bfloat16)
        level_grads[level] = (
            jnp.einsum("thp,thq->hpq", gated, grad_rows, preferred_element_type=jnp.float32)
            * inv_dim
        )
    forward_sums = {}
    for level in cross_levels:
        forward_sums[level] = jnp.zeros(block_state.shape, jnp.float32)
    backward_sum = jnp.zeros(block_state.shape, jnp.float32)
    running = block_state
    running_grads = dict(level_grads)
    for bit_index in range(seq_bits):
        used_level = level_of_bit(bit_index)
        received = from_partner(running, "seq", bit_index)
        upper_half = (jnp.right_shift(seq_place, bit_index) & 1).astype(jnp.float32)
        forward_sums[used_level] = forward_sums[used_level] + upper_half * received
        running = running + received
    for bit_index in range(seq_bits):
        used_level = level_of_bit(bit_index)
        remaining = [level for level in cross_levels if level >= used_level]
        outgoing = jnp.stack([running_grads[level] for level in remaining])
        received = from_partner(outgoing, "seq", bit_index)
        upper_half = (jnp.right_shift(seq_place, bit_index) & 1).astype(jnp.float32)
        backward_sum = backward_sum + (1.0 - upper_half) * received[0]
        for position, level in enumerate(remaining):
            if level >= level_of_bit(bit_index + 1):
                running_grads[level] = running_grads[level] + received[position]
    query_cross = jnp.zeros((tok_count, heads_here, HEAD_DIM), jnp.float32)
    cross_terms = {}
    for level in cross_levels:
        projected = jnp.einsum(
            "thq,hpq->thp",
            grad_rows,
            forward_sums[level].astype(jnp.bfloat16),
            preferred_element_type=jnp.float32,
        )
        query_cross = query_cross + weight[:, :, level, None] * projected
        cross_terms[level] = jnp.sum(query_rows * projected, -1)
    empty_gate = jnp.zeros((tok_count, heads_here), jnp.float32)
    gate_cross = jnp.stack([cross_terms.get(level, empty_gate) for level in range(LEVELS)], -1)
    later_state = backward_sum.astype(jnp.bfloat16)
    key_cross = jnp.einsum(
        "shq,hpq->shp", value_rows, later_state, preferred_element_type=jnp.float32
    )
    value_cross = jnp.einsum(
        "shp,hpq->shq", key_rows, later_state, preferred_element_type=jnp.float32
    )
    span_index = jnp.arange(spans_here)
    local_level = span_level(span_index[:, None], span_index[None, :])
    onehot = (local_level[:, :, None] == jnp.arange(LEVELS)[None, None, :]).astype(jnp.float32)
    tok_onehot = jnp.repeat(onehot, SPAN, axis=0)
    positions = jnp.arange(tok_count)
    causal = (positions[None, :] <= positions[:, None]).astype(jnp.float32)
    query_parts = []
    key_parts = []
    value_parts = []
    gate_parts = []
    for head_index in range(heads_here):
        query_head = query_rows[:, head_index]
        key_head = key_rows[:, head_index]
        value_head = value_rows[:, head_index]
        grad_head = grad_rows[:, head_index]
        scores = (
            lax.dot_general(
                query_head, key_head, (((1,), (1,)), ((), ())), preferred_element_type=jnp.float32
            )
            * inv_dim
        )
        grad_probs = lax.dot_general(
            grad_head, value_head, (((1,), (1,)), ((), ())), preferred_element_type=jnp.float32
        )
        level_table = jnp.sum(tok_onehot * weight[:, head_index, None, :], -1)
        pair_weight = jnp.repeat(level_table, SPAN, axis=1) * causal
        weighted_scores = (pair_weight * scores).astype(jnp.bfloat16)
        weighted_grads = (pair_weight * grad_probs).astype(jnp.bfloat16)
        value_parts.append(contract_rows(weighted_scores, grad_head))
        key_parts.append(contract_rows(weighted_grads, query_head) * inv_dim)
        query_parts.append(
            jnp.dot(weighted_grads, key_head, preferred_element_type=jnp.float32) * inv_dim
        )
        row_sums = (scores * grad_probs * causal).reshape(tok_count, spans_here, SPAN).sum(-1)
        gate_parts.append(jnp.sum(row_sums[:, :, None] * tok_onehot, 1))
    query_in = jnp.stack(query_parts, axis=1)
    key_in = jnp.stack(key_parts, axis=1)
    value_in = jnp.stack(value_parts, axis=1)
    gate_in = jnp.stack(gate_parts, axis=1)
    grad_queries = (
        (query_in + query_cross).astype(jnp.bfloat16).reshape(tok_count, heads_here * HEAD_DIM)
    )
    grad_keys = (key_in + key_cross).astype(jnp.bfloat16).reshape(tok_count, heads_here * HEAD_DIM)
    grad_values = (
        (value_in + value_cross).astype(jnp.bfloat16).reshape(tok_count, heads_here * HEAD_DIM)
    )
    grad_gates = (gate_in + gate_cross) * allowed_tok[:, None, :]
    grad_logits = (
        (grad_gates * gates * (1.0 - gates))
        .reshape(tok_count, heads_here * LEVELS)
        .astype(jnp.bfloat16)
    )
    all_logit_grads = lax.all_gather(grad_logits, "head", axis=1, tiled=True)
    weight_part = contract_rows(layer_input, all_logit_grads)
    grad_weight = lax.psum(weight_part, "seq") * (1.0 / math.sqrt(tok_count * seq_count))
    return (grad_queries, grad_keys, grad_values, grad_weight)


def solution(mesh):
    placed = (
        P("seq", "head"),
        P("head", None),
        P("seq", "head"),
        P("seq", "head"),
        P("seq", "head"),
        P("seq", "head"),
        P("seq"),
    )
    return jax.shard_map(
        shards,
        mesh=mesh,
        in_specs=placed,
        out_specs=(P("seq", "head"), P("seq", "head"), P("seq", "head"), P("head", None)),
        check_vma=False,
    )
```

profile of v0, /device:TPU:1, one launch (start us, length us, event | category | flops | bytes accessed | tf_op | source)
XLA Modules:
  0.0 332.6 jit_solution(2746119506795361715)
XLA Ops:
  7.2 1.4 copy.166
  9.7 3.3 collective-permute-start
  13.1 1.2 fusion.92
  14.5 1.4 fusion.65
  15.9 1.3 fusion.64
  17.2 1.3 fusion.63
  18.9 1.3 copy.188
  20.2 2.8 bitcast_reduce_fusion.3
  22.9 1.3 bitcast_reduce_fusion.2
  24.2 1.9 bitcast_reduce_fusion.1
  26.1 1.3 bitcast_reduce_fusion
  32.6 1.4 fusion.80
  34.0 1.7 add.227
  35.6 2.3 convolution_bitcast_fusion.5
  40.1 3.1 collective-permute-done.1
  43.2 1.8 add.229
  44.9 1.0 collective-permute-start.2
  52.5 1.0 pad_maximum_fusion
  53.6 1.7 collective-permute-start.6
  55.3 1.2 multiply_reduce_fusion.3
  61.9 2.0 fusion.37
  66.8 1.1 fusion.25
  71.4 1.0 fusion.11
  72.4 1.0 fusion.10
  73.5 1.2 fusion.60
  76.4 1.1 add.231
  77.4 1.9 collective-permute-start.3
  79.6 1.0 fusion.8
  80.6 5.1 %collective-permute-done.3 = f32[4,128,128]{2,1,0:T(8,128)S(1)} collective-permute-done((f32[4,128,128]{2,1,0:T(8,128)S(1)}, f32[4,128,128]{2,1,0:T(8,128)S(1)}, u32[]{:S(2)}, u32[]{:S(2)}) %collective-permute-start.3) | collective-permute-done | bytes 262176 | tf_op jit(solution)/shard_map/ppermute | solution.py:16
  85.8 3.0 collective-permute-start.4
  89.1 11.1 %collective-permute-done.4 = f32[4,128,128]{2,1,0:T(8,128)S(1)} collective-permute-done((f32[4,128,128]{2,1,0:T(8,128)S(1)}, f32[4,128,128]{2,1,0:T(8,128)S(1)}, u32[]{:S(2)}, u32[]{:S(2)}) %collective-permute-start.4) | collective-permute-done | bytes 262176 | tf_op jit(solution)/shard_map/ppermute | solution.py:16
  100.3 6.5 %collective-permute-start.5 = (f32[4,128,128]{2,1,0:T(8,128)S(1)}, f32[4,128,128]{2,1,0:T(8,128)S(1)}, u32[]{:S(2)}, u32[]{:S(2)}) collective-permute-start(f32[4,128,128]{2,1,0:T(8,128)S(1)} %add.234), channel_id=1, source_target_pairs={{0,128},{4,132},{8,136},{12,140},{16,144},{20,148},{24,152},{28,15... | collective-permute-start | bytes 786440 | tf_op jit(solution)/shard_map/ppermute | solution.py:16
  106.7 1.1 fusion.55
  108.7 1.8 collective-permute-start.8
  110.5 1.2 convolution_bitcast_fusion.3
  111.7 3.6 %collective-permute-done.5 = f32[4,128,128]{2,1,0:T(8,128)S(1)} collective-permute-done((f32[4,128,128]{2,1,0:T(8,128)S(1)}, f32[4,128,128]{2,1,0:T(8,128)S(1)}, u32[]{:S(2)}, u32[]{:S(2)}) %collective-permute-start.5) | collective-permute-done | bytes 262176 | tf_op jit(solution)/shard_map/ppermute | solution.py:16
  115.4 1.7 fusion.20
  117.2 5.5 %collective-permute-done.8 = f32[2,4,128,128]{3,2,1,0:T(8,128)} collective-permute-done((f32[2,4,128,128]{3,2,1,0:T(8,128)}, f32[2,4,128,128]{3,2,1,0:T(8,128)}, u32[]{:S(2)}, u32[]{:S(2)}) %collective-permute-start.8) | collective-permute-done | bytes 524320 | tf_op jit(solution)/shard_map/ppermute | solution.py:16
  122.7 1.1 fusion.46
  124.0 9.6 %all_gather.3 = bf16[512,128]{0,1:T(8,128)(2,1)S(1)} all-gather(bf16[512,32]{0,1:T(8,128)(2,1)S(1)} %fusion.79), channel_id=1, replica_groups=mesh['seq'=64,'head'=4] {'head'}, dimensions={1}, use_global_device_ids=true | all-gather | bytes 163840 | tf_op jit(solution)/shard_map/all_gather | solution.py:162
  133.6 1.9 collective-permute-start.10
  135.5 1.1 convolution_bitcast_fusion.6
  136.7 6.0 %collective-permute-done.10 = f32[1,4,128,128]{3,2,1,0:T(8,128)S(1)} collective-permute-done((f32[1,4,128,128]{3,2,1,0:T(8,128)S(1)}, f32[1,4,128,128]{3,2,1,0:T(8,128)S(1)}, u32[]{:S(2)}, u32[]{:S(2)}) %collective-permute-start.10) | collective-permute-done | bytes 262176 | tf_op jit(solution)/shard_map/ppermute | solution.py:16
  143.4 4.8 %collective-permute-start.11 = (f32[1,4,128,128]{3,2,1,0:T(8,128)}, f32[1,4,128,128]{3,2,1,0:T(8,128)}, u32[]{:S(2)}, u32[]{:S(2)}) collective-permute-start(f32[1,4,128,128]{3,2,1,0:T(8,128)} %fusion.61), channel_id=1, source_target_pairs={{0,128},{4,132},{8,136},{12,140},{16,144},{20,148},{24,152},{28,15... | collective-permute-start | bytes 786440 | tf_op jit(solution)/shard_map/ppermute | solution.py:16
  148.2 1.0 convolution_bitcast_fusion.7
  150.2 168.9 %all-reduce.2.cloned.1.call-done = f32[1024,128]{0,1:T(8,128)} async-done(((f32[1024,128]{0,1:T(8,128)}), f32[1024,128]{0,1:T(8,128)}) %all-reduce.2.cloned.1.call-update) | async-done | bytes 524304 | tf_op jit(solution)/shard_map/psum | solution.py:164
  319.1 1.1 broadcast_multiply_fusion
  321.2 1.3 fusion.52
  (225 shorter events, 36.8 us)
Async XLA Ops:
  7.2 5.9 %copy-start = (bf16[512,1024]{1,0:T(8,128)(2,1)S(1)}, bf16[512,1024]{1,0:T(8,128)(2,1)}, u32[]{:S(2)}) copy-start(bf16[512,1024]{1,0:T(8,128)(2,1)} %param.7) | copy-start | bytes 3145732
  7.2 1.4 copy-start.22
  7.2 30.7 %reduce-scatter.2.cloned.1.call-start = ((), (), s32[]{:S(2)}) async-start(), calls=%async_computation.1 | async-start | bytes 327680 | tf_op jit(solution)/shard_map/reduce_scatter | solution.py:43
  8.9 9.7 %copy-start.9 = (bf16[512,512]{0,1:T(8,128)(2,1)}, bf16[512,512]{0,1:T(8,128)(2,1)S(1)}, u32[]{:S(2)}) copy-start(bf16[512,512]{0,1:T(8,128)(2,1)S(1)} %copy.164) | copy-start | bytes 1572868
  9.4 3.6 %copy-start.34 = (bf16[1024,128]{1,0:T(8,128)(2,1)S(1)}, bf16[1024,128]{1,0:T(8,128)(2,1)}, u32[]{:S(2)}) copy-start(bf16[1024,128]{1,0:T(8,128)(2,1)} %param.8) | copy-start | bytes 786436
  9.7 24.2 %collective-permute-start = (f32[4,128,128]{2,1,0:T(8,128)S(1)}, f32[4,128,128]{2,1,0:T(8,128)}, u32[]{:S(2)}, u32[]{:S(2)}) collective-permute-start(f32[4,128,128]{2,1,0:T(8,128)S(1)} %convolution_multiply_fusion.16), channel_id=1, source_target_pairs={{0,4},{4,0},{8,12},{12,8},{16,20},{20,16},{24,28},{28,24},{32,36},... | collective-permute-start | bytes 786440 | tf_op jit(solution)/shard_map/ppermute | solution.py:16
  14.3 304.8 %all-reduce.2.cloned.1.call-start = ((), (), s32[]{:S(2)}) async-start(), calls=%async_computation.2 | async-start | bytes 1048576 | tf_op jit(solution)/shard_map/psum | solution.py:164
  20.1 2.8 copy-start.3
  20.1 2.8 copy-start.6
  35.6 7.5 %collective-permute-start.1 = (f32[4,128,128]{2,1,0:T(8,128)}, f32[4,128,128]{2,1,0:T(8,128)S(1)}, u32[]{:S(2)}, u32[]{:S(2)}) collective-permute-start(f32[4,128,128]{2,1,0:T(8,128)} %add.227), channel_id=1, source_target_pairs={{0,8},{4,12},{8,0},{12,4},{16,24},{20,28},{24,16},{28,20},{32,40},... | collective-permute-start | bytes 786440 | tf_op jit(solution)/shard_map/ppermute | solution.py:16
  43.2 1.8 copy-start.20
  44.9 31.4 %collective-permute-start.2 = (f32[4,128,128]{2,1,0:T(8,128)}, f32[4,128,128]{2,1,0:T(8,128)}, u32[]{:S(2)}, u32[]{:S(2)}) collective-permute-start(f32[4,128,128]{2,1,0:T(8,128)} %add.229), channel_id=1, source_target_pairs={{0,16},{4,20},{8,24},{12,28},{16,0},{20,4},{24,8},{28,12},{32,48},... | collective-permute-start | bytes 786440 | tf_op jit(solution)/shard_map/ppermute | solution.py:16
  52.5 2.8 copy-start.35
  52.5 2.8 copy-start.36
  52.5 2.8 copy-start.37
  52.5 2.8 copy-start.38
  53.6 19.9 %collective-permute-start.6 = (f32[4,4,128,128]{3,2,1,0:T(8,128)}, f32[4,4,128,128]{3,2,1,0:T(8,128)}, u32[]{:S(2)}, u32[]{:S(2)}) collective-permute-start(f32[4,4,128,128]{3,2,1,0:T(8,128)} %pad_maximum_fusion), channel_id=1, source_target_pairs={{0,4},{4,0},{8,12},{12,8},{16,20},{20,16},{24,28},{28,24},{32,36},... | collective-permute-start | bytes 3145736 | tf_op jit(solution)/shard_map/ppermute | solution.py:16
  61.9 2.0 copy-start.4
  61.9 2.2 copy-start.13
  64.1 1.5 copy-start.12
  74.8 32.0 %collective-permute-start.7 = (f32[3,4,128,128]{3,2,1,0:T(8,128)S(1)}, f32[3,4,128,128]{3,2,1,0:T(8,128)S(1)}, u32[]{:S(2)}, u32[]{:S(2)}) collective-permute-start(f32[3,4,128,128]{3,2,1,0:T(8,128)S(1)} %pad_maximum_fusion.1), channel_id=1, source_target_pairs={{0,8},{4,12},{8,0},{12,4},{16,24},{20,28},{24,16},{28,20},{32,40},... | collective-permute-start | bytes 2359304 | tf_op jit(solution)/shard_map/ppermute | solution.py:16
  77.4 8.3 %collective-permute-start.3 = (f32[4,128,128]{2,1,0:T(8,128)S(1)}, f32[4,128,128]{2,1,0:T(8,128)S(1)}, u32[]{:S(2)}, u32[]{:S(2)}) collective-permute-start(f32[4,128,128]{2,1,0:T(8,128)S(1)} %add.231), channel_id=1, source_target_pairs={{0,32},{4,36},{8,40},{12,44},{16,48},{20,52},{24,56},{28,60},{32,0... | collective-permute-start | bytes 786440 | tf_op jit(solution)/shard_map/ppermute | solution.py:16
  80.6 8.2 %copy-start.21 = (f32[4,128,128]{2,1,0:T(8,128)S(1)}, f32[4,128,128]{2,1,0:T(8,128)}, u32[]{:S(2)}) copy-start(f32[4,128,128]{2,1,0:T(8,128)} %copy-done.20) | copy-start | bytes 786436
  85.8 14.4 %collective-permute-start.4 = (f32[4,128,128]{2,1,0:T(8,128)S(1)}, f32[4,128,128]{2,1,0:T(8,128)S(1)}, u32[]{:S(2)}, u32[]{:S(2)}) collective-permute-start(f32[4,128,128]{2,1,0:T(8,128)S(1)} %add.232), channel_id=1, source_target_pairs={{0,64},{4,68},{8,72},{12,76},{16,80},{20,84},{24,88},{28,92},{32,9... | collective-permute-start | bytes 786440 | tf_op jit(solution)/shard_map/ppermute | solution.py:16
  100.3 15.1 %collective-permute-start.5 = (f32[4,128,128]{2,1,0:T(8,128)S(1)}, f32[4,128,128]{2,1,0:T(8,128)S(1)}, u32[]{:S(2)}, u32[]{:S(2)}) collective-permute-start(f32[4,128,128]{2,1,0:T(8,128)S(1)} %add.234), channel_id=1, source_target_pairs={{0,128},{4,132},{8,136},{12,140},{16,144},{20,148},{24,152},{28,15... | collective-permute-start | bytes 786440 | tf_op jit(solution)/shard_map/ppermute | solution.py:16
  108.7 6.7 %copy-start.19 = (f32[512,4,128]{0,2,1:T(8,128)S(1)}, f32[512,4,128]{0,2,1:T(8,128)}, u32[]{:S(2)}) copy-start(f32[512,4,128]{0,2,1:T(8,128)} %convolution_bitcast_fusion.5) | copy-start | bytes 3145732
  108.7 6.7 %copy-start.53 = (f32[512,4]{0,1:T(4,128)S(1)}, f32[512,4]{0,1:T(4,128)}, u32[]{:S(2)}) copy-start(f32[512,4]{0,1:T(4,128)} %copy-done.52) | copy-start | bytes 24580
  108.7 6.7 %copy-start.55 = (f32[512,4]{0,1:T(4,128)S(1)}, f32[512,4]{0,1:T(4,128)}, u32[]{:S(2)}) copy-start(f32[512,4]{0,1:T(4,128)} %copy-done.54) | copy-start | bytes 24580
  108.7 6.7 %copy-start.57 = (f32[512,4]{0,1:T(4,128)S(1)}, f32[512,4]{0,1:T(4,128)}, u32[]{:S(2)}) copy-start(f32[512,4]{0,1:T(4,128)} %copy-done.56) | copy-start | bytes 24580
  108.7 6.7 %copy-start.59 = (f32[512,4]{0,1:T(4,128)S(1)}, f32[512,4]{0,1:T(4,128)}, u32[]{:S(2)}) copy-start(f32[512,4]{0,1:T(4,128)} %copy-done.58) | copy-start | bytes 24580
  108.7 14.0 %collective-permute-start.8 = (f32[2,4,128,128]{3,2,1,0:T(8,128)}, f32[2,4,128,128]{3,2,1,0:T(8,128)}, u32[]{:S(2)}, u32[]{:S(2)}) collective-permute-start(f32[2,4,128,128]{3,2,1,0:T(8,128)} %pad_maximum_fusion.2), channel_id=1, source_target_pairs={{0,16},{4,20},{8,24},{12,28},{16,0},{20,4},{24,8},{28,12},{32,48},... | collective-permute-start | bytes 1572872 | tf_op jit(solution)/shard_map/ppermute | solution.py:16
  117.2 6.7 %copy-start.33 = (f32[512,32]{0,1:T(8,128)S(1)}, f32[512,32]{0,1:T(8,128)}, u32[]{:S(2)}) copy-start(f32[512,32]{0,1:T(8,128)} %reduce-scatter.2.cloned.1.call-done) | copy-start | bytes 196612
  117.2 6.7 %copy-start.49 = (f32[512,1,8]{0,2,1:T(8,128)S(1)}, f32[512,1,8]{0,2,1:T(8,128)}, u32[]{:S(2)}) copy-start(f32[512,1,8]{0,2,1:T(8,128)} %stack.153) | copy-start | bytes 49156
  117.2 6.7 %copy-start.50 = (f32[512,1,8]{0,2,1:T(8,128)S(1)}, f32[512,1,8]{0,2,1:T(8,128)}, u32[]{:S(2)}) copy-start(f32[512,1,8]{0,2,1:T(8,128)} %stack.154) | copy-start | bytes 49156
  117.2 6.7 %copy-start.51 = (f32[512,1,8]{0,2,1:T(8,128)S(1)}, f32[512,1,8]{0,2,1:T(8,128)}, u32[]{:S(2)}) copy-start(f32[512,1,8]{0,2,1:T(8,128)} %stack.155) | copy-start | bytes 49156
  123.8 9.8 %collective-permute-start.9 = (f32[1,4,128,128]{3,2,1,0:T(8,128)S(1)}, f32[1,4,128,128]{3,2,1,0:T(8,128)S(1)}, u32[]{:S(2)}, u32[]{:S(2)}) collective-permute-start(f32[1,4,128,128]{3,2,1,0:T(8,128)S(1)} %bitcast.429), channel_id=1, source_target_pairs={{0,32},{4,36},{8,40},{12,44},{16,48},{20,52},{24,56},{28,60},{32,0... | collective-permute-start | bytes 786440 | tf_op jit(solution)/shard_map/ppermute | solution.py:16
  133.6 9.0 %collective-permute-start.10 = (f32[1,4,128,128]{3,2,1,0:T(8,128)S(1)}, f32[1,4,128,128]{3,2,1,0:T(8,128)S(1)}, u32[]{:S(2)}, u32[]{:S(2)}) collective-permute-start(f32[1,4,128,128]{3,2,1,0:T(8,128)S(1)} %fusion.72), channel_id=1, source_target_pairs={{0,64},{4,68},{8,72},{12,76},{16,80},{20,84},{24,88},{28,92},{32,9... | collective-permute-start | bytes 786440 | tf_op jit(solution)/shard_map/ppermute | solution.py:16
  136.7 11.5 %copy-start.18 = (bf16[512,512]{0,1:T(8,128)(2,1)S(1)}, bf16[512,512]{0,1:T(8,128)(2,1)}, u32[]{:S(2)}) copy-start(bf16[512,512]{0,1:T(8,128)(2,1)} %get-tuple-element.60) | copy-start | bytes 1572868
  143.4 5.8 %copy-start.24 = (bf16[512,4,128]{0,2,1:T(8,128)(2,1)S(1)}, bf16[512,4,128]{0,2,1:T(8,128)(2,1)}, u32[]{:S(2)}) copy-start(bf16[512,4,128]{0,2,1:T(8,128)(2,1)} %get-tuple-element.40) | copy-start | bytes 1572868
  143.4 177.8 %collective-permute-start.11 = (f32[1,4,128,128]{3,2,1,0:T(8,128)}, f32[1,4,128,128]{3,2,1,0:T(8,128)}, u32[]{:S(2)}, u32[]{:S(2)}) collective-permute-start(f32[1,4,128,128]{3,2,1,0:T(8,128)} %fusion.61), channel_id=1, source_target_pairs={{0,128},{4,132},{8,136},{12,140},{16,144},{20,148},{24,152},{28,15... | collective-permute-start | bytes 786440 | tf_op jit(solution)/shard_map/ppermute | solution.py:16
  321.1 1.4 copy-start.8
  321.1 1.4 copy-start.26
  321.2 1.4 copy-start.28
  321.2 1.5 copy-start.29
  321.2 1.6 copy-start.32
  322.7 1.4 copy-start.30
  322.7 1.4 copy-start.31
  323.1 1.3 copy-start.27
  (32 other events, 28.0 us)
Sparse Core Ops, SparseCore 0:
  14.4 22.0 reduce-scatter.1
  136.8 182.1 all-reduce.1
where the time goes:
time: 335 us; the launch traced here: 333 us
  waiting for transfers between devices  203 us (61%)
  matrix products  30.5 us (9%)
  local copies, waits for them, and re-layouts  26.7 us (8%)
  starting transfers between devices  26.5 us (8%)
  other arithmetic  21.4 us (6%)
  between operations  14.6 us (4%)
  blocking collectives  9.6 us (3%)
    psum x1, waiting for transfers between devices, shards(): lax.psum(weight_part, 'seq') * (1.0 / math.sqrt(tok_count * seq_count))  169 us
    ppermute x12, waiting for transfers between devices, from_partner(): return lax.ppermute(value, axis, pairs)  34.4 us
    ppermute x12, starting transfers between devices, from_partner(): return lax.ppermute(value, axis, pairs)  26.4 us
    unnamed x142, local copies, waits for them, and re-layouts  16 us
    all_gather x1, blocking collectives, shards(): all_logit_grads = lax.all_gather(grad_logits, 'head', axis=1, tiled=True)  9.6 us
    dot_general x9, matrix products, contract_rows(): lax.dot_general(left, right, (((0,), (0,)), ((), ())), preferred_element_...  9.28 us
    dot_general x4, matrix products, shards(): lax.dot_general(query_head, key_head, (((1,), (1,)), ((), ())), preferred...  7.26 us
  transfers between devices with their start and end apart: 14, of which 7 were waited for; matrix products, arithmetic and copies ran while one was open for 18% of the time, Pallas kernels for 0%

commit v1 on v0

v1 whole, which is shorter than its diff:
```python
import functools
import math

import jax
import jax.numpy as jnp
from jax import lax
from jax.experimental import pallas as pl
from jax.experimental.pallas import tpu as pltpu
from jax.sharding import PartitionSpec as P

F32 = jnp.float32
BF16 = jnp.bfloat16
TOK = 512
DIM = 128
SPAN = 64
LEVELS = 8
CHIPS = 32
INV = 1.0 / DIM
VMEM_LIMIT = 24 * 1024 * 1024


def mm(left, right, left_dim=1, right_dim=0):
    return lax.dot_general(
        left, right, (((left_dim,), (right_dim,)), ((), ())), preferred_element_type=F32
    )


def aligned(index, size):
    return pl.ds(pl.multiple_of(index * size, size), size)


def call(body, out_shape, args, in_specs=None, out_specs=None, grid=(), scratch=(), cost=(10**7, 10**6)):
    whole = pl.BlockSpec(memory_space=pltpu.VMEM)
    many = isinstance(out_shape, (tuple, list))
    return pl.pallas_call(
        body,
        out_shape=out_shape,
        grid=grid,
        in_specs=in_specs or [whole] * len(args),
        out_specs=out_specs or ([whole] * len(out_shape) if many else whole),
        scratch_shapes=list(scratch),
        compiler_params=pltpu.CompilerParams(vmem_limit_bytes=VMEM_LIMIT),
        cost_estimate=pl.CostEstimate(flops=cost[0], bytes_accessed=cost[1], transcendentals=0),
    )(*args)


def shape(dims, dtype):
    return jax.ShapeDtypeStruct(dims, dtype)


def logits_body(x_ref, w_ref, o0, o1, o2, o3, scr):
    head = lax.axis_index("head")
    scr[...] = mm(w_ref[...], x_ref[...], 0, 1)
    for step, out in enumerate((o0, o1, o2, o3)):
        out[...] = scr[aligned(lax.rem(head + step, 4), 32), :]


def state_body(k_ref, v_ref, o_ref):
    o_ref[...] = mm(k_ref[...], v_ref[...], 0, 0) * INV


def allowed_mask(reach_ref):
    lane = lax.broadcasted_iota(jnp.int32, (LEVELS, TOK), 1) // SPAN
    level = lax.broadcasted_iota(jnp.int32, (LEVELS, TOK), 0)
    reach = jnp.zeros((LEVELS, TOK), jnp.int32)
    for span in range(TOK // SPAN):
        reach = jnp.where(lane == span, reach_ref[span], reach)
    return (level <= reach).astype(F32)


def level_body(q_ref, g_ref, l0, l1, l2, l3, reach_ref, gates_ref, msg_ref, keep_ref, w_scr):
    core = lax.axis_index("seq") & 1
    gates = jax.nn.sigmoid((l0[...] + l1[...]) + (l2[...] + l3[...]))
    gates_ref[...] = gates
    allowed = allowed_mask(reach_ref)
    for head in range(4):
        w_scr[8 * head : 8 * head + 8, :] = gates[8 * head : 8 * head + 8, :] * allowed
    for slot in range(4):
        kept = slot < 2
        head = 2 * core + slot if kept else 2 * (1 - core) + slot - 2
        query = q_ref[:, aligned(head, DIM)].astype(F32).T
        weight = w_scr[aligned(head, 8), :]
        gated = jnp.concatenate(
            [(weight[level : level + 1, :] * query).astype(BF16) for level in range(4, 8)], axis=0
        )
        grads = mm(gated, g_ref[:, aligned(head, DIM)]) * INV
        msg_ref[aligned(head, DIM), :] = grads[:DIM]
        for level in range(3):
            part = grads[DIM * (level + 1) : DIM * (level + 2)]
            row = 256 * level + DIM * (slot % 2)
            if kept:
                keep_ref[row : row + DIM, :] = part
            else:
                msg_ref[512 + row : 512 + row + DIM, :] = part


def mid1_body(r_ref, keep_ref, recv_ref, o_ref):
    own = [r_ref[chip] for chip in range(CHIPS)]
    pairs = [own[chip] + own[chip ^ 1] for chip in range(CHIPS)]
    zero = jnp.zeros((8, DIM), F32)
    before = [zero]
    for group in range(7):
        before.append(before[-1] + (pairs[4 * group] + pairs[4 * group + 2]))
    for chip in range(CHIPS):
        rows = [
            own[chip ^ 1] if chip & 1 else zero,
            pairs[chip ^ 2] if chip & 2 else zero,
            before[chip >> 2],
        ]
        for level in range(3):
            row = 256 * level + 8 * chip
            rows.append(keep_ref[row : row + 8, :] + recv_ref[512 + row : 512 + row + 8, :])
        o_ref[chip] = jnp.concatenate(rows, axis=0).astype(BF16)


def mid2_body(r_ref, states_ref, later_ref):
    got = [r_ref[chip].astype(F32) for chip in range(CHIPS)]
    for chip in range(0, CHIPS, 2):
        for level in range(3):
            both = [got[chip + i][8 * level : 8 * level + 8] for i in range(2)]
            row = 256 * level + 8 * chip
            states_ref[row : row + 16, :] = jnp.concatenate(both, axis=0).astype(BF16)
    zero = jnp.zeros((8, DIM), F32)
    after = [zero]
    for group in range(7, 0, -1):
        total = zero
        for chip in range(4 * group, 4 * group + 4):
            total = total + got[chip][40:48]
        after.append(after[-1] + total)
    after = after[::-1]
    for chip in range(CHIPS):
        total = after[chip >> 2]
        if not chip & 2:
            total = total + (got[chip ^ 2][32:40] + got[chip ^ 3][32:40])
        if not chip & 1:
            total = total + got[chip ^ 1][24:32]
        later_ref[chip] = total


def intra_body(q_ref, k_ref, v_ref, g_ref, gates_ref, reach_ref, dk_ref, dv_ref, dq_ref, rows_ref, p_scr, w_scr):
    weight = gates_ref[...] * allowed_mask(reach_ref)
    src = lax.broadcasted_iota(jnp.int32, (DIM, DIM), 0)
    dst = lax.broadcasted_iota(jnp.int32, (DIM, DIM), 1)
    same = (src // SPAN) == (dst // SPAN)
    mask0 = (same & (src <= dst)).astype(F32)
    mask1 = ((src // SPAN) < (dst // SPAN)).astype(F32)
    tiles = TOK // DIM
    key_t = k_ref[...].astype(F32).T.astype(BF16)
    row_parts = []
    for a in range(tiles):
        cols = slice(DIM * a, DIM * (a + 1))
        end = DIM * (a + 1)
        scores = mm(k_ref[:end, :], q_ref[cols, :], 1, 1) * INV
        probs = mm(v_ref[:end, :], g_ref[cols, :], 1, 1)
        prod = scores * probs
        sums = [None] * 4
        weights = []
        for b in range(a):
            level = (a ^ b).bit_length() + 1
            part = jnp.sum(prod[DIM * b : DIM * (b + 1)], axis=0, keepdims=True)
            sums[level] = part if sums[level] is None else sums[level] + part
            weights.append(jnp.broadcast_to(weight[level : level + 1, cols], (DIM, DIM)))
        diagonal = prod[DIM * a :]
        sums[0] = jnp.sum(diagonal * mask0, axis=0, keepdims=True)
        sums[1] = jnp.sum(diagonal * mask1, axis=0, keepdims=True)
        weights.append(weight[0:1, cols] * mask0 + weight[1:2, cols] * mask1)
        none = jnp.zeros((1, DIM), F32)
        sums = [none if part is None else part for part in sums]
        row_parts.append(jnp.concatenate(sums + [none] * 4, axis=0))
        pair = jnp.concatenate(weights, axis=0)
        p_scr[:end, cols] = (pair * scores).astype(BF16)
        weighted = (pair * probs).astype(BF16)
        w_scr[:end, cols] = weighted
        dq_ref[:, cols] = mm(key_t[:, :end], weighted) * INV
    rows_ref[...] = jnp.concatenate(row_parts, axis=1)
    for b in range(tiles):
        rows = slice(DIM * b, DIM * (b + 1))
        start = DIM * b
        dv_ref[rows, :] = mm(p_scr[rows, start:], g_ref[start:, :])
        dk_ref[rows, :] = mm(w_scr[rows, start:], q_ref[start:, :]) * INV


def cross_body(q_ref, g_ref, sib_ref, mine_ref, other_ref, gates_ref, reach_ref, dqt_ref, rows_ref, dq_ref, gl_ref):
    half = pl.program_id(0)
    core = lax.axis_index("seq") & 1
    allowed = allowed_mask(reach_ref)
    upper = (core == 1).astype(F32)
    outs = []
    for i in range(2):
        lanes = slice(DIM * i, DIM * (i + 1))
        rows = slice(DIM * i, DIM * (i + 1))
        levels = [(sib_ref[rows, :] * upper).astype(BF16)]
        for level in range(3):
            at = slice(256 * level + DIM * i, 256 * level + DIM * (i + 1))
            levels.append(jnp.where(half == core, mine_ref[at, :], other_ref[at, :]))
        projected = mm(jnp.concatenate(levels, axis=0), g_ref[:, lanes], 1, 1)
        query = q_ref[:, lanes].astype(F32).T
        gates = gates_ref[8 * i : 8 * i + 8, :]
        weight = gates * allowed
        total = dqt_ref[rows, :]
        parts = []
        for level in range(4):
            term = projected[DIM * level : DIM * (level + 1)]
            total = total + weight[4 + level : 5 + level, :] * term
            parts.append(jnp.sum(query * term, axis=0, keepdims=True))
        dq_ref[:, lanes] = total.T.astype(BF16)
        cross = jnp.concatenate([jnp.zeros((4, TOK), F32)] + parts, axis=0)
        grads = (rows_ref[8 * i : 8 * i + 8, :] + cross) * allowed
        outs.append(grads * gates * (1.0 - gates))
    gl_ref[...] = jnp.concatenate(outs, axis=0).astype(BF16)


def gradw_body(x_ref, g0, g1, g2, g3, keep_ref, send_ref, scr, full):
    head = lax.axis_index("head")
    core = lax.axis_index("seq") & 1
    for step, part in enumerate((g0, g1, g2, g3)):
        scr[aligned(lax.rem(head + 4 - step, 4), 32), :] = part[...]
    full[...] = mm(scr[...], x_ref[...]).T
    keep_ref[...] = full[aligned(core, 512), :]
    send_ref[...] = full[aligned(1 - core, 512), :]


def pack3_body(keep_ref, recv_ref, later_ref, o_ref):
    for chip in range(CHIPS):
        rows = slice(16 * chip, 16 * chip + 16)
        o_ref[chip, 0:16, :] = keep_ref[rows, :] + recv_ref[rows, :]
        o_ref[chip, 16:24, :] = later_ref[chip]


def mid3_body(scale, r_ref, sums_ref, later_ref):
    total = r_ref[0, 0:16, :]
    for chip in range(1, CHIPS):
        total = total + r_ref[chip, 0:16, :]
    total = total * scale
    for chip in range(CHIPS):
        sums_ref[chip] = total
    for chip in range(CHIPS):
        later_ref[8 * chip : 8 * chip + 8, :] = r_ref[chip, 16:24, :]


def final_body(k_ref, v_ref, sib_ref, mine_ref, other_ref, dki_ref, dvi_ref, dk_ref, dv_ref):
    half = pl.program_id(0) // 2
    core = lax.axis_index("seq") & 1
    later = jnp.where(half == core, mine_ref[...], other_ref[...])
    lower = (core == 0).astype(F32)
    later = (later + sib_ref[...] * lower).astype(BF16)
    dk_ref[...] = (dki_ref[...] + mm(v_ref[...], later, 1, 1)).astype(BF16)
    dv_ref[...] = (dvi_ref[...] + mm(k_ref[...], later, 1, 0)).astype(BF16)


def shards(layer_input, gate_weight, queries, key_vectors, value_vectors, grad_output, reach_level):
    seq_count = lax.axis_size("seq")
    core = lax.axis_index("seq") & 1
    groups = [[2 * chip + c for chip in range(CHIPS)] for c in range(2)]
    swap = [(d, d ^ 1) for d in range(seq_count)]

    def sibling(value):
        return lax.ppermute(value, "seq", swap)

    def exchange(value):
        return lax.all_to_all(value, "seq", 0, 0, axis_index_groups=groups)

    def rotate(value, step):
        return lax.ppermute(value, "head", [(h, (h + step) % 4) for h in range(4)])

    def whole():
        return pl.BlockSpec(memory_space=pltpu.VMEM)

    smem = pl.BlockSpec(memory_space=pltpu.SMEM)
    heads4 = pl.BlockSpec((TOK, DIM), lambda h: (0, h))
    rows4 = pl.BlockSpec((DIM, DIM), lambda h: (h, 0))

    states = call(
        state_body, shape((512, DIM), F32), (key_vectors, value_vectors),
        in_specs=[heads4, heads4], out_specs=rows4, grid=(4,),
    )
    sib_state = sibling(states)

    parts = call(
        logits_body, [shape((32, TOK), F32)] * 4, (layer_input, gate_weight),
        scratch=[pltpu.VMEM((DIM, TOK), F32)],
    )
    logits = [parts[0]] + [rotate(parts[step], step) for step in range(1, 4)]

    pair = lax.dynamic_slice(states + sib_state, (256 * core, 0), (256, DIM))
    got1 = exchange(pair.reshape(CHIPS, 8, DIM))

    gates, msg, keep = call(
        level_body,
        [shape((32, TOK), F32), shape((1280, DIM), F32), shape((768, DIM), F32)],
        (queries, grad_output, *logits, reach_level),
        in_specs=[whole()] * 6 + [smem],
        scratch=[pltpu.VMEM((32, TOK), F32)],
    )
    msg_in = sibling(msg)
    got2 = exchange(call(mid1_body, shape((CHIPS, 48, DIM), BF16), (got1, keep, msg_in)))

    dk_in, dv_in, dq_t, rows = call(
        intra_body,
        [shape((TOK, 512), F32), shape((TOK, 512), F32), shape((512, TOK), F32), shape((32, TOK), F32)],
        (queries, key_vectors, value_vectors, grad_output, gates, reach_level),
        in_specs=[heads4] * 4 + [pl.BlockSpec((8, TOK), lambda h: (h, 0)), smem],
        out_specs=[heads4, heads4, pl.BlockSpec((DIM, TOK), lambda h: (h, 0)), pl.BlockSpec((8, TOK), lambda h: (h, 0))],
        grid=(4,),
        scratch=[pltpu.VMEM((TOK, TOK), BF16), pltpu.VMEM((TOK, TOK), BF16)],
        cost=(2 * 10**9, 8 * 10**6),
    )

    level_half, later_slices = call(
        mid2_body, [shape((768, DIM), BF16), shape((CHIPS, 8, DIM), F32)], (got2,)
    )
    level_other = sibling(level_half)

    heads2 = pl.BlockSpec((TOK, 256), lambda h: (0, h))
    tok16 = pl.BlockSpec((16, TOK), lambda h: (h, 0))
    all768 = pl.BlockSpec((768, DIM), lambda h: (0, 0))
    grad_queries, grad_logits = call(
        cross_body,
        [shape((TOK, 512), BF16), shape((32, TOK), BF16)],
        (queries, grad_output, sib_state, level_half, level_other, gates, reach_level, dq_t, rows),
        in_specs=[
            heads2, heads2, pl.BlockSpec((256, DIM), lambda h: (h, 0)), all768, all768, tok16, smem,
            pl.BlockSpec((256, TOK), lambda h: (h, 0)), tok16,
        ],
        out_specs=[heads2, tok16],
        grid=(2,),
    )

    gl = [grad_logits] + [rotate(grad_logits, step) for step in range(1, 4)]
    w_keep, w_send = call(
        gradw_body, [shape((512, DIM), F32)] * 2, (layer_input, *gl),
        scratch=[pltpu.VMEM((DIM, TOK), BF16), pltpu.VMEM((1024, DIM), F32)],
    )
    w_in = sibling(w_send)
    got3 = exchange(call(pack3_body, shape((CHIPS, 24, DIM), F32), (w_keep, w_in, later_slices)))
    scale = 1.0 / math.sqrt(TOK * seq_count)
    sums, later_half = call(
        functools.partial(mid3_body, scale),
        [shape((CHIPS, 16, DIM), F32), shape((256, DIM), F32)], (got3,),
    )
    got4 = exchange(sums)
    later_other = sibling(later_half)

    half4 = pl.BlockSpec((DIM, DIM), lambda h: (h % 2, 0))
    grad_keys, grad_values = call(
        final_body,
        [shape((TOK, 512), BF16)] * 2,
        (key_vectors, value_vectors, msg_in, later_half, later_other, dk_in, dv_in),
        in_specs=[heads4, heads4, rows4, half4, half4, heads4, heads4],
        out_specs=[heads4, heads4],
        grid=(4,),
    )

    w_half = got4.reshape(512, DIM)
    w_other = sibling(w_half)
    low = jnp.where(core == 0, w_half, w_other)
    high = jnp.where(core == 0, w_other, w_half)
    return grad_queries, grad_keys, grad_values, jnp.concatenate([low, high], axis=0)


def solution(mesh):
    placed = (
        P("seq", "head"),
        P("head", None),
        P("seq", "head"),
        P("seq", "head"),
        P("seq", "head"),
        P("seq", "head"),
        P("seq"),
    )
    return jax.shard_map(
        shards,
        mesh=mesh,
        in_specs=placed,
        out_specs=(P("seq", "head"), P("seq", "head"), P("seq", "head"), P("head", None)),
        check_vma=False,
    )
```

time: 335 us -> 123 us (0.37)
  waiting for transfers between devices: 203 us -> 10.1 us
  blocking collectives: 9.6 us -> 69.7 us
  matrix products: 30.5 us -> 0 us
  other arithmetic: 21.4 us -> 0.88 us
  local copies, waits for them, and re-layouts: 26.7 us -> 6.6 us
  Pallas kernels: 0 us -> 15.3 us
  between operations: 14.6 us -> 0.75 us
  starting transfers between devices: 26.5 us -> 19.7 us
    psum x1 -> x0, waiting for transfers between devices: 169 us -> none  [shards(): lax.psum(weight_part, 'seq') * (1.0 / math.sqrt(tok_count * seq_count))]
    all_to_all x0 -> x4, blocking collectives: none -> 69.7 us  [exchange(): return lax.all_to_all(value, 'seq', 0, 0, axis_index_groups=groups)]
    dot_general x33 -> x0, matrix products: 30.5 us -> none  [the longest x9 9.28 us: contract_rows(): lax.dot_general(left, right, (((0,), (0,)), ((), ())), preferred_element_...]
    ppermute x12, waiting for transfers between devices: 34.4 us -> 10.1 us  [the longest x6 6.09 us: rotate(): return lax.ppermute(value, 'head', [(h, (h + step) % 4) for h in range(4)])]
    pallas_call x0 -> x11, Pallas kernels: none -> 15.3 us  [call(): pl.pallas_call(body, out_shape=out_shape, grid=grid, in_specs=in_specs or...]
    all_gather x1 -> x0, blocking collectives: 9.6 us -> none  [shards(): all_logit_grads = lax.all_gather(grad_logits, 'head', axis=1, tiled=True)]
    unnamed x142 -> x28, local copies, waits for them, and re-layouts: 16 us -> 6.6 us
    convert_element_type x8 -> x0, other arithmetic: 6.95 us -> none  [the longest x4 3.62 us: shards(): weighted_scores = (pair_weight * scores).astype(jnp.bfloat16)]
  transfers between devices with their start and end apart: 14 -> 12, of which waited for: 7 -> 7; matrix products, arithmetic and copies ran while one was open for 18% -> 0% of each run, Pallas kernels for 0% -> 8%
where the time goes in v1:
time: 123 us
  blocking collectives  69.7 us (57%)
  starting transfers between devices  19.7 us (16%)
  Pallas kernels  15.3 us (12%)
  waiting for transfers between devices  10.1 us (8%)
  local copies, waits for them, and re-layouts  6.6 us (5%)
    all_to_all x4, blocking collectives, exchange(): return lax.all_to_all(value, 'seq', 0, 0, axis_index_groups=groups)  69.7 us
    pallas_call x11, Pallas kernels, call(): pl.pallas_call(body, out_shape=out_shape, grid=grid, in_specs=in_specs or...  15.3 us
    ppermute x6, starting transfers between devices, sibling(): return lax.ppermute(value, 'seq', swap)  10.9 us
    ppermute x6, starting transfers between devices, rotate(): return lax.ppermute(value, 'head', [(h, (h + step) % 4) for h in range(4)])  8.75 us
    unnamed x28, local copies, waits for them, and re-layouts  6.6 us
    ppermute x6, waiting for transfers between devices, rotate(): return lax.ppermute(value, 'head', [(h, (h + step) % 4) for h in range(4)])  6.09 us
    ppermute x6, waiting for transfers between devices, sibling(): return lax.ppermute(value, 'seq', swap)  4.02 us
  transfers between devices with their start and end apart: 12, of which 7 were waited for; matrix products, arithmetic and copies ran while one was open for 0% of the time, Pallas kernels for 8%

profile of v1, /device:TPU:1, one launch (start us, length us, event | category | flops | bytes accessed | tf_op | source)
XLA Modules:
  0.0 123.1 jit_solution(302330745774476697)
XLA Ops:
  0.6 0.0 copy-start
  0.6 1.2 copy-done
  1.9 0.9 copy-done.12
  2.8 0.5 shard_map.103
  3.3 2.2 %collective-permute-start.1 = (f32[32,512]{1,0:T(8,128)S(1)}, f32[32,512]{1,0:T(8,128)S(1)}, u32[]{:S(2)}, u32[]{:S(2)}) collective-permute-start(f32[32,512]{1,0:T(8,128)S(1)} %get-tuple-element.26), channel_id=1, source_target_pairs={{0,1},{1,2},{2,3},{3,0},{4,5},{5,6},{6,7},{7,4},{8,9},{9,10},{10,1... | collective-permute-start | bytes 196616 | tf_op jit(solution)/shard_map/ppermute | solution.py:264
  5.5 2.6 %collective-permute-start.2 = (f32[32,512]{1,0:T(8,128)S(1)}, f32[32,512]{1,0:T(8,128)S(1)}, u32[]{:S(2)}, u32[]{:S(2)}) collective-permute-start(f32[32,512]{1,0:T(8,128)S(1)} %get-tuple-element.27), channel_id=1, source_target_pairs={{0,2},{1,3},{2,0},{3,1},{4,6},{5,7},{6,4},{7,5},{8,10},{9,11},{10,... | collective-permute-start | bytes 196616 | tf_op jit(solution)/shard_map/ppermute | solution.py:264
  8.2 1.1 collective-permute-start.3
  9.2 0.0 collective-permute-done.1.l1
  9.2 1.5 %collective-permute-done.2.l2 = f32[32,512]{1,0:T(8,128)S(1)} collective-permute-done((f32[32,512]{1,0:T(8,128)S(1)}, f32[32,512]{1,0:T(8,128)S(1)}, u32[]{:S(2)}, u32[]{:S(2)}) %collective-permute-start.2) | collective-permute-done | bytes 65568 | tf_op jit(solution)/shard_map/ppermute | solution.py:264
  10.8 0.8 collective-permute-done.3.l3
  11.6 0.0 copy-start.4
  11.6 0.0 copy-start.5
  11.6 2.2 %shard_map.104 = (f32[32,512]{1,0:T(8,128)S(1)}, f32[1280,128]{1,0:T(8,128)}, f32[768,128]{1,0:T(8,128)S(1)}) custom-call(bf16[512,512]{1,0:T(8,128)(2,1)S(1)} %copy-done.2, bf16[512,512]{1,0:T(8,128)(2,1)S(1)} %copy-done.3, f32[32,512]{1,0:T(8,128)S(1)} %get-tuple-element.25.l0, f32[32,512]{1,0:T(8,128)S(1)} %collective-permute-done.1.l1, ...), custom_call_target="tpu_custom_call" | custom-call | flops 10000000 | bytes 1000000 | tf_op jit(solution)/shard_map/pallas_call | solution.py:35
  13.8 2.1 %collective-permute-start.4 = (f32[1280,128]{1,0:T(8,128)}, f32[1280,128]{1,0:T(8,128)S(1)}, u32[]{:S(2)}, u32[]{:S(2)}) collective-permute-start(f32[1280,128]{1,0:T(8,128)} %get-tuple-element.30), channel_id=1, source_target_pairs={{0,4},{4,0},{8,12},{12,8},{16,20},{20,16},{24,28},{28,24},{32,36},... | collective-permute-start | bytes 1966088 | tf_op jit(solution)/shard_map/ppermute | solution.py:258
  15.9 1.2 shard_map.102
  17.1 0.1 collective-permute-start
  17.2 1.5 %collective-permute-done.sib_ref = f32[512,128]{1,0:T(8,128)S(1)} collective-permute-done((f32[512,128]{1,0:T(8,128)S(1)}, f32[512,128]{1,0:T(8,128)S(1)}, u32[]{:S(2)}, u32[]{:S(2)}) %collective-permute-start) | collective-permute-done | bytes 262176 | tf_op jit(solution)/shard_map/ppermute | solution.py:258
  18.7 20.6 %all_to_all.20.r_ref = f32[32,8,128]{2,1,0:T(8,128)S(1)} all-to-all(f32[32,8,128]{2,1,0:T(8,128)S(1)} %fusion), channel_id=1, replica_groups={{0,8,16,24,32,40,48,56,64,72,80,88,96,104,112,120,128,136,144,152,160,1..., dimensions={0} | all-to-all | bytes 262144 | tf_op jit(solution)/shard_map/all_to_all | solution.py:261
  39.4 0.0 collective-permute-done.4.recv_ref.sib_ref
  39.4 0.1 shard_map.105
  39.4 16.3 %all_to_all.21.r_ref = bf16[32,48,128]{2,1,0:T(8,128)(2,1)S(1)} all-to-all(bf16[32,48,128]{2,1,0:T(8,128)(2,1)S(1)} %shard_map.105), channel_id=1, replica_groups={{0,8,16,24,32,40,48,56,64,72,80,88,96,104,112,120,128,136,144,152,160,1..., dimensions={0} | all-to-all | bytes 786432 | tf_op jit(solution)/shard_map/all_to_all | solution.py:261
  55.7 0.1 shard_map.106
  55.8 3.4 %collective-permute-start.5 = (bf16[768,128]{1,0:T(8,128)(2,1)S(1)}, bf16[768,128]{1,0:T(8,128)(2,1)S(1)}, u32[]{:S(2)}, u32[]{:S(2)}) collective-permute-start(bf16[768,128]{1,0:T(8,128)(2,1)S(1)} %get-tuple-element.31.mine_ref), channel_id=1, source_target_pairs={{0,4},{4,0},{8,12},{12,8},{16,20},{20,16},{24,28},{28,24},{32,36},... | collective-permute-start | bytes 589832 | tf_op jit(solution)/shard_map/ppermute | solution.py:258
  59.2 5.7 %shard_map.107 = (f32[512,512]{1,0:T(8,128)S(1)}, f32[512,512]{1,0:T(8,128)S(1)}, f32[512,512]{1,0:T(8,128)S(1)}, f32[32,512]{1,0:T(8,128)S(1)}) custom-call(bf16[512,512]{1,0:T(8,128)(2,1)S(1)} %copy-done.2, bf16[512,512]{1,0:T(8,128)(2,1)S(1)} %copy-done.4, bf16[512,512]{1,0:T(8,128)(2,1)S(1)} %copy-done.5, bf16[512,512]{1,0:T(8,128)(2,1)S(1)} %copy-done.3, ...), custom_call_target="tpu_custom_call" | custom-call | flops 2000000000 | bytes 8000000 | tf_op jit(solution)/shard_map/pallas_call | solution.py:35
  64.9 1.0 copy-done.6
  65.9 1.0 copy-done.8
  66.8 0.0 collective-permute-done.5.other_ref
  66.8 2.6 %shard_map.108 = (bf16[512,512]{1,0:T(8,128)(2,1)}, bf16[32,512]{1,0:T(8,128)(2,1)S(1)}) custom-call(bf16[512,512]{1,0:T(8,128)(2,1)S(1)} %copy-done.2, bf16[512,512]{1,0:T(8,128)(2,1)S(1)} %copy-done.3, f32[512,128]{1,0:T(8,128)S(1)} %collective-permute-done.sib_ref, bf16[768,128]{1,0:T(8,128)(2,1)S(1)} %get-tuple-element.31.mine_ref, ...), custom_call_target="tpu_custom_call" | custom-call | flops 10000000 | bytes 1000000 | tf_op jit(solution)/shard_map/pallas_call | solution.py:35
  69.5 2.3 %collective-permute-start.8 = (bf16[32,512]{1,0:T(8,128)(2,1)S(1)}, bf16[32,512]{1,0:T(8,128)(2,1)S(1)}, u32[]{:S(2)}, u32[]{:S(2)}) collective-permute-start(bf16[32,512]{1,0:T(8,128)(2,1)S(1)} %get-tuple-element.36.g0), channel_id=1, source_target_pairs={{0,3},{1,0},{2,1},{3,2},{4,7},{5,4},{6,5},{7,6},{8,11},{9,8},{10,9... | collective-permute-start | bytes 98312 | tf_op jit(solution)/shard_map/ppermute | solution.py:264
  71.7 0.0 collective-permute-start.7
  71.7 0.6 collective-permute-start.6
  72.3 0.4 collective-permute-done.8.g3
  72.8 3.3 %collective-permute-done.7.g2 = bf16[32,512]{1,0:T(8,128)(2,1)S(1)} collective-permute-done((bf16[32,512]{1,0:T(8,128)(2,1)S(1)}, bf16[32,512]{1,0:T(8,128)(2,1)S(1)}, u32[]{:S(2)}, u32[]{:S(2)}) %collective-permute-start.7) | collective-permute-done | bytes 32800 | tf_op jit(solution)/shard_map/ppermute | solution.py:264
  76.1 0.0 collective-permute-done.6.g1
  76.1 0.5 shard_map.109
  76.6 1.5 %collective-permute-start.9 = (f32[512,128]{1,0:T(8,128)S(1)}, f32[512,128]{1,0:T(8,128)S(1)}, u32[]{:S(2)}, u32[]{:S(2)}) collective-permute-start(f32[512,128]{1,0:T(8,128)S(1)} %get-tuple-element.38), channel_id=1, source_target_pairs={{0,4},{4,0},{8,12},{12,8},{16,20},{20,16},{24,28},{28,24},{32,36},... | collective-permute-start | bytes 786440 | tf_op jit(solution)/shard_map/ppermute | solution.py:258
  78.1 1.2 collective-permute-done.9.recv_ref
  79.3 17.6 %all_to_all.22.r_ref = f32[32,24,128]{2,1,0:T(8,128)S(1)} all-to-all(f32[32,24,128]{2,1,0:T(8,128)S(1)} %shard_map.110), channel_id=1, replica_groups={{0,8,16,24,32,40,48,56,64,72,80,88,96,104,112,120,128,136,144,152,160,1..., dimensions={0} | all-to-all | bytes 786432 | tf_op jit(solution)/shard_map/all_to_all | solution.py:261
  97.0 0.1 shard_map.111
  97.0 15.2 %all_to_all.23 = f32[32,16,128]{2,1,0:T(8,128)S(1)} all-to-all(f32[32,16,128]{2,1,0:T(8,128)S(1)} %get-tuple-element.45), channel_id=1, replica_groups={{0,8,16,24,32,40,48,56,64,72,80,88,96,104,112,120,128,136,144,152,160,1..., dimensions={0} | all-to-all | bytes 524288 | tf_op jit(solution)/shard_map/all_to_all | solution.py:261
  112.2 3.7 %collective-permute-start.11 = (f32[512,128]{1,0:T(8,128)S(1)}, f32[512,128]{1,0:T(8,128)S(1)}, u32[]{:S(2)}, u32[]{:S(2)}) collective-permute-start(f32[512,128]{1,0:T(8,128)S(1)} %bitcast.5), channel_id=1, source_target_pairs={{0,4},{4,0},{8,12},{12,8},{16,20},{20,16},{24,28},{28,24},{32,36},... | collective-permute-start | bytes 786440 | tf_op jit(solution)/shard_map/ppermute | solution.py:258
  115.9 0.0 collective-permute-start.10
  115.9 1.3 %collective-permute-done.10.other_ref = f32[256,128]{1,0:T(8,128)S(1)} collective-permute-done((f32[256,128]{1,0:T(8,128)S(1)}, f32[256,128]{1,0:T(8,128)S(1)}, u32[]{:S(2)}, u32[]{:S(2)}) %collective-permute-start.10) | collective-permute-done | bytes 131104 | tf_op jit(solution)/shard_map/ppermute | solution.py:258
  117.3 1.2 copy-done.7
  118.5 1.2 copy-done.9
  119.7 2.5 %shard_map.112 = (bf16[512,512]{1,0:T(8,128)(2,1)}, bf16[512,512]{1,0:T(8,128)(2,1)}) custom-call(bf16[512,512]{1,0:T(8,128)(2,1)S(1)} %copy-done.4, bf16[512,512]{1,0:T(8,128)(2,1)S(1)} %copy-done.5, f32[1280,128]{1,0:T(8,128)S(1)} %collective-permute-done.4.recv_ref.sib_ref, f32[256,128]{1,0:T(8,128)S(1)} %get-tuple-element.40.mine_ref, ...), custom_call_target="tpu_custom_call" | custom-call | flops 10000000 | bytes 1000000 | tf_op jit(solution)/shard_map/pallas_call | solution.py:35
  122.2 0.0 collective-permute-done.11
  122.3 0.8 pad_maximum_fusion
  (22 shorter events, 0.1 us)
Async XLA Ops:
  0.6 1.2 copy-start
  1.9 0.9 copy-start.12
  2.8 8.8 %copy-start.2 = (bf16[512,512]{1,0:T(8,128)(2,1)S(1)}, bf16[512,512]{1,0:T(8,128)(2,1)}, u32[]{:S(2)}) copy-start(bf16[512,512]{1,0:T(8,128)(2,1)} %q_ref.5) | copy-start | bytes 1572868
  2.8 8.8 %copy-start.3 = (bf16[512,512]{1,0:T(8,128)(2,1)S(1)}, bf16[512,512]{1,0:T(8,128)(2,1)}, u32[]{:S(2)}) copy-start(bf16[512,512]{1,0:T(8,128)(2,1)} %g_ref.5) | copy-start | bytes 1572868
  3.3 5.9 %collective-permute-start.1 = (f32[32,512]{1,0:T(8,128)S(1)}, f32[32,512]{1,0:T(8,128)S(1)}, u32[]{:S(2)}, u32[]{:S(2)}) collective-permute-start(f32[32,512]{1,0:T(8,128)S(1)} %get-tuple-element.26), channel_id=1, source_target_pairs={{0,1},{1,2},{2,3},{3,0},{4,5},{5,6},{6,7},{7,4},{8,9},{9,10},{10,1... | collective-permute-start | bytes 196616 | tf_op jit(solution)/shard_map/ppermute | solution.py:264
  5.5 5.2 %collective-permute-start.2 = (f32[32,512]{1,0:T(8,128)S(1)}, f32[32,512]{1,0:T(8,128)S(1)}, u32[]{:S(2)}, u32[]{:S(2)}) collective-permute-start(f32[32,512]{1,0:T(8,128)S(1)} %get-tuple-element.27), channel_id=1, source_target_pairs={{0,2},{1,3},{2,0},{3,1},{4,6},{5,7},{6,4},{7,5},{8,10},{9,11},{10,... | collective-permute-start | bytes 196616 | tf_op jit(solution)/shard_map/ppermute | solution.py:264
  8.1 3.4 %copy-start.13 = (s32[8]{0:T(128)S(1)}, s32[8]{0:T(128)}, u32[]{:S(2)}) copy-start(s32[8]{0:T(128)} %reach_ref.5) | copy-start | bytes 100
  8.2 3.4 %collective-permute-start.3 = (f32[32,512]{1,0:T(8,128)S(1)}, f32[32,512]{1,0:T(8,128)S(1)}, u32[]{:S(2)}, u32[]{:S(2)}) collective-permute-start(f32[32,512]{1,0:T(8,128)S(1)} %get-tuple-element.28), channel_id=1, source_target_pairs={{0,3},{1,0},{2,1},{3,2},{4,7},{5,4},{6,5},{7,6},{8,11},{9,8},{10,9... | collective-permute-start | bytes 196616 | tf_op jit(solution)/shard_map/ppermute | solution.py:264
  11.6 4.3 %copy-start.4 = (bf16[512,512]{1,0:T(8,128)(2,1)S(1)}, bf16[512,512]{1,0:T(8,128)(2,1)}, u32[]{:S(2)}) copy-start(bf16[512,512]{1,0:T(8,128)(2,1)} %k_ref.5) | copy-start | bytes 1572868
  11.6 4.3 %copy-start.5 = (bf16[512,512]{1,0:T(8,128)(2,1)S(1)}, bf16[512,512]{1,0:T(8,128)(2,1)}, u32[]{:S(2)}) copy-start(bf16[512,512]{1,0:T(8,128)(2,1)} %v_ref.5) | copy-start | bytes 1572868
  13.8 3.3 %copy-start.10 = (f32[768,128]{1,0:T(8,128)}, f32[768,128]{1,0:T(8,128)S(1)}, u32[]{:S(2)}) copy-start(f32[768,128]{1,0:T(8,128)S(1)} %get-tuple-element.29.keep_ref) | copy-start | bytes 1179652
  13.8 25.6 %collective-permute-start.4 = (f32[1280,128]{1,0:T(8,128)}, f32[1280,128]{1,0:T(8,128)S(1)}, u32[]{:S(2)}, u32[]{:S(2)}) collective-permute-start(f32[1280,128]{1,0:T(8,128)} %get-tuple-element.30), channel_id=1, source_target_pairs={{0,4},{4,0},{8,12},{12,8},{16,20},{20,16},{24,28},{28,24},{32,36},... | collective-permute-start | bytes 1966088 | tf_op jit(solution)/shard_map/ppermute | solution.py:258
  17.1 1.6 %collective-permute-start = (f32[512,128]{1,0:T(8,128)S(1)}, f32[512,128]{1,0:T(8,128)S(1)}, u32[]{:S(2)}, u32[]{:S(2)}) collective-permute-start(f32[512,128]{1,0:T(8,128)S(1)} %shard_map.102), channel_id=1, source_target_pairs={{0,4},{4,0},{8,12},{12,8},{16,20},{20,16},{24,28},{28,24},{32,36},... | collective-permute-start | bytes 786440 | tf_op jit(solution)/shard_map/ppermute | solution.py:258
  17.2 22.2 %copy-start.11 = (f32[768,128]{1,0:T(8,128)S(1)}, f32[768,128]{1,0:T(8,128)}, u32[]{:S(2)}) copy-start(f32[768,128]{1,0:T(8,128)} %copy-done.10) | copy-start | bytes 1179652
  55.8 11.1 %collective-permute-start.5 = (bf16[768,128]{1,0:T(8,128)(2,1)S(1)}, bf16[768,128]{1,0:T(8,128)(2,1)S(1)}, u32[]{:S(2)}, u32[]{:S(2)}) collective-permute-start(bf16[768,128]{1,0:T(8,128)(2,1)S(1)} %get-tuple-element.31.mine_ref), channel_id=1, source_target_pairs={{0,4},{4,0},{8,12},{12,8},{16,20},{20,16},{24,28},{28,24},{32,36},... | collective-permute-start | bytes 589832 | tf_op jit(solution)/shard_map/ppermute | solution.py:258
  64.9 1.0 copy-start.6
  65.9 1.0 copy-start.8
  66.8 9.2 %copy-start.1 = (bf16[512,1024]{1,0:T(8,128)(2,1)S(1)}, bf16[512,1024]{1,0:T(8,128)(2,1)}, u32[]{:S(2)}) copy-start(bf16[512,1024]{1,0:T(8,128)(2,1)} %x_ref.3) | copy-start | bytes 3145732
  69.5 3.3 %collective-permute-start.8 = (bf16[32,512]{1,0:T(8,128)(2,1)S(1)}, bf16[32,512]{1,0:T(8,128)(2,1)S(1)}, u32[]{:S(2)}, u32[]{:S(2)}) collective-permute-start(bf16[32,512]{1,0:T(8,128)(2,1)S(1)} %get-tuple-element.36.g0), channel_id=1, source_target_pairs={{0,3},{1,0},{2,1},{3,2},{4,7},{5,4},{6,5},{7,6},{8,11},{9,8},{10,9... | collective-permute-start | bytes 98312 | tf_op jit(solution)/shard_map/ppermute | solution.py:264
  71.7 4.3 %collective-permute-start.7 = (bf16[32,512]{1,0:T(8,128)(2,1)S(1)}, bf16[32,512]{1,0:T(8,128)(2,1)S(1)}, u32[]{:S(2)}, u32[]{:S(2)}) collective-permute-start(bf16[32,512]{1,0:T(8,128)(2,1)S(1)} %get-tuple-element.36.g0), channel_id=1, source_target_pairs={{0,2},{1,3},{2,0},{3,1},{4,6},{5,7},{6,4},{7,5},{8,10},{9,11},{10,... | collective-permute-start | bytes 98312 | tf_op jit(solution)/shard_map/ppermute | solution.py:264
  71.7 4.3 %collective-permute-start.6 = (bf16[32,512]{1,0:T(8,128)(2,1)S(1)}, bf16[32,512]{1,0:T(8,128)(2,1)S(1)}, u32[]{:S(2)}, u32[]{:S(2)}) collective-permute-start(bf16[32,512]{1,0:T(8,128)(2,1)S(1)} %get-tuple-element.36.g0), channel_id=1, source_target_pairs={{0,1},{1,2},{2,3},{3,0},{4,5},{5,6},{6,7},{7,4},{8,9},{9,10},{10,1... | collective-permute-start | bytes 98312 | tf_op jit(solution)/shard_map/ppermute | solution.py:264
  76.6 2.7 %collective-permute-start.9 = (f32[512,128]{1,0:T(8,128)S(1)}, f32[512,128]{1,0:T(8,128)S(1)}, u32[]{:S(2)}, u32[]{:S(2)}) collective-permute-start(f32[512,128]{1,0:T(8,128)S(1)} %get-tuple-element.38), channel_id=1, source_target_pairs={{0,4},{4,0},{8,12},{12,8},{16,20},{20,16},{24,28},{28,24},{32,36},... | collective-permute-start | bytes 786440 | tf_op jit(solution)/shard_map/ppermute | solution.py:258
  112.2 10.0 %collective-permute-start.11 = (f32[512,128]{1,0:T(8,128)S(1)}, f32[512,128]{1,0:T(8,128)S(1)}, u32[]{:S(2)}, u32[]{:S(2)}) collective-permute-start(f32[512,128]{1,0:T(8,128)S(1)} %bitcast.5), channel_id=1, source_target_pairs={{0,4},{4,0},{8,12},{12,8},{16,20},{20,16},{24,28},{28,24},{32,36},... | collective-permute-start | bytes 786440 | tf_op jit(solution)/shard_map/ppermute | solution.py:258
  115.9 1.3 %collective-permute-start.10 = (f32[256,128]{1,0:T(8,128)S(1)}, f32[256,128]{1,0:T(8,128)S(1)}, u32[]{:S(2)}, u32[]{:S(2)}) collective-permute-start(f32[256,128]{1,0:T(8,128)S(1)} %get-tuple-element.40.mine_ref), channel_id=1, source_target_pairs={{0,4},{4,0},{8,12},{12,8},{16,20},{20,16},{24,28},{28,24},{32,36},... | collective-permute-start | bytes 393224 | tf_op jit(solution)/shard_map/ppermute | solution.py:258
  117.3 1.2 copy-start.7
  118.5 1.2 copy-start.9

commit v2 on v1

v2 whole, which is shorter than its diff:
```python
import functools
import math

import jax
import jax.numpy as jnp
from jax import lax
from jax.experimental import pallas as pl
from jax.experimental.pallas import tpu as pltpu
from jax.sharding import PartitionSpec as P

F32 = jnp.float32
BF16 = jnp.bfloat16
TOK = 512
DIM = 128
SPAN = 64
LEVELS = 8
CHIPS = 32
INV = 1.0 / DIM
VMEM_LIMIT = 24 * 1024 * 1024


def mm(left, right, left_dim=1, right_dim=0):
    return lax.dot_general(
        left, right, (((left_dim,), (right_dim,)), ((), ())), preferred_element_type=F32
    )


def aligned(index, size):
    return pl.ds(pl.multiple_of(index * size, size), size)


def call(
    body, out_shape, args, in_specs=None, out_specs=None, grid=(), scratch=(), cost=(10**7, 10**6), after=()
):
    whole = pl.BlockSpec(memory_space=pltpu.VMEM)
    many = isinstance(out_shape, (tuple, list))
    used = len(args)
    in_specs = list(in_specs or [whole] * used) + [pl.BlockSpec(memory_space=pl.ANY)] * len(after)
    args = (*args, *after)

    def kernel(*refs):
        body(*refs[:used], *refs[len(args) :])

    return pl.pallas_call(
        kernel,
        out_shape=out_shape,
        grid=grid,
        in_specs=in_specs,
        out_specs=out_specs or ([whole] * len(out_shape) if many else whole),
        scratch_shapes=list(scratch),
        compiler_params=pltpu.CompilerParams(vmem_limit_bytes=VMEM_LIMIT),
        cost_estimate=pl.CostEstimate(flops=cost[0], bytes_accessed=cost[1], transcendentals=0),
    )(*args)


def shape(dims, dtype):
    return jax.ShapeDtypeStruct(dims, dtype)


def logits_body(x_ref, w_ref, o0, o1, o2, o3, scr):
    head = lax.axis_index("head")
    scr[...] = mm(w_ref[...], x_ref[...], 0, 1)
    for step, out in enumerate((o0, o1, o2, o3)):
        out[...] = scr[aligned(lax.rem(head + step, 4), 32), :]


def state_body(k_ref, v_ref, o_ref):
    o_ref[...] = mm(k_ref[...], v_ref[...], 0, 0) * INV


def allowed_mask(reach_ref):
    lane = lax.broadcasted_iota(jnp.int32, (LEVELS, TOK), 1) // SPAN
    level = lax.broadcasted_iota(jnp.int32, (LEVELS, TOK), 0)
    reach = jnp.zeros((LEVELS, TOK), jnp.int32)
    for span in range(TOK // SPAN):
        reach = jnp.where(lane == span, reach_ref[span], reach)
    return (level <= reach).astype(F32)


def level_body(q_ref, g_ref, l0, l1, l2, l3, reach_ref, gates_ref, near_ref, keep_ref, send_ref, w_scr):
    core = lax.axis_index("seq") & 1
    gates = jax.nn.sigmoid((l0[...] + l1[...]) + (l2[...] + l3[...]))
    gates_ref[...] = gates
    allowed = allowed_mask(reach_ref)
    for head in range(4):
        w_scr[8 * head : 8 * head + 8, :] = gates[8 * head : 8 * head + 8, :] * allowed
    for slot in range(4):
        head = 2 * core + slot if slot < 2 else 2 * (1 - core) + slot - 2
        out = keep_ref if slot < 2 else send_ref
        query = q_ref[:, aligned(head, DIM)].astype(F32).T
        weight = w_scr[aligned(head, 8), :]
        gated = jnp.concatenate(
            [(weight[level : level + 1, :] * query).astype(BF16) for level in range(4, 8)], axis=0
        )
        grads = mm(gated, g_ref[:, aligned(head, DIM)]) * INV
        near_ref[aligned(head, DIM), :] = grads[:DIM]
        for level in range(3):
            row = 256 * level + DIM * (slot % 2)
            out[row : row + DIM, :] = grads[DIM * (level + 1) : DIM * (level + 2)]


def pack1_body(state_ref, sib_ref, keep_ref, recv_ref, o_ref):
    core = lax.axis_index("seq") & 1
    for chip in range(CHIPS):
        at = pl.ds(pl.multiple_of(256 * core + 8 * chip, 8), 8)
        rows = [state_ref[at, :] + sib_ref[at, :]]
        for level in range(3):
            row = 256 * level + 8 * chip
            rows.append(keep_ref[row : row + 8, :] + recv_ref[row : row + 8, :])
        o_ref[chip] = jnp.concatenate(rows, axis=0).astype(BF16)


def mid1_body(r_ref, o_ref):
    got = [r_ref[chip].astype(F32) for chip in range(CHIPS)]
    own = [part[0:8] for part in got]
    pairs = [own[chip] + own[chip ^ 1] for chip in range(CHIPS)]
    zero = jnp.zeros((8, DIM), F32)
    before = [zero]
    for group in range(7):
        before.append(before[-1] + (pairs[4 * group] + pairs[4 * group + 2]))
    after = [zero]
    for group in range(7, 0, -1):
        total = [got[4 * group + i][24:32] for i in range(4)]
        after.append(after[-1] + ((total[0] + total[1]) + (total[2] + total[3])))
    after = after[::-1]
    for chip in range(CHIPS):
        later = after[chip >> 2]
        if not chip & 2:
            later = later + (got[chip ^ 2][16:24] + got[chip ^ 3][16:24])
        if not chip & 1:
            later = later + got[chip ^ 1][8:16]
        rows = [
            own[chip ^ 1] if chip & 1 else zero,
            pairs[chip ^ 2] if chip & 2 else zero,
            before[chip >> 2],
            later,
        ]
        o_ref[chip] = jnp.concatenate(rows, axis=0).astype(BF16)


def mid2_body(r_ref, o_ref):
    for chip in range(0, CHIPS, 2):
        got = [r_ref[chip + i].astype(F32) for i in range(2)]
        for level in range(4):
            both = [part[8 * level : 8 * level + 8] for part in got]
            row = 256 * level + 8 * chip
            o_ref[row : row + 16, :] = jnp.concatenate(both, axis=0).astype(BF16)


def intra_body(q_ref, k_ref, v_ref, g_ref, gates_ref, reach_ref, dk_ref, dv_ref, dq_ref, rows_ref, p_scr, w_scr):
    weight = gates_ref[...] * allowed_mask(reach_ref)
    src = lax.broadcasted_iota(jnp.int32, (DIM, DIM), 0)
    dst = lax.broadcasted_iota(jnp.int32, (DIM, DIM), 1)
    same = (src // SPAN) == (dst // SPAN)
    mask0 = (same & (src <= dst)).astype(F32)
    mask1 = ((src // SPAN) < (dst // SPAN)).astype(F32)
    tiles = TOK // DIM
    key_t = k_ref[...].astype(F32).T.astype(BF16)
    row_parts = []
    for a in range(tiles):
        cols = slice(DIM * a, DIM * (a + 1))
        end = DIM * (a + 1)
        scores = mm(k_ref[:end, :], q_ref[cols, :], 1, 1) * INV
        probs = mm(v_ref[:end, :], g_ref[cols, :], 1, 1)
        prod = scores * probs
        sums = [None] * 4
        weights = []
        for b in range(a):
            level = (a ^ b).bit_length() + 1
            part = jnp.sum(prod[DIM * b : DIM * (b + 1)], axis=0, keepdims=True)
            sums[level] = part if sums[level] is None else sums[level] + part
            weights.append(jnp.broadcast_to(weight[level : level + 1, cols], (DIM, DIM)))
        diagonal = prod[DIM * a :]
        sums[0] = jnp.sum(diagonal * mask0, axis=0, keepdims=True)
        sums[1] = jnp.sum(diagonal * mask1, axis=0, keepdims=True)
        weights.append(weight[0:1, cols] * mask0 + weight[1:2, cols] * mask1)
        none = jnp.zeros((1, DIM), F32)
        sums = [none if part is None else part for part in sums]
        row_parts.append(jnp.concatenate(sums + [none] * 4, axis=0))
        pair = jnp.concatenate(weights, axis=0)
        p_scr[:end, cols] = (pair * scores).astype(BF16)
        weighted = (pair * probs).astype(BF16)
        w_scr[:end, cols] = weighted
        dq_ref[:, cols] = mm(key_t[:, :end], weighted) * INV
    rows_ref[...] = jnp.concatenate(row_parts, axis=1)
    for b in range(tiles):
        rows = slice(DIM * b, DIM * (b + 1))
        start = DIM * b
        dv_ref[rows, :] = mm(p_scr[rows, start:], g_ref[start:, :])
        dk_ref[rows, :] = mm(w_scr[rows, start:], q_ref[start:, :]) * INV


def cross_body(q_ref, g_ref, sib_ref, mine_ref, other_ref, gates_ref, reach_ref, rows_ref, dqt_ref, gl_ref):
    half = pl.program_id(0)
    core = lax.axis_index("seq") & 1
    allowed = allowed_mask(reach_ref)
    upper = (core == 1).astype(F32)
    outs = []
    for i in range(2):
        lanes = slice(DIM * i, DIM * (i + 1))
        rows = slice(DIM * i, DIM * (i + 1))
        levels = [(sib_ref[rows, :] * upper).astype(BF16)]
        for level in range(3):
            at = slice(256 * level + DIM * i, 256 * level + DIM * (i + 1))
            levels.append(jnp.where(half == core, mine_ref[at, :], other_ref[at, :]))
        projected = mm(jnp.concatenate(levels, axis=0), g_ref[:, lanes], 1, 1)
        query = q_ref[:, lanes].astype(F32).T
        gates = gates_ref[8 * i : 8 * i + 8, :]
        weight = gates * allowed
        total = None
        parts = []
        for level in range(4):
            term = projected[DIM * level : DIM * (level + 1)]
            weighted = weight[4 + level : 5 + level, :] * term
            total = weighted if total is None else total + weighted
            parts.append(jnp.sum(query * term, axis=0, keepdims=True))
        dqt_ref[rows, :] = total
        cross = jnp.concatenate([jnp.zeros((4, TOK), F32)] + parts, axis=0)
        grads = (rows_ref[8 * i : 8 * i + 8, :] + cross) * allowed
        outs.append(grads * gates * (1.0 - gates))
    gl_ref[...] = jnp.concatenate(outs, axis=0).astype(BF16)


def queries_body(in_ref, cross_ref, o_ref):
    o_ref[...] = (in_ref[...] + cross_ref[...]).T.astype(BF16)


def gradw_body(x_ref, g0, g1, g2, g3, keep_ref, send_ref, scr, full):
    head = lax.axis_index("head")
    core = lax.axis_index("seq") & 1
    for step, part in enumerate((g0, g1, g2, g3)):
        scr[aligned(lax.rem(head + 4 - step, 4), 32), :] = part[...]
    full[...] = mm(scr[...], x_ref[...]).T
    keep_ref[...] = full[aligned(core, 512), :]
    send_ref[...] = full[aligned(1 - core, 512), :]


def pack3_body(keep_ref, recv_ref, o_ref):
    for chip in range(CHIPS):
        rows = slice(16 * chip, 16 * chip + 16)
        o_ref[chip] = keep_ref[rows, :] + recv_ref[rows, :]


def mid3_body(scale, r_ref, o_ref):
    total = r_ref[0]
    for chip in range(1, CHIPS):
        total = total + r_ref[chip]
    total = (total * scale).astype(BF16)
    for chip in range(CHIPS):
        o_ref[chip] = total


def join_body(mine_ref, other_ref, o_ref):
    core = lax.axis_index("seq") & 1
    o_ref[aligned(core, 512), :] = mine_ref[...].astype(F32)
    o_ref[aligned(1 - core, 512), :] = other_ref[...].astype(F32)


def final_body(k_ref, v_ref, near_ref, mine_ref, other_ref, dki_ref, dvi_ref, dk_ref, dv_ref):
    half = pl.program_id(0) // 2
    core = lax.axis_index("seq") & 1
    later = jnp.where(half == core, mine_ref[...], other_ref[...]).astype(F32)
    lower = (core == 0).astype(F32)
    later = (later + near_ref[...] * lower).astype(BF16)
    dk_ref[...] = (dki_ref[...] + mm(v_ref[...], later, 1, 1)).astype(BF16)
    dv_ref[...] = (dvi_ref[...] + mm(k_ref[...], later, 1, 0)).astype(BF16)


def shards(layer_input, gate_weight, queries, key_vectors, value_vectors, grad_output, reach_level):
    seq_count = lax.axis_size("seq")
    groups = [[2 * chip + c for chip in range(CHIPS)] for c in range(2)]
    swap = [(d, d ^ 1) for d in range(seq_count)]

    def sibling(value):
        return lax.ppermute(value, "seq", swap)

    def exchange(value):
        return lax.all_to_all(value, "seq", 0, 0, axis_index_groups=groups)

    def rotate(value, step):
        return lax.ppermute(value, "head", [(h, (h + step) % 4) for h in range(4)])

    whole = pl.BlockSpec(memory_space=pltpu.VMEM)
    smem = pl.BlockSpec(memory_space=pltpu.SMEM)
    heads4 = pl.BlockSpec((TOK, DIM), lambda h: (0, h))
    rows4 = pl.BlockSpec((DIM, DIM), lambda h: (h, 0))
    rows4_tok = pl.BlockSpec((DIM, TOK), lambda h: (h, 0))
    gates4 = pl.BlockSpec((8, TOK), lambda h: (h, 0))

    parts = call(
        logits_body, [shape((32, TOK), F32)] * 4, (layer_input, gate_weight),
        scratch=[pltpu.VMEM((DIM, TOK), F32)],
    )
    logits = [parts[0]] + [rotate(parts[step], step) for step in range(1, 4)]
    states = call(
        state_body, shape((512, DIM), F32), (key_vectors, value_vectors),
        in_specs=[heads4, heads4], out_specs=rows4, grid=(4,), after=(parts[0],),
    )
    sib_state = sibling(states)

    gates, near, keep, send = call(
        level_body,
        [shape((32, TOK), F32), shape((512, DIM), F32), shape((768, DIM), F32), shape((768, DIM), F32)],
        (queries, grad_output, *logits, reach_level),
        in_specs=[whole] * 6 + [smem],
        scratch=[pltpu.VMEM((32, TOK), F32)],
        after=(states,),
    )

    slices = call(pack1_body, shape((CHIPS, 32, DIM), BF16), (states, sib_state, keep, sibling(send)))
    got1 = exchange(slices)
    near_in = sibling(near)
    dk_in, dv_in, dq_in, rows = call(
        intra_body,
        [shape((TOK, 512), F32), shape((TOK, 512), F32), shape((512, TOK), F32), shape((32, TOK), F32)],
        (queries, key_vectors, value_vectors, grad_output, gates, reach_level),
        in_specs=[heads4] * 4 + [gates4, smem],
        out_specs=[heads4, heads4, rows4_tok, gates4],
        grid=(4,),
        scratch=[pltpu.VMEM((TOK, TOK), BF16), pltpu.VMEM((TOK, TOK), BF16)],
        cost=(2 * 10**9, 8 * 10**6),
        after=(slices,),
    )
    got2 = exchange(call(mid1_body, shape((CHIPS, 32, DIM), BF16), (got1,), after=(rows,)))
    mine = call(mid2_body, shape((1024, DIM), BF16), (got2,))
    other = sibling(mine)

    heads2 = pl.BlockSpec((TOK, 256), lambda h: (0, h))
    tok16 = pl.BlockSpec((16, TOK), lambda h: (h, 0))
    all768 = pl.BlockSpec((768, DIM), lambda h: (0, 0))
    dq_cross, grad_logits = call(
        cross_body,
        [shape((512, TOK), F32), shape((32, TOK), BF16)],
        (queries, grad_output, sib_state, mine, other, gates, reach_level, rows),
        in_specs=[
            heads2, heads2, pl.BlockSpec((256, DIM), lambda h: (h, 0)), all768, all768, tok16, smem, tok16,
        ],
        out_specs=[pl.BlockSpec((256, TOK), lambda h: (h, 0)), tok16],
        grid=(2,),
    )

    gl = [grad_logits] + [rotate(grad_logits, step) for step in range(1, 4)]
    grad_queries = call(
        queries_body, shape((TOK, 512), BF16), (dq_in, dq_cross),
        in_specs=[rows4_tok, rows4_tok], out_specs=heads4, grid=(4,),
    )
    half4 = pl.BlockSpec((DIM, DIM), lambda h: (6 + h % 2, 0))
    grad_keys, grad_values = call(
        final_body,
        [shape((TOK, 512), BF16)] * 2,
        (key_vectors, value_vectors, near_in, mine, other, dk_in, dv_in),
        in_specs=[heads4, heads4, rows4, half4, half4, heads4, heads4],
        out_specs=[heads4, heads4],
        grid=(4,),
        after=(grad_logits,),
    )
    w_keep, w_send = call(
        gradw_body, [shape((512, DIM), F32)] * 2, (layer_input, *gl),
        scratch=[pltpu.VMEM((DIM, TOK), BF16), pltpu.VMEM((1024, DIM), F32)],
        after=(grad_queries, grad_keys),
    )
    got3 = exchange(call(pack3_body, shape((CHIPS, 16, DIM), F32), (w_keep, sibling(w_send))))
    scale = 1.0 / math.sqrt(TOK * seq_count)
    sums = call(functools.partial(mid3_body, scale), shape((CHIPS, 16, DIM), BF16), (got3,))
    w_half = exchange(sums).reshape(512, DIM)
    grad_weight = call(join_body, shape((1024, DIM), F32), (w_half, sibling(w_half)))
    return grad_queries, grad_keys, grad_values, grad_weight


def solution(mesh):
    placed = (
        P("seq", "head"),
        P("head", None),
        P("seq", "head"),
        P("seq", "head"),
        P("seq", "head"),
        P("seq", "head"),
        P("seq"),
    )
    return jax.shard_map(
        shards,
        mesh=mesh,
        in_specs=placed,
        out_specs=(P("seq", "head"), P("seq", "head"), P("seq", "head"), P("head", None)),
        check_vma=False,
    )
```

time: 123 us -> 109 us (0.89)
  blocking collectives: 69.7 us -> 44.7 us
  starting transfers between devices: 19.7 us -> 30.4 us
  Pallas kernels: 15.3 us -> 17.8 us
    all_to_all x4 -> x3, blocking collectives: 69.7 us -> 44.7 us  [exchange(): return lax.all_to_all(value, 'seq', 0, 0, axis_index_groups=groups)]
    all_to_all x0 -> x1, starting transfers between devices: none -> 11.1 us  [exchange(): return lax.all_to_all(value, 'seq', 0, 0, axis_index_groups=groups)]
    ppermute x6, waiting for transfers between devices: 6.09 us -> 1.13 us  [rotate(): return lax.ppermute(value, 'head', [(h, (h + step) % 4) for h in range(4)])]
    all_to_all x0 -> x1, waiting for transfers between devices: none -> 3.9 us  [exchange(): return lax.all_to_all(value, 'seq', 0, 0, axis_index_groups=groups)]
    pallas_call x11 -> x14, Pallas kernels: 15.3 us -> 17.8 us  [call(): pl.pallas_call(kernel, out_shape=out_shape, grid=grid, in_specs=in_specs,...]
    unnamed x28 -> x32, local copies, waits for them, and re-layouts: 6.6 us -> 5.89 us
  transfers between devices with their start and end apart: 12 -> 13, of which waited for: 7 -> 7; matrix products, arithmetic and copies ran while one was open for 0% -> 0% of each run, Pallas kernels for 8% -> 12%
where the time goes in v2:
time: 109 us
  blocking collectives  44.7 us (41%)
  starting transfers between devices  30.4 us (28%)
  Pallas kernels  17.8 us (16%)
  waiting for transfers between devices  9.25 us (8%)
  local copies, waits for them, and re-layouts  5.89 us (5%)
    all_to_all x3, blocking collectives, exchange(): return lax.all_to_all(value, 'seq', 0, 0, axis_index_groups=groups)  44.7 us
    pallas_call x14, Pallas kernels, call(): pl.pallas_call(kernel, out_shape=out_shape, grid=grid, in_specs=in_specs,...  17.8 us
    all_to_all x1, starting transfers between devices, exchange(): return lax.all_to_all(value, 'seq', 0, 0, axis_index_groups=groups)  11.1 us
    ppermute x6, starting transfers between devices, sibling(): return lax.ppermute(value, 'seq', swap)  9.85 us
    ppermute x6, starting transfers between devices, rotate(): return lax.ppermute(value, 'head', [(h, (h + step) % 4) for h in range(4)])  9.42 us
    unnamed x32, local copies, waits for them, and re-layouts  5.89 us
    ppermute x6, waiting for transfers between devices, sibling(): return lax.ppermute(value, 'seq', swap)  4.22 us
    all_to_all x1, waiting for transfers between devices, exchange(): return lax.all_to_all(value, 'seq', 0, 0, axis_index_groups=groups)  3.9 us
  transfers between devices with their start and end apart: 13, of which 7 were waited for; matrix products, arithmetic and copies ran while one was open for 0% of the time, Pallas kernels for 12%

profile of v2, /device:TPU:1, one launch (start us, length us, event | category | flops | bytes accessed | tf_op | source)
XLA Modules:
  0.0 108.8 jit_solution(4547314569938025330)
XLA Ops:
  0.6 0.0 copy-start
  0.6 1.2 %copy-done = bf16[512,1024]{1,0:T(8,128)(2,1)S(1)} copy-done((bf16[512,1024]{1,0:T(8,128)(2,1)S(1)}, bf16[512,1024]{1,0:T(8,128)(2,1)}, u32[]{:S(2)}) %copy-start) | copy-done | bytes 1048600
  1.9 0.9 copy-done.12
  2.8 0.5 shard_map.102
  3.3 2.2 %collective-permute-start = (f32[32,512]{1,0:T(8,128)S(1)}, f32[32,512]{1,0:T(8,128)S(1)}, u32[]{:S(2)}, u32[]{:S(2)}) collective-permute-start(f32[32,512]{1,0:T(8,128)S(1)} %get-tuple-element.23), channel_id=1, source_target_pairs={{0,1},{1,2},{2,3},{3,0},{4,5},{5,6},{6,7},{7,4},{8,9},{9,10},{10,1... | collective-permute-start | bytes 196616 | tf_op jit(solution)/shard_map/ppermute | solution.py:281
  5.5 2.6 %collective-permute-start.1 = (f32[32,512]{1,0:T(8,128)S(1)}, f32[32,512]{1,0:T(8,128)S(1)}, u32[]{:S(2)}, u32[]{:S(2)}) collective-permute-start(f32[32,512]{1,0:T(8,128)S(1)} %get-tuple-element.24), channel_id=1, source_target_pairs={{0,2},{1,3},{2,0},{3,1},{4,6},{5,7},{6,4},{7,5},{8,10},{9,11},{10,... | collective-permute-start | bytes 196616 | tf_op jit(solution)/shard_map/ppermute | solution.py:281
  8.1 1.1 collective-permute-start.2
  9.2 0.0 copy-start.13
  9.2 1.2 %shard_map.103.refs_7_.refs_0_ = f32[512,128]{1,0:T(8,128)S(1)} custom-call(bf16[512,512]{1,0:T(8,128)(2,1)S(1)} %copy-done.5, bf16[512,512]{1,0:T(8,128)(2,1)S(1)} %copy-done.6, f32[32,512]{1,0:T(8,128)S(1)} %get-tuple-element.22.refs_2_), custom_call_target="tpu_custom_call" | custom-call | flops 10000000 | bytes 1000000 | tf_op jit(solution)/shard_map/pallas_call | solution.py:44
  10.4 0.0 collective-permute-done.refs_3_
  10.4 0.3 collective-permute-done.1.refs_4_
  10.8 0.8 collective-permute-done.2.refs_5_
  11.6 1.3 %shard_map.104 = (f32[32,512]{1,0:T(8,128)S(1)}, f32[512,128]{1,0:T(8,128)S(1)}, f32[768,128]{1,0:T(8,128)S(1)}, f32[768,128]{1,0:T(8,128)S(1)}) custom-call(bf16[512,512]{1,0:T(8,128)(2,1)S(1)} %copy-done.3, bf16[512,512]{1,0:T(8,128)(2,1)S(1)} %copy-done.4, f32[32,512]{1,0:T(8,128)S(1)} %get-tuple-element.22.refs_2_, ...), custom_call_target="tpu_custom_call" | custom-call | flops 10000000 | bytes 1000000 | tf_op jit(solution)/shard_map/pallas_call | solution.py:44
  12.9 0.0 copy-start.14
  12.9 0.7 copy-done.14
  13.6 2.1 %collective-permute-start.4 = (f32[768,128]{1,0:T(8,128)S(1)}, f32[768,128]{1,0:T(8,128)S(1)}, u32[]{:S(2)}, u32[]{:S(2)}) collective-permute-start(f32[768,128]{1,0:T(8,128)S(1)} %get-tuple-element.28), channel_id=1, source_target_pairs={{0,4},{4,0},{8,12},{12,8},{16,20},{20,16},{24,28},{28,24},{32,36},... | collective-permute-start | bytes 1179656 | tf_op jit(solution)/shard_map/ppermute | solution.py:275
  15.7 1.7 %collective-permute-done.3.refs_1_.refs_2_ = f32[512,128]{1,0:T(8,128)S(1)} collective-permute-done((f32[512,128]{1,0:T(8,128)S(1)}, f32[512,128]{1,0:T(8,128)S(1)}, u32[]{:S(2)}, u32[]{:S(2)}) %collective-permute-start.3) | collective-permute-done | bytes 262176 | tf_op jit(solution)/shard_map/ppermute | solution.py:275
  17.5 0.8 shard_map.105.refs_6_
  18.2 11.1 %all-to-all-start = ((bf16[32,32,128]{2,1,0:T(8,128)(2,1)}), bf16[32,32,128]{2,1,0:T(8,128)(2,1)}, u32[]{:S(2)}, u32[]{:S(2)}) async-start(bf16[32,32,128]{2,1,0:T(8,128)(2,1)} %shard_map.105.refs_6_), calls=%async_computation | async-start | bytes 524288 | tf_op jit(solution)/shard_map/all_to_all | solution.py:278
  29.4 5.7 %shard_map.106 = (f32[512,512]{1,0:T(8,128)S(1)}, f32[512,512]{1,0:T(8,128)S(1)}, f32[512,512]{1,0:T(8,128)S(1)}, f32[32,512]{1,0:T(8,128)S(1)}) custom-call(bf16[512,512]{1,0:T(8,128)(2,1)S(1)} %copy-done.3, bf16[512,512]{1,0:T(8,128)(2,1)S(1)} %copy-done.5, bf16[512,512]{1,0:T(8,128)(2,1)S(1)} %copy-done.6, bf16[512,512]{1,0:T(8,128)(2,1)S(1)} %copy-done.4, ...), custom_call_target="tpu_custom_call" | custom-call | flops 2000000000 | bytes 8000000 | tf_op jit(solution)/shard_map/pallas_call | solution.py:44
  35.1 1.0 copy-done.7
  36.1 1.0 copy-done.9
  37.0 3.9 %all-to-all-done.refs_0_ = bf16[32,32,128]{2,1,0:T(8,128)(2,1)} async-done(((bf16[32,32,128]{2,1,0:T(8,128)(2,1)}), bf16[32,32,128]{2,1,0:T(8,128)(2,1)}, u32[]{:S(2)}, u32[]{:S(2)}) %all-to-all-start) | async-done | bytes 262176 | tf_op jit(solution)/shard_map/all_to_all | solution.py:278
  40.9 1.0 shard_map.107
  41.9 15.7 %all_to_all.20.refs_0_ = bf16[32,32,128]{2,1,0:T(8,128)(2,1)S(1)} all-to-all(bf16[32,32,128]{2,1,0:T(8,128)(2,1)S(1)} %shard_map.107), channel_id=1, replica_groups={{0,8,16,24,32,40,48,56,64,72,80,88,96,104,112,120,128,136,144,152,160,1..., dimensions={0} | all-to-all | bytes 524288 | tf_op jit(solution)/shard_map/all_to_all | solution.py:278
  57.7 3.0 %collective-permute-start.5 = (bf16[1024,128]{1,0:T(8,128)(2,1)S(1)}, bf16[1024,128]{1,0:T(8,128)(2,1)S(1)}, u32[]{:S(2)}, u32[]{:S(2)}) collective-permute-start(bf16[1024,128]{1,0:T(8,128)(2,1)S(1)} %shard_map.108.refs_3_), channel_id=1, source_target_pairs={{0,4},{4,0},{8,12},{12,8},{16,20},{20,16},{24,28},{28,24},{32,36},... | collective-permute-start | bytes 786440 | tf_op jit(solution)/shard_map/ppermute | solution.py:275
  60.7 0.8 collective-permute-start.6
  61.6 0.3 collective-permute-done.5.refs_4_
  61.9 1.7 %shard_map.109 = (f32[512,512]{1,0:T(8,128)S(1)}, bf16[32,512]{1,0:T(8,128)(2,1)S(1)}) custom-call(bf16[512,512]{1,0:T(8,128)(2,1)S(1)} %copy-done.3, bf16[512,512]{1,0:T(8,128)(2,1)S(1)} %copy-done.4, f32[512,128]{1,0:T(8,128)S(1)} %collective-permute-done.3.refs_1_.refs_2_, bf16[1024,128]{1,0:T(8,128)(2,1)S(1)} %shard_map.108.refs_3_, ...), custom_call_target="tpu_custom_call" | custom-call | flops 10000000 | bytes 1000000 | tf_op jit(solution)/shard_map/pallas_call | solution.py:44
  63.6 0.1 collective-permute-start.7
  63.7 3.4 %collective-permute-start.8 = (bf16[32,512]{1,0:T(8,128)(2,1)S(1)}, bf16[32,512]{1,0:T(8,128)(2,1)S(1)}, u32[]{:S(2)}, u32[]{:S(2)}) collective-permute-start(bf16[32,512]{1,0:T(8,128)(2,1)S(1)} %get-tuple-element.35.refs_7_.refs_1_), channel_id=1, source_target_pairs={{0,2},{1,3},{2,0},{3,1},{4,6},{5,7},{6,4},{7,5},{8,10},{9,11},{10,... | collective-permute-start | bytes 98312 | tf_op jit(solution)/shard_map/ppermute | solution.py:281
  67.1 1.7 %shard_map.110.refs_5_ = bf16[512,512]{1,0:T(8,128)(2,1)} custom-call(f32[512,512]{1,0:T(8,128)S(1)} %get-tuple-element.29.refs_0_, f32[512,512]{1,0:T(8,128)S(1)} %get-tuple-element.31.refs_1_), custom_call_target="tpu_custom_call" | custom-call | flops 10000000 | bytes 1000000 | tf_op jit(solution)/shard_map/pallas_call | solution.py:44
  68.8 0.0 collective-permute-done.6.refs_2_
  68.8 0.0 copy-start.1
  68.8 0.0 copy-start.2
  68.8 2.5 %shard_map.111 = (bf16[512,512]{1,0:T(8,128)(2,1)}, bf16[512,512]{1,0:T(8,128)(2,1)}) custom-call(bf16[512,512]{1,0:T(8,128)(2,1)S(1)} %copy-done.5, bf16[512,512]{1,0:T(8,128)(2,1)S(1)} %copy-done.6, f32[512,128]{1,0:T(8,128)S(1)} %collective-permute-done.6.refs_2_, bf16[1024,128]{1,0:T(8,128)(2,1)S(1)} %shard_map.108.refs_3_, ...), custom_call_target="tpu_custom_call" | custom-call | flops 10000000 | bytes 1000000 | tf_op jit(solution)/shard_map/pallas_call | solution.py:44
  71.4 0.0 collective-permute-done.7.refs_2_
  71.4 0.0 collective-permute-done.9.refs_4_
  71.4 0.0 copy-start.11
  71.4 1.0 copy-done.11
  72.5 0.5 shard_map.112
  73.0 1.1 %collective-permute-start.10 = (f32[512,128]{1,0:T(8,128)S(1)}, f32[512,128]{1,0:T(8,128)S(1)}, u32[]{:S(2)}, u32[]{:S(2)}) collective-permute-start(f32[512,128]{1,0:T(8,128)S(1)} %get-tuple-element.39), channel_id=1, source_target_pairs={{0,4},{4,0},{8,12},{12,8},{16,20},{20,16},{24,28},{28,24},{32,36},... | collective-permute-start | bytes 786440 | tf_op jit(solution)/shard_map/ppermute | solution.py:275
  74.1 1.2 %collective-permute-done.10.refs_1_ = f32[512,128]{1,0:T(8,128)S(1)} collective-permute-done((f32[512,128]{1,0:T(8,128)S(1)}, f32[512,128]{1,0:T(8,128)S(1)}, u32[]{:S(2)}, u32[]{:S(2)}) %collective-permute-start.10) | collective-permute-done | bytes 262176 | tf_op jit(solution)/shard_map/ppermute | solution.py:275
  75.3 15.2 %all_to_all.21.refs_0_ = f32[32,16,128]{2,1,0:T(8,128)S(1)} all-to-all(f32[32,16,128]{2,1,0:T(8,128)S(1)} %shard_map.113), channel_id=1, replica_groups={{0,8,16,24,32,40,48,56,64,72,80,88,96,104,112,120,128,136,144,152,160,1..., dimensions={0} | all-to-all | bytes 524288 | tf_op jit(solution)/shard_map/all_to_all | solution.py:278
  90.5 13.7 %all_to_all.22 = bf16[32,16,128]{2,1,0:T(8,128)(2,1)S(1)} all-to-all(bf16[32,16,128]{2,1,0:T(8,128)(2,1)S(1)} %shard_map.114), channel_id=1, replica_groups={{0,8,16,24,32,40,48,56,64,72,80,88,96,104,112,120,128,136,144,152,160,1..., dimensions={0} | all-to-all | bytes 262144 | tf_op jit(solution)/shard_map/all_to_all | solution.py:278
  104.3 2.7 %collective-permute-start.11 = (bf16[512,128]{1,0:T(8,128)(2,1)S(1)}, bf16[512,128]{1,0:T(8,128)(2,1)S(1)}, u32[]{:S(2)}, u32[]{:S(2)}) collective-permute-start(bf16[512,128]{1,0:T(8,128)(2,1)S(1)} %bitcast.1), channel_id=1, source_target_pairs={{0,4},{4,0},{8,12},{12,8},{16,20},{20,16},{24,28},{28,24},{32,36},... | collective-permute-start | bytes 393224 | tf_op jit(solution)/shard_map/ppermute | solution.py:275
  107.0 1.0 collective-permute-done.11.refs_1_
  108.0 0.8 shard_map.115
  (27 shorter events, 0.2 us)
Async XLA Ops:
  0.6 1.2 %copy-start = (bf16[512,1024]{1,0:T(8,128)(2,1)S(1)}, bf16[512,1024]{1,0:T(8,128)(2,1)}, u32[]{:S(2)}) copy-start(bf16[512,1024]{1,0:T(8,128)(2,1)} %refs_0_.13) | copy-start | bytes 3145732
  1.9 0.9 copy-start.12
  2.8 6.4 %copy-start.5 = (bf16[512,512]{1,0:T(8,128)(2,1)S(1)}, bf16[512,512]{1,0:T(8,128)(2,1)}, u32[]{:S(2)}) copy-start(bf16[512,512]{1,0:T(8,128)(2,1)} %refs_0_.12) | copy-start | bytes 1572868
  2.8 6.4 %copy-start.6 = (bf16[512,512]{1,0:T(8,128)(2,1)S(1)}, bf16[512,512]{1,0:T(8,128)(2,1)}, u32[]{:S(2)}) copy-start(bf16[512,512]{1,0:T(8,128)(2,1)} %refs_1_.11) | copy-start | bytes 1572868
  3.3 7.1 %collective-permute-start = (f32[32,512]{1,0:T(8,128)S(1)}, f32[32,512]{1,0:T(8,128)S(1)}, u32[]{:S(2)}, u32[]{:S(2)}) collective-permute-start(f32[32,512]{1,0:T(8,128)S(1)} %get-tuple-element.23), channel_id=1, source_target_pairs={{0,1},{1,2},{2,3},{3,0},{4,5},{5,6},{6,7},{7,4},{8,9},{9,10},{10,1... | collective-permute-start | bytes 196616 | tf_op jit(solution)/shard_map/ppermute | solution.py:281
  5.5 5.2 %collective-permute-start.1 = (f32[32,512]{1,0:T(8,128)S(1)}, f32[32,512]{1,0:T(8,128)S(1)}, u32[]{:S(2)}, u32[]{:S(2)}) collective-permute-start(f32[32,512]{1,0:T(8,128)S(1)} %get-tuple-element.24), channel_id=1, source_target_pairs={{0,2},{1,3},{2,0},{3,1},{4,6},{5,7},{6,4},{7,5},{8,10},{9,11},{10,... | collective-permute-start | bytes 196616 | tf_op jit(solution)/shard_map/ppermute | solution.py:281
  8.1 3.4 %collective-permute-start.2 = (f32[32,512]{1,0:T(8,128)S(1)}, f32[32,512]{1,0:T(8,128)S(1)}, u32[]{:S(2)}, u32[]{:S(2)}) collective-permute-start(f32[32,512]{1,0:T(8,128)S(1)} %get-tuple-element.25), channel_id=1, source_target_pairs={{0,3},{1,0},{2,1},{3,2},{4,7},{5,4},{6,5},{7,6},{8,11},{9,8},{10,9... | collective-permute-start | bytes 196616 | tf_op jit(solution)/shard_map/ppermute | solution.py:281
  9.2 2.3 %copy-start.3 = (bf16[512,512]{1,0:T(8,128)(2,1)S(1)}, bf16[512,512]{1,0:T(8,128)(2,1)}, u32[]{:S(2)}) copy-start(bf16[512,512]{1,0:T(8,128)(2,1)} %refs_0_.11) | copy-start | bytes 1572868
  9.2 2.3 %copy-start.4 = (bf16[512,512]{1,0:T(8,128)(2,1)S(1)}, bf16[512,512]{1,0:T(8,128)(2,1)}, u32[]{:S(2)}) copy-start(bf16[512,512]{1,0:T(8,128)(2,1)} %refs_1_.10) | copy-start | bytes 1572868
  9.2 2.3 %copy-start.13 = (s32[8]{0:T(128)S(1)}, s32[8]{0:T(128)}, u32[]{:S(2)}) copy-start(s32[8]{0:T(128)} %refs_6_.3) | copy-start | bytes 100
  12.9 0.7 copy-start.14
  13.6 3.9 %collective-permute-start.4 = (f32[768,128]{1,0:T(8,128)S(1)}, f32[768,128]{1,0:T(8,128)S(1)}, u32[]{:S(2)}, u32[]{:S(2)}) collective-permute-start(f32[768,128]{1,0:T(8,128)S(1)} %get-tuple-element.28), channel_id=1, source_target_pairs={{0,4},{4,0},{8,12},{12,8},{16,20},{20,16},{24,28},{28,24},{32,36},... | collective-permute-start | bytes 1179656 | tf_op jit(solution)/shard_map/ppermute | solution.py:275
  15.7 1.7 %collective-permute-start.3 = (f32[512,128]{1,0:T(8,128)S(1)}, f32[512,128]{1,0:T(8,128)S(1)}, u32[]{:S(2)}, u32[]{:S(2)}) collective-permute-start(f32[512,128]{1,0:T(8,128)S(1)} %shard_map.103.refs_7_.refs_0_), channel_id=1, source_target_pairs={{0,4},{4,0},{8,12},{12,8},{16,20},{20,16},{24,28},{28,24},{32,36},... | collective-permute-start | bytes 786440 | tf_op jit(solution)/shard_map/ppermute | solution.py:275
  18.2 22.7 %all-to-all-start = ((bf16[32,32,128]{2,1,0:T(8,128)(2,1)}), bf16[32,32,128]{2,1,0:T(8,128)(2,1)}, u32[]{:S(2)}, u32[]{:S(2)}) async-start(bf16[32,32,128]{2,1,0:T(8,128)(2,1)} %shard_map.105.refs_6_), calls=%async_computation | async-start | bytes 524288 | tf_op jit(solution)/shard_map/all_to_all | solution.py:278
  35.1 1.0 copy-start.7
  36.1 1.0 copy-start.9
  57.7 3.1 %copy-start.15 = (f32[512,128]{1,0:T(8,128)S(1)}, f32[512,128]{1,0:T(8,128)}, u32[]{:S(2)}) copy-start(f32[512,128]{1,0:T(8,128)} %copy-done.14) | copy-start | bytes 786436
  57.7 4.2 %collective-permute-start.5 = (bf16[1024,128]{1,0:T(8,128)(2,1)S(1)}, bf16[1024,128]{1,0:T(8,128)(2,1)S(1)}, u32[]{:S(2)}, u32[]{:S(2)}) collective-permute-start(bf16[1024,128]{1,0:T(8,128)(2,1)S(1)} %shard_map.108.refs_3_), channel_id=1, source_target_pairs={{0,4},{4,0},{8,12},{12,8},{16,20},{20,16},{24,28},{28,24},{32,36},... | collective-permute-start | bytes 786440 | tf_op jit(solution)/shard_map/ppermute | solution.py:275
  60.7 8.1 %collective-permute-start.6 = (f32[512,128]{1,0:T(8,128)S(1)}, f32[512,128]{1,0:T(8,128)S(1)}, u32[]{:S(2)}, u32[]{:S(2)}) collective-permute-start(f32[512,128]{1,0:T(8,128)S(1)} %copy-done.15), channel_id=1, source_target_pairs={{0,4},{4,0},{8,12},{12,8},{16,20},{20,16},{24,28},{28,24},{32,36},... | collective-permute-start | bytes 786440 | tf_op jit(solution)/shard_map/ppermute | solution.py:275
  63.6 7.8 %collective-permute-start.7 = (bf16[32,512]{1,0:T(8,128)(2,1)S(1)}, bf16[32,512]{1,0:T(8,128)(2,1)S(1)}, u32[]{:S(2)}, u32[]{:S(2)}) collective-permute-start(bf16[32,512]{1,0:T(8,128)(2,1)S(1)} %get-tuple-element.35.refs_7_.refs_1_), channel_id=1, source_target_pairs={{0,1},{1,2},{2,3},{3,0},{4,5},{5,6},{6,7},{7,4},{8,9},{9,10},{10,1... | collective-permute-start | bytes 98312 | tf_op jit(solution)/shard_map/ppermute | solution.py:281
  63.7 7.7 %collective-permute-start.8 = (bf16[32,512]{1,0:T(8,128)(2,1)S(1)}, bf16[32,512]{1,0:T(8,128)(2,1)S(1)}, u32[]{:S(2)}, u32[]{:S(2)}) collective-permute-start(bf16[32,512]{1,0:T(8,128)(2,1)S(1)} %get-tuple-element.35.refs_7_.refs_1_), channel_id=1, source_target_pairs={{0,2},{1,3},{2,0},{3,1},{4,6},{5,7},{6,4},{7,5},{8,10},{9,11},{10,... | collective-permute-start | bytes 98312 | tf_op jit(solution)/shard_map/ppermute | solution.py:281
  67.1 4.3 %collective-permute-start.9 = (bf16[32,512]{1,0:T(8,128)(2,1)S(1)}, bf16[32,512]{1,0:T(8,128)(2,1)S(1)}, u32[]{:S(2)}, u32[]{:S(2)}) collective-permute-start(bf16[32,512]{1,0:T(8,128)(2,1)S(1)} %get-tuple-element.35.refs_7_.refs_1_), channel_id=1, source_target_pairs={{0,3},{1,0},{2,1},{3,2},{4,7},{5,4},{6,5},{7,6},{8,11},{9,8},{10,9... | collective-permute-start | bytes 98312 | tf_op jit(solution)/shard_map/ppermute | solution.py:281
  67.1 1.7 %copy-start.8 = (f32[512,512]{1,0:T(8,128)S(1)}, f32[512,512]{1,0:T(8,128)}, u32[]{:S(2)}) copy-start(f32[512,512]{1,0:T(8,128)} %copy-done.7) | copy-start | bytes 3145732
  67.1 1.7 %copy-start.10 = (f32[512,512]{1,0:T(8,128)S(1)}, f32[512,512]{1,0:T(8,128)}, u32[]{:S(2)}) copy-start(f32[512,512]{1,0:T(8,128)} %copy-done.9) | copy-start | bytes 3145732
  68.8 2.6 %copy-start.1 = (bf16[512,1024]{1,0:T(8,128)(2,1)S(1)}, bf16[512,1024]{1,0:T(8,128)(2,1)}, u32[]{:S(2)}) copy-start(bf16[512,1024]{1,0:T(8,128)(2,1)} %refs_0_.13) | copy-start | bytes 3145732
  68.8 2.6 %copy-start.2 = (bf16[512,512]{1,0:T(8,128)(2,1)S(1)}, bf16[512,512]{1,0:T(8,128)(2,1)}, u32[]{:S(2)}) copy-start(bf16[512,512]{1,0:T(8,128)(2,1)} %shard_map.110.refs_5_) | copy-start | bytes 1572868
  71.4 1.0 copy-start.11
  73.0 2.3 %collective-permute-start.10 = (f32[512,128]{1,0:T(8,128)S(1)}, f32[512,128]{1,0:T(8,128)S(1)}, u32[]{:S(2)}, u32[]{:S(2)}) collective-permute-start(f32[512,128]{1,0:T(8,128)S(1)} %get-tuple-element.39), channel_id=1, source_target_pairs={{0,4},{4,0},{8,12},{12,8},{16,20},{20,16},{24,28},{28,24},{32,36},... | collective-permute-start | bytes 786440 | tf_op jit(solution)/shard_map/ppermute | solution.py:275
  104.3 3.7 %collective-permute-start.11 = (bf16[512,128]{1,0:T(8,128)(2,1)S(1)}, bf16[512,128]{1,0:T(8,128)(2,1)S(1)}, u32[]{:S(2)}, u32[]{:S(2)}) collective-permute-start(bf16[512,128]{1,0:T(8,128)(2,1)S(1)} %bitcast.1), channel_id=1, source_target_pairs={{0,4},{4,0},{8,12},{12,8},{16,20},{20,16},{24,28},{28,24},{32,36},... | collective-permute-start | bytes 393224 | tf_op jit(solution)/shard_map/ppermute | solution.py:275

commit v3 on v2

v3 whole, which is shorter than its diff:
```python
import functools
import math

import jax
import jax.numpy as jnp
from jax import lax
from jax.experimental import pallas as pl
from jax.experimental.pallas import tpu as pltpu
from jax.sharding import PartitionSpec as P

F32 = jnp.float32
BF16 = jnp.bfloat16
TOK = 512
DIM = 128
SPAN = 64
LEVELS = 8
CHIPS = 32
INV = 1.0 / DIM
VMEM_LIMIT = 24 * 1024 * 1024
VMEM_ALL = 60 * 1024 * 1024


def mm(left, right, left_dim=1, right_dim=0):
    return lax.dot_general(
        left, right, (((left_dim,), (right_dim,)), ((), ())), preferred_element_type=F32
    )


def aligned(index, size):
    return pl.ds(pl.multiple_of(index * size, size), size)


def call(
    body, out_shape, args, in_specs=None, out_specs=None, grid=(), scratch=(), cost=(10**7, 10**6), after=(),
    limit=VMEM_LIMIT,
):
    whole = pl.BlockSpec(memory_space=pltpu.VMEM)
    many = isinstance(out_shape, (tuple, list))
    used = len(args)
    in_specs = list(in_specs or [whole] * used) + [pl.BlockSpec(memory_space=pl.ANY)] * len(after)
    args = (*args, *after)

    def kernel(*refs):
        body(*refs[:used], *refs[len(args) :])

    return pl.pallas_call(
        kernel,
        out_shape=out_shape,
        grid=grid,
        in_specs=in_specs,
        out_specs=out_specs or ([whole] * len(out_shape) if many else whole),
        scratch_shapes=list(scratch),
        compiler_params=pltpu.CompilerParams(vmem_limit_bytes=limit),
        cost_estimate=pl.CostEstimate(flops=cost[0], bytes_accessed=cost[1], transcendentals=0),
    )(*args)


def shape(dims, dtype):
    return jax.ShapeDtypeStruct(dims, dtype)


def logits_body(x_ref, w_ref, o0, o1, o2, o3, scr):
    head = lax.axis_index("head")
    scr[...] = mm(w_ref[...], x_ref[...], 0, 1)
    for step, out in enumerate((o0, o1, o2, o3)):
        out[...] = scr[aligned(lax.rem(head + step, 4), 32), :]


def state_body(q_ref, k_ref, v_ref, reach_ref, state_ref, qt_ref, allowed_ref):
    state_ref[...] = mm(k_ref[...], v_ref[...], 0, 0) * INV
    qt_ref[...] = q_ref[...].astype(F32).T.astype(BF16)
    lane = lax.broadcasted_iota(jnp.int32, (LEVELS, TOK), 1) // SPAN
    level = lax.broadcasted_iota(jnp.int32, (LEVELS, TOK), 0)
    reach = jnp.zeros((LEVELS, TOK), jnp.int32)
    for span in range(TOK // SPAN):
        reach = jnp.where(lane == span, reach_ref[span], reach)
    allowed_ref[...] = (level <= reach).astype(F32)


def level_grads(qt_ref, g_ref, gates_ref, allowed, head, levels):
    lanes = aligned(head, DIM)
    query = qt_ref[lanes, :].astype(F32)
    weight = gates_ref[aligned(head, 8), :] * allowed
    gated = jnp.concatenate([(weight[level : level + 1, :] * query).astype(BF16) for level in levels], axis=0)
    return mm(gated, g_ref[:, lanes]) * INV


def level_send_body(qt_ref, g_ref, l0, l1, l2, l3, allowed_ref, gates_ref, send_ref):
    core = lax.axis_index("seq") & 1
    gates_ref[...] = jax.nn.sigmoid((l0[...] + l1[...]) + (l2[...] + l3[...]))
    allowed = allowed_ref[...]
    for slot in range(2):
        grads = level_grads(qt_ref, g_ref, gates_ref, allowed, 2 * (1 - core) + slot, range(5, 8))
        for level in range(3):
            row = 256 * level + DIM * slot
            send_ref[row : row + DIM, :] = grads[DIM * level : DIM * (level + 1)].astype(BF16)


def level_keep_body(qt_ref, g_ref, gates_ref, allowed_ref, near_ref, keep_ref):
    core = lax.axis_index("seq") & 1
    allowed = allowed_ref[...]
    for slot in range(2):
        head = 2 * core + slot
        grads = level_grads(qt_ref, g_ref, gates_ref, allowed, head, range(4, 8))
        near_ref[aligned(head, DIM), :] = grads[:DIM].astype(BF16)
        for level in range(3):
            row = 256 * level + DIM * slot
            keep_ref[row : row + DIM, :] = grads[DIM * (level + 1) : DIM * (level + 2)]
        head = 2 * (1 - core) + slot
        near_ref[aligned(head, DIM), :] = level_grads(qt_ref, g_ref, gates_ref, allowed, head, (4,)).astype(BF16)


def pack1_body(state_ref, sib_ref, keep_ref, recv_ref, o_ref, scr):
    core = lax.axis_index("seq") & 1
    half = aligned(core, 256)
    scr[0:256, :] = state_ref[half, :] + sib_ref[half, :]
    scr[256:1024, :] = keep_ref[...] + recv_ref[...].astype(F32)
    for chip in range(CHIPS):
        rows = [scr[256 * level + 8 * chip : 256 * level + 8 * chip + 8, :] for level in range(4)]
        o_ref[chip] = jnp.concatenate(rows, axis=0).astype(BF16)


def mid1_body(r_ref, o_ref):
    got = [r_ref[chip].astype(F32) for chip in range(CHIPS)]
    own = [part[0:8] for part in got]
    pairs = [own[chip] + own[chip ^ 1] for chip in range(CHIPS)]
    zero = jnp.zeros((8, DIM), F32)
    before = [zero]
    for group in range(7):
        before.append(before[-1] + (pairs[4 * group] + pairs[4 * group + 2]))
    after = [zero]
    for group in range(7, 0, -1):
        total = [got[4 * group + i][24:32] for i in range(4)]
        after.append(after[-1] + ((total[0] + total[1]) + (total[2] + total[3])))
    after = after[::-1]
    for chip in range(CHIPS):
        later = after[chip >> 2]
        if not chip & 2:
            later = later + (got[chip ^ 2][16:24] + got[chip ^ 3][16:24])
        if not chip & 1:
            later = later + got[chip ^ 1][8:16]
        rows = [
            own[chip ^ 1] if chip & 1 else zero,
            pairs[chip ^ 2] if chip & 2 else zero,
            before[chip >> 2],
            later,
        ]
        o_ref[chip] = jnp.concatenate(rows, axis=0).astype(BF16)


def mid2_body(r_ref, near_ref, o_ref):
    for chip in range(0, CHIPS, 2):
        got = [r_ref[chip + i].astype(F32) for i in range(2)]
        for level in range(4):
            both = [part[8 * level : 8 * level + 8] for part in got]
            row = 256 * level + 8 * chip
            o_ref[row : row + 16, :] = jnp.concatenate(both, axis=0).astype(BF16)
    o_ref[1024:1536, :] = near_ref[...]


def causal_masks():
    src = lax.broadcasted_iota(jnp.int32, (DIM, DIM), 0)
    dst = lax.broadcasted_iota(jnp.int32, (DIM, DIM), 1)
    same = (src // SPAN) == (dst // SPAN)
    return (same & (src <= dst)).astype(F32), ((src // SPAN) < (dst // SPAN)).astype(F32)


def intra_body(
    q_ref, k_ref, v_ref, g_ref, sib_ref, gates_ref, allowed_ref, dk_ref, dv_ref, dq_ref, rows_ref, p_scr, w_scr
):
    core = lax.axis_index("seq") & 1
    weight = gates_ref[...] * allowed_ref[...]
    mask0, mask1 = causal_masks()
    tiles = TOK // DIM
    key_t = k_ref[...].astype(F32).T.astype(BF16)
    query_t = q_ref[...].astype(F32).T
    near = (sib_ref[...] * (core == 1).astype(F32)).astype(BF16)
    projected = mm(near, g_ref[...], 1, 1)
    near_row = jnp.sum(query_t * projected, axis=0, keepdims=True)
    none = jnp.zeros((1, DIM), F32)
    for a in range(tiles):
        cols = slice(DIM * a, DIM * (a + 1))
        end = DIM * (a + 1)
        scores = mm(k_ref[:end, :], q_ref[cols, :], 1, 1) * INV
        probs = mm(v_ref[:end, :], g_ref[cols, :], 1, 1)
        prod = scores * probs
        sums = [none] * 8
        sums[4] = near_row[:, cols]
        weights = []
        for b in range(a):
            level = (a ^ b).bit_length() + 1
            sums[level] = sums[level] + jnp.sum(prod[DIM * b : DIM * (b + 1)], axis=0, keepdims=True)
            weights.append(jnp.broadcast_to(weight[level : level + 1, cols], (DIM, DIM)))
        sums[0] = jnp.sum(prod[DIM * a :] * mask0, axis=0, keepdims=True)
        sums[1] = jnp.sum(prod[DIM * a :] * mask1, axis=0, keepdims=True)
        weights.append(weight[0:1, cols] * mask0 + weight[1:2, cols] * mask1)
        rows_ref[:, cols] = jnp.concatenate(sums, axis=0)
        pair = jnp.concatenate(weights, axis=0)
        p_scr[:end, cols] = (pair * scores).astype(BF16)
        weighted = (pair * probs).astype(BF16)
        w_scr[:end, cols] = weighted
        dq_ref[:, cols] = mm(key_t[:, :end], weighted) * INV + weight[4:5, cols] * projected[:, cols]
    for b in range(tiles):
        rows = slice(DIM * b, DIM * (b + 1))
        start = DIM * b
        dv_ref[rows, :] = mm(p_scr[rows, start:], g_ref[start:, :])
        dk_ref[rows, :] = mm(w_scr[rows, start:], q_ref[start:, :]) * INV


def far_projection(head, g_ref, mine_ref, other_ref):
    core = lax.axis_index("seq") & 1
    states = []
    for level in range(3):
        at = slice(256 * level + DIM * (head % 2), 256 * level + DIM * (head % 2 + 1))
        states.append(jnp.where(head // 2 == core, mine_ref[at, :], other_ref[at, :]))
    projected = mm(jnp.concatenate(states, axis=0), g_ref[:, DIM * head : DIM * (head + 1)], 1, 1)
    return [projected[DIM * level : DIM * (level + 1)] for level in range(3)]


def cross_body(qt_ref, g_ref, mine_ref, other_ref, gates_ref, allowed_ref, rows_ref, gl_ref):
    allowed = allowed_ref[...]
    outs = []
    for head in range(4):
        query = qt_ref[DIM * head : DIM * (head + 1), :].astype(F32)
        parts = [jnp.zeros((5, TOK), F32)]
        for term in far_projection(head, g_ref, mine_ref, other_ref):
            parts.append(jnp.sum(query * term, axis=0, keepdims=True))
        gates = gates_ref[8 * head : 8 * head + 8, :]
        grads = (rows_ref[8 * head : 8 * head + 8, :] + jnp.concatenate(parts, axis=0)) * allowed
        outs.append(grads * gates * (1.0 - gates))
    gl_ref[...] = jnp.concatenate(outs, axis=0).astype(BF16)


def queries_body(g_ref, mine_ref, other_ref, gates_ref, allowed_ref, in_ref, dq_hbm, token_ref, dq_ref, sems):
    allowed = allowed_ref[...]
    copies = []
    for head in range(4):
        lanes = slice(DIM * head, DIM * (head + 1))
        weight = gates_ref[8 * head : 8 * head + 8, :] * allowed
        total = in_ref[lanes, :]
        for level, term in enumerate(far_projection(head, g_ref, mine_ref, other_ref)):
            total = total + weight[5 + level : 6 + level, :] * term
        dq_ref[:, lanes] = total.T.astype(BF16)
        copies.append(pltpu.make_async_copy(dq_ref.at[:, lanes], dq_hbm.at[:, lanes], sems.at[head]))
        copies[-1].start()
    token_ref[...] = jnp.zeros_like(token_ref)
    for copy in copies:
        copy.wait()


def gradw_body(x_ref, g0, g1, g2, g3, keep_ref, send_ref, scr, full):
    head = lax.axis_index("head")
    core = lax.axis_index("seq") & 1
    for step, part in enumerate((g0, g1, g2, g3)):
        scr[aligned(lax.rem(head + 4 - step, 4), 32), :] = part[...]
    full[...] = mm(scr[...], x_ref[...]).T
    keep_ref[...] = full[aligned(core, 512), :]
    send_ref[...] = full[aligned(1 - core, 512), :]


def pack3_body(keep_ref, recv_ref, o_ref):
    for chip in range(CHIPS):
        rows = slice(16 * chip, 16 * chip + 16)
        o_ref[chip] = keep_ref[rows, :] + recv_ref[rows, :]


def mid3_body(scale, r_ref, o_ref):
    total = r_ref[0]
    for chip in range(1, CHIPS):
        total = total + r_ref[chip]
    total = (total * scale).astype(BF16)
    for chip in range(CHIPS):
        o_ref[chip] = total


def finish_body(
    k_ref, v_ref, mine_ref, other_ref, dki_ref, dvi_ref, w_mine_ref, w_other_ref,
    dk_hbm, dv_hbm, w_hbm, dk_ref, dv_ref, w_ref, sems,
):
    core = lax.axis_index("seq") & 1
    w_ref[aligned(core, 512), :] = w_mine_ref[...].astype(F32)
    w_ref[aligned(1 - core, 512), :] = w_other_ref[...].astype(F32)
    copies = [pltpu.make_async_copy(w_ref, w_hbm, sems.at[8])]
    copies[0].start()
    for head in range(4):
        lanes = slice(DIM * head, DIM * (head + 1))
        part = slice(768 + DIM * (head % 2), 768 + DIM * (head % 2 + 1))
        later = jnp.where(head // 2 == core, mine_ref[part, :], other_ref[part, :]).astype(F32)
        near = other_ref[1024 + DIM * head : 1024 + DIM * (head + 1), :].astype(F32)
        later = (later + near * (core == 0).astype(F32)).astype(BF16)
        dk_ref[:, lanes] = (dki_ref[:, lanes] + mm(v_ref[:, lanes], later, 1, 1)).astype(BF16)
        copies.append(pltpu.make_async_copy(dk_ref.at[:, lanes], dk_hbm.at[:, lanes], sems.at[head]))
        copies[-1].start()
        dv_ref[:, lanes] = (dvi_ref[:, lanes] + mm(k_ref[:, lanes], later, 1, 0)).astype(BF16)
        copies.append(pltpu.make_async_copy(dv_ref.at[:, lanes], dv_hbm.at[:, lanes], sems.at[4 + head]))
        copies[-1].start()
    for copy in copies:
        copy.wait()


def shards(layer_input, gate_weight, queries, key_vectors, value_vectors, grad_output, reach_level):
    seq_count = lax.axis_size("seq")
    groups = [[2 * chip + c for chip in range(CHIPS)] for c in range(2)]
    swap = [(d, d ^ 1) for d in range(seq_count)]

    def sibling(value):
        return lax.ppermute(value, "seq", swap)

    def exchange(value):
        return lax.all_to_all(value, "seq", 0, 0, axis_index_groups=groups)

    def rotate(value, step):
        return lax.ppermute(value, "head", [(h, (h + step) % 4) for h in range(4)])

    whole = pl.BlockSpec(memory_space=pltpu.VMEM)
    smem = pl.BlockSpec(memory_space=pltpu.SMEM)
    hbm = pl.BlockSpec(memory_space=pl.ANY)

    block = pltpu.VMEM((TOK, 512), BF16)
    heads4 = pl.BlockSpec((TOK, DIM), lambda h: (0, h))
    gates4 = pl.BlockSpec((8, TOK), lambda h: (h, 0))
    rows4_tok = pl.BlockSpec((DIM, TOK), lambda h: (h, 0))
    first8 = pl.BlockSpec((8, TOK), lambda h: (0, 0))

    parts = call(
        logits_body, [shape((32, TOK), F32)] * 4, (layer_input, gate_weight), scratch=[pltpu.VMEM((DIM, TOK), F32)]
    )
    logits = [parts[0]] + [rotate(parts[step], step) for step in range(1, 4)]
    states, queries_t, allowed = call(
        state_body,
        [shape((512, DIM), F32), shape((512, TOK), BF16), shape((LEVELS, TOK), F32)],
        (queries, key_vectors, value_vectors, reach_level),
        in_specs=[heads4] * 3 + [smem],
        out_specs=[pl.BlockSpec((DIM, DIM), lambda h: (h, 0)), rows4_tok, first8],
        grid=(4,),
        after=(parts[0],),
    )
    sib_state = sibling(states)
    gates, send = call(
        level_send_body, [shape((32, TOK), F32), shape((768, DIM), BF16)],
        (queries_t, grad_output, *logits, allowed),
        after=(states,),
    )
    near, keep = call(
        level_keep_body, [shape((512, DIM), BF16), shape((768, DIM), F32)],
        (queries_t, grad_output, gates, allowed),
    )

    slices = call(
        pack1_body, shape((CHIPS, 32, DIM), BF16), (states, sib_state, keep, sibling(send)),
        scratch=[pltpu.VMEM((1024, DIM), F32)],
    )
    got1 = exchange(slices)
    dk_in, dv_in, dq_in, rows = call(
        intra_body,
        [shape((TOK, 512), F32), shape((TOK, 512), F32), shape((512, TOK), F32), shape((32, TOK), F32)],
        (queries, key_vectors, value_vectors, grad_output, sib_state, gates, allowed),
        in_specs=[heads4] * 4
        + [pl.BlockSpec((DIM, DIM), lambda h: (h, 0)), gates4, first8],
        out_specs=[heads4, heads4, rows4_tok, gates4],
        grid=(4,),
        scratch=[pltpu.VMEM((TOK, TOK), BF16), pltpu.VMEM((TOK, TOK), BF16)],
        cost=(2 * 10**9, 8 * 10**6),
        after=(slices,),
        limit=VMEM_ALL,
    )
    got2 = exchange(call(mid1_body, shape((CHIPS, 32, DIM), BF16), (got1,), after=(rows,)))
    mine = call(mid2_body, shape((1536, DIM), BF16), (got2, near))
    other = sibling(mine)
    grad_logits = call(
        cross_body, shape((32, TOK), BF16), (queries_t, grad_output, mine, other, gates, allowed, rows)
    )

    gl = [grad_logits] + [rotate(grad_logits, step) for step in range(1, 4)]
    grad_queries, token = call(
        queries_body, [shape((TOK, 512), BF16), shape((8, DIM), F32)],
        (grad_output, mine, other, gates, allowed, dq_in),
        out_specs=[hbm, whole],
        scratch=[block, pltpu.SemaphoreType.DMA((4,))],
        after=(grad_logits,),
    )
    w_keep, w_send = call(
        gradw_body, [shape((512, DIM), F32)] * 2, (layer_input, *gl),
        scratch=[pltpu.VMEM((DIM, TOK), BF16), pltpu.VMEM((1024, DIM), F32)],
        after=(token,),
    )
    got3 = exchange(call(pack3_body, shape((CHIPS, 16, DIM), F32), (w_keep, sibling(w_send))))
    scale = 1.0 / math.sqrt(TOK * seq_count)
    sums = call(functools.partial(mid3_body, scale), shape((CHIPS, 16, DIM), BF16), (got3,))
    w_half = exchange(sums).reshape(512, DIM)
    grad_keys, grad_values, grad_weight = call(
        finish_body,
        [shape((TOK, 512), BF16)] * 2 + [shape((1024, DIM), F32)],
        (key_vectors, value_vectors, mine, other, dk_in, dv_in, w_half, sibling(w_half)),
        out_specs=[hbm] * 3,
        scratch=[block, block, pltpu.VMEM((1024, DIM), F32), pltpu.SemaphoreType.DMA((9,))],
    )
    return grad_queries, grad_keys, grad_values, grad_weight


def solution(mesh):
    placed = (
        P("seq", "head"),
        P("head", None),
        P("seq", "head"),
        P("seq", "head"),
        P("seq", "head"),
        P("seq", "head"),
        P("seq"),
    )
    return jax.shard_map(
        shards,
        mesh=mesh,
        in_specs=placed,
        out_specs=(P("seq", "head"), P("seq", "head"), P("seq", "head"), P("head", None)),
        check_vma=False,
    )
```

time: 109 us -> 105 us (0.963)
  Pallas kernels: 17.8 us -> 15.1 us
  waiting for transfers between devices: 9.25 us -> 11.7 us
  local copies, waits for them, and re-layouts: 5.89 us -> 4.12 us
  blocking collectives: 44.7 us -> 43.6 us
    pallas_call x14, Pallas kernels: 17.8 us -> 15.1 us  [call(): pl.pallas_call(kernel, out_shape=out_shape, grid=grid, in_specs=in_specs,...]
    unnamed x32 -> x42, local copies, waits for them, and re-layouts: 5.89 us -> 4.12 us
    ppermute x6, waiting for transfers between devices: 1.13 us -> 2.58 us  [rotate(): return lax.ppermute(value, 'head', [(h, (h + step) % 4) for h in range(4)])]
    ppermute x6 -> x5, waiting for transfers between devices: 4.22 us -> 4.39 us  [sibling(): return lax.ppermute(value, 'seq', swap)]
    ppermute x6 -> x5, starting transfers between devices: 9.85 us -> 9.88 us  [sibling(): return lax.ppermute(value, 'seq', swap)]
  transfers between devices with their start and end apart: 13 -> 12, of which waited for: 7 -> 7; matrix products, arithmetic and copies ran while one was open for 0% -> 0% of each run, Pallas kernels for 12% -> 11%
where the time goes in v3:
time: 105 us
  blocking collectives  43.6 us (42%)
  starting transfers between devices  29.4 us (28%)
  Pallas kernels  15.1 us (14%)
  waiting for transfers between devices  11.7 us (11%)
  local copies, waits for them, and re-layouts  4.12 us (4%)
    all_to_all x3, blocking collectives, exchange(): return lax.all_to_all(value, 'seq', 0, 0, axis_index_groups=groups)  43.6 us
    pallas_call x14, Pallas kernels, call(): pl.pallas_call(kernel, out_shape=out_shape, grid=grid, in_specs=in_specs,...  15.1 us
    all_to_all x1, starting transfers between devices, exchange(): return lax.all_to_all(value, 'seq', 0, 0, axis_index_groups=groups)  11 us
    ppermute x5, starting transfers between devices, sibling(): return lax.ppermute(value, 'seq', swap)  9.88 us
    ppermute x6, starting transfers between devices, rotate(): return lax.ppermute(value, 'head', [(h, (h + step) % 4) for h in range(4)])  8.53 us
    all_to_all x1, waiting for transfers between devices, exchange(): return lax.all_to_all(value, 'seq', 0, 0, axis_index_groups=groups)  4.69 us
    ppermute x5, waiting for transfers between devices, sibling(): return lax.ppermute(value, 'seq', swap)  4.39 us
    unnamed x42, local copies, waits for them, and re-layouts  4.12 us
  transfers between devices with their start and end apart: 12, of which 7 were waited for; matrix products, arithmetic and copies ran while one was open for 0% of the time, Pallas kernels for 11%

profile of v3, /device:TPU:1, one launch (start us, length us, event | category | flops | bytes accessed | tf_op | source)
XLA Modules:
  0.0 104.8 jit_solution(17601001982720585941)
XLA Ops:
  0.6 0.0 copy-start.2
  0.6 1.2 %copy-done.2 = bf16[512,1024]{1,0:T(8,128)(2,1)S(1)} copy-done((bf16[512,1024]{1,0:T(8,128)(2,1)S(1)}, bf16[512,1024]{1,0:T(8,128)(2,1)}, u32[]{:S(2)}) %copy-start.2) | copy-done | bytes 1048600
  1.9 0.9 copy-done.16
  2.8 0.5 shard_map.102
  3.3 2.2 %collective-permute-start.1 = (f32[32,512]{1,0:T(8,128)S(1)}, f32[32,512]{1,0:T(8,128)S(1)}, u32[]{:S(2)}, u32[]{:S(2)}) collective-permute-start(f32[32,512]{1,0:T(8,128)S(1)} %get-tuple-element.29), channel_id=1, source_target_pairs={{0,1},{1,2},{2,3},{3,0},{4,5},{5,6},{6,7},{7,4},{8,9},{9,10},{10,1... | collective-permute-start | bytes 196616 | tf_op jit(solution)/shard_map/ppermute | solution.py:313
  5.5 2.6 %collective-permute-start.2 = (f32[32,512]{1,0:T(8,128)S(1)}, f32[32,512]{1,0:T(8,128)S(1)}, u32[]{:S(2)}, u32[]{:S(2)}) collective-permute-start(f32[32,512]{1,0:T(8,128)S(1)} %get-tuple-element.30), channel_id=1, source_target_pairs={{0,2},{1,3},{2,0},{3,1},{4,6},{5,7},{6,4},{7,5},{8,10},{9,11},{10,... | collective-permute-start | bytes 196616 | tf_op jit(solution)/shard_map/ppermute | solution.py:313
  8.2 1.1 %collective-permute-start.3 = (f32[32,512]{1,0:T(8,128)S(1)}, f32[32,512]{1,0:T(8,128)S(1)}, u32[]{:S(2)}, u32[]{:S(2)}) collective-permute-start(f32[32,512]{1,0:T(8,128)S(1)} %get-tuple-element.31), channel_id=1, source_target_pairs={{0,3},{1,0},{2,1},{3,2},{4,7},{5,4},{6,5},{7,6},{8,11},{9,8},{10,9... | collective-permute-start | bytes 196616 | tf_op jit(solution)/shard_map/ppermute | solution.py:313
  9.2 0.0 copy-done.4
  9.2 0.0 copy-done.20
  9.2 1.0 copy-done.13
  10.3 1.8 %shard_map.103 = (f32[512,128]{1,0:T(8,128)S(1)}, bf16[512,512]{1,0:T(8,128)(2,1)S(1)}, f32[8,512]{1,0:T(8,128)S(1)}) custom-call(bf16[512,512]{1,0:T(8,128)(2,1)S(1)} %copy-done.13, bf16[512,512]{1,0:T(8,128)(2,1)S(1)} %copy-done.4, bf16[512,512]{1,0:T(8,128)(2,1)S(1)} %copy-done.6, s32[8]{0:T(128)S(1)} %copy-done.20, ...), custom_call_target="tpu_custom_call" | custom-call | flops 10000000 | bytes 1000000 | tf_op jit(solution)/shard_map/pallas_call | solution.py:46
  12.1 1.6 %collective-permute-start = (f32[512,128]{1,0:T(8,128)S(1)}, f32[512,128]{1,0:T(8,128)S(1)}, u32[]{:S(2)}, u32[]{:S(2)}) collective-permute-start(f32[512,128]{1,0:T(8,128)S(1)} %get-tuple-element.27.refs_7_.refs_0_), channel_id=1, source_target_pairs={{0,4},{4,0},{8,12},{12,8},{16,20},{20,16},{24,28},{28,24},{32,36},... | collective-permute-start | bytes 786440 | tf_op jit(solution)/shard_map/ppermute | solution.py:307
  13.7 0.0 collective-permute-done.1.refs_3_
  13.7 0.0 collective-permute-done.2.refs_4_
  13.7 0.0 collective-permute-done.3.refs_5_
  13.7 0.4 shard_map.104
  14.1 0.0 copy-start.11
  14.1 0.1 collective-permute-start.4
  14.2 0.5 shard_map.105
  14.7 0.9 collective-permute-done.4.refs_3_
  15.6 0.0 collective-permute-done.refs_1_.refs_4_
  15.6 0.8 shard_map.106.refs_7_
  16.4 11.0 %all-to-all-start = ((bf16[32,32,128]{2,1,0:T(8,128)(2,1)}), bf16[32,32,128]{2,1,0:T(8,128)(2,1)S(1)}, u32[]{:S(2)}, u32[]{:S(2)}) async-start(bf16[32,32,128]{2,1,0:T(8,128)(2,1)} %shard_map.106.refs_7_), calls=%async_computation | async-start | bytes 524288 | tf_op jit(solution)/shard_map/all_to_all | solution.py:310
  27.5 7.1 %shard_map.107 = (f32[512,512]{1,0:T(8,128)}, f32[512,512]{1,0:T(8,128)}, f32[512,512]{1,0:T(8,128)}, f32[32,512]{1,0:T(8,128)}) custom-call(bf16[512,512]{1,0:T(8,128)(2,1)} %refs_0_.8, bf16[512,512]{1,0:T(8,128)(2,1)} %refs_0_.11, bf16[512,512]{1,0:T(8,128)(2,1)} %refs_1_.13, bf16[512,512]{1,0:T(8,128)(2,1)} %refs_0_.9, f32[512,128]{1,0:T(8,128)} %copy-done.19, ...), custom_call_target="tpu_custom_call" | custom-call | flops 2000000000 | bytes 8000000 | tf_op jit(solution)/shard_map/pallas_call | solution.py:46
  34.6 4.7 %all-to-all-done.refs_0_ = bf16[32,32,128]{2,1,0:T(8,128)(2,1)S(1)} async-done(((bf16[32,32,128]{2,1,0:T(8,128)(2,1)}), bf16[32,32,128]{2,1,0:T(8,128)(2,1)S(1)}, u32[]{:S(2)}, u32[]{:S(2)}) %all-to-all-start) | async-done | bytes 262176 | tf_op jit(solution)/shard_map/all_to_all | solution.py:310
  39.3 0.8 copy-done.17
  40.2 14.8 %all_to_all.20.refs_0_ = bf16[32,32,128]{2,1,0:T(8,128)(2,1)S(1)} all-to-all(bf16[32,32,128]{2,1,0:T(8,128)(2,1)S(1)} %shard_map.108), channel_id=1, replica_groups={{0,8,16,24,32,40,48,56,64,72,80,88,96,104,112,120,128,136,144,152,160,1..., dimensions={0} | all-to-all | bytes 524288 | tf_op jit(solution)/shard_map/all_to_all | solution.py:310
  55.0 0.1 shard_map.109.refs_2_.refs_1_
  55.0 3.5 %collective-permute-start.5 = (bf16[1536,128]{1,0:T(8,128)(2,1)S(1)}, bf16[1536,128]{1,0:T(8,128)(2,1)S(1)}, u32[]{:S(2)}, u32[]{:S(2)}) collective-permute-start(bf16[1536,128]{1,0:T(8,128)(2,1)S(1)} %shard_map.109.refs_2_.refs_1_), channel_id=1, source_target_pairs={{0,4},{4,0},{8,12},{12,8},{16,20},{20,16},{24,28},{28,24},{32,36},... | collective-permute-start | bytes 1179656 | tf_op jit(solution)/shard_map/ppermute | solution.py:307
  58.6 1.3 %collective-permute-done.5.refs_3_.refs_2_ = bf16[1536,128]{1,0:T(8,128)(2,1)S(1)} collective-permute-done((bf16[1536,128]{1,0:T(8,128)(2,1)S(1)}, bf16[1536,128]{1,0:T(8,128)(2,1)S(1)}, u32[]{:S(2)}, u32[]{:S(2)}) %collective-permute-start.5) | collective-permute-done | bytes 393248 | tf_op jit(solution)/shard_map/ppermute | solution.py:307
  59.9 0.6 shard_map.110.refs_6_.refs_1_
  60.5 2.0 %collective-permute-start.8 = (bf16[32,512]{1,0:T(8,128)(2,1)S(1)}, bf16[32,512]{1,0:T(8,128)(2,1)S(1)}, u32[]{:S(2)}, u32[]{:S(2)}) collective-permute-start(bf16[32,512]{1,0:T(8,128)(2,1)S(1)} %shard_map.110.refs_6_.refs_1_), channel_id=1, source_target_pairs={{0,3},{1,0},{2,1},{3,2},{4,7},{5,4},{6,5},{7,6},{8,11},{9,8},{10,9... | collective-permute-start | bytes 98312 | tf_op jit(solution)/shard_map/ppermute | solution.py:313
  62.5 0.3 collective-permute-start.7
  62.8 0.4 collective-permute-start.6
  63.2 1.3 %shard_map.111 = (bf16[512,512]{1,0:T(8,128)(2,1)}, f32[8,128]{1,0:T(8,128)S(1)}) custom-call(bf16[512,512]{1,0:T(8,128)(2,1)S(1)} %copy-done.1, bf16[1536,128]{1,0:T(8,128)(2,1)S(1)} %shard_map.109.refs_2_.refs_1_, bf16[1536,128]{1,0:T(8,128)(2,1)S(1)} %collective-permute-done.5.refs_3_.refs_2_, f32[32,512]{1,0:T(8,128)S(1)} %copy-done.12, ...), custom_call_target="tpu_custom_call" | custom-call | flops 10000000 | bytes 1000000 | tf_op jit(solution)/shard_map/pallas_call | solution.py:46
  64.5 0.0 collective-permute-done.8.refs_4_
  64.5 2.3 %collective-permute-done.7.refs_3_ = bf16[32,512]{1,0:T(8,128)(2,1)S(1)} collective-permute-done((bf16[32,512]{1,0:T(8,128)(2,1)S(1)}, bf16[32,512]{1,0:T(8,128)(2,1)S(1)}, u32[]{:S(2)}, u32[]{:S(2)}) %collective-permute-start.7) | collective-permute-done | bytes 32800 | tf_op jit(solution)/shard_map/ppermute | solution.py:313
  66.8 0.3 collective-permute-done.6.refs_2_
  67.1 0.5 shard_map.112
  67.6 1.9 %collective-permute-start.9 = (f32[512,128]{1,0:T(8,128)S(1)}, f32[512,128]{1,0:T(8,128)S(1)}, u32[]{:S(2)}, u32[]{:S(2)}) collective-permute-start(f32[512,128]{1,0:T(8,128)S(1)} %get-tuple-element.44), channel_id=1, source_target_pairs={{0,4},{4,0},{8,12},{12,8},{16,20},{20,16},{24,28},{28,24},{32,36},... | collective-permute-start | bytes 786440 | tf_op jit(solution)/shard_map/ppermute | solution.py:307
  69.5 1.2 %collective-permute-done.9.refs_1_ = f32[512,128]{1,0:T(8,128)S(1)} collective-permute-done((f32[512,128]{1,0:T(8,128)S(1)}, f32[512,128]{1,0:T(8,128)S(1)}, u32[]{:S(2)}, u32[]{:S(2)}) %collective-permute-start.9) | collective-permute-done | bytes 262176 | tf_op jit(solution)/shard_map/ppermute | solution.py:307
  70.7 0.0 copy-start.5
  70.7 0.0 copy-start.7
  70.7 15.1 %all_to_all.21.refs_0_ = f32[32,16,128]{2,1,0:T(8,128)S(1)} all-to-all(f32[32,16,128]{2,1,0:T(8,128)S(1)} %shard_map.113), channel_id=1, replica_groups={{0,8,16,24,32,40,48,56,64,72,80,88,96,104,112,120,128,136,144,152,160,1..., dimensions={0} | all-to-all | bytes 524288 | tf_op jit(solution)/shard_map/all_to_all | solution.py:310
  85.9 13.7 %all_to_all.22 = bf16[32,16,128]{2,1,0:T(8,128)(2,1)S(1)} all-to-all(bf16[32,16,128]{2,1,0:T(8,128)(2,1)S(1)} %shard_map.114), channel_id=1, replica_groups={{0,8,16,24,32,40,48,56,64,72,80,88,96,104,112,120,128,136,144,152,160,1..., dimensions={0} | all-to-all | bytes 262144 | tf_op jit(solution)/shard_map/all_to_all | solution.py:310
  99.6 2.7 %collective-permute-start.10 = (bf16[512,128]{1,0:T(8,128)(2,1)S(1)}, bf16[512,128]{1,0:T(8,128)(2,1)S(1)}, u32[]{:S(2)}, u32[]{:S(2)}) collective-permute-start(bf16[512,128]{1,0:T(8,128)(2,1)S(1)} %bitcast.1), channel_id=1, source_target_pairs={{0,4},{4,0},{8,12},{12,8},{16,20},{20,16},{24,28},{28,24},{32,36},... | collective-permute-start | bytes 393224 | tf_op jit(solution)/shard_map/ppermute | solution.py:307
  102.4 1.0 collective-permute-done.10.refs_7_
  103.4 1.4 %shard_map.115 = (bf16[512,512]{1,0:T(8,128)(2,1)}, bf16[512,512]{1,0:T(8,128)(2,1)}, f32[1024,128]{1,0:T(8,128)}) custom-call(bf16[512,512]{1,0:T(8,128)(2,1)S(1)} %copy-done.5, bf16[512,512]{1,0:T(8,128)(2,1)S(1)} %copy-done.7, bf16[1536,128]{1,0:T(8,128)(2,1)S(1)} %shard_map.109.refs_2_.refs_1_, ...), custom_call_target="tpu_custom_call" | custom-call | flops 10000000 | bytes 1000000 | tf_op jit(solution)/shard_map/pallas_call | solution.py:46
  (35 shorter events, 0.2 us)
Async XLA Ops:
  0.6 1.2 %copy-start.2 = (bf16[512,1024]{1,0:T(8,128)(2,1)S(1)}, bf16[512,1024]{1,0:T(8,128)(2,1)}, u32[]{:S(2)}) copy-start(bf16[512,1024]{1,0:T(8,128)(2,1)} %refs_0_.10) | copy-start | bytes 3145732
  1.9 0.9 copy-start.16
  2.8 6.4 %copy-start.4 = (bf16[512,512]{1,0:T(8,128)(2,1)S(1)}, bf16[512,512]{1,0:T(8,128)(2,1)}, u32[]{:S(2)}) copy-start(bf16[512,512]{1,0:T(8,128)(2,1)} %refs_0_.11) | copy-start | bytes 1572868
  2.8 6.4 %copy-start.6 = (bf16[512,512]{1,0:T(8,128)(2,1)S(1)}, bf16[512,512]{1,0:T(8,128)(2,1)}, u32[]{:S(2)}) copy-start(bf16[512,512]{1,0:T(8,128)(2,1)} %refs_1_.13) | copy-start | bytes 1572868
  3.3 10.3 %collective-permute-start.1 = (f32[32,512]{1,0:T(8,128)S(1)}, f32[32,512]{1,0:T(8,128)S(1)}, u32[]{:S(2)}, u32[]{:S(2)}) collective-permute-start(f32[32,512]{1,0:T(8,128)S(1)} %get-tuple-element.29), channel_id=1, source_target_pairs={{0,1},{1,2},{2,3},{3,0},{4,5},{5,6},{6,7},{7,4},{8,9},{9,10},{10,1... | collective-permute-start | bytes 196616 | tf_op jit(solution)/shard_map/ppermute | solution.py:313
  5.5 8.1 %collective-permute-start.2 = (f32[32,512]{1,0:T(8,128)S(1)}, f32[32,512]{1,0:T(8,128)S(1)}, u32[]{:S(2)}, u32[]{:S(2)}) collective-permute-start(f32[32,512]{1,0:T(8,128)S(1)} %get-tuple-element.30), channel_id=1, source_target_pairs={{0,2},{1,3},{2,0},{3,1},{4,6},{5,7},{6,4},{7,5},{8,10},{9,11},{10,... | collective-permute-start | bytes 196616 | tf_op jit(solution)/shard_map/ppermute | solution.py:313
  8.1 1.1 %copy-start.20 = (s32[8]{0:T(128)S(1)}, s32[8]{0:T(128)}, u32[]{:S(2)}) copy-start(s32[8]{0:T(128)} %refs_3_.2) | copy-start | bytes 100
  8.2 5.5 %collective-permute-start.3 = (f32[32,512]{1,0:T(8,128)S(1)}, f32[32,512]{1,0:T(8,128)S(1)}, u32[]{:S(2)}, u32[]{:S(2)}) collective-permute-start(f32[32,512]{1,0:T(8,128)S(1)} %get-tuple-element.31), channel_id=1, source_target_pairs={{0,3},{1,0},{2,1},{3,2},{4,7},{5,4},{6,5},{7,6},{8,11},{9,8},{10,9... | collective-permute-start | bytes 196616 | tf_op jit(solution)/shard_map/ppermute | solution.py:313
  9.2 1.0 copy-start.13
  10.3 3.4 %copy-start = (bf16[512,512]{1,0:T(8,128)(2,1)S(1)}, bf16[512,512]{1,0:T(8,128)(2,1)}, u32[]{:S(2)}) copy-start(bf16[512,512]{1,0:T(8,128)(2,1)} %refs_0_.9) | copy-start | bytes 1572868
  12.0 2.2 %copy-start.14 = (f32[8,512]{1,0:T(8,128)}, f32[8,512]{1,0:T(8,128)S(1)}, u32[]{:S(2)}) copy-start(f32[8,512]{1,0:T(8,128)S(1)} %get-tuple-element.32.refs_6_.refs_3_.refs_5_.refs_4_) | copy-start | bytes 49156
  12.1 3.6 %collective-permute-start = (f32[512,128]{1,0:T(8,128)S(1)}, f32[512,128]{1,0:T(8,128)S(1)}, u32[]{:S(2)}, u32[]{:S(2)}) collective-permute-start(f32[512,128]{1,0:T(8,128)S(1)} %get-tuple-element.27.refs_7_.refs_0_), channel_id=1, source_target_pairs={{0,4},{4,0},{8,12},{12,8},{16,20},{20,16},{24,28},{28,24},{32,36},... | collective-permute-start | bytes 786440 | tf_op jit(solution)/shard_map/ppermute | solution.py:307
  14.1 0.6 copy-start.11
  14.1 1.5 %collective-permute-start.4 = (bf16[768,128]{1,0:T(8,128)(2,1)S(1)}, bf16[768,128]{1,0:T(8,128)(2,1)S(1)}, u32[]{:S(2)}, u32[]{:S(2)}) collective-permute-start(bf16[768,128]{1,0:T(8,128)(2,1)S(1)} %get-tuple-element.35), channel_id=1, source_target_pairs={{0,4},{4,0},{8,12},{12,8},{16,20},{20,16},{24,28},{28,24},{32,36},... | collective-permute-start | bytes 589832 | tf_op jit(solution)/shard_map/ppermute | solution.py:307
  15.6 0.8 copy-start.19
  16.4 22.9 %all-to-all-start = ((bf16[32,32,128]{2,1,0:T(8,128)(2,1)}), bf16[32,32,128]{2,1,0:T(8,128)(2,1)S(1)}, u32[]{:S(2)}, u32[]{:S(2)}) async-start(bf16[32,32,128]{2,1,0:T(8,128)(2,1)} %shard_map.106.refs_7_), calls=%async_computation | async-start | bytes 524288 | tf_op jit(solution)/shard_map/all_to_all | solution.py:310
  39.3 0.8 copy-start.17
  54.9 5.0 %copy-start.1 = (bf16[512,512]{1,0:T(8,128)(2,1)S(1)}, bf16[512,512]{1,0:T(8,128)(2,1)}, u32[]{:S(2)}) copy-start(bf16[512,512]{1,0:T(8,128)(2,1)} %refs_0_.9) | copy-start | bytes 1572868
  54.9 5.0 %copy-start.12 = (f32[32,512]{1,0:T(8,128)S(1)}, f32[32,512]{1,0:T(8,128)}, u32[]{:S(2)}) copy-start(f32[32,512]{1,0:T(8,128)} %copy-done.11) | copy-start | bytes 196612
  55.0 5.0 %copy-start.15 = (f32[8,512]{1,0:T(8,128)S(1)}, f32[8,512]{1,0:T(8,128)}, u32[]{:S(2)}) copy-start(f32[8,512]{1,0:T(8,128)} %copy-done.14) | copy-start | bytes 49156
  55.0 5.0 %copy-start.18 = (f32[32,512]{1,0:T(8,128)S(1)}, f32[32,512]{1,0:T(8,128)}, u32[]{:S(2)}) copy-start(f32[32,512]{1,0:T(8,128)} %get-tuple-element.36.refs_1_.refs_6_) | copy-start | bytes 196612
  55.0 8.1 %copy-start.8 = (f32[512,512]{1,0:T(8,128)S(1)}, f32[512,512]{1,0:T(8,128)}, u32[]{:S(2)}) copy-start(f32[512,512]{1,0:T(8,128)} %get-tuple-element.38.refs_5_) | copy-start | bytes 3145732
  55.0 4.9 %collective-permute-start.5 = (bf16[1536,128]{1,0:T(8,128)(2,1)S(1)}, bf16[1536,128]{1,0:T(8,128)(2,1)S(1)}, u32[]{:S(2)}, u32[]{:S(2)}) collective-permute-start(bf16[1536,128]{1,0:T(8,128)(2,1)S(1)} %shard_map.109.refs_2_.refs_1_), channel_id=1, source_target_pairs={{0,4},{4,0},{8,12},{12,8},{16,20},{20,16},{24,28},{28,24},{32,36},... | collective-permute-start | bytes 1179656 | tf_op jit(solution)/shard_map/ppermute | solution.py:307
  60.5 4.0 %collective-permute-start.8 = (bf16[32,512]{1,0:T(8,128)(2,1)S(1)}, bf16[32,512]{1,0:T(8,128)(2,1)S(1)}, u32[]{:S(2)}, u32[]{:S(2)}) collective-permute-start(bf16[32,512]{1,0:T(8,128)(2,1)S(1)} %shard_map.110.refs_6_.refs_1_), channel_id=1, source_target_pairs={{0,3},{1,0},{2,1},{3,2},{4,7},{5,4},{6,5},{7,6},{8,11},{9,8},{10,9... | collective-permute-start | bytes 98312 | tf_op jit(solution)/shard_map/ppermute | solution.py:313
  62.5 4.3 %collective-permute-start.7 = (bf16[32,512]{1,0:T(8,128)(2,1)S(1)}, bf16[32,512]{1,0:T(8,128)(2,1)S(1)}, u32[]{:S(2)}, u32[]{:S(2)}) collective-permute-start(bf16[32,512]{1,0:T(8,128)(2,1)S(1)} %shard_map.110.refs_6_.refs_1_), channel_id=1, source_target_pairs={{0,2},{1,3},{2,0},{3,1},{4,6},{5,7},{6,4},{7,5},{8,10},{9,11},{10,... | collective-permute-start | bytes 98312 | tf_op jit(solution)/shard_map/ppermute | solution.py:313
  62.8 4.3 %collective-permute-start.6 = (bf16[32,512]{1,0:T(8,128)(2,1)S(1)}, bf16[32,512]{1,0:T(8,128)(2,1)S(1)}, u32[]{:S(2)}, u32[]{:S(2)}) collective-permute-start(bf16[32,512]{1,0:T(8,128)(2,1)S(1)} %shard_map.110.refs_6_.refs_1_), channel_id=1, source_target_pairs={{0,1},{1,2},{2,3},{3,0},{4,5},{5,6},{6,7},{7,4},{8,9},{9,10},{10,1... | collective-permute-start | bytes 98312 | tf_op jit(solution)/shard_map/ppermute | solution.py:313
  63.2 3.9 %copy-start.3 = (bf16[512,1024]{1,0:T(8,128)(2,1)S(1)}, bf16[512,1024]{1,0:T(8,128)(2,1)}, u32[]{:S(2)}) copy-start(bf16[512,1024]{1,0:T(8,128)(2,1)} %refs_0_.10) | copy-start | bytes 3145732
  67.1 36.2 %copy-start.9 = (f32[512,512]{1,0:T(8,128)S(1)}, f32[512,512]{1,0:T(8,128)}, u32[]{:S(2)}) copy-start(f32[512,512]{1,0:T(8,128)} %get-tuple-element.40.refs_4_) | copy-start | bytes 3145732
  67.1 36.2 %copy-start.10 = (f32[512,512]{1,0:T(8,128)S(1)}, f32[512,512]{1,0:T(8,128)}, u32[]{:S(2)}) copy-start(f32[512,512]{1,0:T(8,128)} %get-tuple-element.41.refs_5_) | copy-start | bytes 3145732
  67.6 3.0 %collective-permute-start.9 = (f32[512,128]{1,0:T(8,128)S(1)}, f32[512,128]{1,0:T(8,128)S(1)}, u32[]{:S(2)}, u32[]{:S(2)}) collective-permute-start(f32[512,128]{1,0:T(8,128)S(1)} %get-tuple-element.44), channel_id=1, source_target_pairs={{0,4},{4,0},{8,12},{12,8},{16,20},{20,16},{24,28},{28,24},{32,36},... | collective-permute-start | bytes 786440 | tf_op jit(solution)/shard_map/ppermute | solution.py:307
  70.7 32.7 %copy-start.5 = (bf16[512,512]{1,0:T(8,128)(2,1)S(1)}, bf16[512,512]{1,0:T(8,128)(2,1)}, u32[]{:S(2)}) copy-start(bf16[512,512]{1,0:T(8,128)(2,1)} %refs_0_.11) | copy-start | bytes 1572868
  70.7 32.7 %copy-start.7 = (bf16[512,512]{1,0:T(8,128)(2,1)S(1)}, bf16[512,512]{1,0:T(8,128)(2,1)}, u32[]{:S(2)}) copy-start(bf16[512,512]{1,0:T(8,128)(2,1)} %refs_1_.13) | copy-start | bytes 1572868
  99.6 3.7 %collective-permute-start.10 = (bf16[512,128]{1,0:T(8,128)(2,1)S(1)}, bf16[512,128]{1,0:T(8,128)(2,1)S(1)}, u32[]{:S(2)}, u32[]{:S(2)}) collective-permute-start(bf16[512,128]{1,0:T(8,128)(2,1)S(1)} %bitcast.1), channel_id=1, source_target_pairs={{0,4},{4,0},{8,12},{12,8},{16,20},{20,16},{24,28},{28,24},{32,36},... | collective-permute-start | bytes 393224 | tf_op jit(solution)/shard_map/ppermute | solution.py:307

commit v4 on v2

v4 whole, which is shorter than its diff:
```python
import functools
import math

import jax
import jax.numpy as jnp
from jax import lax
from jax.experimental import pallas as pl
from jax.experimental.pallas import tpu as pltpu
from jax.sharding import PartitionSpec as P

F32 = jnp.float32
BF16 = jnp.bfloat16
TOK = 512
DIM = 128
SPAN = 64
LEVELS = 8
CHIPS = 32
INV = 1.0 / DIM
VMEM_LIMIT = 24 * 1024 * 1024
VMEM_ALL = 60 * 1024 * 1024


def mm(left, right, left_dim=1, right_dim=0):
    return lax.dot_general(
        left, right, (((left_dim,), (right_dim,)), ((), ())), preferred_element_type=F32
    )


def aligned(index, size):
    return pl.ds(pl.multiple_of(index * size, size), size)


def call(
    body, out_shape, args, in_specs=None, out_specs=None, grid=(), scratch=(), cost=(10**7, 10**6), after=(),
    limit=VMEM_LIMIT,
):
    whole = pl.BlockSpec(memory_space=pltpu.VMEM)
    many = isinstance(out_shape, (tuple, list))
    used = len(args)
    in_specs = list(in_specs or [whole] * used) + [pl.BlockSpec(memory_space=pl.ANY)] * len(after)
    args = (*args, *after)

    def kernel(*refs):
        body(*refs[:used], *refs[len(args) :])

    return pl.pallas_call(
        kernel,
        out_shape=out_shape,
        grid=grid,
        in_specs=in_specs,
        out_specs=out_specs or ([whole] * len(out_shape) if many else whole),
        scratch_shapes=list(scratch),
        compiler_params=pltpu.CompilerParams(vmem_limit_bytes=limit),
        cost_estimate=pl.CostEstimate(flops=cost[0], bytes_accessed=cost[1], transcendentals=0),
    )(*args)


def shape(dims, dtype):
    return jax.ShapeDtypeStruct(dims, dtype)


def front_body(
    x_hbm, w_hbm, q_hbm, k_hbm, v_hbm, g_hbm, reach_ref, p0, p1, p2, p3, own_hbm, leaving_hbm,
    x_ref, w_ref, part_ref, own_ref, leaving_ref, in_sems, out_sems,
):
    head = lax.axis_index("head")
    core = lax.axis_index("seq") & 1
    ins, outs = [], []

    def load(src, dst):
        ins.append(pltpu.make_async_copy(src, dst, in_sems.at[len(ins)]))
        ins[-1].start()

    def store(src, dst):
        outs.append(pltpu.make_async_copy(src, dst, out_sems.at[len(outs)]))
        outs[-1].start()

    load(w_hbm, w_ref)
    load(x_hbm, x_ref)
    for side, ref in ((1 - core, leaving_ref), (core, own_ref)):
        for i, src in enumerate((q_hbm, k_hbm, v_hbm, g_hbm)):
            load(src.at[:, aligned(side, 256)], ref.at[pl.ds(TOK * i, TOK), :])
    lane = lax.broadcasted_iota(jnp.int32, (LEVELS, TOK), 1) // SPAN
    level = lax.broadcasted_iota(jnp.int32, (LEVELS, TOK), 0)
    reach = jnp.zeros((LEVELS, TOK), jnp.int32)
    for span in range(TOK // SPAN):
        reach = jnp.where(lane == span, reach_ref[span], reach)
    allowed = (level <= reach).astype(F32)
    allowed = jnp.concatenate([allowed[:, :256], allowed[:, 256:]], axis=0).astype(BF16)
    leaving_ref[4 * TOK :, :] = allowed
    own_ref[4 * TOK :, :] = allowed
    ins[0].wait()
    ins[1].wait()
    part_ref[...] = mm(w_ref[...], x_ref[...], 0, 1)
    for step, out in enumerate((p0, p1, p2, p3)):
        store(part_ref.at[aligned(lax.rem(head + step, 4), 32), :], out)
    for copy in ins[2:6]:
        copy.wait()
    store(leaving_ref, leaving_hbm)
    for copy in ins[6:]:
        copy.wait()
    store(own_ref, own_hbm)
    for copy in outs:
        copy.wait()


def gather_body(l0, l1, l2, l3, keep_ref, send_ref):
    core = lax.axis_index("seq") & 1
    keep = aligned(core, 16)
    send = aligned(1 - core, 16)
    keep_ref[...] = (l0[keep, :] + l1[keep, :]) + (l2[keep, :] + l3[keep, :])
    send_ref[...] = (l0[send, :] + l1[send, :]) + (l2[send, :] + l3[send, :])


Q, K, V, G = (slice(TOK * i, TOK * (i + 1)) for i in range(4))


def state_body(own_ref, sib_ref, so_ref, ss_ref, qto_ref, qts_ref, ao_ref, as_ref):
    for ref, state, query_t, mask in ((own_ref, so_ref, qto_ref, ao_ref), (sib_ref, ss_ref, qts_ref, as_ref)):
        for i in range(2):
            lanes = slice(DIM * i, DIM * (i + 1))
            state[lanes, :] = mm(ref[K, lanes], ref[V, lanes], 0, 0) * INV
            query_t[lanes, :] = ref[Q, lanes].astype(F32).T.astype(BF16)
        allowed = ref[4 * TOK :, :].astype(F32)
        mask[...] = jnp.concatenate([allowed[:8], allowed[8:]], axis=1)


def span_masks():
    src = lax.broadcasted_iota(jnp.int32, (256, 256), 0)
    dst = lax.broadcasted_iota(jnp.int32, (256, 256), 1)
    near, far = src // SPAN, dst // SPAN
    return [
        ((near == far) & (src <= dst)).astype(F32),
        ((near < far) & (near // 2 == far // 2)).astype(F32),
        (near // 2 < far // 2).astype(F32),
    ]


def rows_body(own_ref, sib_ref, qto_ref, qts_ref, so_ref, ss_ref, ro_ref, rs_ref):
    core = lax.axis_index("seq") & 1
    masks = span_masks()
    none = jnp.zeros((1, 256), F32)
    for block, (ref, query_t, state, out) in enumerate(
        ((own_ref, qto_ref, ss_ref, ro_ref), (sib_ref, qts_ref, so_ref, rs_ref))
    ):
        upper = (core != block).astype(F32)
        for i in range(2):
            lanes = slice(DIM * i, DIM * (i + 1))
            near = (state[lanes, :] * upper).astype(BF16)
            projected = mm(near, ref[G, lanes], 1, 1)
            near_row = jnp.sum(query_t[lanes, :].astype(F32) * projected, axis=0, keepdims=True)
            for a in range(2):
                cols = slice(256 * a, 256 * a + 256)
                end = 256 * a + 256
                scores = mm(ref[TOK : TOK + end, lanes], ref[cols, lanes], 1, 1) * INV
                prod = scores * mm(ref[2 * TOK : 2 * TOK + end, lanes], ref[3 * TOK + 256 * a : 3 * TOK + end, lanes], 1, 1)
                diagonal = prod[256 * a :]
                sums = [jnp.sum(diagonal * mask, axis=0, keepdims=True) for mask in masks]
                sums.append(jnp.sum(prod[:256], axis=0, keepdims=True) if a else none)
                sums.append(near_row[:, cols])
                out[8 * i : 8 * i + 8, cols] = jnp.concatenate(sums + [none] * 3, axis=0)


def level_body(
    own_ref, sib_ref, qto_ref, qts_ref, ao_ref, as_ref, so_ref, ss_ref, lo_ref, ls_ref,
    go_ref, gs_ref, near_ref, o_ref, scr,
):
    core = lax.axis_index("seq") & 1
    gates = [jax.nn.sigmoid(lo_ref[...]), jax.nn.sigmoid(ls_ref[...])]
    go_ref[...] = gates[0]
    gs_ref[...] = gates[1]
    scr[0:256, :] = so_ref[...] + ss_ref[...]
    for i in range(2):
        lanes = slice(DIM * i, DIM * (i + 1))
        grads = []
        for block, (ref, query_t, mask) in enumerate(((own_ref, qto_ref, ao_ref), (sib_ref, qts_ref, as_ref))):
            query = query_t[lanes, :].astype(F32)
            weight = gates[block][8 * i : 8 * i + 8] * mask[...]
            gated = [(weight[level : level + 1, :] * query).astype(BF16) for level in range(4, 8)]
            grads.append(mm(jnp.concatenate(gated, axis=0), ref[G, lanes]))
        near_ref[lanes, :] = jnp.where(core == 1, grads[0][:DIM], grads[1][:DIM]) * INV
        total = (grads[0][DIM:] + grads[1][DIM:]) * INV
        for level in range(3):
            row = 256 * (level + 1) + DIM * i
            scr[row : row + DIM, :] = total[DIM * level : DIM * (level + 1)]
    for chip in range(CHIPS):
        rows = [scr[256 * level + 8 * chip : 256 * level + 8 * chip + 8, :] for level in range(4)]
        o_ref[chip] = jnp.concatenate(rows, axis=0).astype(BF16)


def mid1_body(r_ref, o_ref):
    got = [r_ref[chip].astype(F32) for chip in range(CHIPS)]
    own = [part[0:8] for part in got]
    pairs = [own[chip] + own[chip ^ 1] for chip in range(CHIPS)]
    zero = jnp.zeros((8, DIM), F32)
    before = [zero]
    for group in range(7):
        before.append(before[-1] + (pairs[4 * group] + pairs[4 * group + 2]))
    after = [zero]
    for group in range(7, 0, -1):
        total = [got[4 * group + i][24:32] for i in range(4)]
        after.append(after[-1] + ((total[0] + total[1]) + (total[2] + total[3])))
    after = after[::-1]
    for chip in range(CHIPS):
        later = after[chip >> 2]
        if not chip & 2:
            later = later + (got[chip ^ 2][16:24] + got[chip ^ 3][16:24])
        if not chip & 1:
            later = later + got[chip ^ 1][8:16]
        rows = [
            own[chip ^ 1] if chip & 1 else zero,
            pairs[chip ^ 2] if chip & 2 else zero,
            before[chip >> 2],
            later,
        ]
        o_ref[chip] = jnp.concatenate(rows, axis=0).astype(BF16)


def mid2_body(r_ref, o_ref):
    for chip in range(0, CHIPS, 2):
        got = [r_ref[chip + i].astype(F32) for i in range(2)]
        for level in range(4):
            both = [part[8 * level : 8 * level + 8] for part in got]
            row = 256 * level + 8 * chip
            o_ref[row : row + 16, :] = jnp.concatenate(both, axis=0).astype(BF16)


def far_projection(i, ref, mine_ref):
    lanes = slice(DIM * i, DIM * (i + 1))
    states = [mine_ref[256 * level + DIM * i : 256 * level + DIM * (i + 1), :] for level in range(3)]
    projected = mm(jnp.concatenate(states, axis=0), ref[G, lanes], 1, 1)
    return [projected[DIM * level : DIM * (level + 1)] for level in range(3)]


def cross_body(
    own_ref, sib_ref, qto_ref, qts_ref, ao_ref, as_ref, go_ref, gs_ref, ro_ref, rs_ref, mine_ref, gl_ref
):
    outs = []
    for ref, query_t, mask, gates_ref, rows_ref in (
        (own_ref, qto_ref, ao_ref, go_ref, ro_ref), (sib_ref, qts_ref, as_ref, gs_ref, rs_ref),
    ):
        for i in range(2):
            query = query_t[DIM * i : DIM * (i + 1), :].astype(F32)
            parts = [jnp.zeros((5, TOK), F32)]
            for term in far_projection(i, ref, mine_ref):
                parts.append(jnp.sum(query * term, axis=0, keepdims=True))
            rows = slice(8 * i, 8 * i + 8)
            gates = gates_ref[rows, :]
            grads = (rows_ref[rows, :] + jnp.concatenate(parts, axis=0)) * mask[...]
            outs.append(grads * gates * (1.0 - gates))
    gl_ref[...] = jnp.concatenate(outs, axis=0).astype(BF16)


def tail_body(block, blk_ref, state_ref, near_ref, mask_ref, gates_ref, mine_ref, out_ref, token_ref):
    core = lax.axis_index("seq") & 1
    masks = span_masks()
    upper = (core != block).astype(F32)
    for i in range(2):
        lanes = slice(DIM * i, DIM * (i + 1))
        query, key, value, grad = blk_ref[Q, lanes], blk_ref[K, lanes], blk_ref[V, lanes], blk_ref[G, lanes]
        weight = gates_ref[8 * i : 8 * i + 8, :] * mask_ref[...]
        key_t = key.astype(F32).T.astype(BF16)
        states = [(state_ref[lanes, :] * upper).astype(BF16)]
        for level in range(3):
            states.append(mine_ref[256 * level + DIM * i : 256 * level + DIM * (i + 1), :])
        projected = mm(jnp.concatenate(states, axis=0), grad, 1, 1)
        later = mine_ref[768 + DIM * i : 768 + DIM * (i + 1), :].astype(F32)
        later = (later + near_ref[lanes, :] * (1.0 - upper)).astype(BF16)
        dk = mm(value, later, 1, 1)
        dv = mm(key, later)
        for a in range(2):
            cols = slice(256 * a, 256 * a + 256)
            end = 256 * a + 256
            pair = sum(weight[level : level + 1, cols] * masks[level] for level in range(3))
            if a:
                pair = jnp.concatenate([jnp.broadcast_to(weight[3:4, cols], (256, 256)), pair], axis=0)
            scored = (pair * (mm(key[:end], query[cols], 1, 1) * INV)).astype(BF16)
            weighted = (pair * mm(value[:end], grad[cols], 1, 1)).astype(BF16)
            total = mm(key_t[:, :end], weighted) * INV
            for level in range(4):
                total = total + weight[4 + level : 5 + level, cols] * projected[DIM * level : DIM * (level + 1), cols]
            out_ref[cols, lanes] = total.T.astype(BF16)
            more_k = mm(weighted, query[cols]) * INV
            more_v = mm(scored, grad[cols])
            if a:
                dk, dv = dk + more_k, dv + more_v
            else:
                dk = jnp.concatenate([dk[:256] + more_k, dk[256:]], axis=0)
                dv = jnp.concatenate([dv[:256] + more_v, dv[256:]], axis=0)
        out_ref[K, lanes] = dk.astype(BF16)
        out_ref[V, lanes] = dv.astype(BF16)
    token_ref[...] = jnp.zeros_like(token_ref)


def gradw_body(xo_ref, xs_ref, g0, g1, g2, g3, o_ref, own_scr, sib_scr, full):
    head = lax.axis_index("head")
    for step, part in enumerate((g0, g1, g2, g3)):
        rows = aligned(lax.rem(head + 4 - step, 4), 16)
        own_scr[rows, :] = part[0:16, :]
        sib_scr[rows, :] = part[16:32, :]
    full[...] = mm(own_scr[...], xo_ref[...]) + mm(sib_scr[...], xs_ref[...])
    for chip in range(CHIPS):
        group, block = chip % 4, chip // 4
        o_ref[chip] = full[16 * group : 16 * group + 16, DIM * block : DIM * (block + 1)]


def mid3_body(scale, r_ref, o_ref):
    total = r_ref[0]
    for chip in range(1, CHIPS):
        total = total + r_ref[chip]
    total = (total * scale).astype(BF16)
    for chip in range(CHIPS):
        o_ref[chip] = total


def place_body(own_ref, recv_ref, dq_hbm, dk_hbm, dv_hbm, sems):
    core = lax.axis_index("seq") & 1
    copies = []
    for i, out in enumerate((dq_hbm, dk_hbm, dv_hbm)):
        rows = pl.ds(TOK * i, TOK)
        copies.append(pltpu.make_async_copy(own_ref.at[rows, :], out.at[:, aligned(core, 256)], sems.at[2 * i]))
        copies.append(pltpu.make_async_copy(recv_ref.at[rows, :], out.at[:, aligned(1 - core, 256)], sems.at[2 * i + 1]))
    for copy in copies:
        copy.start()
    for copy in copies:
        copy.wait()


def join_body(w_mine_ref, w_other_ref, w_hbm, full, w_ref, sems):
    core = lax.axis_index("seq") & 1
    copies = []
    for block in range(8):
        lanes = slice(DIM * block, DIM * (block + 1))
        for group in range(4):
            full[aligned(2 * group + core, 16), :] = w_mine_ref[4 * block + group].astype(F32)
            full[aligned(2 * group + 1 - core, 16), :] = w_other_ref[4 * block + group].astype(F32)
        w_ref[lanes, :] = full[...].T
        if block % 4 == 3:
            rows = pl.ds(512 * (block // 4), 512)
            copies.append(pltpu.make_async_copy(w_ref.at[rows, :], w_hbm.at[rows, :], sems.at[block // 4]))
            copies[-1].start()
    for copy in copies:
        copy.wait()


def shards(layer_input, gate_weight, queries, key_vectors, value_vectors, grad_output, reach_level):
    seq_count = lax.axis_size("seq")
    groups = [[2 * chip + c for chip in range(CHIPS)] for c in range(2)]
    swap = [(d, d ^ 1) for d in range(seq_count)]

    def sibling(value):
        return lax.ppermute(value, "seq", swap)

    def exchange(value):
        return lax.all_to_all(value, "seq", 0, 0, axis_index_groups=groups)

    def rotate(value, step):
        return lax.ppermute(value, "head", [(h, (h + step) % 4) for h in range(4)])

    whole = pl.BlockSpec(memory_space=pltpu.VMEM)
    smem = pl.BlockSpec(memory_space=pltpu.SMEM)
    hbm = pl.BlockSpec(memory_space=pl.ANY)

    tok16 = shape((16, TOK), F32)
    mask8 = shape((LEVELS, TOK), F32)
    half = shape((256, DIM), F32)

    *parts, own, leaving = call(
        front_body,
        [shape((32, TOK), F32)] * 4 + [shape((4 * TOK + 16, 256), BF16)] * 2,
        (layer_input, gate_weight, queries, key_vectors, value_vectors, grad_output, reach_level),
        in_specs=[hbm] * 6 + [smem],
        out_specs=[hbm] * 6,
        scratch=[
            pltpu.VMEM((TOK, 1024), BF16), pltpu.VMEM((1024, DIM), BF16), pltpu.VMEM((DIM, TOK), F32),
            pltpu.VMEM((4 * TOK + 16, 256), BF16), pltpu.VMEM((4 * TOK + 16, 256), BF16),
            pltpu.SemaphoreType.DMA((10,)), pltpu.SemaphoreType.DMA((6,)),
        ],
        limit=VMEM_ALL,
    )
    logits = [parts[0]] + [rotate(parts[step], step) for step in range(1, 4)]
    sib = sibling(leaving)
    sib_input = sibling(layer_input)
    state_own, state_sib, qt_own, qt_sib, allow_own, allow_sib = call(
        state_body, [half, half, shape((256, TOK), BF16), shape((256, TOK), BF16), mask8, mask8], (own, sib)
    )
    rows_own, rows_sib = call(
        rows_body, [tok16, tok16], (own, sib, qt_own, qt_sib, state_own, state_sib)
    )
    logits_own, logits_send = call(gather_body, [tok16, tok16], tuple(logits), after=(rows_own,))

    gates_own, gates_sib, near, slices = call(
        level_body, [tok16, tok16, half, shape((CHIPS, 32, DIM), BF16)],
        (own, sib, qt_own, qt_sib, allow_own, allow_sib, state_own, state_sib, logits_own, sibling(logits_send)),
        scratch=[pltpu.VMEM((1024, DIM), F32)],
        after=(sib_input,),
    )
    got1 = exchange(slices)

    got2 = exchange(call(mid1_body, shape((CHIPS, 32, DIM), BF16), (got1,)))
    mine = call(mid2_body, shape((1024, DIM), BF16), (got2,))
    grad_logits = call(
        cross_body, shape((32, TOK), BF16),
        (own, sib, qt_own, qt_sib, allow_own, allow_sib, gates_own, gates_sib, rows_own, rows_sib, mine),
    )

    gl = [grad_logits] + [rotate(grad_logits, step) for step in range(1, 4)]
    def tail(which, blk, state, allowed, gates, after):
        return call(
            functools.partial(tail_body, which), [shape((3 * TOK, 256), BF16), shape((8, DIM), F32)],
            (blk, state, near, allowed, gates, mine), after=after, cost=(4 * 10**9, 16 * 10**6),
        )

    out_sib, token = tail(1, sib, state_own, allow_sib, gates_sib, (grad_logits,))
    out_recv = sibling(out_sib)
    out_own, token = tail(0, own, state_sib, allow_own, gates_own, (token,))
    slices = call(
        gradw_body, shape((CHIPS, 16, DIM), F32), (layer_input, sib_input, *gl),
        scratch=[pltpu.VMEM((64, TOK), BF16), pltpu.VMEM((64, TOK), BF16), pltpu.VMEM((64, 1024), F32)],
        after=(token,),
    )
    got3 = exchange(slices)
    scale = 1.0 / math.sqrt(TOK * seq_count)
    w_half = exchange(call(functools.partial(mid3_body, scale), shape((CHIPS, 16, DIM), BF16), (got3,)))
    grads = call(
        place_body, [shape((TOK, 512), BF16)] * 3, (out_own, out_recv),
        out_specs=[hbm] * 3, scratch=[pltpu.SemaphoreType.DMA((6,))], after=(w_half,),
    )
    grad_weight = call(
        join_body, shape((1024, DIM), F32), (w_half, sibling(w_half)),
        out_specs=hbm,
        scratch=[pltpu.VMEM((DIM, DIM), F32), pltpu.VMEM((1024, DIM), F32), pltpu.SemaphoreType.DMA((2,))],
    )
    return (*grads, grad_weight)


def solution(mesh):
    placed = (
        P("seq", "head"),
        P("head", None),
        P("seq", "head"),
        P("seq", "head"),
        P("seq", "head"),
        P("seq", "head"),
        P("seq"),
    )
    return jax.shard_map(
        shards,
        mesh=mesh,
        in_specs=placed,
        out_specs=(P("seq", "head"), P("seq", "head"), P("seq", "head"), P("head", None)),
        check_vma=False,
    )
```

time: 109 us -> 101 us (0.927)
  blocking collectives: 44.7 us -> 50.2 us
  starting transfers between devices: 30.4 us -> 25 us
  local copies, waits for them, and re-layouts: 5.89 us -> 1.24 us
  Pallas kernels: 17.8 us -> 14.8 us
  waiting for transfers between devices: 9.25 us -> 8.13 us
    all_to_all x1, starting transfers between devices: 11.1 us -> 5.07 us  [exchange(): return lax.all_to_all(value, 'seq', 0, 0, axis_index_groups=groups)]
    all_to_all x3, blocking collectives: 44.7 us -> 50.2 us  [exchange(): return lax.all_to_all(value, 'seq', 0, 0, axis_index_groups=groups)]
    unnamed x32 -> x8, local copies, waits for them, and re-layouts: 5.89 us -> 1.24 us
    ppermute x6 -> x5, starting transfers between devices: 9.85 us -> 13.6 us  [sibling(): return lax.ppermute(value, 'seq', swap)]
    ppermute x6 -> x5, waiting for transfers between devices: 4.22 us -> 0.87 us  [sibling(): return lax.ppermute(value, 'seq', swap)]
    all_to_all x1, waiting for transfers between devices: 3.9 us -> 7.14 us  [exchange(): return lax.all_to_all(value, 'seq', 0, 0, axis_index_groups=groups)]
    ppermute x6, starting transfers between devices: 9.42 us -> 6.28 us  [rotate(): return lax.ppermute(value, 'head', [(h, (h + step) % 4) for h in range(4)])]
    pallas_call x14, Pallas kernels: 17.8 us -> 14.8 us  [call(): pl.pallas_call(kernel, out_shape=out_shape, grid=grid, in_specs=in_specs,...]
  transfers between devices with their start and end apart: 13 -> 12, of which waited for: 7 -> 3; matrix products, arithmetic and copies ran while one was open for 0% -> 0% of each run, Pallas kernels for 12% -> 7%
where the time goes in v4:
time: 101 us; the launch traced here: 100 us
  blocking collectives  50.2 us (50%)
  starting transfers between devices  25 us (25%)
  Pallas kernels  14.8 us (15%)
  waiting for transfers between devices  8.13 us (8%)
  local copies, waits for them, and re-layouts  1.24 us (1%)
    all_to_all x3, blocking collectives, exchange(): return lax.all_to_all(value, 'seq', 0, 0, axis_index_groups=groups)  50.2 us
    pallas_call x14, Pallas kernels, call(): pl.pallas_call(kernel, out_shape=out_shape, grid=grid, in_specs=in_specs,...  14.8 us
    ppermute x5, starting transfers between devices, sibling(): return lax.ppermute(value, 'seq', swap)  13.6 us
    all_to_all x1, waiting for transfers between devices, exchange(): return lax.all_to_all(value, 'seq', 0, 0, axis_index_groups=groups)  7.14 us
    ppermute x6, starting transfers between devices, rotate(): return lax.ppermute(value, 'head', [(h, (h + step) % 4) for h in range(4)])  6.28 us
    all_to_all x1, starting transfers between devices, exchange(): return lax.all_to_all(value, 'seq', 0, 0, axis_index_groups=groups)  5.07 us
  transfers between devices with their start and end apart: 12, of which 3 were waited for; matrix products, arithmetic and copies ran while one was open for 0% of the time, Pallas kernels for 7%

profile of v4, /device:TPU:1, one launch (start us, length us, event | category | flops | bytes accessed | tf_op | source)
XLA Modules:
  0.0 100.3 jit_solution(17697888913979035182)
XLA Ops:
  0.6 0.0 copy-start.2
  0.6 4.2 %shard_map.102 = (f32[32,512]{1,0:T(8,128)}, f32[32,512]{1,0:T(8,128)}, f32[32,512]{1,0:T(8,128)}, f32[32,512]{1,0:T(8,128)}, bf16[2064,256]{1,0:T(8,128)(2,1)}, /*index=5*/bf16[2064,256]{1,0:T(8,128)(2,1)}) custom-call(bf16[512,1024]{1,0:T(8,128)(2,1)} %refs_0_.3, bf16[1024,128]{1,0:T(8,128)(2,1)} %refs_1_.1, bf16[512,512]{1,0:T(8,128)(2,1)} %refs_2_.1, ...), custom_call_target="tpu_custom_call" | custom-call | flops 10000000 | bytes 1000000 | tf_op jit(solution)/shard_map/pallas_call | solution.py:46
  4.9 3.3 %collective-permute-start = (bf16[2064,256]{1,0:T(8,128)(2,1)}, bf16[2064,256]{1,0:T(8,128)(2,1)S(1)}, u32[]{:S(2)}, u32[]{:S(2)}) collective-permute-start(bf16[2064,256]{1,0:T(8,128)(2,1)} %get-tuple-element.32), channel_id=1, source_target_pairs={{0,4},{4,0},{8,12},{12,8},{16,20},{20,16},{24,28},{28,24},{32,36},... | collective-permute-start | bytes 3170312 | tf_op jit(solution)/shard_map/ppermute | solution.py:352
  8.2 0.0 copy-done.2
  8.2 0.1 collective-permute-start.5
  8.3 0.0 collective-permute-start.1
  8.3 2.2 %collective-permute-start.2 = (f32[32,512]{1,0:T(8,128)}, f32[32,512]{1,0:T(8,128)S(1)}, u32[]{:S(2)}, u32[]{:S(2)}) collective-permute-start(f32[32,512]{1,0:T(8,128)} %get-tuple-element.41), channel_id=1, source_target_pairs={{0,2},{1,3},{2,0},{3,1},{4,6},{5,7},{6,4},{7,5},{8,10},{9,11},{10,... | collective-permute-start | bytes 196616 | tf_op jit(solution)/shard_map/ppermute | solution.py:358
  10.5 1.1 %collective-permute-start.3 = (f32[32,512]{1,0:T(8,128)}, f32[32,512]{1,0:T(8,128)S(1)}, u32[]{:S(2)}, u32[]{:S(2)}) collective-permute-start(f32[32,512]{1,0:T(8,128)} %get-tuple-element.42), channel_id=1, source_target_pairs={{0,3},{1,0},{2,1},{3,2},{4,7},{5,4},{6,5},{7,6},{8,11},{9,8},{10,9... | collective-permute-start | bytes 196616 | tf_op jit(solution)/shard_map/ppermute | solution.py:358
  11.5 0.0 collective-permute-done.refs_1_.refs_0_
  11.5 0.0 copy-start
  11.6 1.2 %copy-done = bf16[2064,256]{1,0:T(8,128)(2,1)S(1)} copy-done((bf16[2064,256]{1,0:T(8,128)(2,1)S(1)}, bf16[2064,256]{1,0:T(8,128)(2,1)}, u32[]{:S(2)}) %copy-start) | copy-done | bytes 1056792
  12.8 0.5 shard_map.103
  13.3 0.0 copy-start.3
  13.3 0.0 copy-start.1
  13.3 1.2 %shard_map.104 = (f32[16,512]{1,0:T(8,128)S(1)}, f32[16,512]{1,0:T(8,128)S(1)}) custom-call(bf16[2064,256]{1,0:T(8,128)(2,1)S(1)} %copy-done, bf16[2064,256]{1,0:T(8,128)(2,1)S(1)} %collective-permute-done.refs_1_.refs_0_, bf16[256,512]{1,0:T(8,128)(2,1)S(1)} %get-tuple-element.34.refs_2_, bf16[256,512]{1,0:T(8,128)(2,1)S(1)} %get-tuple-element.35.refs_3_, ...), custom_call_target="tpu_custom_call" | custom-call | flops 10000000 | bytes 1000000 | tf_op jit(solution)/shard_map/pallas_call | solution.py:46
  14.5 0.0 collective-permute-done.1.refs_1_
  14.5 0.0 collective-permute-done.2.refs_2_
  14.5 0.1 collective-permute-done.3.refs_3_
  14.6 0.0 copy-done.3
  14.7 1.6 %collective-permute-start.4 = (f32[16,512]{1,0:T(8,128)S(1)}, f32[16,512]{1,0:T(8,128)S(1)}, u32[]{:S(2)}, u32[]{:S(2)}) collective-permute-start(f32[16,512]{1,0:T(8,128)S(1)} %get-tuple-element.45), channel_id=1, source_target_pairs={{0,4},{4,0},{8,12},{12,8},{16,20},{20,16},{24,28},{28,24},{32,36},... | collective-permute-start | bytes 98312 | tf_op jit(solution)/shard_map/ppermute | solution.py:352
  16.3 0.0 collective-permute-done.5.refs_10_.refs_1_
  16.3 0.9 collective-permute-done.4.refs_9_
  17.2 0.0 copy-done.1
  17.2 0.7 shard_map.106
  17.9 22.2 %all_to_all.20.refs_0_ = bf16[32,32,128]{2,1,0:T(8,128)(2,1)S(1)} all-to-all(bf16[32,32,128]{2,1,0:T(8,128)(2,1)S(1)} %get-tuple-element.48), channel_id=1, replica_groups={{0,8,16,24,32,40,48,56,64,72,80,88,96,104,112,120,128,136,144,152,160,1..., dimensions={0} | all-to-all | bytes 524288 | tf_op jit(solution)/shard_map/all_to_all | solution.py:355
  40.1 15.0 %all_to_all.21.refs_0_ = bf16[32,32,128]{2,1,0:T(8,128)(2,1)S(1)} all-to-all(bf16[32,32,128]{2,1,0:T(8,128)(2,1)S(1)} %shard_map.107), channel_id=1, replica_groups={{0,8,16,24,32,40,48,56,64,72,80,88,96,104,112,120,128,136,144,152,160,1..., dimensions={0} | all-to-all | bytes 524288 | tf_op jit(solution)/shard_map/all_to_all | solution.py:355
  55.1 0.6 shard_map.109.refs_6_.refs_2_
  55.7 2.4 %collective-permute-start.9 = (bf16[32,512]{1,0:T(8,128)(2,1)S(1)}, bf16[32,512]{1,0:T(8,128)(2,1)S(1)}, u32[]{:S(2)}, u32[]{:S(2)}) collective-permute-start(bf16[32,512]{1,0:T(8,128)(2,1)S(1)} %shard_map.109.refs_6_.refs_2_), channel_id=1, source_target_pairs={{0,3},{1,0},{2,1},{3,2},{4,7},{5,4},{6,5},{7,6},{8,11},{9,8},{10,9... | collective-permute-start | bytes 98312 | tf_op jit(solution)/shard_map/ppermute | solution.py:358
  58.1 0.0 collective-permute-start.8
  58.1 0.7 collective-permute-start.7
  58.8 2.0 %shard_map.110 = (bf16[1536,256]{1,0:T(8,128)(2,1)S(1)}, f32[8,128]{1,0:T(8,128)S(1)}) custom-call(bf16[2064,256]{1,0:T(8,128)(2,1)S(1)} %collective-permute-done.refs_1_.refs_0_, f32[256,128]{1,0:T(8,128)S(1)} %get-tuple-element.38.refs_4_.refs_6_.refs_1_, f32[256,128]{1,0:T(8,128)S(1)} %get-tuple-element.46.refs_2_, ...), custom_call_target="tpu_custom_call" | custom-call | flops 4000000000 | bytes 16000000 | tf_op jit(solution)/shard_map/pallas_call | solution.py:46
  60.8 2.0 %shard_map.111 = (bf16[1536,256]{1,0:T(8,128)(2,1)S(1)}, f32[8,128]{1,0:T(8,128)S(1)}) custom-call(bf16[2064,256]{1,0:T(8,128)(2,1)S(1)} %copy-done.1, f32[256,128]{1,0:T(8,128)S(1)} %get-tuple-element.33.refs_5_.refs_7_.refs_1_, f32[256,128]{1,0:T(8,128)S(1)} %get-tuple-element.46.refs_2_, f32[8,512]{1,0:T(8,128)S(1)} %get-tuple-element.36.refs_4_.refs_3_, ...), custom_call_target="tpu_custom_call" | custom-call | flops 4000000000 | bytes 16000000 | tf_op jit(solution)/shard_map/pallas_call | solution.py:46
  62.8 0.0 collective-permute-done.9.refs_5_
  62.8 0.0 collective-permute-done.8.refs_4_
  62.8 0.0 collective-permute-done.7.refs_3_
  62.8 1.2 %shard_map.112 = f32[32,16,128]{2,1,0:T(8,128)} custom-call(bf16[512,1024]{1,0:T(8,128)(2,1)S(1)} %copy-done.2, bf16[512,1024]{1,0:T(8,128)(2,1)S(1)} %collective-permute-done.5.refs_10_.refs_1_, bf16[32,512]{1,0:T(8,128)(2,1)S(1)} %shard_map.109.refs_6_.refs_2_, bf16[32,512]{1,0:T(8,128)(2,1)S(1)} %collective-permute-done.7.refs_3_, ...), custom_call_target="tpu_custom_call" | custom-call | flops 10000000 | bytes 1000000 | tf_op jit(solution)/shard_map/pallas_call | solution.py:46
  64.0 5.1 %all-to-all-start.2 = ((f32[32,16,128]{2,1,0:T(8,128)}), f32[32,16,128]{2,1,0:T(8,128)S(1)}, u32[]{:S(2)}, u32[]{:S(2)}) async-start(f32[32,16,128]{2,1,0:T(8,128)} %shard_map.112), calls=%async_computation.2 | async-start | bytes 524288 | tf_op jit(solution)/shard_map/all_to_all | solution.py:355
  69.1 3.3 %collective-permute-start.6 = (bf16[1536,256]{1,0:T(8,128)(2,1)S(1)}, bf16[1536,256]{1,0:T(8,128)(2,1)S(1)}, u32[]{:S(2)}, u32[]{:S(2)}) collective-permute-start(bf16[1536,256]{1,0:T(8,128)(2,1)S(1)} %get-tuple-element.53), channel_id=1, source_target_pairs={{0,4},{4,0},{8,12},{12,8},{16,20},{20,16},{24,28},{28,24},{32,36},... | collective-permute-start | bytes 2359304 | tf_op jit(solution)/shard_map/ppermute | solution.py:352
  72.4 7.1 %all-to-all-done.2.refs_0_ = f32[32,16,128]{2,1,0:T(8,128)S(1)} async-done(((f32[32,16,128]{2,1,0:T(8,128)}), f32[32,16,128]{2,1,0:T(8,128)S(1)}, u32[]{:S(2)}, u32[]{:S(2)}) %all-to-all-start.2) | async-done | bytes 262176 | tf_op jit(solution)/shard_map/all_to_all | solution.py:355
  79.5 13.0 %all_to_all.22.refs_2_.refs_0_ = bf16[32,16,128]{2,1,0:T(8,128)(2,1)S(1)} all-to-all(bf16[32,16,128]{2,1,0:T(8,128)(2,1)S(1)} %shard_map.113), channel_id=1, replica_groups={{0,8,16,24,32,40,48,56,64,72,80,88,96,104,112,120,128,136,144,152,160,1..., dimensions={0} | all-to-all | bytes 262144 | tf_op jit(solution)/shard_map/all_to_all | solution.py:355
  92.6 5.3 %collective-permute-start.10 = (bf16[32,16,128]{2,1,0:T(8,128)(2,1)S(1)}, bf16[32,16,128]{2,1,0:T(8,128)(2,1)S(1)}, u32[]{:S(2)}, u32[]{:S(2)}) collective-permute-start(bf16[32,16,128]{2,1,0:T(8,128)(2,1)S(1)} %all_to_all.22.refs_2_.refs_0_), channel_id=1, source_target_pairs={{0,4},{4,0},{8,12},{12,8},{16,20},{20,16},{24,28},{28,24},{32,36},... | collective-permute-start | bytes 393224 | tf_op jit(solution)/shard_map/ppermute | solution.py:352
  97.9 0.0 collective-permute-done.6.refs_1_
  97.9 1.2 %shard_map.114 = (bf16[512,512]{1,0:T(8,128)(2,1)}, bf16[512,512]{1,0:T(8,128)(2,1)}, bf16[512,512]{1,0:T(8,128)(2,1)}) custom-call(bf16[1536,256]{1,0:T(8,128)(2,1)S(1)} %get-tuple-element.52.refs_0_, bf16[1536,256]{1,0:T(8,128)(2,1)S(1)} %collective-permute-done.6.refs_1_, bf16[32,16,128]{2,1,0:T(8,128)(2,1)S(1)} %all_to_all.22.refs_2_.refs_0_), custom_call_target="tpu_custom_call" | custom-call | flops 10000000 | bytes 1000000 | tf_op jit(solution)/shard_map/pallas_call | solution.py:46
  99.1 0.0 collective-permute-done.10.refs_1_
  99.1 1.1 %shard_map.115 = f32[1024,128]{1,0:T(8,128)} custom-call(bf16[32,16,128]{2,1,0:T(8,128)(2,1)S(1)} %all_to_all.22.refs_2_.refs_0_, bf16[32,16,128]{2,1,0:T(8,128)(2,1)S(1)} %collective-permute-done.10.refs_1_), custom_call_target="tpu_custom_call" | custom-call | flops 10000000 | bytes 1000000 | tf_op jit(solution)/shard_map/pallas_call | solution.py:46
  (4 shorter events, 0.1 us)
Async XLA Ops:
  0.6 7.6 %copy-start.2 = (bf16[512,1024]{1,0:T(8,128)(2,1)S(1)}, bf16[512,1024]{1,0:T(8,128)(2,1)}, u32[]{:S(2)}) copy-start(bf16[512,1024]{1,0:T(8,128)(2,1)} %refs_0_.3) | copy-start | bytes 3145732
  4.9 6.7 %collective-permute-start = (bf16[2064,256]{1,0:T(8,128)(2,1)}, bf16[2064,256]{1,0:T(8,128)(2,1)S(1)}, u32[]{:S(2)}, u32[]{:S(2)}) collective-permute-start(bf16[2064,256]{1,0:T(8,128)(2,1)} %get-tuple-element.32), channel_id=1, source_target_pairs={{0,4},{4,0},{8,12},{12,8},{16,20},{20,16},{24,28},{28,24},{32,36},... | collective-permute-start | bytes 3170312 | tf_op jit(solution)/shard_map/ppermute | solution.py:352
  8.2 8.1 %collective-permute-start.5 = (bf16[512,1024]{1,0:T(8,128)(2,1)S(1)}, bf16[512,1024]{1,0:T(8,128)(2,1)S(1)}, u32[]{:S(2)}, u32[]{:S(2)}) collective-permute-start(bf16[512,1024]{1,0:T(8,128)(2,1)S(1)} %copy-done.2), channel_id=1, source_target_pairs={{0,4},{4,0},{8,12},{12,8},{16,20},{20,16},{24,28},{28,24},{32,36},... | collective-permute-start | bytes 3145736 | tf_op jit(solution)/shard_map/ppermute | solution.py:352
  8.3 6.2 %collective-permute-start.1 = (f32[32,512]{1,0:T(8,128)}, f32[32,512]{1,0:T(8,128)S(1)}, u32[]{:S(2)}, u32[]{:S(2)}) collective-permute-start(f32[32,512]{1,0:T(8,128)} %get-tuple-element.40), channel_id=1, source_target_pairs={{0,1},{1,2},{2,3},{3,0},{4,5},{5,6},{6,7},{7,4},{8,9},{9,10},{10,1... | collective-permute-start | bytes 196616 | tf_op jit(solution)/shard_map/ppermute | solution.py:358
  8.3 6.2 %collective-permute-start.2 = (f32[32,512]{1,0:T(8,128)}, f32[32,512]{1,0:T(8,128)S(1)}, u32[]{:S(2)}, u32[]{:S(2)}) collective-permute-start(f32[32,512]{1,0:T(8,128)} %get-tuple-element.41), channel_id=1, source_target_pairs={{0,2},{1,3},{2,0},{3,1},{4,6},{5,7},{6,4},{7,5},{8,10},{9,11},{10,... | collective-permute-start | bytes 196616 | tf_op jit(solution)/shard_map/ppermute | solution.py:358
  10.5 4.2 %collective-permute-start.3 = (f32[32,512]{1,0:T(8,128)}, f32[32,512]{1,0:T(8,128)S(1)}, u32[]{:S(2)}, u32[]{:S(2)}) collective-permute-start(f32[32,512]{1,0:T(8,128)} %get-tuple-element.42), channel_id=1, source_target_pairs={{0,3},{1,0},{2,1},{3,2},{4,7},{5,4},{6,5},{7,6},{8,11},{9,8},{10,9... | collective-permute-start | bytes 196616 | tf_op jit(solution)/shard_map/ppermute | solution.py:358
  11.5 1.2 %copy-start = (bf16[2064,256]{1,0:T(8,128)(2,1)S(1)}, bf16[2064,256]{1,0:T(8,128)(2,1)}, u32[]{:S(2)}) copy-start(bf16[2064,256]{1,0:T(8,128)(2,1)} %get-tuple-element.31.refs_0_) | copy-start | bytes 3170308
  13.3 1.4 %copy-start.3 = (f32[32,512]{1,0:T(8,128)S(1)}, f32[32,512]{1,0:T(8,128)}, u32[]{:S(2)}) copy-start(f32[32,512]{1,0:T(8,128)} %get-tuple-element.39.refs_0_) | copy-start | bytes 196612
  13.3 3.9 %copy-start.1 = (bf16[2064,256]{1,0:T(8,128)(2,1)S(1)}, bf16[2064,256]{1,0:T(8,128)(2,1)}, u32[]{:S(2)}) copy-start(bf16[2064,256]{1,0:T(8,128)(2,1)} %get-tuple-element.31.refs_0_) | copy-start | bytes 3170308
  14.7 2.5 %collective-permute-start.4 = (f32[16,512]{1,0:T(8,128)S(1)}, f32[16,512]{1,0:T(8,128)S(1)}, u32[]{:S(2)}, u32[]{:S(2)}) collective-permute-start(f32[16,512]{1,0:T(8,128)S(1)} %get-tuple-element.45), channel_id=1, source_target_pairs={{0,4},{4,0},{8,12},{12,8},{16,20},{20,16},{24,28},{28,24},{32,36},... | collective-permute-start | bytes 98312 | tf_op jit(solution)/shard_map/ppermute | solution.py:352
  55.7 7.1 %collective-permute-start.9 = (bf16[32,512]{1,0:T(8,128)(2,1)S(1)}, bf16[32,512]{1,0:T(8,128)(2,1)S(1)}, u32[]{:S(2)}, u32[]{:S(2)}) collective-permute-start(bf16[32,512]{1,0:T(8,128)(2,1)S(1)} %shard_map.109.refs_6_.refs_2_), channel_id=1, source_target_pairs={{0,3},{1,0},{2,1},{3,2},{4,7},{5,4},{6,5},{7,6},{8,11},{9,8},{10,9... | collective-permute-start | bytes 98312 | tf_op jit(solution)/shard_map/ppermute | solution.py:358
  58.1 4.7 %collective-permute-start.8 = (bf16[32,512]{1,0:T(8,128)(2,1)S(1)}, bf16[32,512]{1,0:T(8,128)(2,1)S(1)}, u32[]{:S(2)}, u32[]{:S(2)}) collective-permute-start(bf16[32,512]{1,0:T(8,128)(2,1)S(1)} %shard_map.109.refs_6_.refs_2_), channel_id=1, source_target_pairs={{0,2},{1,3},{2,0},{3,1},{4,6},{5,7},{6,4},{7,5},{8,10},{9,11},{10,... | collective-permute-start | bytes 98312 | tf_op jit(solution)/shard_map/ppermute | solution.py:358
  58.1 4.7 %collective-permute-start.7 = (bf16[32,512]{1,0:T(8,128)(2,1)S(1)}, bf16[32,512]{1,0:T(8,128)(2,1)S(1)}, u32[]{:S(2)}, u32[]{:S(2)}) collective-permute-start(bf16[32,512]{1,0:T(8,128)(2,1)S(1)} %shard_map.109.refs_6_.refs_2_), channel_id=1, source_target_pairs={{0,1},{1,2},{2,3},{3,0},{4,5},{5,6},{6,7},{7,4},{8,9},{9,10},{10,1... | collective-permute-start | bytes 98312 | tf_op jit(solution)/shard_map/ppermute | solution.py:358
  64.0 15.5 %all-to-all-start.2 = ((f32[32,16,128]{2,1,0:T(8,128)}), f32[32,16,128]{2,1,0:T(8,128)S(1)}, u32[]{:S(2)}, u32[]{:S(2)}) async-start(f32[32,16,128]{2,1,0:T(8,128)} %shard_map.112), calls=%async_computation.2 | async-start | bytes 524288 | tf_op jit(solution)/shard_map/all_to_all | solution.py:355
  69.1 28.8 %collective-permute-start.6 = (bf16[1536,256]{1,0:T(8,128)(2,1)S(1)}, bf16[1536,256]{1,0:T(8,128)(2,1)S(1)}, u32[]{:S(2)}, u32[]{:S(2)}) collective-permute-start(bf16[1536,256]{1,0:T(8,128)(2,1)S(1)} %get-tuple-element.53), channel_id=1, source_target_pairs={{0,4},{4,0},{8,12},{12,8},{16,20},{20,16},{24,28},{28,24},{32,36},... | collective-permute-start | bytes 2359304 | tf_op jit(solution)/shard_map/ppermute | solution.py:352
  92.6 6.5 %collective-permute-start.10 = (bf16[32,16,128]{2,1,0:T(8,128)(2,1)S(1)}, bf16[32,16,128]{2,1,0:T(8,128)(2,1)S(1)}, u32[]{:S(2)}, u32[]{:S(2)}) collective-permute-start(bf16[32,16,128]{2,1,0:T(8,128)(2,1)S(1)} %all_to_all.22.refs_2_.refs_0_), channel_id=1, source_target_pairs={{0,4},{4,0},{8,12},{12,8},{16,20},{20,16},{24,28},{28,24},{32,36},... | collective-permute-start | bytes 393224 | tf_op jit(solution)/shard_map/ppermute | solution.py:352

commit v5 on v4

--- a/solution.py
+++ b/solution.py
@@ -60,8 +60,8 @@
 
 
 def front_body(
-    x_hbm, w_hbm, q_hbm, k_hbm, v_hbm, g_hbm, reach_ref, p0, p1, p2, p3, own_hbm, leaving_hbm,
-    x_ref, w_ref, part_ref, own_ref, leaving_ref, in_sems, out_sems,
+    x_hbm, w_hbm, q_hbm, k_hbm, v_hbm, g_hbm, reach_hbm, p0, p1, p2, p3, own_hbm, leaving_hbm,
+    x_ref, w_ref, part_ref, own_ref, leaving_ref, reach_ref, in_sems, out_sems,
 ):
     head = lax.axis_index("head")
     core = lax.axis_index("seq") & 1
@@ -80,6 +80,13 @@
     for side, ref in ((1 - core, leaving_ref), (core, own_ref)):
         for i, src in enumerate((q_hbm, k_hbm, v_hbm, g_hbm)):
             load(src.at[:, aligned(side, 256)], ref.at[pl.ds(TOK * i, TOK), :])
+    load(reach_hbm, reach_ref)
+    ins[0].wait()
+    ins[1].wait()
+    part_ref[...] = mm(w_ref[...], x_ref[...], 0, 1)
+    for step, out in enumerate((p0, p1, p2, p3)):
+        store(part_ref.at[aligned(lax.rem(head + step, 4), 32), :], out)
+    ins[10].wait()
     lane = lax.broadcasted_iota(jnp.int32, (LEVELS, TOK), 1) // SPAN
     level = lax.broadcasted_iota(jnp.int32, (LEVELS, TOK), 0)
     reach = jnp.zeros((LEVELS, TOK), jnp.int32)
@@ -89,15 +96,10 @@
     allowed = jnp.concatenate([allowed[:, :256], allowed[:, 256:]], axis=0).astype(BF16)
     leaving_ref[4 * TOK :, :] = allowed
     own_ref[4 * TOK :, :] = allowed
-    ins[0].wait()
-    ins[1].wait()
-    part_ref[...] = mm(w_ref[...], x_ref[...], 0, 1)
-    for step, out in enumerate((p0, p1, p2, p3)):
-        store(part_ref.at[aligned(lax.rem(head + step, 4), 32), :], out)
     for copy in ins[2:6]:
         copy.wait()
     store(leaving_ref, leaving_hbm)
-    for copy in ins[6:]:
+    for copy in ins[6:10]:
         copy.wait()
     store(own_ref, own_hbm)
     for copy in outs:
@@ -115,12 +117,15 @@
 Q, K, V, G = (slice(TOK * i, TOK * (i + 1)) for i in range(4))
 
 
-def state_body(own_ref, sib_ref, so_ref, ss_ref, qto_ref, qts_ref, ao_ref, as_ref):
-    for ref, state, query_t, mask in ((own_ref, so_ref, qto_ref, ao_ref), (sib_ref, ss_ref, qts_ref, as_ref)):
+def state_body(own_ref, sib_ref, so_ref, ss_ref, qto_ref, qts_ref, kto_ref, kts_ref, ao_ref, as_ref):
+    for ref, state, query_t, key_t, mask in (
+        (own_ref, so_ref, qto_ref, kto_ref, ao_ref), (sib_ref, ss_ref, qts_ref, kts_ref, as_ref),
+    ):
         for i in range(2):
             lanes = slice(DIM * i, DIM * (i + 1))
             state[lanes, :] = mm(ref[K, lanes], ref[V, lanes], 0, 0) * INV
-            query_t[lanes, :] = ref[Q, lanes].astype(F32).T.astype(BF16)
+            query_t[lanes, :] = ref[Q, lanes].T
+            key_t[lanes, :] = ref[K, lanes].T
         allowed = ref[4 * TOK :, :].astype(F32)
         mask[...] = jnp.concatenate([allowed[:8], allowed[8:]], axis=1)
 
@@ -136,13 +141,13 @@
     ]
 
 
-def rows_body(own_ref, sib_ref, qto_ref, qts_ref, so_ref, ss_ref, ro_ref, rs_ref):
+def rows_body(own_ref, sib_ref, qto_ref, qts_ref, so_ref, ss_ref, ro_ref, rs_ref, sco_ref, pro_ref, scs_ref, prs_ref):
     core = lax.axis_index("seq") & 1
     masks = span_masks()
     none = jnp.zeros((1, 256), F32)
-    for block, (ref, query_t, state, out) in enumerate(
-        ((own_ref, qto_ref, ss_ref, ro_ref), (sib_ref, qts_ref, so_ref, rs_ref))
-    ):
+    for block, (ref, query_t, state, out, score_ref, prob_ref) in enumerate((
+        (own_ref, qto_ref, ss_ref, ro_ref, sco_ref, pro_ref), (sib_ref, qts_ref, so_ref, rs_ref, scs_ref, prs_ref),
+    )):
         upper = (core != block).astype(F32)
         for i in range(2):
             lanes = slice(DIM * i, DIM * (i + 1))
@@ -153,7 +158,11 @@
                 cols = slice(256 * a, 256 * a + 256)
                 end = 256 * a + 256
                 scores = mm(ref[TOK : TOK + end, lanes], ref[cols, lanes], 1, 1) * INV
-                prod = scores * mm(ref[2 * TOK : 2 * TOK + end, lanes], ref[3 * TOK + 256 * a : 3 * TOK + end, lanes], 1, 1)
+                probs = mm(ref[2 * TOK : 2 * TOK + end, lanes], ref[3 * TOK + 256 * a : 3 * TOK + end, lanes], 1, 1)
+                kept = slice(768 * i + 256 * a, 768 * i + 256 * a + end)
+                score_ref[kept, :] = scores
+                prob_ref[kept, :] = probs
+                prod = scores * probs
                 diagonal = prod[256 * a :]
                 sums = [jnp.sum(diagonal * mask, axis=0, keepdims=True) for mask in masks]
                 sums.append(jnp.sum(prod[:256], axis=0, keepdims=True) if a else none)
@@ -233,25 +242,33 @@
 
 
 def cross_body(
-    own_ref, sib_ref, qto_ref, qts_ref, ao_ref, as_ref, go_ref, gs_ref, ro_ref, rs_ref, mine_ref, gl_ref
+    own_ref, sib_ref, qto_ref, qts_ref, ao_ref, as_ref, go_ref, gs_ref, ro_ref, rs_ref, mine_ref, gl_ref, co_ref, cs_ref
 ):
     outs = []
-    for ref, query_t, mask, gates_ref, rows_ref in (
-        (own_ref, qto_ref, ao_ref, go_ref, ro_ref), (sib_ref, qts_ref, as_ref, gs_ref, rs_ref),
+    for ref, query_t, mask, gates_ref, rows_ref, cross_ref in (
+        (own_ref, qto_ref, ao_ref, go_ref, ro_ref, co_ref), (sib_ref, qts_ref, as_ref, gs_ref, rs_ref, cs_ref),
     ):
         for i in range(2):
             query = query_t[DIM * i : DIM * (i + 1), :].astype(F32)
-            parts = [jnp.zeros((5, TOK), F32)]
-            for term in far_projection(i, ref, mine_ref):
-                parts.append(jnp.sum(query * term, axis=0, keepdims=True))
             rows = slice(8 * i, 8 * i + 8)
             gates = gates_ref[rows, :]
+            weight = gates * mask[...]
+            parts = [jnp.zeros((5, TOK), F32)]
+            total = None
+            for level, term in enumerate(far_projection(i, ref, mine_ref)):
+                parts.append(jnp.sum(query * term, axis=0, keepdims=True))
+                weighted = weight[5 + level : 6 + level, :] * term
+                total = weighted if total is None else total + weighted
+            cross_ref[DIM * i : DIM * (i + 1), :] = total
             grads = (rows_ref[rows, :] + jnp.concatenate(parts, axis=0)) * mask[...]
             outs.append(grads * gates * (1.0 - gates))
     gl_ref[...] = jnp.concatenate(outs, axis=0).astype(BF16)
 
 
-def tail_body(block, blk_ref, state_ref, near_ref, mask_ref, gates_ref, mine_ref, out_ref, token_ref):
+def tail_body(
+    block, blk_ref, kt_ref, state_ref, near_ref, mask_ref, gates_ref, mine_ref, cross_ref, score_ref, prob_ref,
+    out_ref, token_ref,
+):
     core = lax.axis_index("seq") & 1
     masks = span_masks()
     upper = (core != block).astype(F32)
@@ -259,11 +276,7 @@
         lanes = slice(DIM * i, DIM * (i + 1))
         query, key, value, grad = blk_ref[Q, lanes], blk_ref[K, lanes], blk_ref[V, lanes], blk_ref[G, lanes]
         weight = gates_ref[8 * i : 8 * i + 8, :] * mask_ref[...]
-        key_t = key.astype(F32).T.astype(BF16)
-        states = [(state_ref[lanes, :] * upper).astype(BF16)]
-        for level in range(3):
-            states.append(mine_ref[256 * level + DIM * i : 256 * level + DIM * (i + 1), :])
-        projected = mm(jnp.concatenate(states, axis=0), grad, 1, 1)
+        near = mm((state_ref[lanes, :] * upper).astype(BF16), grad, 1, 1)
         later = mine_ref[768 + DIM * i : 768 + DIM * (i + 1), :].astype(F32)
         later = (later + near_ref[lanes, :] * (1.0 - upper)).astype(BF16)
         dk = mm(value, later, 1, 1)
@@ -271,15 +284,15 @@
         for a in range(2):
             cols = slice(256 * a, 256 * a + 256)
             end = 256 * a + 256
+            kept = slice(768 * i + 256 * a, 768 * i + 256 * a + end)
             pair = sum(weight[level : level + 1, cols] * masks[level] for level in range(3))
             if a:
                 pair = jnp.concatenate([jnp.broadcast_to(weight[3:4, cols], (256, 256)), pair], axis=0)
-            scored = (pair * (mm(key[:end], query[cols], 1, 1) * INV)).astype(BF16)
-            weighted = (pair * mm(value[:end], grad[cols], 1, 1)).astype(BF16)
-            total = mm(key_t[:, :end], weighted) * INV
-            for level in range(4):
-                total = total + weight[4 + level : 5 + level, cols] * projected[DIM * level : DIM * (level + 1), cols]
-            out_ref[cols, lanes] = total.T.astype(BF16)
+            scored = (pair * score_ref[kept, :]).astype(BF16)
+            weighted = (pair * prob_ref[kept, :]).astype(BF16)
+            total = mm(kt_ref[lanes, :end], weighted) * INV
+            total = total + weight[4:5, cols] * near[:, cols] + cross_ref[lanes, cols]
+            out_ref[cols, lanes] = total.astype(BF16).T
             more_k = mm(weighted, query[cols]) * INV
             more_v = mm(scored, grad[cols])
             if a:
@@ -301,19 +314,20 @@
     full[...] = mm(own_scr[...], xo_ref[...]) + mm(sib_scr[...], xs_ref[...])
     for chip in range(CHIPS):
         group, block = chip % 4, chip // 4
-        o_ref[chip] = full[16 * group : 16 * group + 16, DIM * block : DIM * (block + 1)]
+        o_ref[chip] = full[16 * group : 16 * group + 16, DIM * block : DIM * (block + 1)].astype(BF16)
 
 
 def mid3_body(scale, r_ref, o_ref):
-    total = r_ref[0]
+    total = r_ref[0].astype(F32)
     for chip in range(1, CHIPS):
-        total = total + r_ref[chip]
+        total = total + r_ref[chip].astype(F32)
     total = (total * scale).astype(BF16)
     for chip in range(CHIPS):
         o_ref[chip] = total
 
 
-def place_body(own_ref, recv_ref, dq_hbm, dk_hbm, dv_hbm, sems):
+def place_body(own_ref, recv_ref, dq_hbm, dk_hbm, dv_hbm, token_ref, sems):
+    token_ref[...] = jnp.zeros_like(token_ref)
     core = lax.axis_index("seq") & 1
     copies = []
     for i, out in enumerate((dq_hbm, dk_hbm, dv_hbm)):
@@ -358,7 +372,6 @@
         return lax.ppermute(value, "head", [(h, (h + step) % 4) for h in range(4)])
 
     whole = pl.BlockSpec(memory_space=pltpu.VMEM)
-    smem = pl.BlockSpec(memory_space=pltpu.SMEM)
     hbm = pl.BlockSpec(memory_space=pl.ANY)
 
     tok16 = shape((16, TOK), F32)
@@ -369,23 +382,24 @@
         front_body,
         [shape((32, TOK), F32)] * 4 + [shape((4 * TOK + 16, 256), BF16)] * 2,
         (layer_input, gate_weight, queries, key_vectors, value_vectors, grad_output, reach_level),
-        in_specs=[hbm] * 6 + [smem],
+        in_specs=[hbm] * 7,
         out_specs=[hbm] * 6,
         scratch=[
             pltpu.VMEM((TOK, 1024), BF16), pltpu.VMEM((1024, DIM), BF16), pltpu.VMEM((DIM, TOK), F32),
             pltpu.VMEM((4 * TOK + 16, 256), BF16), pltpu.VMEM((4 * TOK + 16, 256), BF16),
-            pltpu.SemaphoreType.DMA((10,)), pltpu.SemaphoreType.DMA((6,)),
+            pltpu.SMEM((LEVELS,), jnp.int32), pltpu.SemaphoreType.DMA((11,)), pltpu.SemaphoreType.DMA((6,)),
         ],
         limit=VMEM_ALL,
     )
     logits = [parts[0]] + [rotate(parts[step], step) for step in range(1, 4)]
     sib = sibling(leaving)
     sib_input = sibling(layer_input)
-    state_own, state_sib, qt_own, qt_sib, allow_own, allow_sib = call(
-        state_body, [half, half, shape((256, TOK), BF16), shape((256, TOK), BF16), mask8, mask8], (own, sib)
-    )
-    rows_own, rows_sib = call(
-        rows_body, [tok16, tok16], (own, sib, qt_own, qt_sib, state_own, state_sib)
+    state_own, state_sib, qt_own, qt_sib, kt_own, kt_sib, allow_own, allow_sib = call(
+        state_body, [half, half] + [shape((256, TOK), BF16)] * 4 + [mask8, mask8], (own, sib)
+    )
+    pairs = shape((1536, 256), F32)
+    rows_own, rows_sib, sc_own, pr_own, sc_sib, pr_sib = call(
+        rows_body, [tok16, tok16] + [pairs] * 4, (own, sib, qt_own, qt_sib, state_own, state_sib)
     )
     logits_own, logits_send = call(gather_body, [tok16, tok16], tuple(logits), after=(rows_own,))
 
@@ -399,36 +413,38 @@
 
     got2 = exchange(call(mid1_body, shape((CHIPS, 32, DIM), BF16), (got1,)))
     mine = call(mid2_body, shape((1024, DIM), BF16), (got2,))
-    grad_logits = call(
-        cross_body, shape((32, TOK), BF16),
+    tok256 = shape((256, TOK), F32)
+    grad_logits, cross_own, cross_sib = call(
+        cross_body, [shape((32, TOK), BF16), tok256, tok256],
         (own, sib, qt_own, qt_sib, allow_own, allow_sib, gates_own, gates_sib, rows_own, rows_sib, mine),
     )
 
     gl = [grad_logits] + [rotate(grad_logits, step) for step in range(1, 4)]
-    def tail(which, blk, state, allowed, gates, after):
+    def tail(which, blk, key_t, state, allowed, gates, cross, scores, probs, after):
         return call(
             functools.partial(tail_body, which), [shape((3 * TOK, 256), BF16), shape((8, DIM), F32)],
-            (blk, state, near, allowed, gates, mine), after=after, cost=(4 * 10**9, 16 * 10**6),
+            (blk, key_t, state, near, allowed, gates, mine, cross, scores, probs), after=after, cost=(4 * 10**9, 16 * 10**6),
         )
 
-    out_sib, token = tail(1, sib, state_own, allow_sib, gates_sib, (grad_logits,))
+    out_sib, token = tail(1, sib, kt_sib, state_own, allow_sib, gates_sib, cross_sib, sc_sib, pr_sib, (grad_logits,))
     out_recv = sibling(out_sib)
-    out_own, token = tail(0, own, state_sib, allow_own, gates_own, (token,))
+    out_own, token = tail(0, own, kt_own, state_sib, allow_own, gates_own, cross_own, sc_own, pr_own, (token,))
     slices = call(
-        gradw_body, shape((CHIPS, 16, DIM), F32), (layer_input, sib_input, *gl),
+        gradw_body, shape((CHIPS, 16, DIM), BF16), (layer_input, sib_input, *gl),
         scratch=[pltpu.VMEM((64, TOK), BF16), pltpu.VMEM((64, TOK), BF16), pltpu.VMEM((64, 1024), F32)],
         after=(token,),
     )
     got3 = exchange(slices)
     scale = 1.0 / math.sqrt(TOK * seq_count)
     w_half = exchange(call(functools.partial(mid3_body, scale), shape((CHIPS, 16, DIM), BF16), (got3,)))
-    grads = call(
-        place_body, [shape((TOK, 512), BF16)] * 3, (out_own, out_recv),
-        out_specs=[hbm] * 3, scratch=[pltpu.SemaphoreType.DMA((6,))], after=(w_half,),
+    *grads, token = call(
+        place_body, [shape((TOK, 512), BF16)] * 3 + [shape((8, DIM), F32)], (out_own, out_recv),
+        out_specs=[hbm] * 3 + [whole], scratch=[pltpu.SemaphoreType.DMA((6,))], after=(w_half,),
     )
     grad_weight = call(
         join_body, shape((1024, DIM), F32), (w_half, sibling(w_half)),
         out_specs=hbm,
+        after=(token,),
         scratch=[pltpu.VMEM((DIM, DIM), F32), pltpu.VMEM((1024, DIM), F32), pltpu.SemaphoreType.DMA((2,))],
     )
     return (*grads, grad_weight)

time: 101 us -> 97.8 us (0.968)
  blocking collectives: 50.2 us -> 62.5 us
  waiting for transfers between devices: 8.13 us -> 1 us
  starting transfers between devices: 25 us -> 20.3 us
  Pallas kernels: 14.8 us -> 11.6 us
    all_to_all x3 -> x4, blocking collectives: 50.2 us -> 62.5 us  [exchange(): return lax.all_to_all(value, 'seq', 0, 0, axis_index_groups=groups)]
    all_to_all x1 -> x0, waiting for transfers between devices: 7.14 us -> none  [exchange(): return lax.all_to_all(value, 'seq', 0, 0, axis_index_groups=groups)]
    all_to_all x1 -> x0, starting transfers between devices: 5.07 us -> none  [exchange(): return lax.all_to_all(value, 'seq', 0, 0, axis_index_groups=groups)]
    pallas_call x14, Pallas kernels: 14.8 us -> 11.6 us  [call(): pl.pallas_call(kernel, out_shape=out_shape, grid=grid, in_specs=in_specs,...]
  transfers between devices with their start and end apart: 12 -> 11, of which waited for: 3 -> 2; matrix products, arithmetic and copies ran while one was open for 0% -> 0% of each run, Pallas kernels for 7% -> 6%
where the time goes in v5:
time: 97.8 us; the launch traced here: 97.5 us
  blocking collectives  62.5 us (64%)
  starting transfers between devices  20.3 us (21%)
  Pallas kernels  11.6 us (12%)
  local copies, waits for them, and re-layouts  1.24 us (1%)
  waiting for transfers between devices  1 us (1%)
    all_to_all x4, blocking collectives, exchange(): return lax.all_to_all(value, 'seq', 0, 0, axis_index_groups=groups)  62.5 us
    ppermute x5, starting transfers between devices, sibling(): return lax.ppermute(value, 'seq', swap)  13.4 us
    pallas_call x14, Pallas kernels, call(): pl.pallas_call(kernel, out_shape=out_shape, grid=grid, in_specs=in_specs,...  11.6 us
    ppermute x6, starting transfers between devices, rotate(): return lax.ppermute(value, 'head', [(h, (h + step) % 4) for h in range(4)])  6.87 us
  transfers between devices with their start and end apart: 11, of which 2 were waited for; matrix products, arithmetic and copies ran while one was open for 0% of the time, Pallas kernels for 6%

profile of v5, /device:TPU:1, one launch (start us, length us, event | category | flops | bytes accessed | tf_op | source)
XLA Modules:
  0.0 97.5 jit_solution(387171409092373451)
XLA Ops:
  0.6 0.0 copy-start.2
  0.6 3.5 %shard_map.102 = (f32[32,512]{1,0:T(8,128)}, f32[32,512]{1,0:T(8,128)}, f32[32,512]{1,0:T(8,128)}, f32[32,512]{1,0:T(8,128)}, bf16[2064,256]{1,0:T(8,128)(2,1)}, /*index=5*/bf16[2064,256]{1,0:T(8,128)(2,1)}) custom-call(bf16[512,1024]{1,0:T(8,128)(2,1)} %refs_0_.3, bf16[1024,128]{1,0:T(8,128)(2,1)} %refs_1_.1, bf16[512,512]{1,0:T(8,128)(2,1)} %refs_2_.1, ...), custom_call_target="tpu_custom_call" | custom-call | flops 10000000 | bytes 1000000 | tf_op jit(solution)/shard_map/pallas_call | solution.py:46
  4.2 3.3 %collective-permute-start = (bf16[2064,256]{1,0:T(8,128)(2,1)}, bf16[2064,256]{1,0:T(8,128)(2,1)S(1)}, u32[]{:S(2)}, u32[]{:S(2)}) collective-permute-start(bf16[2064,256]{1,0:T(8,128)(2,1)} %get-tuple-element.42), channel_id=1, source_target_pairs={{0,4},{4,0},{8,12},{12,8},{16,20},{20,16},{24,28},{28,24},{32,36},... | collective-permute-start | bytes 3170312 | tf_op jit(solution)/shard_map/ppermute | solution.py:366
  7.5 0.0 copy-done.2
  7.5 0.1 collective-permute-start.5
  7.6 0.0 collective-permute-start.1
  7.6 2.2 %collective-permute-start.2 = (f32[32,512]{1,0:T(8,128)}, f32[32,512]{1,0:T(8,128)S(1)}, u32[]{:S(2)}, u32[]{:S(2)}) collective-permute-start(f32[32,512]{1,0:T(8,128)} %get-tuple-element.52), channel_id=1, source_target_pairs={{0,2},{1,3},{2,0},{3,1},{4,6},{5,7},{6,4},{7,5},{8,10},{9,11},{10,... | collective-permute-start | bytes 196616 | tf_op jit(solution)/shard_map/ppermute | solution.py:372
  9.8 1.1 %collective-permute-start.3 = (f32[32,512]{1,0:T(8,128)}, f32[32,512]{1,0:T(8,128)S(1)}, u32[]{:S(2)}, u32[]{:S(2)}) collective-permute-start(f32[32,512]{1,0:T(8,128)} %get-tuple-element.53), channel_id=1, source_target_pairs={{0,3},{1,0},{2,1},{3,2},{4,7},{5,4},{6,5},{7,6},{8,11},{9,8},{10,9... | collective-permute-start | bytes 196616 | tf_op jit(solution)/shard_map/ppermute | solution.py:372
  10.9 0.0 collective-permute-done.refs_1_.refs_0_
  10.9 0.0 copy-start
  10.9 1.2 %copy-done = bf16[2064,256]{1,0:T(8,128)(2,1)S(1)} copy-done((bf16[2064,256]{1,0:T(8,128)(2,1)S(1)}, bf16[2064,256]{1,0:T(8,128)(2,1)}, u32[]{:S(2)}) %copy-start) | copy-done | bytes 1056792
  12.1 0.5 shard_map.103
  12.6 0.0 copy-start.3
  12.6 0.0 copy-start.1
  12.6 1.2 %shard_map.104 = (f32[16,512]{1,0:T(8,128)S(1)}, f32[16,512]{1,0:T(8,128)S(1)}, f32[1536,256]{1,0:T(8,128)S(1)}, f32[1536,256]{1,0:T(8,128)S(1)}, f32[1536,256]{1,0:T(8,128)S(1)}, /*index=5*/f32[1536,256]{1,0:T(8,128)S(1)}) custom-call(bf16[2064,256]{1,0:T(8,128)(2,1)S(1)} %copy-done, bf16[2064,256]{1,0:T(8,128)(2,1)S(1)} %collective-permute-done.refs_1_.refs_0_, ...), custom_call_target="tpu_custom_call" | custom-call | flops 10000000 | bytes 1000000 | tf_op jit(solution)/shard_map/pallas_call | solution.py:46
  13.8 0.0 collective-permute-done.1.refs_1_
  13.8 0.0 collective-permute-done.2.refs_2_
  13.9 0.1 collective-permute-done.3.refs_3_
  14.0 0.0 copy-done.3
  14.0 1.6 %collective-permute-start.4 = (f32[16,512]{1,0:T(8,128)S(1)}, f32[16,512]{1,0:T(8,128)S(1)}, u32[]{:S(2)}, u32[]{:S(2)}) collective-permute-start(f32[16,512]{1,0:T(8,128)S(1)} %get-tuple-element.56), channel_id=1, source_target_pairs={{0,4},{4,0},{8,12},{12,8},{16,20},{20,16},{24,28},{28,24},{32,36},... | collective-permute-start | bytes 98312 | tf_op jit(solution)/shard_map/ppermute | solution.py:366
  15.6 0.0 collective-permute-done.5.refs_10_.refs_1_
  15.6 0.9 collective-permute-done.4.refs_9_
  16.5 0.0 copy-done.1
  16.5 0.7 shard_map.106
  17.2 22.2 %all_to_all.20.refs_0_ = bf16[32,32,128]{2,1,0:T(8,128)(2,1)S(1)} all-to-all(bf16[32,32,128]{2,1,0:T(8,128)(2,1)S(1)} %get-tuple-element.59), channel_id=1, replica_groups={{0,8,16,24,32,40,48,56,64,72,80,88,96,104,112,120,128,136,144,152,160,1..., dimensions={0} | all-to-all | bytes 524288 | tf_op jit(solution)/shard_map/all_to_all | solution.py:369
  39.4 15.0 %all_to_all.21.refs_0_ = bf16[32,32,128]{2,1,0:T(8,128)(2,1)S(1)} all-to-all(bf16[32,32,128]{2,1,0:T(8,128)(2,1)S(1)} %shard_map.107), channel_id=1, replica_groups={{0,8,16,24,32,40,48,56,64,72,80,88,96,104,112,120,128,136,144,152,160,1..., dimensions={0} | all-to-all | bytes 524288 | tf_op jit(solution)/shard_map/all_to_all | solution.py:369
  54.5 0.7 shard_map.109
  55.2 0.4 collective-permute-start.7
  55.5 3.2 %collective-permute-start.8 = (bf16[32,512]{1,0:T(8,128)(2,1)S(1)}, bf16[32,512]{1,0:T(8,128)(2,1)S(1)}, u32[]{:S(2)}, u32[]{:S(2)}) collective-permute-start(bf16[32,512]{1,0:T(8,128)(2,1)S(1)} %get-tuple-element.69.refs_10_.refs_2_), channel_id=1, source_target_pairs={{0,2},{1,3},{2,0},{3,1},{4,6},{5,7},{6,4},{7,5},{8,10},{9,11},{10,... | collective-permute-start | bytes 98312 | tf_op jit(solution)/shard_map/ppermute | solution.py:372
  58.7 0.1 collective-permute-start.9
  58.8 1.1 %shard_map.110 = (bf16[1536,256]{1,0:T(8,128)(2,1)S(1)}, f32[8,128]{1,0:T(8,128)S(1)}) custom-call(bf16[2064,256]{1,0:T(8,128)(2,1)S(1)} %collective-permute-done.refs_1_.refs_0_, bf16[256,512]{1,0:T(8,128)(2,1)S(1)} %get-tuple-element.65.refs_1_, f32[256,128]{1,0:T(8,128)S(1)} %get-tuple-element.49.refs_4_.refs_6_.refs_2_, ...), custom_call_target="tpu_custom_call" | custom-call | flops 4000000000 | bytes 16000000 | tf_op jit(solution)/shard_map/pallas_call | solution.py:46
  59.9 4.4 %collective-permute-start.6 = (bf16[1536,256]{1,0:T(8,128)(2,1)S(1)}, bf16[1536,256]{1,0:T(8,128)(2,1)S(1)}, u32[]{:S(2)}, u32[]{:S(2)}) collective-permute-start(bf16[1536,256]{1,0:T(8,128)(2,1)S(1)} %get-tuple-element.72), channel_id=1, source_target_pairs={{0,4},{4,0},{8,12},{12,8},{16,20},{20,16},{24,28},{28,24},{32,36},... | collective-permute-start | bytes 2359304 | tf_op jit(solution)/shard_map/ppermute | solution.py:366
  64.3 0.9 shard_map.111
  65.2 0.0 collective-permute-done.7.refs_3_
  65.2 0.0 collective-permute-done.8.refs_4_
  65.2 0.0 collective-permute-done.9.refs_5_
  65.2 0.5 shard_map.112
  65.7 12.7 %all_to_all.22.refs_0_ = bf16[32,16,128]{2,1,0:T(8,128)(2,1)S(1)} all-to-all(bf16[32,16,128]{2,1,0:T(8,128)(2,1)S(1)} %shard_map.112), channel_id=1, replica_groups={{0,8,16,24,32,40,48,56,64,72,80,88,96,104,112,120,128,136,144,152,160,1..., dimensions={0} | all-to-all | bytes 262144 | tf_op jit(solution)/shard_map/all_to_all | solution.py:369
  78.5 12.6 %all_to_all.23.refs_2_.refs_0_ = bf16[32,16,128]{2,1,0:T(8,128)(2,1)S(1)} all-to-all(bf16[32,16,128]{2,1,0:T(8,128)(2,1)S(1)} %shard_map.113), channel_id=1, replica_groups={{0,8,16,24,32,40,48,56,64,72,80,88,96,104,112,120,128,136,144,152,160,1..., dimensions={0} | all-to-all | bytes 262144 | tf_op jit(solution)/shard_map/all_to_all | solution.py:369
  91.1 3.9 %collective-permute-start.10 = (bf16[32,16,128]{2,1,0:T(8,128)(2,1)S(1)}, bf16[32,16,128]{2,1,0:T(8,128)(2,1)S(1)}, u32[]{:S(2)}, u32[]{:S(2)}) collective-permute-start(bf16[32,16,128]{2,1,0:T(8,128)(2,1)S(1)} %all_to_all.23.refs_2_.refs_0_), channel_id=1, source_target_pairs={{0,4},{4,0},{8,12},{12,8},{16,20},{20,16},{24,28},{28,24},{32,36},... | collective-permute-start | bytes 393224 | tf_op jit(solution)/shard_map/ppermute | solution.py:366
  95.1 0.0 collective-permute-done.6.refs_1_
  95.1 1.2 %shard_map.114 = (bf16[512,512]{1,0:T(8,128)(2,1)}, bf16[512,512]{1,0:T(8,128)(2,1)}, bf16[512,512]{1,0:T(8,128)(2,1)}, f32[8,128]{1,0:T(8,128)S(1)}) custom-call(bf16[1536,256]{1,0:T(8,128)(2,1)S(1)} %get-tuple-element.71.refs_0_, bf16[1536,256]{1,0:T(8,128)(2,1)S(1)} %collective-permute-done.6.refs_1_, bf16[32,16,128]{2,1,0:T(8,128)(2,1)S(1)} %all_to_all.23.refs_2_.refs_0_), custom_call_target="tpu_custom_call" | custom-call | flops 10000000 | bytes 1000000 | tf_op jit(solution)/shard_map/pallas_call | solution.py:46
  96.3 0.0 collective-permute-done.10.refs_1_
  96.3 1.1 %shard_map.115 = f32[1024,128]{1,0:T(8,128)} custom-call(bf16[32,16,128]{2,1,0:T(8,128)(2,1)S(1)} %all_to_all.23.refs_2_.refs_0_, bf16[32,16,128]{2,1,0:T(8,128)(2,1)S(1)} %collective-permute-done.10.refs_1_, f32[8,128]{1,0:T(8,128)S(1)} %get-tuple-element.77.refs_2_), custom_call_target="tpu_custom_call" | custom-call | flops 10000000 | bytes 1000000 | tf_op jit(solution)/shard_map/pallas_call | solution.py:46
  (4 shorter events, 0.1 us)
Async XLA Ops:
  0.6 6.9 %copy-start.2 = (bf16[512,1024]{1,0:T(8,128)(2,1)S(1)}, bf16[512,1024]{1,0:T(8,128)(2,1)}, u32[]{:S(2)}) copy-start(bf16[512,1024]{1,0:T(8,128)(2,1)} %refs_0_.3) | copy-start | bytes 3145732
  4.2 6.7 %collective-permute-start = (bf16[2064,256]{1,0:T(8,128)(2,1)}, bf16[2064,256]{1,0:T(8,128)(2,1)S(1)}, u32[]{:S(2)}, u32[]{:S(2)}) collective-permute-start(bf16[2064,256]{1,0:T(8,128)(2,1)} %get-tuple-element.42), channel_id=1, source_target_pairs={{0,4},{4,0},{8,12},{12,8},{16,20},{20,16},{24,28},{28,24},{32,36},... | collective-permute-start | bytes 3170312 | tf_op jit(solution)/shard_map/ppermute | solution.py:366
  7.5 8.1 %collective-permute-start.5 = (bf16[512,1024]{1,0:T(8,128)(2,1)S(1)}, bf16[512,1024]{1,0:T(8,128)(2,1)S(1)}, u32[]{:S(2)}, u32[]{:S(2)}) collective-permute-start(bf16[512,1024]{1,0:T(8,128)(2,1)S(1)} %copy-done.2), channel_id=1, source_target_pairs={{0,4},{4,0},{8,12},{12,8},{16,20},{20,16},{24,28},{28,24},{32,36},... | collective-permute-start | bytes 3145736 | tf_op jit(solution)/shard_map/ppermute | solution.py:366
  7.6 6.2 %collective-permute-start.1 = (f32[32,512]{1,0:T(8,128)}, f32[32,512]{1,0:T(8,128)S(1)}, u32[]{:S(2)}, u32[]{:S(2)}) collective-permute-start(f32[32,512]{1,0:T(8,128)} %get-tuple-element.51), channel_id=1, source_target_pairs={{0,1},{1,2},{2,3},{3,0},{4,5},{5,6},{6,7},{7,4},{8,9},{9,10},{10,1... | collective-permute-start | bytes 196616 | tf_op jit(solution)/shard_map/ppermute | solution.py:372
  7.6 6.2 %collective-permute-start.2 = (f32[32,512]{1,0:T(8,128)}, f32[32,512]{1,0:T(8,128)S(1)}, u32[]{:S(2)}, u32[]{:S(2)}) collective-permute-start(f32[32,512]{1,0:T(8,128)} %get-tuple-element.52), channel_id=1, source_target_pairs={{0,2},{1,3},{2,0},{3,1},{4,6},{5,7},{6,4},{7,5},{8,10},{9,11},{10,... | collective-permute-start | bytes 196616 | tf_op jit(solution)/shard_map/ppermute | solution.py:372
  9.8 4.2 %collective-permute-start.3 = (f32[32,512]{1,0:T(8,128)}, f32[32,512]{1,0:T(8,128)S(1)}, u32[]{:S(2)}, u32[]{:S(2)}) collective-permute-start(f32[32,512]{1,0:T(8,128)} %get-tuple-element.53), channel_id=1, source_target_pairs={{0,3},{1,0},{2,1},{3,2},{4,7},{5,4},{6,5},{7,6},{8,11},{9,8},{10,9... | collective-permute-start | bytes 196616 | tf_op jit(solution)/shard_map/ppermute | solution.py:372
  10.9 1.2 %copy-start = (bf16[2064,256]{1,0:T(8,128)(2,1)S(1)}, bf16[2064,256]{1,0:T(8,128)(2,1)}, u32[]{:S(2)}) copy-start(bf16[2064,256]{1,0:T(8,128)(2,1)} %get-tuple-element.41.refs_0_) | copy-start | bytes 3170308
  12.6 1.4 %copy-start.3 = (f32[32,512]{1,0:T(8,128)S(1)}, f32[32,512]{1,0:T(8,128)}, u32[]{:S(2)}) copy-start(f32[32,512]{1,0:T(8,128)} %get-tuple-element.50.refs_0_) | copy-start | bytes 196612
  12.6 3.9 %copy-start.1 = (bf16[2064,256]{1,0:T(8,128)(2,1)S(1)}, bf16[2064,256]{1,0:T(8,128)(2,1)}, u32[]{:S(2)}) copy-start(bf16[2064,256]{1,0:T(8,128)(2,1)} %get-tuple-element.41.refs_0_) | copy-start | bytes 3170308
  14.0 2.5 %collective-permute-start.4 = (f32[16,512]{1,0:T(8,128)S(1)}, f32[16,512]{1,0:T(8,128)S(1)}, u32[]{:S(2)}, u32[]{:S(2)}) collective-permute-start(f32[16,512]{1,0:T(8,128)S(1)} %get-tuple-element.56), channel_id=1, source_target_pairs={{0,4},{4,0},{8,12},{12,8},{16,20},{20,16},{24,28},{28,24},{32,36},... | collective-permute-start | bytes 98312 | tf_op jit(solution)/shard_map/ppermute | solution.py:366
  55.2 10.1 %collective-permute-start.7 = (bf16[32,512]{1,0:T(8,128)(2,1)S(1)}, bf16[32,512]{1,0:T(8,128)(2,1)S(1)}, u32[]{:S(2)}, u32[]{:S(2)}) collective-permute-start(bf16[32,512]{1,0:T(8,128)(2,1)S(1)} %get-tuple-element.69.refs_10_.refs_2_), channel_id=1, source_target_pairs={{0,1},{1,2},{2,3},{3,0},{4,5},{5,6},{6,7},{7,4},{8,9},{9,10},{10,1... | collective-permute-start | bytes 98312 | tf_op jit(solution)/shard_map/ppermute | solution.py:372
  55.5 9.7 %collective-permute-start.8 = (bf16[32,512]{1,0:T(8,128)(2,1)S(1)}, bf16[32,512]{1,0:T(8,128)(2,1)S(1)}, u32[]{:S(2)}, u32[]{:S(2)}) collective-permute-start(bf16[32,512]{1,0:T(8,128)(2,1)S(1)} %get-tuple-element.69.refs_10_.refs_2_), channel_id=1, source_target_pairs={{0,2},{1,3},{2,0},{3,1},{4,6},{5,7},{6,4},{7,5},{8,10},{9,11},{10,... | collective-permute-start | bytes 98312 | tf_op jit(solution)/shard_map/ppermute | solution.py:372
  58.7 6.5 %collective-permute-start.9 = (bf16[32,512]{1,0:T(8,128)(2,1)S(1)}, bf16[32,512]{1,0:T(8,128)(2,1)S(1)}, u32[]{:S(2)}, u32[]{:S(2)}) collective-permute-start(bf16[32,512]{1,0:T(8,128)(2,1)S(1)} %get-tuple-element.69.refs_10_.refs_2_), channel_id=1, source_target_pairs={{0,3},{1,0},{2,1},{3,2},{4,7},{5,4},{6,5},{7,6},{8,11},{9,8},{10,9... | collective-permute-start | bytes 98312 | tf_op jit(solution)/shard_map/ppermute | solution.py:372
  59.9 35.2 %collective-permute-start.6 = (bf16[1536,256]{1,0:T(8,128)(2,1)S(1)}, bf16[1536,256]{1,0:T(8,128)(2,1)S(1)}, u32[]{:S(2)}, u32[]{:S(2)}) collective-permute-start(bf16[1536,256]{1,0:T(8,128)(2,1)S(1)} %get-tuple-element.72), channel_id=1, source_target_pairs={{0,4},{4,0},{8,12},{12,8},{16,20},{20,16},{24,28},{28,24},{32,36},... | collective-permute-start | bytes 2359304 | tf_op jit(solution)/shard_map/ppermute | solution.py:366
  91.1 5.1 %collective-permute-start.10 = (bf16[32,16,128]{2,1,0:T(8,128)(2,1)S(1)}, bf16[32,16,128]{2,1,0:T(8,128)(2,1)S(1)}, u32[]{:S(2)}, u32[]{:S(2)}) collective-permute-start(bf16[32,16,128]{2,1,0:T(8,128)(2,1)S(1)} %all_to_all.23.refs_2_.refs_0_), channel_id=1, source_target_pairs={{0,4},{4,0},{8,12},{12,8},{16,20},{20,16},{24,28},{28,24},{32,36},... | collective-permute-start | bytes 393224 | tf_op jit(solution)/shard_map/ppermute | solution.py:366

commit v6 on v5

--- a/solution.py
+++ b/solution.py
@@ -117,7 +117,7 @@
 Q, K, V, G = (slice(TOK * i, TOK * (i + 1)) for i in range(4))
 
 
-def state_body(own_ref, sib_ref, so_ref, ss_ref, qto_ref, qts_ref, kto_ref, kts_ref, ao_ref, as_ref):
+def state_body(own_ref, sib_ref, so_ref, ss_ref, qto_ref, qts_ref, kto_ref, kts_ref, ao_ref, as_ref, pair_ref):
     for ref, state, query_t, key_t, mask in (
         (own_ref, so_ref, qto_ref, kto_ref, ao_ref), (sib_ref, ss_ref, qts_ref, kts_ref, as_ref),
     ):
@@ -128,6 +128,7 @@
             key_t[lanes, :] = ref[K, lanes].T
         allowed = ref[4 * TOK :, :].astype(F32)
         mask[...] = jnp.concatenate([allowed[:8], allowed[8:]], axis=1)
+    pair_ref[...] = (so_ref[...] + ss_ref[...]).astype(BF16)
 
 
 def span_masks():
@@ -216,33 +217,29 @@
             later = later + (got[chip ^ 2][16:24] + got[chip ^ 3][16:24])
         if not chip & 1:
             later = later + got[chip ^ 1][8:16]
-        rows = [
-            own[chip ^ 1] if chip & 1 else zero,
-            pairs[chip ^ 2] if chip & 2 else zero,
-            before[chip >> 2],
-            later,
-        ]
+        rows = [pairs[chip ^ 2] if chip & 2 else zero, before[chip >> 2], later]
         o_ref[chip] = jnp.concatenate(rows, axis=0).astype(BF16)
 
 
 def mid2_body(r_ref, o_ref):
     for chip in range(0, CHIPS, 2):
         got = [r_ref[chip + i].astype(F32) for i in range(2)]
-        for level in range(4):
+        for level in range(3):
             both = [part[8 * level : 8 * level + 8] for part in got]
             row = 256 * level + 8 * chip
             o_ref[row : row + 16, :] = jnp.concatenate(both, axis=0).astype(BF16)
 
 
-def far_projection(i, ref, mine_ref):
+def far_projection(i, ref, next_ref, mine_ref):
     lanes = slice(DIM * i, DIM * (i + 1))
-    states = [mine_ref[256 * level + DIM * i : 256 * level + DIM * (i + 1), :] for level in range(3)]
+    states = [next_ref[lanes, :]]
+    states += [mine_ref[256 * level + DIM * i : 256 * level + DIM * (i + 1), :] for level in range(2)]
     projected = mm(jnp.concatenate(states, axis=0), ref[G, lanes], 1, 1)
     return [projected[DIM * level : DIM * (level + 1)] for level in range(3)]
 
 
 def cross_body(
-    own_ref, sib_ref, qto_ref, qts_ref, ao_ref, as_ref, go_ref, gs_ref, ro_ref, rs_ref, mine_ref, gl_ref, co_ref, cs_ref
+    own_ref, sib_ref, qto_ref, qts_ref, ao_ref, as_ref, go_ref, gs_ref, ro_ref, rs_ref, next_ref, mine_ref, gl_ref, co_ref, cs_ref
 ):
     outs = []
     for ref, query_t, mask, gates_ref, rows_ref, cross_ref in (
@@ -255,7 +252,7 @@
             weight = gates * mask[...]
             parts = [jnp.zeros((5, TOK), F32)]
             total = None
-            for level, term in enumerate(far_projection(i, ref, mine_ref)):
+            for level, term in enumerate(far_projection(i, ref, next_ref, mine_ref)):
                 parts.append(jnp.sum(query * term, axis=0, keepdims=True))
                 weighted = weight[5 + level : 6 + level, :] * term
                 total = weighted if total is None else total + weighted
@@ -277,7 +274,7 @@
         query, key, value, grad = blk_ref[Q, lanes], blk_ref[K, lanes], blk_ref[V, lanes], blk_ref[G, lanes]
         weight = gates_ref[8 * i : 8 * i + 8, :] * mask_ref[...]
         near = mm((state_ref[lanes, :] * upper).astype(BF16), grad, 1, 1)
-        later = mine_ref[768 + DIM * i : 768 + DIM * (i + 1), :].astype(F32)
+        later = mine_ref[512 + DIM * i : 512 + DIM * (i + 1), :].astype(F32)
         later = (later + near_ref[lanes, :] * (1.0 - upper)).astype(BF16)
         dk = mm(value, later, 1, 1)
         dv = mm(key, later)
@@ -394,29 +391,31 @@
     logits = [parts[0]] + [rotate(parts[step], step) for step in range(1, 4)]
     sib = sibling(leaving)
     sib_input = sibling(layer_input)
-    state_own, state_sib, qt_own, qt_sib, kt_own, kt_sib, allow_own, allow_sib = call(
-        state_body, [half, half] + [shape((256, TOK), BF16)] * 4 + [mask8, mask8], (own, sib)
-    )
+    state_own, state_sib, qt_own, qt_sib, kt_own, kt_sib, allow_own, allow_sib, pair_state = call(
+        state_body, [half, half] + [shape((256, TOK), BF16)] * 4 + [mask8, mask8, shape((256, DIM), BF16)],
+        (own, sib),
+    )
+    next_state = lax.ppermute(pair_state, "seq", [(d, d ^ 2) for d in range(seq_count) if not d & 2])
     pairs = shape((1536, 256), F32)
     rows_own, rows_sib, sc_own, pr_own, sc_sib, pr_sib = call(
         rows_body, [tok16, tok16] + [pairs] * 4, (own, sib, qt_own, qt_sib, state_own, state_sib)
     )
-    logits_own, logits_send = call(gather_body, [tok16, tok16], tuple(logits), after=(rows_own,))
+    logits_own, logits_send = call(gather_body, [tok16, tok16], tuple(logits))
 
     gates_own, gates_sib, near, slices = call(
         level_body, [tok16, tok16, half, shape((CHIPS, 32, DIM), BF16)],
         (own, sib, qt_own, qt_sib, allow_own, allow_sib, state_own, state_sib, logits_own, sibling(logits_send)),
         scratch=[pltpu.VMEM((1024, DIM), F32)],
-        after=(sib_input,),
+        after=(sib_input, next_state, rows_own),
     )
     got1 = exchange(slices)
 
-    got2 = exchange(call(mid1_body, shape((CHIPS, 32, DIM), BF16), (got1,)))
-    mine = call(mid2_body, shape((1024, DIM), BF16), (got2,))
+    got2 = exchange(call(mid1_body, shape((CHIPS, 24, DIM), BF16), (got1,)))
+    mine = call(mid2_body, shape((768, DIM), BF16), (got2,))
     tok256 = shape((256, TOK), F32)
     grad_logits, cross_own, cross_sib = call(
         cross_body, [shape((32, TOK), BF16), tok256, tok256],
-        (own, sib, qt_own, qt_sib, allow_own, allow_sib, gates_own, gates_sib, rows_own, rows_sib, mine),
+        (own, sib, qt_own, qt_sib, allow_own, allow_sib, gates_own, gates_sib, rows_own, rows_sib, next_state, mine),
     )
 
     gl = [grad_logits] + [rotate(grad_logits, step) for step in range(1, 4)]

time: 97.8 us -> 96.8 us (0.990)
  blocking collectives: 62.5 us -> 60.8 us
  starting transfers between devices: 20.3 us -> 21.9 us
    ppermute x0 -> x1, starting transfers between devices: none -> 3.12 us  [shards(): lax.ppermute(pair_state, 'seq', [(d, d ^ 2) for d in range(seq_count) if...]
    all_to_all x4, blocking collectives: 62.5 us -> 60.8 us  [exchange(): return lax.all_to_all(value, 'seq', 0, 0, axis_index_groups=groups)]
  transfers between devices with their start and end apart: 11 -> 12, of which waited for: 2 -> 0; matrix products, arithmetic and copies ran while one was open for 0% -> 0% of each run, Pallas kernels for 6% -> 6%
where the time goes in v6:
time: 96.8 us; the launch traced here: 96.5 us
  blocking collectives  60.8 us (63%)
  starting transfers between devices  21.9 us (23%)
  Pallas kernels  11.6 us (12%)
  local copies, waits for them, and re-layouts  1.24 us (1%)
  between operations  0.99 us (1%)
    all_to_all x4, blocking collectives, exchange(): return lax.all_to_all(value, 'seq', 0, 0, axis_index_groups=groups)  60.8 us
    ppermute x5, starting transfers between devices, sibling(): return lax.ppermute(value, 'seq', swap)  12.6 us
    pallas_call x14, Pallas kernels, call(): pl.pallas_call(kernel, out_shape=out_shape, grid=grid, in_specs=in_specs,...  11.6 us
    ppermute x6, starting transfers between devices, rotate(): return lax.ppermute(value, 'head', [(h, (h + step) % 4) for h in range(4)])  6.22 us
    ppermute x1, starting transfers between devices, shards(): lax.ppermute(pair_state, 'seq', [(d, d ^ 2) for d in range(seq_count) if...  3.12 us
  transfers between devices with their start and end apart: 12, of which 0 were waited for; matrix products, arithmetic and copies ran while one was open for 0% of the time, Pallas kernels for 6%

profile of v6, /device:TPU:1, one launch (start us, length us, event | category | flops | bytes accessed | tf_op | source)
XLA Modules:
  0.0 96.5 jit_solution(17236964964455750347)
XLA Ops:
  0.6 0.0 copy-start.2
  0.6 3.6 %shard_map.102 = (f32[32,512]{1,0:T(8,128)}, f32[32,512]{1,0:T(8,128)}, f32[32,512]{1,0:T(8,128)}, f32[32,512]{1,0:T(8,128)}, bf16[2064,256]{1,0:T(8,128)(2,1)}, /*index=5*/bf16[2064,256]{1,0:T(8,128)(2,1)}) custom-call(bf16[512,1024]{1,0:T(8,128)(2,1)} %refs_0_.3, bf16[1024,128]{1,0:T(8,128)(2,1)} %refs_1_.1, bf16[512,512]{1,0:T(8,128)(2,1)} %refs_2_.1, ...), custom_call_target="tpu_custom_call" | custom-call | flops 10000000 | bytes 1000000 | tf_op jit(solution)/shard_map/pallas_call | solution.py:46
  4.2 3.3 %collective-permute-start = (bf16[2064,256]{1,0:T(8,128)(2,1)}, bf16[2064,256]{1,0:T(8,128)(2,1)S(1)}, u32[]{:S(2)}, u32[]{:S(2)}) collective-permute-start(bf16[2064,256]{1,0:T(8,128)(2,1)} %get-tuple-element.43), channel_id=1, source_target_pairs={{0,4},{4,0},{8,12},{12,8},{16,20},{20,16},{24,28},{28,24},{32,36},... | collective-permute-start | bytes 3170312 | tf_op jit(solution)/shard_map/ppermute | solution.py:363
  7.5 0.0 copy-done.2
  7.5 0.1 collective-permute-start.5
  7.6 0.0 collective-permute-start.1
  7.6 2.2 %collective-permute-start.2 = (f32[32,512]{1,0:T(8,128)}, f32[32,512]{1,0:T(8,128)S(1)}, u32[]{:S(2)}, u32[]{:S(2)}) collective-permute-start(f32[32,512]{1,0:T(8,128)} %get-tuple-element.53), channel_id=1, source_target_pairs={{0,2},{1,3},{2,0},{3,1},{4,6},{5,7},{6,4},{7,5},{8,10},{9,11},{10,... | collective-permute-start | bytes 196616 | tf_op jit(solution)/shard_map/ppermute | solution.py:369
  9.8 1.1 %collective-permute-start.3 = (f32[32,512]{1,0:T(8,128)}, f32[32,512]{1,0:T(8,128)S(1)}, u32[]{:S(2)}, u32[]{:S(2)}) collective-permute-start(f32[32,512]{1,0:T(8,128)} %get-tuple-element.54), channel_id=1, source_target_pairs={{0,3},{1,0},{2,1},{3,2},{4,7},{5,4},{6,5},{7,6},{8,11},{9,8},{10,9... | collective-permute-start | bytes 196616 | tf_op jit(solution)/shard_map/ppermute | solution.py:369
  10.9 0.0 collective-permute-done.refs_1_.refs_0_
  10.9 0.0 copy-start
  10.9 1.2 %copy-done = bf16[2064,256]{1,0:T(8,128)(2,1)S(1)} copy-done((bf16[2064,256]{1,0:T(8,128)(2,1)S(1)}, bf16[2064,256]{1,0:T(8,128)(2,1)}, u32[]{:S(2)}) %copy-start) | copy-done | bytes 1056792
  12.1 0.0 copy-start.3
  12.1 0.0 copy-start.1
  12.1 0.5 shard_map.103
  12.6 3.1 %collective-permute-start.6 = (bf16[256,128]{1,0:T(8,128)(2,1)S(1)}, bf16[256,128]{1,0:T(8,128)(2,1)S(1)}, u32[]{:S(2)}, u32[]{:S(2)}) collective-permute-start(bf16[256,128]{1,0:T(8,128)(2,1)S(1)} %get-tuple-element.57), channel_id=1, source_target_pairs={{0,8},{4,12},{16,24},{20,28},{32,40},{36,44},{48,56},{52,60},{64,7... | collective-permute-start | bytes 196616 | tf_op jit(solution)/shard_map/ppermute | solution.py:398
  15.8 0.0 collective-permute-done.1.refs_1_
  15.8 0.0 collective-permute-done.2.refs_2_
  15.8 0.0 collective-permute-done.3.refs_3_
  15.8 0.0 copy-done.3
  15.8 1.6 %collective-permute-start.4 = (f32[16,512]{1,0:T(8,128)S(1)}, f32[16,512]{1,0:T(8,128)S(1)}, u32[]{:S(2)}, u32[]{:S(2)}) collective-permute-start(f32[16,512]{1,0:T(8,128)S(1)} %get-tuple-element.56), channel_id=1, source_target_pairs={{0,4},{4,0},{8,12},{12,8},{16,20},{20,16},{24,28},{28,24},{32,36},... | collective-permute-start | bytes 98312 | tf_op jit(solution)/shard_map/ppermute | solution.py:363
  17.5 0.0 copy-done.1
  17.5 1.2 %shard_map.105 = (f32[16,512]{1,0:T(8,128)S(1)}, f32[16,512]{1,0:T(8,128)S(1)}, f32[1536,256]{1,0:T(8,128)S(1)}, f32[1536,256]{1,0:T(8,128)S(1)}, f32[1536,256]{1,0:T(8,128)S(1)}, /*index=5*/f32[1536,256]{1,0:T(8,128)S(1)}) custom-call(bf16[2064,256]{1,0:T(8,128)(2,1)S(1)} %copy-done.1, bf16[2064,256]{1,0:T(8,128)(2,1)S(1)} %collective-permute-done.refs_1_.refs_0_, ...), custom_call_target="tpu_custom_call" | custom-call | flops 10000000 | bytes 1000000 | tf_op jit(solution)/shard_map/pallas_call | solution.py:46
  18.6 0.0 collective-permute-done.4.refs_9_
  18.7 0.0 collective-permute-done.5.refs_10_.refs_1_
  18.7 0.0 collective-permute-done.6.refs_11_.refs_10_
  18.7 0.7 shard_map.106
  19.4 20.9 %all_to_all.20.refs_0_ = bf16[32,32,128]{2,1,0:T(8,128)(2,1)S(1)} all-to-all(bf16[32,32,128]{2,1,0:T(8,128)(2,1)S(1)} %get-tuple-element.61), channel_id=1, replica_groups={{0,8,16,24,32,40,48,56,64,72,80,88,96,104,112,120,128,136,144,152,160,1..., dimensions={0} | all-to-all | bytes 524288 | tf_op jit(solution)/shard_map/all_to_all | solution.py:366
  40.4 14.8 %all_to_all.21.refs_0_ = bf16[32,24,128]{2,1,0:T(8,128)(2,1)S(1)} all-to-all(bf16[32,24,128]{2,1,0:T(8,128)(2,1)S(1)} %shard_map.107), channel_id=1, replica_groups={{0,8,16,24,32,40,48,56,64,72,80,88,96,104,112,120,128,136,144,152,160,1..., dimensions={0} | all-to-all | bytes 393216 | tf_op jit(solution)/shard_map/all_to_all | solution.py:366
  55.3 0.7 shard_map.109
  56.0 0.5 collective-permute-start.8
  56.4 1.7 %collective-permute-start.9 = (bf16[32,512]{1,0:T(8,128)(2,1)S(1)}, bf16[32,512]{1,0:T(8,128)(2,1)S(1)}, u32[]{:S(2)}, u32[]{:S(2)}) collective-permute-start(bf16[32,512]{1,0:T(8,128)(2,1)S(1)} %get-tuple-element.71.refs_10_.refs_2_), channel_id=1, source_target_pairs={{0,2},{1,3},{2,0},{3,1},{4,6},{5,7},{6,4},{7,5},{8,10},{9,11},{10,... | collective-permute-start | bytes 98312 | tf_op jit(solution)/shard_map/ppermute | solution.py:369
  58.1 0.8 collective-permute-start.10
  58.9 1.1 %shard_map.110 = (bf16[1536,256]{1,0:T(8,128)(2,1)S(1)}, f32[8,128]{1,0:T(8,128)S(1)}) custom-call(bf16[2064,256]{1,0:T(8,128)(2,1)S(1)} %collective-permute-done.refs_1_.refs_0_, bf16[256,512]{1,0:T(8,128)(2,1)S(1)} %get-tuple-element.67.refs_1_, f32[256,128]{1,0:T(8,128)S(1)} %get-tuple-element.50.refs_4_.refs_6_.refs_2_, ...), custom_call_target="tpu_custom_call" | custom-call | flops 4000000000 | bytes 16000000 | tf_op jit(solution)/shard_map/pallas_call | solution.py:46
  60.0 4.3 %collective-permute-start.7 = (bf16[1536,256]{1,0:T(8,128)(2,1)S(1)}, bf16[1536,256]{1,0:T(8,128)(2,1)S(1)}, u32[]{:S(2)}, u32[]{:S(2)}) collective-permute-start(bf16[1536,256]{1,0:T(8,128)(2,1)S(1)} %get-tuple-element.74), channel_id=1, source_target_pairs={{0,4},{4,0},{8,12},{12,8},{16,20},{20,16},{24,28},{28,24},{32,36},... | collective-permute-start | bytes 2359304 | tf_op jit(solution)/shard_map/ppermute | solution.py:363
  64.3 1.0 shard_map.111
  65.3 0.0 collective-permute-done.8.refs_3_
  65.3 0.0 collective-permute-done.9.refs_4_
  65.3 0.0 collective-permute-done.10.refs_5_
  65.3 0.5 shard_map.112
  65.8 12.3 %all_to_all.22.refs_0_ = bf16[32,16,128]{2,1,0:T(8,128)(2,1)S(1)} all-to-all(bf16[32,16,128]{2,1,0:T(8,128)(2,1)S(1)} %shard_map.112), channel_id=1, replica_groups={{0,8,16,24,32,40,48,56,64,72,80,88,96,104,112,120,128,136,144,152,160,1..., dimensions={0} | all-to-all | bytes 262144 | tf_op jit(solution)/shard_map/all_to_all | solution.py:366
  78.2 12.7 %all_to_all.23.refs_2_.refs_0_ = bf16[32,16,128]{2,1,0:T(8,128)(2,1)S(1)} all-to-all(bf16[32,16,128]{2,1,0:T(8,128)(2,1)S(1)} %shard_map.113), channel_id=1, replica_groups={{0,8,16,24,32,40,48,56,64,72,80,88,96,104,112,120,128,136,144,152,160,1..., dimensions={0} | all-to-all | bytes 262144 | tf_op jit(solution)/shard_map/all_to_all | solution.py:366
  90.9 3.2 %collective-permute-start.11 = (bf16[32,16,128]{2,1,0:T(8,128)(2,1)S(1)}, bf16[32,16,128]{2,1,0:T(8,128)(2,1)S(1)}, u32[]{:S(2)}, u32[]{:S(2)}) collective-permute-start(bf16[32,16,128]{2,1,0:T(8,128)(2,1)S(1)} %all_to_all.23.refs_2_.refs_0_), channel_id=1, source_target_pairs={{0,4},{4,0},{8,12},{12,8},{16,20},{20,16},{24,28},{28,24},{32,36},... | collective-permute-start | bytes 393224 | tf_op jit(solution)/shard_map/ppermute | solution.py:363
  94.1 0.0 collective-permute-done.7.refs_1_
  94.1 1.2 %shard_map.114 = (bf16[512,512]{1,0:T(8,128)(2,1)}, bf16[512,512]{1,0:T(8,128)(2,1)}, bf16[512,512]{1,0:T(8,128)(2,1)}, f32[8,128]{1,0:T(8,128)S(1)}) custom-call(bf16[1536,256]{1,0:T(8,128)(2,1)S(1)} %get-tuple-element.73.refs_0_, bf16[1536,256]{1,0:T(8,128)(2,1)S(1)} %collective-permute-done.7.refs_1_, bf16[32,16,128]{2,1,0:T(8,128)(2,1)S(1)} %all_to_all.23.refs_2_.refs_0_), custom_call_target="tpu_custom_call" | custom-call | flops 10000000 | bytes 1000000 | tf_op jit(solution)/shard_map/pallas_call | solution.py:46
  95.3 0.0 collective-permute-done.11.refs_1_
  95.3 1.1 %shard_map.115 = f32[1024,128]{1,0:T(8,128)} custom-call(bf16[32,16,128]{2,1,0:T(8,128)(2,1)S(1)} %all_to_all.23.refs_2_.refs_0_, bf16[32,16,128]{2,1,0:T(8,128)(2,1)S(1)} %collective-permute-done.11.refs_1_, f32[8,128]{1,0:T(8,128)S(1)} %get-tuple-element.79.refs_2_), custom_call_target="tpu_custom_call" | custom-call | flops 10000000 | bytes 1000000 | tf_op jit(solution)/shard_map/pallas_call | solution.py:46
  (4 shorter events, 0.1 us)
Async XLA Ops:
  0.6 6.9 %copy-start.2 = (bf16[512,1024]{1,0:T(8,128)(2,1)S(1)}, bf16[512,1024]{1,0:T(8,128)(2,1)}, u32[]{:S(2)}) copy-start(bf16[512,1024]{1,0:T(8,128)(2,1)} %refs_0_.3) | copy-start | bytes 3145732
  4.2 6.7 %collective-permute-start = (bf16[2064,256]{1,0:T(8,128)(2,1)}, bf16[2064,256]{1,0:T(8,128)(2,1)S(1)}, u32[]{:S(2)}, u32[]{:S(2)}) collective-permute-start(bf16[2064,256]{1,0:T(8,128)(2,1)} %get-tuple-element.43), channel_id=1, source_target_pairs={{0,4},{4,0},{8,12},{12,8},{16,20},{20,16},{24,28},{28,24},{32,36},... | collective-permute-start | bytes 3170312 | tf_op jit(solution)/shard_map/ppermute | solution.py:363
  7.5 11.1 %collective-permute-start.5 = (bf16[512,1024]{1,0:T(8,128)(2,1)S(1)}, bf16[512,1024]{1,0:T(8,128)(2,1)S(1)}, u32[]{:S(2)}, u32[]{:S(2)}) collective-permute-start(bf16[512,1024]{1,0:T(8,128)(2,1)S(1)} %copy-done.2), channel_id=1, source_target_pairs={{0,4},{4,0},{8,12},{12,8},{16,20},{20,16},{24,28},{28,24},{32,36},... | collective-permute-start | bytes 3145736 | tf_op jit(solution)/shard_map/ppermute | solution.py:363
  7.6 8.1 %collective-permute-start.1 = (f32[32,512]{1,0:T(8,128)}, f32[32,512]{1,0:T(8,128)S(1)}, u32[]{:S(2)}, u32[]{:S(2)}) collective-permute-start(f32[32,512]{1,0:T(8,128)} %get-tuple-element.52), channel_id=1, source_target_pairs={{0,1},{1,2},{2,3},{3,0},{4,5},{5,6},{6,7},{7,4},{8,9},{9,10},{10,1... | collective-permute-start | bytes 196616 | tf_op jit(solution)/shard_map/ppermute | solution.py:369
  7.6 8.1 %collective-permute-start.2 = (f32[32,512]{1,0:T(8,128)}, f32[32,512]{1,0:T(8,128)S(1)}, u32[]{:S(2)}, u32[]{:S(2)}) collective-permute-start(f32[32,512]{1,0:T(8,128)} %get-tuple-element.53), channel_id=1, source_target_pairs={{0,2},{1,3},{2,0},{3,1},{4,6},{5,7},{6,4},{7,5},{8,10},{9,11},{10,... | collective-permute-start | bytes 196616 | tf_op jit(solution)/shard_map/ppermute | solution.py:369
  9.8 6.0 %collective-permute-start.3 = (f32[32,512]{1,0:T(8,128)}, f32[32,512]{1,0:T(8,128)S(1)}, u32[]{:S(2)}, u32[]{:S(2)}) collective-permute-start(f32[32,512]{1,0:T(8,128)} %get-tuple-element.54), channel_id=1, source_target_pairs={{0,3},{1,0},{2,1},{3,2},{4,7},{5,4},{6,5},{7,6},{8,11},{9,8},{10,9... | collective-permute-start | bytes 196616 | tf_op jit(solution)/shard_map/ppermute | solution.py:369
  10.9 1.2 %copy-start = (bf16[2064,256]{1,0:T(8,128)(2,1)S(1)}, bf16[2064,256]{1,0:T(8,128)(2,1)}, u32[]{:S(2)}) copy-start(bf16[2064,256]{1,0:T(8,128)(2,1)} %get-tuple-element.42.refs_0_) | copy-start | bytes 3170308
  12.1 3.7 %copy-start.3 = (f32[32,512]{1,0:T(8,128)S(1)}, f32[32,512]{1,0:T(8,128)}, u32[]{:S(2)}) copy-start(f32[32,512]{1,0:T(8,128)} %get-tuple-element.51.refs_0_) | copy-start | bytes 196612
  12.1 5.3 %copy-start.1 = (bf16[2064,256]{1,0:T(8,128)(2,1)S(1)}, bf16[2064,256]{1,0:T(8,128)(2,1)}, u32[]{:S(2)}) copy-start(bf16[2064,256]{1,0:T(8,128)(2,1)} %get-tuple-element.42.refs_0_) | copy-start | bytes 3170308
  12.6 6.0 %collective-permute-start.6 = (bf16[256,128]{1,0:T(8,128)(2,1)S(1)}, bf16[256,128]{1,0:T(8,128)(2,1)S(1)}, u32[]{:S(2)}, u32[]{:S(2)}) collective-permute-start(bf16[256,128]{1,0:T(8,128)(2,1)S(1)} %get-tuple-element.57), channel_id=1, source_target_pairs={{0,8},{4,12},{16,24},{20,28},{32,40},{36,44},{48,56},{52,60},{64,7... | collective-permute-start | bytes 196616 | tf_op jit(solution)/shard_map/ppermute | solution.py:398
  15.8 2.8 %collective-permute-start.4 = (f32[16,512]{1,0:T(8,128)S(1)}, f32[16,512]{1,0:T(8,128)S(1)}, u32[]{:S(2)}, u32[]{:S(2)}) collective-permute-start(f32[16,512]{1,0:T(8,128)S(1)} %get-tuple-element.56), channel_id=1, source_target_pairs={{0,4},{4,0},{8,12},{12,8},{16,20},{20,16},{24,28},{28,24},{32,36},... | collective-permute-start | bytes 98312 | tf_op jit(solution)/shard_map/ppermute | solution.py:363
  56.0 9.3 %collective-permute-start.8 = (bf16[32,512]{1,0:T(8,128)(2,1)S(1)}, bf16[32,512]{1,0:T(8,128)(2,1)S(1)}, u32[]{:S(2)}, u32[]{:S(2)}) collective-permute-start(bf16[32,512]{1,0:T(8,128)(2,1)S(1)} %get-tuple-element.71.refs_10_.refs_2_), channel_id=1, source_target_pairs={{0,1},{1,2},{2,3},{3,0},{4,5},{5,6},{6,7},{7,4},{8,9},{9,10},{10,1... | collective-permute-start | bytes 98312 | tf_op jit(solution)/shard_map/ppermute | solution.py:369
  56.4 8.9 %collective-permute-start.9 = (bf16[32,512]{1,0:T(8,128)(2,1)S(1)}, bf16[32,512]{1,0:T(8,128)(2,1)S(1)}, u32[]{:S(2)}, u32[]{:S(2)}) collective-permute-start(bf16[32,512]{1,0:T(8,128)(2,1)S(1)} %get-tuple-element.71.refs_10_.refs_2_), channel_id=1, source_target_pairs={{0,2},{1,3},{2,0},{3,1},{4,6},{5,7},{6,4},{7,5},{8,10},{9,11},{10,... | collective-permute-start | bytes 98312 | tf_op jit(solution)/shard_map/ppermute | solution.py:369
  58.1 7.2 %collective-permute-start.10 = (bf16[32,512]{1,0:T(8,128)(2,1)S(1)}, bf16[32,512]{1,0:T(8,128)(2,1)S(1)}, u32[]{:S(2)}, u32[]{:S(2)}) collective-permute-start(bf16[32,512]{1,0:T(8,128)(2,1)S(1)} %get-tuple-element.71.refs_10_.refs_2_), channel_id=1, source_target_pairs={{0,3},{1,0},{2,1},{3,2},{4,7},{5,4},{6,5},{7,6},{8,11},{9,8},{10,9... | collective-permute-start | bytes 98312 | tf_op jit(solution)/shard_map/ppermute | solution.py:369
  60.0 34.1 %collective-permute-start.7 = (bf16[1536,256]{1,0:T(8,128)(2,1)S(1)}, bf16[1536,256]{1,0:T(8,128)(2,1)S(1)}, u32[]{:S(2)}, u32[]{:S(2)}) collective-permute-start(bf16[1536,256]{1,0:T(8,128)(2,1)S(1)} %get-tuple-element.74), channel_id=1, source_target_pairs={{0,4},{4,0},{8,12},{12,8},{16,20},{20,16},{24,28},{28,24},{32,36},... | collective-permute-start | bytes 2359304 | tf_op jit(solution)/shard_map/ppermute | solution.py:363
  90.9 4.4 %collective-permute-start.11 = (bf16[32,16,128]{2,1,0:T(8,128)(2,1)S(1)}, bf16[32,16,128]{2,1,0:T(8,128)(2,1)S(1)}, u32[]{:S(2)}, u32[]{:S(2)}) collective-permute-start(bf16[32,16,128]{2,1,0:T(8,128)(2,1)S(1)} %all_to_all.23.refs_2_.refs_0_), channel_id=1, source_target_pairs={{0,4},{4,0},{8,12},{12,8},{16,20},{20,16},{24,28},{28,24},{32,36},... | collective-permute-start | bytes 393224 | tf_op jit(solution)/shard_map/ppermute | solution.py:363

commit v7 on v6

--- a/solution.py
+++ b/solution.py
@@ -302,25 +302,39 @@
     token_ref[...] = jnp.zeros_like(token_ref)
 
 
-def gradw_body(xo_ref, xs_ref, g0, g1, g2, g3, o_ref, own_scr, sib_scr, full):
+def gradw_body(xo_ref, xs_ref, g0, g1, g2, g3, o0, o1, o2, o3, own_scr, sib_scr, full):
     head = lax.axis_index("head")
     for step, part in enumerate((g0, g1, g2, g3)):
         rows = aligned(lax.rem(head + 4 - step, 4), 16)
         own_scr[rows, :] = part[0:16, :]
         sib_scr[rows, :] = part[16:32, :]
     full[...] = mm(own_scr[...], xo_ref[...]) + mm(sib_scr[...], xs_ref[...])
-    for chip in range(CHIPS):
-        group, block = chip % 4, chip // 4
-        o_ref[chip] = full[16 * group : 16 * group + 16, DIM * block : DIM * (block + 1)].astype(BF16)
-
-
-def mid3_body(scale, r_ref, o_ref):
+    place = (lax.axis_index("seq") // 2) % 4
+    for step, out in enumerate((o0, o1, o2, o3)):
+        start = 256 * lax.rem(place + step, 4)
+        for block in range(2):
+            part = full[:, pl.ds(pl.multiple_of(start + DIM * block, DIM), DIM)]
+            out[64 * block : 64 * block + 64, :] = part.astype(out.dtype)
+
+
+def sum_x_body(own_ref, r1, r2, r3, o_ref):
+    total = (own_ref[...] + r1[...].astype(F32)) + (r2[...].astype(F32) + r3[...].astype(F32))
+    total = total.astype(BF16)
+    for place in range(8):
+        o_ref[place] = total
+
+
+def sum_z_body(scale, r_ref, o_ref):
     total = r_ref[0].astype(F32)
-    for chip in range(1, CHIPS):
-        total = total + r_ref[chip].astype(F32)
-    total = (total * scale).astype(BF16)
-    for chip in range(CHIPS):
-        o_ref[chip] = total
+    for place in range(1, 8):
+        total = total + r_ref[place].astype(F32)
+    o_ref[...] = (total * scale).astype(BF16)
+
+
+def both_body(mine_ref, other_ref, o_ref):
+    core = lax.axis_index("seq") & 1
+    o_ref[aligned(core, DIM), :] = mine_ref[...]
+    o_ref[aligned(1 - core, DIM), :] = other_ref[...]
 
 
 def place_body(own_ref, recv_ref, dq_hbm, dk_hbm, dv_hbm, token_ref, sems):
@@ -337,19 +351,24 @@
         copy.wait()
 
 
-def join_body(w_mine_ref, w_other_ref, w_hbm, full, w_ref, sems):
-    core = lax.axis_index("seq") & 1
+def join_body(r0, r1, r2, r3, w_hbm, w_ref, sems):
+    place = (lax.axis_index("seq") // 2) % 4
     copies = []
-    for block in range(8):
-        lanes = slice(DIM * block, DIM * (block + 1))
-        for group in range(4):
-            full[aligned(2 * group + core, 16), :] = w_mine_ref[4 * block + group].astype(F32)
-            full[aligned(2 * group + 1 - core, 16), :] = w_other_ref[4 * block + group].astype(F32)
-        w_ref[lanes, :] = full[...].T
-        if block % 4 == 3:
-            rows = pl.ds(512 * (block // 4), 512)
-            copies.append(pltpu.make_async_copy(w_ref.at[rows, :], w_hbm.at[rows, :], sems.at[block // 4]))
-            copies[-1].start()
+    for step, ref in enumerate((r0, r1, r2, r3)):
+        data = ref[...].astype(F32)
+        for block in range(2):
+            parts = [
+                data[DIM * half + 64 * block + 16 * group : DIM * half + 64 * block + 16 * group + 16]
+                for group in range(4)
+                for half in range(2)
+            ]
+            at = 2 * step + block
+            w_ref[DIM * at : DIM * (at + 1), :] = jnp.concatenate(parts, axis=0).T
+        rows = aligned(lax.rem(place + 4 - step, 4), 256)
+        copies.append(
+            pltpu.make_async_copy(w_ref.at[pl.ds(256 * step, 256), :], w_hbm.at[rows, :], sems.at[step])
+        )
+        copies[-1].start()
     for copy in copies:
         copy.wait()
 
@@ -364,6 +383,10 @@
 
     def exchange(value):
         return lax.all_to_all(value, "seq", 0, 0, axis_index_groups=groups)
+
+    def rotate_x(value, step):
+        pairs = [(d, d // 8 * 8 + (d + 2 * step) % 8) for d in range(seq_count)]
+        return lax.ppermute(value, "seq", pairs)
 
     def rotate(value, step):
         return lax.ppermute(value, "head", [(h, (h + step) % 4) for h in range(4)])
@@ -428,23 +451,30 @@
     out_sib, token = tail(1, sib, kt_sib, state_own, allow_sib, gates_sib, cross_sib, sc_sib, pr_sib, (grad_logits,))
     out_recv = sibling(out_sib)
     out_own, token = tail(0, own, kt_own, state_sib, allow_own, gates_own, cross_own, sc_own, pr_own, (token,))
-    slices = call(
-        gradw_body, shape((CHIPS, 16, DIM), BF16), (layer_input, sib_input, *gl),
+    quarter = shape((DIM, DIM), BF16)
+    sums = call(
+        gradw_body, [shape((DIM, DIM), F32)] + [quarter] * 3, (layer_input, sib_input, *gl),
         scratch=[pltpu.VMEM((64, TOK), BF16), pltpu.VMEM((64, TOK), BF16), pltpu.VMEM((64, 1024), F32)],
         after=(token,),
     )
-    got3 = exchange(slices)
+    got3 = [sums[0]] + [rotate_x(sums[step], step) for step in range(1, 4)]
+    spread = call(sum_x_body, shape((8, DIM, DIM), BF16), tuple(got3))
+    columns = [[8 * z + place for z in range(8)] for place in range(8)]
+    got4 = lax.all_to_all(spread, "seq", 0, 0, axis_index_groups=columns)
     scale = 1.0 / math.sqrt(TOK * seq_count)
-    w_half = exchange(call(functools.partial(mid3_body, scale), shape((CHIPS, 16, DIM), BF16), (got3,)))
+    mine_sum = call(functools.partial(sum_z_body, scale), quarter, (got4,))
+    other_sum = sibling(mine_sum)
     *grads, token = call(
         place_body, [shape((TOK, 512), BF16)] * 3 + [shape((8, DIM), F32)], (out_own, out_recv),
-        out_specs=[hbm] * 3 + [whole], scratch=[pltpu.SemaphoreType.DMA((6,))], after=(w_half,),
-    )
+        out_specs=[hbm] * 3 + [whole], scratch=[pltpu.SemaphoreType.DMA((6,))], after=(mine_sum,),
+    )
+    both = call(both_body, shape((256, DIM), BF16), (mine_sum, other_sum))
+    got5 = [both] + [rotate_x(both, step) for step in range(1, 4)]
     grad_weight = call(
-        join_body, shape((1024, DIM), F32), (w_half, sibling(w_half)),
+        join_body, shape((1024, DIM), F32), tuple(got5),
         out_specs=hbm,
         after=(token,),
-        scratch=[pltpu.VMEM((DIM, DIM), F32), pltpu.VMEM((1024, DIM), F32), pltpu.SemaphoreType.DMA((2,))],
+        scratch=[pltpu.VMEM((1024, DIM), F32), pltpu.SemaphoreType.DMA((4,))],
     )
     return (*grads, grad_weight)
 

time: 96.8 us -> 95.8 us (0.990)
  blocking collectives: 60.8 us -> 47.4 us
  starting transfers between devices: 21.9 us -> 29.3 us
  waiting for transfers between devices: 0.03 us -> 5.11 us
    all_to_all x4 -> x2, blocking collectives: 60.8 us -> 35.8 us  [exchange(): return lax.all_to_all(value, 'seq', 0, 0, axis_index_groups=groups)]
    all_to_all x0 -> x1, blocking collectives: none -> 11.6 us  [shards(): got4 = lax.all_to_all(spread, 'seq', 0, 0, axis_index_groups=columns)]
    ppermute x0 -> x6, starting transfers between devices: none -> 6.92 us  [rotate_x(): return lax.ppermute(value, 'seq', pairs)]
    ppermute x0 -> x6, waiting for transfers between devices: none -> 4.22 us  [rotate_x(): return lax.ppermute(value, 'seq', pairs)]
    pallas_call x14 -> x16, Pallas kernels: 11.6 us -> 11.5 us  [call(): pl.pallas_call(kernel, out_shape=out_shape, grid=grid, in_specs=in_specs,...]
  transfers between devices with their start and end apart: 12 -> 18, of which waited for: 0 -> 6; matrix products, arithmetic and copies ran while one was open for 0% -> 0% of each run, Pallas kernels for 6% -> 6%
where the time goes in v7:
time: 95.8 us; the launch traced here: 95.5 us
  blocking collectives  47.4 us (49%)
  starting transfers between devices  29.3 us (31%)
  Pallas kernels  11.5 us (12%)
  waiting for transfers between devices  5.11 us (5%)
  local copies, waits for them, and re-layouts  1.24 us (1%)
  between operations  1 us (1%)
    all_to_all x2, blocking collectives, exchange(): return lax.all_to_all(value, 'seq', 0, 0, axis_index_groups=groups)  35.8 us
    ppermute x5, starting transfers between devices, sibling(): return lax.ppermute(value, 'seq', swap)  13.1 us
    all_to_all x1, blocking collectives, shards(): got4 = lax.all_to_all(spread, 'seq', 0, 0, axis_index_groups=columns)  11.6 us
    pallas_call x16, Pallas kernels, call(): pl.pallas_call(kernel, out_shape=out_shape, grid=grid, in_specs=in_specs,...  11.5 us
    ppermute x6, starting transfers between devices, rotate_x(): return lax.ppermute(value, 'seq', pairs)  6.92 us
    ppermute x6, starting transfers between devices, rotate(): return lax.ppermute(value, 'head', [(h, (h + step) % 4) for h in range(4)])  6.22 us
    ppermute x6, waiting for transfers between devices, rotate_x(): return lax.ppermute(value, 'seq', pairs)  4.22 us
    ppermute x1, starting transfers between devices, shards(): lax.ppermute(pair_state, 'seq', [(d, d ^ 2) for d in range(seq_count) if...  3.12 us
  transfers between devices with their start and end apart: 18, of which 6 were waited for; matrix products, arithmetic and copies ran while one was open for 0% of the time, Pallas kernels for 6%

profile of v7, /device:TPU:1, one launch (start us, length us, event | category | flops | bytes accessed | tf_op | source)
XLA Modules:
  0.0 95.5 jit_solution(18124725794368417305)
XLA Ops:
  0.6 3.5 %shard_map.102 = (f32[32,512]{1,0:T(8,128)}, f32[32,512]{1,0:T(8,128)}, f32[32,512]{1,0:T(8,128)}, f32[32,512]{1,0:T(8,128)}, bf16[2064,256]{1,0:T(8,128)(2,1)}, /*index=5*/bf16[2064,256]{1,0:T(8,128)(2,1)}) custom-call(bf16[512,1024]{1,0:T(8,128)(2,1)} %refs_0_.3, bf16[1024,128]{1,0:T(8,128)(2,1)} %refs_1_.1, bf16[512,512]{1,0:T(8,128)(2,1)} %refs_2_.1, ...), custom_call_target="tpu_custom_call" | custom-call | flops 10000000 | bytes 1000000 | tf_op jit(solution)/shard_map/pallas_call | solution.py:46
  4.2 3.3 %collective-permute-start = (bf16[2064,256]{1,0:T(8,128)(2,1)}, bf16[2064,256]{1,0:T(8,128)(2,1)S(1)}, u32[]{:S(2)}, u32[]{:S(2)}) collective-permute-start(bf16[2064,256]{1,0:T(8,128)(2,1)} %get-tuple-element.47), channel_id=1, source_target_pairs={{0,4},{4,0},{8,12},{12,8},{16,20},{20,16},{24,28},{28,24},{32,36},... | collective-permute-start | bytes 3170312 | tf_op jit(solution)/shard_map/ppermute | solution.py:382
  7.5 0.1 collective-permute-start.5
  7.6 0.0 collective-permute-start.1
  7.6 2.2 %collective-permute-start.2 = (f32[32,512]{1,0:T(8,128)}, f32[32,512]{1,0:T(8,128)S(1)}, u32[]{:S(2)}, u32[]{:S(2)}) collective-permute-start(f32[32,512]{1,0:T(8,128)} %get-tuple-element.57), channel_id=1, source_target_pairs={{0,2},{1,3},{2,0},{3,1},{4,6},{5,7},{6,4},{7,5},{8,10},{9,11},{10,... | collective-permute-start | bytes 196616 | tf_op jit(solution)/shard_map/ppermute | solution.py:392
  9.8 1.1 %collective-permute-start.3 = (f32[32,512]{1,0:T(8,128)}, f32[32,512]{1,0:T(8,128)S(1)}, u32[]{:S(2)}, u32[]{:S(2)}) collective-permute-start(f32[32,512]{1,0:T(8,128)} %get-tuple-element.58), channel_id=1, source_target_pairs={{0,3},{1,0},{2,1},{3,2},{4,7},{5,4},{6,5},{7,6},{8,11},{9,8},{10,9... | collective-permute-start | bytes 196616 | tf_op jit(solution)/shard_map/ppermute | solution.py:392
  10.9 0.0 collective-permute-done.refs_1_.refs_0_
  10.9 1.2 %copy-done = bf16[2064,256]{1,0:T(8,128)(2,1)S(1)} copy-done((bf16[2064,256]{1,0:T(8,128)(2,1)S(1)}, bf16[2064,256]{1,0:T(8,128)(2,1)}, u32[]{:S(2)}) %copy-start) | copy-done | bytes 1056792
  12.1 0.5 shard_map.103
  12.6 3.1 %collective-permute-start.6 = (bf16[256,128]{1,0:T(8,128)(2,1)S(1)}, bf16[256,128]{1,0:T(8,128)(2,1)S(1)}, u32[]{:S(2)}, u32[]{:S(2)}) collective-permute-start(bf16[256,128]{1,0:T(8,128)(2,1)S(1)} %get-tuple-element.61), channel_id=1, source_target_pairs={{0,8},{4,12},{16,24},{20,28},{32,40},{36,44},{48,56},{52,60},{64,7... | collective-permute-start | bytes 196616 | tf_op jit(solution)/shard_map/ppermute | solution.py:421
  15.7 0.0 collective-permute-done.1.refs_1_
  15.7 0.0 collective-permute-done.2.refs_2_
  15.8 0.0 collective-permute-done.3.refs_3_
  15.8 1.6 %collective-permute-start.4 = (f32[16,512]{1,0:T(8,128)S(1)}, f32[16,512]{1,0:T(8,128)S(1)}, u32[]{:S(2)}, u32[]{:S(2)}) collective-permute-start(f32[16,512]{1,0:T(8,128)S(1)} %get-tuple-element.60), channel_id=1, source_target_pairs={{0,4},{4,0},{8,12},{12,8},{16,20},{20,16},{24,28},{28,24},{32,36},... | collective-permute-start | bytes 98312 | tf_op jit(solution)/shard_map/ppermute | solution.py:382
  17.4 1.2 %shard_map.105 = (f32[16,512]{1,0:T(8,128)S(1)}, f32[16,512]{1,0:T(8,128)S(1)}, f32[1536,256]{1,0:T(8,128)S(1)}, f32[1536,256]{1,0:T(8,128)S(1)}, f32[1536,256]{1,0:T(8,128)S(1)}, /*index=5*/f32[1536,256]{1,0:T(8,128)S(1)}) custom-call(bf16[2064,256]{1,0:T(8,128)(2,1)S(1)} %copy-done.1, bf16[2064,256]{1,0:T(8,128)(2,1)S(1)} %collective-permute-done.refs_1_.refs_0_, ...), custom_call_target="tpu_custom_call" | custom-call | flops 10000000 | bytes 1000000 | tf_op jit(solution)/shard_map/pallas_call | solution.py:46
  18.6 0.0 collective-permute-done.4.refs_9_
  18.6 0.0 collective-permute-done.5.refs_10_.refs_1_
  18.6 0.0 collective-permute-done.6.refs_11_.refs_10_
  18.7 0.7 shard_map.106
  19.4 20.9 %all_to_all.15.refs_0_ = bf16[32,32,128]{2,1,0:T(8,128)(2,1)S(1)} all-to-all(bf16[32,32,128]{2,1,0:T(8,128)(2,1)S(1)} %get-tuple-element.65), channel_id=1, replica_groups={{0,8,16,24,32,40,48,56,64,72,80,88,96,104,112,120,128,136,144,152,160,1..., dimensions={0} | all-to-all | bytes 524288 | tf_op jit(solution)/shard_map/all_to_all | solution.py:385
  40.4 14.8 %all_to_all.16.refs_0_ = bf16[32,24,128]{2,1,0:T(8,128)(2,1)S(1)} all-to-all(bf16[32,24,128]{2,1,0:T(8,128)(2,1)S(1)} %shard_map.107), channel_id=1, replica_groups={{0,8,16,24,32,40,48,56,64,72,80,88,96,104,112,120,128,136,144,152,160,1..., dimensions={0} | all-to-all | bytes 393216 | tf_op jit(solution)/shard_map/all_to_all | solution.py:385
  55.2 0.7 shard_map.109
  55.9 0.5 collective-permute-start.8
  56.4 1.7 %collective-permute-start.9 = (bf16[32,512]{1,0:T(8,128)(2,1)S(1)}, bf16[32,512]{1,0:T(8,128)(2,1)S(1)}, u32[]{:S(2)}, u32[]{:S(2)}) collective-permute-start(bf16[32,512]{1,0:T(8,128)(2,1)S(1)} %get-tuple-element.75.refs_10_.refs_2_), channel_id=1, source_target_pairs={{0,2},{1,3},{2,0},{3,1},{4,6},{5,7},{6,4},{7,5},{8,10},{9,11},{10,... | collective-permute-start | bytes 98312 | tf_op jit(solution)/shard_map/ppermute | solution.py:392
  58.1 0.8 collective-permute-start.10
  58.9 1.1 %shard_map.110 = (bf16[1536,256]{1,0:T(8,128)(2,1)S(1)}, f32[8,128]{1,0:T(8,128)S(1)}) custom-call(bf16[2064,256]{1,0:T(8,128)(2,1)S(1)} %collective-permute-done.refs_1_.refs_0_, bf16[256,512]{1,0:T(8,128)(2,1)S(1)} %get-tuple-element.71.refs_1_, f32[256,128]{1,0:T(8,128)S(1)} %get-tuple-element.54.refs_4_.refs_6_.refs_2_, ...), custom_call_target="tpu_custom_call" | custom-call | flops 4000000000 | bytes 16000000 | tf_op jit(solution)/shard_map/pallas_call | solution.py:46
  60.0 4.3 %collective-permute-start.7 = (bf16[1536,256]{1,0:T(8,128)(2,1)S(1)}, bf16[1536,256]{1,0:T(8,128)(2,1)S(1)}, u32[]{:S(2)}, u32[]{:S(2)}) collective-permute-start(bf16[1536,256]{1,0:T(8,128)(2,1)S(1)} %get-tuple-element.78), channel_id=1, source_target_pairs={{0,4},{4,0},{8,12},{12,8},{16,20},{20,16},{24,28},{28,24},{32,36},... | collective-permute-start | bytes 2359304 | tf_op jit(solution)/shard_map/ppermute | solution.py:382
  64.3 1.0 shard_map.111
  65.3 0.0 collective-permute-done.8.refs_3_
  65.3 0.0 collective-permute-done.10.refs_5_
  65.3 0.5 shard_map.112
  65.8 0.1 collective-permute-start.11
  65.9 2.1 %collective-permute-start.12 = (bf16[128,128]{1,0:T(8,128)(2,1)S(1)}, bf16[128,128]{1,0:T(8,128)(2,1)S(1)}, u32[]{:S(2)}, u32[]{:S(2)}) collective-permute-start(bf16[128,128]{1,0:T(8,128)(2,1)S(1)} %get-tuple-element.82), channel_id=1, source_target_pairs={{0,16},{4,20},{8,24},{12,28},{16,0},{20,4},{24,8},{28,12},{32,48},... | collective-permute-start | bytes 98312 | tf_op jit(solution)/shard_map/ppermute | solution.py:389
  68.0 0.9 collective-permute-start.13
  68.9 1.0 %collective-permute-done.11.refs_1_ = bf16[128,128]{1,0:T(8,128)(2,1)S(1)} collective-permute-done((bf16[128,128]{1,0:T(8,128)(2,1)S(1)}, bf16[128,128]{1,0:T(8,128)(2,1)S(1)}, u32[]{:S(2)}, u32[]{:S(2)}) %collective-permute-start.11) | collective-permute-done | bytes 32800 | tf_op jit(solution)/shard_map/ppermute | solution.py:389
  69.9 0.7 collective-permute-done.12.refs_2_
  70.5 0.6 collective-permute-done.13.refs_3_
  71.1 11.6 %all_to_all.17.refs_0_ = bf16[8,128,128]{2,1,0:T(8,128)(2,1)S(1)} all-to-all(bf16[8,128,128]{2,1,0:T(8,128)(2,1)S(1)} %shard_map.113), channel_id=1, replica_groups={{0,32,64,96,128,160,192,224},{4,36,68,100,132,164,196,228},{8,40,72,104..., dimensions={0} | all-to-all | bytes 524288 | tf_op jit(solution)/shard_map/all_to_all | solution.py:463
  82.8 3.7 %collective-permute-start.14 = (bf16[128,128]{1,0:T(8,128)(2,1)S(1)}, bf16[128,128]{1,0:T(8,128)(2,1)S(1)}, u32[]{:S(2)}, u32[]{:S(2)}) collective-permute-start(bf16[128,128]{1,0:T(8,128)(2,1)S(1)} %shard_map.114.refs_2_.refs_0_), channel_id=1, source_target_pairs={{0,4},{4,0},{8,12},{12,8},{16,20},{20,16},{24,28},{28,24},{32,36},... | collective-permute-start | bytes 98312 | tf_op jit(solution)/shard_map/ppermute | solution.py:382
  86.5 0.9 collective-permute-done.14.refs_1_
  87.4 1.3 %collective-permute-start.15 = (bf16[256,128]{1,0:T(8,128)(2,1)S(1)}, bf16[256,128]{1,0:T(8,128)(2,1)S(1)}, u32[]{:S(2)}, u32[]{:S(2)}) collective-permute-start(bf16[256,128]{1,0:T(8,128)(2,1)S(1)} %shard_map.116.refs_0_), channel_id=1, source_target_pairs={{0,8},{4,12},{8,16},{12,20},{16,24},{20,28},{24,0},{28,4},{32,40},... | collective-permute-start | bytes 196616 | tf_op jit(solution)/shard_map/ppermute | solution.py:389
  88.7 2.0 %collective-permute-start.16 = (bf16[256,128]{1,0:T(8,128)(2,1)S(1)}, bf16[256,128]{1,0:T(8,128)(2,1)S(1)}, u32[]{:S(2)}, u32[]{:S(2)}) collective-permute-start(bf16[256,128]{1,0:T(8,128)(2,1)S(1)} %shard_map.116.refs_0_), channel_id=1, source_target_pairs={{0,16},{4,20},{8,24},{12,28},{16,0},{20,4},{24,8},{28,12},{32,48},... | collective-permute-start | bytes 196616 | tf_op jit(solution)/shard_map/ppermute | solution.py:389
  90.7 0.5 collective-permute-start.17
  91.2 0.0 collective-permute-done.7.refs_1_
  91.2 1.2 %shard_map.115 = (bf16[512,512]{1,0:T(8,128)(2,1)}, bf16[512,512]{1,0:T(8,128)(2,1)}, bf16[512,512]{1,0:T(8,128)(2,1)}, f32[8,128]{1,0:T(8,128)S(1)}) custom-call(bf16[1536,256]{1,0:T(8,128)(2,1)S(1)} %get-tuple-element.77.refs_0_, bf16[1536,256]{1,0:T(8,128)(2,1)S(1)} %collective-permute-done.7.refs_1_, bf16[128,128]{1,0:T(8,128)(2,1)S(1)} %shard_map.114.refs_2_.refs_0_), custom_call_target="tpu_custom_call" | custom-call | flops 10000000 | bytes 1000000 | tf_op jit(solution)/shard_map/pallas_call | solution.py:46
  92.4 1.9 %collective-permute-done.16.refs_2_ = bf16[256,128]{1,0:T(8,128)(2,1)S(1)} collective-permute-done((bf16[256,128]{1,0:T(8,128)(2,1)S(1)}, bf16[256,128]{1,0:T(8,128)(2,1)S(1)}, u32[]{:S(2)}, u32[]{:S(2)}) %collective-permute-start.16) | collective-permute-done | bytes 65568 | tf_op jit(solution)/shard_map/ppermute | solution.py:389
  94.3 0.1 collective-permute-done.17.refs_3_
  94.4 0.9 shard_map.117
  (15 shorter events, 0.2 us)
Async XLA Ops:
  0.6 6.9 %copy-start.2 = (bf16[512,1024]{1,0:T(8,128)(2,1)S(1)}, bf16[512,1024]{1,0:T(8,128)(2,1)}, u32[]{:S(2)}) copy-start(bf16[512,1024]{1,0:T(8,128)(2,1)} %refs_0_.3) | copy-start | bytes 3145732
  4.2 6.7 %collective-permute-start = (bf16[2064,256]{1,0:T(8,128)(2,1)}, bf16[2064,256]{1,0:T(8,128)(2,1)S(1)}, u32[]{:S(2)}, u32[]{:S(2)}) collective-permute-start(bf16[2064,256]{1,0:T(8,128)(2,1)} %get-tuple-element.47), channel_id=1, source_target_pairs={{0,4},{4,0},{8,12},{12,8},{16,20},{20,16},{24,28},{28,24},{32,36},... | collective-permute-start | bytes 3170312 | tf_op jit(solution)/shard_map/ppermute | solution.py:382
  7.5 11.1 %collective-permute-start.5 = (bf16[512,1024]{1,0:T(8,128)(2,1)S(1)}, bf16[512,1024]{1,0:T(8,128)(2,1)S(1)}, u32[]{:S(2)}, u32[]{:S(2)}) collective-permute-start(bf16[512,1024]{1,0:T(8,128)(2,1)S(1)} %copy-done.2), channel_id=1, source_target_pairs={{0,4},{4,0},{8,12},{12,8},{16,20},{20,16},{24,28},{28,24},{32,36},... | collective-permute-start | bytes 3145736 | tf_op jit(solution)/shard_map/ppermute | solution.py:382
  7.6 8.1 %collective-permute-start.1 = (f32[32,512]{1,0:T(8,128)}, f32[32,512]{1,0:T(8,128)S(1)}, u32[]{:S(2)}, u32[]{:S(2)}) collective-permute-start(f32[32,512]{1,0:T(8,128)} %get-tuple-element.56), channel_id=1, source_target_pairs={{0,1},{1,2},{2,3},{3,0},{4,5},{5,6},{6,7},{7,4},{8,9},{9,10},{10,1... | collective-permute-start | bytes 196616 | tf_op jit(solution)/shard_map/ppermute | solution.py:392
  7.6 8.1 %collective-permute-start.2 = (f32[32,512]{1,0:T(8,128)}, f32[32,512]{1,0:T(8,128)S(1)}, u32[]{:S(2)}, u32[]{:S(2)}) collective-permute-start(f32[32,512]{1,0:T(8,128)} %get-tuple-element.57), channel_id=1, source_target_pairs={{0,2},{1,3},{2,0},{3,1},{4,6},{5,7},{6,4},{7,5},{8,10},{9,11},{10,... | collective-permute-start | bytes 196616 | tf_op jit(solution)/shard_map/ppermute | solution.py:392
  9.8 6.0 %collective-permute-start.3 = (f32[32,512]{1,0:T(8,128)}, f32[32,512]{1,0:T(8,128)S(1)}, u32[]{:S(2)}, u32[]{:S(2)}) collective-permute-start(f32[32,512]{1,0:T(8,128)} %get-tuple-element.58), channel_id=1, source_target_pairs={{0,3},{1,0},{2,1},{3,2},{4,7},{5,4},{6,5},{7,6},{8,11},{9,8},{10,9... | collective-permute-start | bytes 196616 | tf_op jit(solution)/shard_map/ppermute | solution.py:392
  10.9 1.2 %copy-start = (bf16[2064,256]{1,0:T(8,128)(2,1)S(1)}, bf16[2064,256]{1,0:T(8,128)(2,1)}, u32[]{:S(2)}) copy-start(bf16[2064,256]{1,0:T(8,128)(2,1)} %get-tuple-element.46.refs_0_) | copy-start | bytes 3170308
  12.1 3.7 %copy-start.3 = (f32[32,512]{1,0:T(8,128)S(1)}, f32[32,512]{1,0:T(8,128)}, u32[]{:S(2)}) copy-start(f32[32,512]{1,0:T(8,128)} %get-tuple-element.55.refs_0_) | copy-start | bytes 196612
  12.1 5.3 %copy-start.1 = (bf16[2064,256]{1,0:T(8,128)(2,1)S(1)}, bf16[2064,256]{1,0:T(8,128)(2,1)}, u32[]{:S(2)}) copy-start(bf16[2064,256]{1,0:T(8,128)(2,1)} %get-tuple-element.46.refs_0_) | copy-start | bytes 3170308
  12.6 6.0 %collective-permute-start.6 = (bf16[256,128]{1,0:T(8,128)(2,1)S(1)}, bf16[256,128]{1,0:T(8,128)(2,1)S(1)}, u32[]{:S(2)}, u32[]{:S(2)}) collective-permute-start(bf16[256,128]{1,0:T(8,128)(2,1)S(1)} %get-tuple-element.61), channel_id=1, source_target_pairs={{0,8},{4,12},{16,24},{20,28},{32,40},{36,44},{48,56},{52,60},{64,7... | collective-permute-start | bytes 196616 | tf_op jit(solution)/shard_map/ppermute | solution.py:421
  15.8 2.8 %collective-permute-start.4 = (f32[16,512]{1,0:T(8,128)S(1)}, f32[16,512]{1,0:T(8,128)S(1)}, u32[]{:S(2)}, u32[]{:S(2)}) collective-permute-start(f32[16,512]{1,0:T(8,128)S(1)} %get-tuple-element.60), channel_id=1, source_target_pairs={{0,4},{4,0},{8,12},{12,8},{16,20},{20,16},{24,28},{28,24},{32,36},... | collective-permute-start | bytes 98312 | tf_op jit(solution)/shard_map/ppermute | solution.py:382
  55.9 9.3 %collective-permute-start.8 = (bf16[32,512]{1,0:T(8,128)(2,1)S(1)}, bf16[32,512]{1,0:T(8,128)(2,1)S(1)}, u32[]{:S(2)}, u32[]{:S(2)}) collective-permute-start(bf16[32,512]{1,0:T(8,128)(2,1)S(1)} %get-tuple-element.75.refs_10_.refs_2_), channel_id=1, source_target_pairs={{0,1},{1,2},{2,3},{3,0},{4,5},{5,6},{6,7},{7,4},{8,9},{9,10},{10,1... | collective-permute-start | bytes 98312 | tf_op jit(solution)/shard_map/ppermute | solution.py:392
  56.4 8.9 %collective-permute-start.9 = (bf16[32,512]{1,0:T(8,128)(2,1)S(1)}, bf16[32,512]{1,0:T(8,128)(2,1)S(1)}, u32[]{:S(2)}, u32[]{:S(2)}) collective-permute-start(bf16[32,512]{1,0:T(8,128)(2,1)S(1)} %get-tuple-element.75.refs_10_.refs_2_), channel_id=1, source_target_pairs={{0,2},{1,3},{2,0},{3,1},{4,6},{5,7},{6,4},{7,5},{8,10},{9,11},{10,... | collective-permute-start | bytes 98312 | tf_op jit(solution)/shard_map/ppermute | solution.py:392
  58.1 7.2 %collective-permute-start.10 = (bf16[32,512]{1,0:T(8,128)(2,1)S(1)}, bf16[32,512]{1,0:T(8,128)(2,1)S(1)}, u32[]{:S(2)}, u32[]{:S(2)}) collective-permute-start(bf16[32,512]{1,0:T(8,128)(2,1)S(1)} %get-tuple-element.75.refs_10_.refs_2_), channel_id=1, source_target_pairs={{0,3},{1,0},{2,1},{3,2},{4,7},{5,4},{6,5},{7,6},{8,11},{9,8},{10,9... | collective-permute-start | bytes 98312 | tf_op jit(solution)/shard_map/ppermute | solution.py:392
  60.0 31.2 %collective-permute-start.7 = (bf16[1536,256]{1,0:T(8,128)(2,1)S(1)}, bf16[1536,256]{1,0:T(8,128)(2,1)S(1)}, u32[]{:S(2)}, u32[]{:S(2)}) collective-permute-start(bf16[1536,256]{1,0:T(8,128)(2,1)S(1)} %get-tuple-element.78), channel_id=1, source_target_pairs={{0,4},{4,0},{8,12},{12,8},{16,20},{20,16},{24,28},{28,24},{32,36},... | collective-permute-start | bytes 2359304 | tf_op jit(solution)/shard_map/ppermute | solution.py:382
  65.8 4.1 %collective-permute-start.11 = (bf16[128,128]{1,0:T(8,128)(2,1)S(1)}, bf16[128,128]{1,0:T(8,128)(2,1)S(1)}, u32[]{:S(2)}, u32[]{:S(2)}) collective-permute-start(bf16[128,128]{1,0:T(8,128)(2,1)S(1)} %get-tuple-element.81), channel_id=1, source_target_pairs={{0,8},{4,12},{8,16},{12,20},{16,24},{20,28},{24,0},{28,4},{32,40},... | collective-permute-start | bytes 98312 | tf_op jit(solution)/shard_map/ppermute | solution.py:389
  65.9 4.6 %collective-permute-start.12 = (bf16[128,128]{1,0:T(8,128)(2,1)S(1)}, bf16[128,128]{1,0:T(8,128)(2,1)S(1)}, u32[]{:S(2)}, u32[]{:S(2)}) collective-permute-start(bf16[128,128]{1,0:T(8,128)(2,1)S(1)} %get-tuple-element.82), channel_id=1, source_target_pairs={{0,16},{4,20},{8,24},{12,28},{16,0},{20,4},{24,8},{28,12},{32,48},... | collective-permute-start | bytes 98312 | tf_op jit(solution)/shard_map/ppermute | solution.py:389
  68.0 3.1 %collective-permute-start.13 = (bf16[128,128]{1,0:T(8,128)(2,1)S(1)}, bf16[128,128]{1,0:T(8,128)(2,1)S(1)}, u32[]{:S(2)}, u32[]{:S(2)}) collective-permute-start(bf16[128,128]{1,0:T(8,128)(2,1)S(1)} %get-tuple-element.83), channel_id=1, source_target_pairs={{0,24},{4,28},{8,0},{12,4},{16,8},{20,12},{24,16},{28,20},{32,56},... | collective-permute-start | bytes 98312 | tf_op jit(solution)/shard_map/ppermute | solution.py:389
  82.8 4.6 %collective-permute-start.14 = (bf16[128,128]{1,0:T(8,128)(2,1)S(1)}, bf16[128,128]{1,0:T(8,128)(2,1)S(1)}, u32[]{:S(2)}, u32[]{:S(2)}) collective-permute-start(bf16[128,128]{1,0:T(8,128)(2,1)S(1)} %shard_map.114.refs_2_.refs_0_), channel_id=1, source_target_pairs={{0,4},{4,0},{8,12},{12,8},{16,20},{20,16},{24,28},{28,24},{32,36},... | collective-permute-start | bytes 98312 | tf_op jit(solution)/shard_map/ppermute | solution.py:382
  87.4 5.0 %collective-permute-start.15 = (bf16[256,128]{1,0:T(8,128)(2,1)S(1)}, bf16[256,128]{1,0:T(8,128)(2,1)S(1)}, u32[]{:S(2)}, u32[]{:S(2)}) collective-permute-start(bf16[256,128]{1,0:T(8,128)(2,1)S(1)} %shard_map.116.refs_0_), channel_id=1, source_target_pairs={{0,8},{4,12},{8,16},{12,20},{16,24},{20,28},{24,0},{28,4},{32,40},... | collective-permute-start | bytes 196616 | tf_op jit(solution)/shard_map/ppermute | solution.py:389
  88.7 5.6 %collective-permute-start.16 = (bf16[256,128]{1,0:T(8,128)(2,1)S(1)}, bf16[256,128]{1,0:T(8,128)(2,1)S(1)}, u32[]{:S(2)}, u32[]{:S(2)}) collective-permute-start(bf16[256,128]{1,0:T(8,128)(2,1)S(1)} %shard_map.116.refs_0_), channel_id=1, source_target_pairs={{0,16},{4,20},{8,24},{12,28},{16,0},{20,4},{24,8},{28,12},{32,48},... | collective-permute-start | bytes 196616 | tf_op jit(solution)/shard_map/ppermute | solution.py:389
  90.7 3.7 %collective-permute-start.17 = (bf16[256,128]{1,0:T(8,128)(2,1)S(1)}, bf16[256,128]{1,0:T(8,128)(2,1)S(1)}, u32[]{:S(2)}, u32[]{:S(2)}) collective-permute-start(bf16[256,128]{1,0:T(8,128)(2,1)S(1)} %shard_map.116.refs_0_), channel_id=1, source_target_pairs={{0,24},{4,28},{8,0},{12,4},{16,8},{20,12},{24,16},{28,20},{32,56},... | collective-permute-start | bytes 196616 | tf_op jit(solution)/shard_map/ppermute | solution.py:389

commit v8 on v7

--- a/solution.py
+++ b/solution.py
@@ -14,7 +14,6 @@
 DIM = 128
 SPAN = 64
 LEVELS = 8
-CHIPS = 32
 INV = 1.0 / DIM
 VMEM_LIMIT = 24 * 1024 * 1024
 VMEM_ALL = 60 * 1024 * 1024
@@ -117,7 +116,7 @@
 Q, K, V, G = (slice(TOK * i, TOK * (i + 1)) for i in range(4))
 
 
-def state_body(own_ref, sib_ref, so_ref, ss_ref, qto_ref, qts_ref, kto_ref, kts_ref, ao_ref, as_ref, pair_ref):
+def state_body(own_ref, sib_ref, so_ref, ss_ref, qto_ref, qts_ref, kto_ref, kts_ref, ao_ref, as_ref):
     for ref, state, query_t, key_t, mask in (
         (own_ref, so_ref, qto_ref, kto_ref, ao_ref), (sib_ref, ss_ref, qts_ref, kts_ref, as_ref),
     ):
@@ -128,7 +127,6 @@
             key_t[lanes, :] = ref[K, lanes].T
         allowed = ref[4 * TOK :, :].astype(F32)
         mask[...] = jnp.concatenate([allowed[:8], allowed[8:]], axis=1)
-    pair_ref[...] = (so_ref[...] + ss_ref[...]).astype(BF16)
 
 
 def span_masks():
@@ -173,7 +171,7 @@
 
 def level_body(
     own_ref, sib_ref, qto_ref, qts_ref, ao_ref, as_ref, so_ref, ss_ref, lo_ref, ls_ref,
-    go_ref, gs_ref, near_ref, o_ref, scr,
+    go_ref, gs_ref, near_ref, own_slice_ref, m1_ref, m2_ref, m3_ref, scr,
 ):
     core = lax.axis_index("seq") & 1
     gates = [jax.nn.sigmoid(lo_ref[...]), jax.nn.sigmoid(ls_ref[...])]
@@ -193,53 +191,64 @@
         for level in range(3):
             row = 256 * (level + 1) + DIM * i
             scr[row : row + DIM, :] = total[DIM * level : DIM * (level + 1)]
-    for chip in range(CHIPS):
-        rows = [scr[256 * level + 8 * chip : 256 * level + 8 * chip + 8, :] for level in range(4)]
-        o_ref[chip] = jnp.concatenate(rows, axis=0).astype(BF16)
-
-
-def mid1_body(r_ref, o_ref):
-    got = [r_ref[chip].astype(F32) for chip in range(CHIPS)]
-    own = [part[0:8] for part in got]
-    pairs = [own[chip] + own[chip ^ 1] for chip in range(CHIPS)]
-    zero = jnp.zeros((8, DIM), F32)
-    before = [zero]
-    for group in range(7):
-        before.append(before[-1] + (pairs[4 * group] + pairs[4 * group + 2]))
-    after = [zero]
-    for group in range(7, 0, -1):
-        total = [got[4 * group + i][24:32] for i in range(4)]
-        after.append(after[-1] + ((total[0] + total[1]) + (total[2] + total[3])))
-    after = after[::-1]
-    for chip in range(CHIPS):
-        later = after[chip >> 2]
-        if not chip & 2:
-            later = later + (got[chip ^ 2][16:24] + got[chip ^ 3][16:24])
-        if not chip & 1:
-            later = later + got[chip ^ 1][8:16]
-        rows = [pairs[chip ^ 2] if chip & 2 else zero, before[chip >> 2], later]
-        o_ref[chip] = jnp.concatenate(rows, axis=0).astype(BF16)
-
-
-def mid2_body(r_ref, o_ref):
-    for chip in range(0, CHIPS, 2):
-        got = [r_ref[chip + i].astype(F32) for i in range(2)]
-        for level in range(3):
-            both = [part[8 * level : 8 * level + 8] for part in got]
-            row = 256 * level + 8 * chip
-            o_ref[row : row + 16, :] = jnp.concatenate(both, axis=0).astype(BF16)
-
-
-def far_projection(i, ref, next_ref, mine_ref):
+    place = (lax.axis_index("seq") // 2) % 4
+    own_slice_ref[0:64, :] = scr[aligned(place, 64), :]
+    own_slice_ref[64:128, :] = scr[pl.ds(pl.multiple_of(768 + 64 * place, 64), 64), :]
+    for mask, out in ((1, m1_ref), (2, m2_ref), (3, m3_ref)):
+        later = (place >> (mask >> 1)) & 1
+        start = later * (256 if mask == 1 else 512)
+        out[0:256, :] = scr[pl.ds(pl.multiple_of(start, 256), 256), :].astype(BF16)
+        peer = 64 * (place ^ mask)
+        for part in range(2):
+            rows = scr[pl.ds(pl.multiple_of(768 * part + peer, 64), 64), :]
+            out[256 + 64 * part : 320 + 64 * part, :] = rows.astype(BF16)
+
+
+def along_x_body(own_ref, m1_ref, m2_ref, m3_ref, spread_ref, states_ref, later_ref):
+    place = (lax.axis_index("seq") // 2) % 4
+    got = [m1_ref[...].astype(F32), m2_ref[...].astype(F32), m3_ref[...].astype(F32)]
+    level5, level6 = got[0][:256], got[1][:256] + got[2][:256]
+    upper5 = (place & 1).astype(F32)
+    upper6 = (place >> 1).astype(F32)
+    states_ref[0:256, :] = (level5 * upper5).astype(BF16)
+    states_ref[256:512, :] = (level6 * upper6).astype(BF16)
+    later_ref[...] = level5 * (1.0 - upper5) + level6 * (1.0 - upper6)
+    total = own_ref[...] + got[0][256:] + (got[1][256:] + got[2][256:])
+    here = lax.axis_index("seq") // 8
+    for group in range(8):
+        spread_ref[7 - group] = jnp.where(group > here, total[:64], total[64:]).astype(BF16)
+
+
+def along_z_body(r_ref, o_ref):
+    here = lax.axis_index("seq") // 8
+    before = jnp.zeros((64, DIM), F32)
+    after = jnp.zeros((64, DIM), F32)
+    for group in range(8):
+        part = r_ref[7 - group].astype(F32)
+        before = before + part * (here > group).astype(F32)
+        after = after + part * (here < group).astype(F32)
+    o_ref[...] = jnp.concatenate([before, after], axis=0).astype(BF16)
+
+
+def far_body(own_ref, r1, r2, r3, states_ref, near_ref, mine_ref, later_ref):
+    place = (lax.axis_index("seq") // 2) % 4
+    mine_ref[0:512, :] = states_ref[...]
+    for mask, ref in enumerate((own_ref, r1, r2, r3)):
+        peer = 64 * (place ^ mask)
+        mine_ref[pl.ds(pl.multiple_of(512 + peer, 64), 64), :] = ref[0:64, :]
+        rows = pl.ds(pl.multiple_of(peer, 64), 64)
+        later_ref[rows, :] = near_ref[rows, :] + ref[64:128, :].astype(F32)
+
+
+def far_projection(i, ref, mine_ref):
     lanes = slice(DIM * i, DIM * (i + 1))
-    states = [next_ref[lanes, :]]
-    states += [mine_ref[256 * level + DIM * i : 256 * level + DIM * (i + 1), :] for level in range(2)]
+    states = [mine_ref[256 * level + DIM * i : 256 * level + DIM * (i + 1), :] for level in range(3)]
     projected = mm(jnp.concatenate(states, axis=0), ref[G, lanes], 1, 1)
     return [projected[DIM * level : DIM * (level + 1)] for level in range(3)]
 
 
 def cross_body(
-    own_ref, sib_ref, qto_ref, qts_ref, ao_ref, as_ref, go_ref, gs_ref, ro_ref, rs_ref, next_ref, mine_ref, gl_ref, co_ref, cs_ref
+    own_ref, sib_ref, qto_ref, qts_ref, ao_ref, as_ref, go_ref, gs_ref, ro_ref, rs_ref, mine_ref, gl_ref, co_ref, cs_ref
 ):
     outs = []
     for ref, query_t, mask, gates_ref, rows_ref, cross_ref in (
@@ -252,7 +261,7 @@
             weight = gates * mask[...]
             parts = [jnp.zeros((5, TOK), F32)]
             total = None
-            for level, term in enumerate(far_projection(i, ref, next_ref, mine_ref)):
+            for level, term in enumerate(far_projection(i, ref, mine_ref)):
                 parts.append(jnp.sum(query * term, axis=0, keepdims=True))
                 weighted = weight[5 + level : 6 + level, :] * term
                 total = weighted if total is None else total + weighted
@@ -263,7 +272,7 @@
 
 
 def tail_body(
-    block, blk_ref, kt_ref, state_ref, near_ref, mask_ref, gates_ref, mine_ref, cross_ref, score_ref, prob_ref,
+    block, blk_ref, kt_ref, state_ref, near_ref, mask_ref, gates_ref, later_ref, cross_ref, score_ref, prob_ref,
     out_ref, token_ref,
 ):
     core = lax.axis_index("seq") & 1
@@ -274,8 +283,7 @@
         query, key, value, grad = blk_ref[Q, lanes], blk_ref[K, lanes], blk_ref[V, lanes], blk_ref[G, lanes]
         weight = gates_ref[8 * i : 8 * i + 8, :] * mask_ref[...]
         near = mm((state_ref[lanes, :] * upper).astype(BF16), grad, 1, 1)
-        later = mine_ref[512 + DIM * i : 512 + DIM * (i + 1), :].astype(F32)
-        later = (later + near_ref[lanes, :] * (1.0 - upper)).astype(BF16)
+        later = (later_ref[lanes, :] + near_ref[lanes, :] * (1.0 - upper)).astype(BF16)
         dk = mm(value, later, 1, 1)
         dv = mm(key, later)
         for a in range(2):
@@ -375,14 +383,14 @@
 
 def shards(layer_input, gate_weight, queries, key_vectors, value_vectors, grad_output, reach_level):
     seq_count = lax.axis_size("seq")
-    groups = [[2 * chip + c for chip in range(CHIPS)] for c in range(2)]
+    columns = [[8 * z + place for z in reversed(range(8))] for place in range(8)]
     swap = [(d, d ^ 1) for d in range(seq_count)]
 
     def sibling(value):
         return lax.ppermute(value, "seq", swap)
 
-    def exchange(value):
-        return lax.all_to_all(value, "seq", 0, 0, axis_index_groups=groups)
+    def swap_x(value, mask):
+        return lax.ppermute(value, "seq", [(d, d ^ (2 * mask)) for d in range(seq_count)])
 
     def rotate_x(value, step):
         pairs = [(d, d // 8 * 8 + (d + 2 * step) % 8) for d in range(seq_count)]
@@ -414,38 +422,44 @@
     logits = [parts[0]] + [rotate(parts[step], step) for step in range(1, 4)]
     sib = sibling(leaving)
     sib_input = sibling(layer_input)
-    state_own, state_sib, qt_own, qt_sib, kt_own, kt_sib, allow_own, allow_sib, pair_state = call(
-        state_body, [half, half] + [shape((256, TOK), BF16)] * 4 + [mask8, mask8, shape((256, DIM), BF16)],
+    state_own, state_sib, qt_own, qt_sib, kt_own, kt_sib, allow_own, allow_sib = call(
+        state_body, [half, half] + [shape((256, TOK), BF16)] * 4 + [mask8, mask8],
         (own, sib),
     )
-    next_state = lax.ppermute(pair_state, "seq", [(d, d ^ 2) for d in range(seq_count) if not d & 2])
     pairs = shape((1536, 256), F32)
     rows_own, rows_sib, sc_own, pr_own, sc_sib, pr_sib = call(
         rows_body, [tok16, tok16] + [pairs] * 4, (own, sib, qt_own, qt_sib, state_own, state_sib)
     )
-    logits_own, logits_send = call(gather_body, [tok16, tok16], tuple(logits))
-
-    gates_own, gates_sib, near, slices = call(
-        level_body, [tok16, tok16, half, shape((CHIPS, 32, DIM), BF16)],
+    logits_own, logits_send = call(gather_body, [tok16, tok16], tuple(logits), after=(rows_own,))
+
+    message = shape((384, DIM), BF16)
+    eighth = shape((DIM, DIM), BF16)
+    gates_own, gates_sib, near, own_slice, *messages = call(
+        level_body, [tok16, tok16, half, shape((DIM, DIM), F32), message, message, message],
         (own, sib, qt_own, qt_sib, allow_own, allow_sib, state_own, state_sib, logits_own, sibling(logits_send)),
         scratch=[pltpu.VMEM((1024, DIM), F32)],
-        after=(sib_input, next_state, rows_own),
-    )
-    got1 = exchange(slices)
-
-    got2 = exchange(call(mid1_body, shape((CHIPS, 24, DIM), BF16), (got1,)))
-    mine = call(mid2_body, shape((768, DIM), BF16), (got2,))
+        after=(sib_input, rows_own),
+    )
+    spread, close_states, close_later = call(
+        along_x_body, [shape((8, 64, DIM), BF16), shape((512, DIM), BF16), half],
+        (own_slice, *(swap_x(messages[mask - 1], mask) for mask in (1, 2, 3))),
+    )
+    got = call(along_z_body, eighth, (lax.all_to_all(spread, "seq", 0, 0, axis_index_groups=columns),))
+    mine, later = call(
+        far_body, [shape((768, DIM), BF16), half],
+        (got, *(swap_x(got, mask) for mask in (1, 2, 3)), close_states, close_later),
+    )
     tok256 = shape((256, TOK), F32)
     grad_logits, cross_own, cross_sib = call(
         cross_body, [shape((32, TOK), BF16), tok256, tok256],
-        (own, sib, qt_own, qt_sib, allow_own, allow_sib, gates_own, gates_sib, rows_own, rows_sib, next_state, mine),
+        (own, sib, qt_own, qt_sib, allow_own, allow_sib, gates_own, gates_sib, rows_own, rows_sib, mine),
     )
 
     gl = [grad_logits] + [rotate(grad_logits, step) for step in range(1, 4)]
     def tail(which, blk, key_t, state, allowed, gates, cross, scores, probs, after):
         return call(
             functools.partial(tail_body, which), [shape((3 * TOK, 256), BF16), shape((8, DIM), F32)],
-            (blk, key_t, state, near, allowed, gates, mine, cross, scores, probs), after=after, cost=(4 * 10**9, 16 * 10**6),
+            (blk, key_t, state, near, allowed, gates, later, cross, scores, probs), after=after, cost=(4 * 10**9, 16 * 10**6),
         )
 
     out_sib, token = tail(1, sib, kt_sib, state_own, allow_sib, gates_sib, cross_sib, sc_sib, pr_sib, (grad_logits,))
@@ -459,7 +473,6 @@
     )
     got3 = [sums[0]] + [rotate_x(sums[step], step) for step in range(1, 4)]
     spread = call(sum_x_body, shape((8, DIM, DIM), BF16), tuple(got3))
-    columns = [[8 * z + place for z in range(8)] for place in range(8)]
     got4 = lax.all_to_all(spread, "seq", 0, 0, axis_index_groups=columns)
     scale = 1.0 / math.sqrt(TOK * seq_count)
     mine_sum = call(functools.partial(sum_z_body, scale), quarter, (got4,))

time: 95.8 us -> 90 us (0.939)
  blocking collectives: 47.4 us -> 24.3 us
  waiting for transfers between devices: 5.11 us -> 15.2 us
  starting transfers between devices: 29.3 us -> 36.3 us
    all_to_all x2 -> x1, blocking collectives: 35.8 us -> 13.1 us  [shards(): lax.all_to_all(spread, 'seq', 0, 0, axis_index_groups=columns)]
    ppermute x1 -> x6, waiting for transfers between devices: 0.01 us -> 8.54 us  [swap_x(): lax.ppermute(value, 'seq', [(d, d ^ 2 * mask) for d in range(seq_count)])]
    ppermute x1 -> x6, starting transfers between devices: 3.12 us -> 7.88 us  [swap_x(): lax.ppermute(value, 'seq', [(d, d ^ 2 * mask) for d in range(seq_count)])]
    ppermute x5, starting transfers between devices: 13.1 us -> 14.6 us  [sibling(): return lax.ppermute(value, 'seq', swap)]
    pallas_call x16 -> x17, Pallas kernels: 11.5 us -> 11.8 us  [call(): pl.pallas_call(kernel, out_shape=out_shape, grid=grid, in_specs=in_specs,...]
  transfers between devices with their start and end apart: 18 -> 23, of which waited for: 6 -> 14; matrix products, arithmetic and copies ran while one was open for 0% -> 0% of each run, Pallas kernels for 6% -> 6%
where the time goes in v8:
time: 90 us; the launch traced here: 89.8 us
  starting transfers between devices  36.3 us (40%)
  blocking collectives  24.3 us (27%)
  waiting for transfers between devices  15.2 us (17%)
  Pallas kernels  11.8 us (13%)
  local copies, waits for them, and re-layouts  1.24 us (1%)
  between operations  1 us (1%)
    ppermute x5, starting transfers between devices, sibling(): return lax.ppermute(value, 'seq', swap)  14.6 us
    all_to_all x1, blocking collectives, shards(): lax.all_to_all(spread, 'seq', 0, 0, axis_index_groups=columns)  13.1 us
    pallas_call x17, Pallas kernels, call(): pl.pallas_call(kernel, out_shape=out_shape, grid=grid, in_specs=in_specs,...  11.8 us
    all_to_all x1, blocking collectives, shards(): got4 = lax.all_to_all(spread, 'seq', 0, 0, axis_index_groups=columns)  11.1 us
    ppermute x6, waiting for transfers between devices, swap_x(): lax.ppermute(value, 'seq', [(d, d ^ 2 * mask) for d in range(seq_count)])  8.54 us
    ppermute x6, starting transfers between devices, swap_x(): lax.ppermute(value, 'seq', [(d, d ^ 2 * mask) for d in range(seq_count)])  7.88 us
    ppermute x6, starting transfers between devices, rotate_x(): return lax.ppermute(value, 'seq', pairs)  6.96 us
    ppermute x6, starting transfers between devices, rotate(): return lax.ppermute(value, 'head', [(h, (h + step) % 4) for h in range(4)])  6.87 us
  transfers between devices with their start and end apart: 23, of which 14 were waited for; matrix products, arithmetic and copies ran while one was open for 0% of the time, Pallas kernels for 6%

profile of v8, /device:TPU:1, one launch (start us, length us, event | category | flops | bytes accessed | tf_op | source)
XLA Modules:
  0.0 89.8 jit_solution(404924217973124601)
XLA Ops:
  0.6 3.7 %shard_map.102 = (f32[32,512]{1,0:T(8,128)}, f32[32,512]{1,0:T(8,128)}, f32[32,512]{1,0:T(8,128)}, f32[32,512]{1,0:T(8,128)}, bf16[2064,256]{1,0:T(8,128)(2,1)}, /*index=5*/bf16[2064,256]{1,0:T(8,128)(2,1)}) custom-call(bf16[512,1024]{1,0:T(8,128)(2,1)} %refs_0_.3, bf16[1024,128]{1,0:T(8,128)(2,1)} %refs_1_.1, bf16[512,512]{1,0:T(8,128)(2,1)} %refs_2_.1, ...), custom_call_target="tpu_custom_call" | custom-call | flops 10000000 | bytes 1000000 | tf_op jit(solution)/shard_map/pallas_call | solution.py:45
  4.4 3.3 %collective-permute-start = (bf16[2064,256]{1,0:T(8,128)(2,1)}, bf16[2064,256]{1,0:T(8,128)(2,1)S(1)}, u32[]{:S(2)}, u32[]{:S(2)}) collective-permute-start(bf16[2064,256]{1,0:T(8,128)(2,1)} %get-tuple-element.54), channel_id=1, source_target_pairs={{0,4},{4,0},{8,12},{12,8},{16,20},{20,16},{24,28},{28,24},{32,36},... | collective-permute-start | bytes 3170312 | tf_op jit(solution)/shard_map/ppermute | solution.py:390
  7.7 0.1 collective-permute-start.5
  7.8 2.2 %collective-permute-start.2 = (f32[32,512]{1,0:T(8,128)}, f32[32,512]{1,0:T(8,128)S(1)}, u32[]{:S(2)}, u32[]{:S(2)}) collective-permute-start(f32[32,512]{1,0:T(8,128)} %get-tuple-element.64), channel_id=1, source_target_pairs={{0,2},{1,3},{2,0},{3,1},{4,6},{5,7},{6,4},{7,5},{8,10},{9,11},{10,... | collective-permute-start | bytes 196616 | tf_op jit(solution)/shard_map/ppermute | solution.py:400
  10.0 1.1 %collective-permute-start.3 = (f32[32,512]{1,0:T(8,128)}, f32[32,512]{1,0:T(8,128)S(1)}, u32[]{:S(2)}, u32[]{:S(2)}) collective-permute-start(f32[32,512]{1,0:T(8,128)} %get-tuple-element.65), channel_id=1, source_target_pairs={{0,3},{1,0},{2,1},{3,2},{4,7},{5,4},{6,5},{7,6},{8,11},{9,8},{10,9... | collective-permute-start | bytes 196616 | tf_op jit(solution)/shard_map/ppermute | solution.py:400
  11.1 1.2 %copy-done = bf16[2064,256]{1,0:T(8,128)(2,1)S(1)} copy-done((bf16[2064,256]{1,0:T(8,128)(2,1)S(1)}, bf16[2064,256]{1,0:T(8,128)(2,1)}, u32[]{:S(2)}) %copy-start) | copy-done | bytes 1056792
  12.3 0.5 shard_map.103
  12.8 1.2 %shard_map.104 = (f32[16,512]{1,0:T(8,128)S(1)}, f32[16,512]{1,0:T(8,128)S(1)}, f32[1536,256]{1,0:T(8,128)S(1)}, f32[1536,256]{1,0:T(8,128)S(1)}, f32[1536,256]{1,0:T(8,128)S(1)}, /*index=5*/f32[1536,256]{1,0:T(8,128)S(1)}) custom-call(bf16[2064,256]{1,0:T(8,128)(2,1)S(1)} %copy-done, bf16[2064,256]{1,0:T(8,128)(2,1)S(1)} %collective-permute-done.refs_1_.refs_0_, ...), custom_call_target="tpu_custom_call" | custom-call | flops 10000000 | bytes 1000000 | tf_op jit(solution)/shard_map/pallas_call | solution.py:45
  14.0 0.1 collective-permute-done.3.refs_3_
  14.2 1.6 %collective-permute-start.4 = (f32[16,512]{1,0:T(8,128)S(1)}, f32[16,512]{1,0:T(8,128)S(1)}, u32[]{:S(2)}, u32[]{:S(2)}) collective-permute-start(f32[16,512]{1,0:T(8,128)S(1)} %get-tuple-element.68), channel_id=1, source_target_pairs={{0,4},{4,0},{8,12},{12,8},{16,20},{20,16},{24,28},{28,24},{32,36},... | collective-permute-start | bytes 98312 | tf_op jit(solution)/shard_map/ppermute | solution.py:390
  15.8 0.9 collective-permute-done.4.refs_9_
  16.7 0.7 shard_map.106
  17.4 1.0 %collective-permute-start.6 = (bf16[384,128]{1,0:T(8,128)(2,1)S(1)}, bf16[384,128]{1,0:T(8,128)(2,1)S(1)}, u32[]{:S(2)}, u32[]{:S(2)}) collective-permute-start(bf16[384,128]{1,0:T(8,128)(2,1)S(1)} %get-tuple-element.72), channel_id=1, source_target_pairs={{0,8},{4,12},{8,0},{12,4},{16,24},{20,28},{24,16},{28,20},{32,40},... | collective-permute-start | bytes 294920 | tf_op jit(solution)/shard_map/ppermute | solution.py:393
  18.5 2.5 %collective-permute-start.7 = (bf16[384,128]{1,0:T(8,128)(2,1)S(1)}, bf16[384,128]{1,0:T(8,128)(2,1)S(1)}, u32[]{:S(2)}, u32[]{:S(2)}) collective-permute-start(bf16[384,128]{1,0:T(8,128)(2,1)S(1)} %get-tuple-element.73), channel_id=1, source_target_pairs={{0,16},{4,20},{8,24},{12,28},{16,0},{20,4},{24,8},{28,12},{32,48},... | collective-permute-start | bytes 294920 | tf_op jit(solution)/shard_map/ppermute | solution.py:393
  20.9 0.4 collective-permute-start.8
  21.4 0.2 collective-permute-done.6.refs_1_
  21.5 4.1 %collective-permute-done.7.refs_2_ = bf16[384,128]{1,0:T(8,128)(2,1)S(1)} collective-permute-done((bf16[384,128]{1,0:T(8,128)(2,1)S(1)}, bf16[384,128]{1,0:T(8,128)(2,1)S(1)}, u32[]{:S(2)}, u32[]{:S(2)}) %collective-permute-start.7) | collective-permute-done | bytes 98336 | tf_op jit(solution)/shard_map/ppermute | solution.py:393
  25.6 2.6 %collective-permute-done.8.refs_3_ = bf16[384,128]{1,0:T(8,128)(2,1)S(1)} collective-permute-done((bf16[384,128]{1,0:T(8,128)(2,1)S(1)}, bf16[384,128]{1,0:T(8,128)(2,1)S(1)}, u32[]{:S(2)}, u32[]{:S(2)}) %collective-permute-start.8) | collective-permute-done | bytes 98336 | tf_op jit(solution)/shard_map/ppermute | solution.py:393
  28.2 0.1 shard_map.107
  28.3 13.1 %all_to_all.10.refs_0_ = bf16[8,64,128]{2,1,0:T(8,128)(2,1)S(1)} all-to-all(bf16[8,64,128]{2,1,0:T(8,128)(2,1)S(1)} %get-tuple-element.75), channel_id=1, replica_groups={{224,192,160,128,96,64,32,0},{228,196,164,132,100,68,36,4},{232,200,168..., dimensions={0} | all-to-all | bytes 262144 | tf_op jit(solution)/shard_map/all_to_all | solution.py:447
  41.5 0.1 collective-permute-start.9
  41.6 1.6 %collective-permute-start.10 = (bf16[128,128]{1,0:T(8,128)(2,1)S(1)}, bf16[128,128]{1,0:T(8,128)(2,1)S(1)}, u32[]{:S(2)}, u32[]{:S(2)}) collective-permute-start(bf16[128,128]{1,0:T(8,128)(2,1)S(1)} %shard_map.108.refs_0_), channel_id=1, source_target_pairs={{0,16},{4,20},{8,24},{12,28},{16,0},{20,4},{24,8},{28,12},{32,48},... | collective-permute-start | bytes 98312 | tf_op jit(solution)/shard_map/ppermute | solution.py:393
  43.2 2.2 %collective-permute-start.11 = (bf16[128,128]{1,0:T(8,128)(2,1)S(1)}, bf16[128,128]{1,0:T(8,128)(2,1)S(1)}, u32[]{:S(2)}, u32[]{:S(2)}) collective-permute-start(bf16[128,128]{1,0:T(8,128)(2,1)S(1)} %shard_map.108.refs_0_), channel_id=1, source_target_pairs={{0,24},{4,28},{8,16},{12,20},{16,8},{20,12},{24,0},{28,4},{32,56},... | collective-permute-start | bytes 98312 | tf_op jit(solution)/shard_map/ppermute | solution.py:393
  45.4 0.5 collective-permute-done.10.refs_2_
  45.9 1.2 %collective-permute-done.11.refs_3_ = bf16[128,128]{1,0:T(8,128)(2,1)S(1)} collective-permute-done((bf16[128,128]{1,0:T(8,128)(2,1)S(1)}, bf16[128,128]{1,0:T(8,128)(2,1)S(1)}, u32[]{:S(2)}, u32[]{:S(2)}) %collective-permute-start.11) | collective-permute-done | bytes 32800 | tf_op jit(solution)/shard_map/ppermute | solution.py:393
  47.2 0.7 shard_map.110
  47.9 0.4 collective-permute-start.13
  48.3 3.2 %collective-permute-start.14 = (bf16[32,512]{1,0:T(8,128)(2,1)S(1)}, bf16[32,512]{1,0:T(8,128)(2,1)S(1)}, u32[]{:S(2)}, u32[]{:S(2)}) collective-permute-start(bf16[32,512]{1,0:T(8,128)(2,1)S(1)} %get-tuple-element.89.refs_10_.refs_2_), channel_id=1, source_target_pairs={{0,2},{1,3},{2,0},{3,1},{4,6},{5,7},{6,4},{7,5},{8,10},{9,11},{10,... | collective-permute-start | bytes 98312 | tf_op jit(solution)/shard_map/ppermute | solution.py:400
  51.5 1.1 %shard_map.111 = (bf16[1536,256]{1,0:T(8,128)(2,1)S(1)}, f32[8,128]{1,0:T(8,128)S(1)}) custom-call(bf16[2064,256]{1,0:T(8,128)(2,1)S(1)} %collective-permute-done.refs_1_.refs_0_, bf16[256,512]{1,0:T(8,128)(2,1)S(1)} %get-tuple-element.85.refs_1_, f32[256,128]{1,0:T(8,128)S(1)} %get-tuple-element.61.refs_4_.refs_6_.refs_2_, ...), custom_call_target="tpu_custom_call" | custom-call | flops 4000000000 | bytes 16000000 | tf_op jit(solution)/shard_map/pallas_call | solution.py:45
  52.6 4.5 %collective-permute-start.12 = (bf16[1536,256]{1,0:T(8,128)(2,1)S(1)}, bf16[1536,256]{1,0:T(8,128)(2,1)S(1)}, u32[]{:S(2)}, u32[]{:S(2)}) collective-permute-start(bf16[1536,256]{1,0:T(8,128)(2,1)S(1)} %get-tuple-element.92), channel_id=1, source_target_pairs={{0,4},{4,0},{8,12},{12,8},{16,20},{20,16},{24,28},{28,24},{32,36},... | collective-permute-start | bytes 2359304 | tf_op jit(solution)/shard_map/ppermute | solution.py:390
  57.1 0.9 %shard_map.112 = (bf16[1536,256]{1,0:T(8,128)(2,1)S(1)}, f32[8,128]{1,0:T(8,128)S(1)}) custom-call(bf16[2064,256]{1,0:T(8,128)(2,1)S(1)} %copy-done.1, bf16[256,512]{1,0:T(8,128)(2,1)S(1)} %get-tuple-element.55.refs_1_, f32[256,128]{1,0:T(8,128)S(1)} %get-tuple-element.56.refs_5_.refs_7_.refs_2_, f32[256,128]{1,0:T(8,128)S(1)} %get-tuple-element.69.refs_3_, ...), custom_call_target="tpu_custom_call" | custom-call | flops 4000000000 | bytes 16000000 | tf_op jit(solution)/shard_map/pallas_call | solution.py:45
  58.1 0.5 shard_map.113
  58.6 0.1 collective-permute-start.16
  58.7 3.5 %collective-permute-start.17 = (bf16[128,128]{1,0:T(8,128)(2,1)S(1)}, bf16[128,128]{1,0:T(8,128)(2,1)S(1)}, u32[]{:S(2)}, u32[]{:S(2)}) collective-permute-start(bf16[128,128]{1,0:T(8,128)(2,1)S(1)} %get-tuple-element.96), channel_id=1, source_target_pairs={{0,16},{4,20},{8,24},{12,28},{16,0},{20,4},{24,8},{28,12},{32,48},... | collective-permute-start | bytes 98312 | tf_op jit(solution)/shard_map/ppermute | solution.py:397
  62.3 0.4 collective-permute-done.16.refs_1_
  62.7 1.2 %collective-permute-done.17.refs_2_ = bf16[128,128]{1,0:T(8,128)(2,1)S(1)} collective-permute-done((bf16[128,128]{1,0:T(8,128)(2,1)S(1)}, bf16[128,128]{1,0:T(8,128)(2,1)S(1)}, u32[]{:S(2)}, u32[]{:S(2)}) %collective-permute-start.17) | collective-permute-done | bytes 32800 | tf_op jit(solution)/shard_map/ppermute | solution.py:397
  63.9 1.4 %collective-permute-done.18.refs_3_ = bf16[128,128]{1,0:T(8,128)(2,1)S(1)} collective-permute-done((bf16[128,128]{1,0:T(8,128)(2,1)S(1)}, bf16[128,128]{1,0:T(8,128)(2,1)S(1)}, u32[]{:S(2)}, u32[]{:S(2)}) %collective-permute-start.18) | collective-permute-done | bytes 32800 | tf_op jit(solution)/shard_map/ppermute | solution.py:397
  65.4 11.1 %all_to_all.11.refs_0_ = bf16[8,128,128]{2,1,0:T(8,128)(2,1)S(1)} all-to-all(bf16[8,128,128]{2,1,0:T(8,128)(2,1)S(1)} %shard_map.114), channel_id=1, replica_groups={{224,192,160,128,96,64,32,0},{228,196,164,132,100,68,36,4},{232,200,168..., dimensions={0} | all-to-all | bytes 524288 | tf_op jit(solution)/shard_map/all_to_all | solution.py:476
  76.5 5.0 %collective-permute-start.19 = (bf16[128,128]{1,0:T(8,128)(2,1)S(1)}, bf16[128,128]{1,0:T(8,128)(2,1)S(1)}, u32[]{:S(2)}, u32[]{:S(2)}) collective-permute-start(bf16[128,128]{1,0:T(8,128)(2,1)S(1)} %shard_map.115.refs_2_.refs_0_), channel_id=1, source_target_pairs={{0,4},{4,0},{8,12},{12,8},{16,20},{20,16},{24,28},{28,24},{32,36},... | collective-permute-start | bytes 98312 | tf_op jit(solution)/shard_map/ppermute | solution.py:390
  81.5 0.9 collective-permute-done.19.refs_1_
  82.4 0.1 collective-permute-start.20
  82.5 2.1 %collective-permute-start.21 = (bf16[256,128]{1,0:T(8,128)(2,1)S(1)}, bf16[256,128]{1,0:T(8,128)(2,1)S(1)}, u32[]{:S(2)}, u32[]{:S(2)}) collective-permute-start(bf16[256,128]{1,0:T(8,128)(2,1)S(1)} %shard_map.117.refs_0_), channel_id=1, source_target_pairs={{0,16},{4,20},{8,24},{12,28},{16,0},{20,4},{24,8},{28,12},{32,48},... | collective-permute-start | bytes 196616 | tf_op jit(solution)/shard_map/ppermute | solution.py:397
  84.6 1.2 %collective-permute-start.22 = (bf16[256,128]{1,0:T(8,128)(2,1)S(1)}, bf16[256,128]{1,0:T(8,128)(2,1)S(1)}, u32[]{:S(2)}, u32[]{:S(2)}) collective-permute-start(bf16[256,128]{1,0:T(8,128)(2,1)S(1)} %shard_map.117.refs_0_), channel_id=1, source_target_pairs={{0,24},{4,28},{8,0},{12,4},{16,8},{20,12},{24,16},{28,20},{32,56},... | collective-permute-start | bytes 196616 | tf_op jit(solution)/shard_map/ppermute | solution.py:397
  85.8 1.2 %shard_map.116 = (bf16[512,512]{1,0:T(8,128)(2,1)}, bf16[512,512]{1,0:T(8,128)(2,1)}, bf16[512,512]{1,0:T(8,128)(2,1)}, f32[8,128]{1,0:T(8,128)S(1)}) custom-call(bf16[1536,256]{1,0:T(8,128)(2,1)S(1)} %get-tuple-element.91.refs_0_, bf16[1536,256]{1,0:T(8,128)(2,1)S(1)} %collective-permute-done.12.refs_1_, bf16[128,128]{1,0:T(8,128)(2,1)S(1)} %shard_map.115.refs_2_.refs_0_), custom_call_target="tpu_custom_call" | custom-call | flops 10000000 | bytes 1000000 | tf_op jit(solution)/shard_map/pallas_call | solution.py:45
  87.0 0.7 collective-permute-done.20.refs_1_
  87.6 0.6 collective-permute-done.21.refs_2_
  88.2 0.5 collective-permute-done.22.refs_3_
  88.7 0.9 %shard_map.118 = f32[1024,128]{1,0:T(8,128)} custom-call(bf16[256,128]{1,0:T(8,128)(2,1)S(1)} %shard_map.117.refs_0_, bf16[256,128]{1,0:T(8,128)(2,1)S(1)} %collective-permute-done.20.refs_1_, bf16[256,128]{1,0:T(8,128)(2,1)S(1)} %collective-permute-done.21.refs_2_, bf16[256,128]{1,0:T(8,128)(2,1)S(1)} %collective-permute-done.22.refs_3_, ...), custom_call_target="tpu_custom_call" | custom-call | flops 10000000 | bytes 1000000 | tf_op jit(solution)/shard_map/pallas_call | solution.py:45
  (25 shorter events, 0.3 us)
Async XLA Ops:
  0.6 7.1 %copy-start.2 = (bf16[512,1024]{1,0:T(8,128)(2,1)S(1)}, bf16[512,1024]{1,0:T(8,128)(2,1)}, u32[]{:S(2)}) copy-start(bf16[512,1024]{1,0:T(8,128)(2,1)} %refs_0_.3) | copy-start | bytes 3145732
  4.4 6.7 %collective-permute-start = (bf16[2064,256]{1,0:T(8,128)(2,1)}, bf16[2064,256]{1,0:T(8,128)(2,1)S(1)}, u32[]{:S(2)}, u32[]{:S(2)}) collective-permute-start(bf16[2064,256]{1,0:T(8,128)(2,1)} %get-tuple-element.54), channel_id=1, source_target_pairs={{0,4},{4,0},{8,12},{12,8},{16,20},{20,16},{24,28},{28,24},{32,36},... | collective-permute-start | bytes 3170312 | tf_op jit(solution)/shard_map/ppermute | solution.py:390
  7.7 8.1 %collective-permute-start.5 = (bf16[512,1024]{1,0:T(8,128)(2,1)S(1)}, bf16[512,1024]{1,0:T(8,128)(2,1)S(1)}, u32[]{:S(2)}, u32[]{:S(2)}) collective-permute-start(bf16[512,1024]{1,0:T(8,128)(2,1)S(1)} %copy-done.2), channel_id=1, source_target_pairs={{0,4},{4,0},{8,12},{12,8},{16,20},{20,16},{24,28},{28,24},{32,36},... | collective-permute-start | bytes 3145736 | tf_op jit(solution)/shard_map/ppermute | solution.py:390
  7.8 6.2 %collective-permute-start.1 = (f32[32,512]{1,0:T(8,128)}, f32[32,512]{1,0:T(8,128)S(1)}, u32[]{:S(2)}, u32[]{:S(2)}) collective-permute-start(f32[32,512]{1,0:T(8,128)} %get-tuple-element.63), channel_id=1, source_target_pairs={{0,1},{1,2},{2,3},{3,0},{4,5},{5,6},{6,7},{7,4},{8,9},{9,10},{10,1... | collective-permute-start | bytes 196616 | tf_op jit(solution)/shard_map/ppermute | solution.py:400
  7.8 6.2 %collective-permute-start.2 = (f32[32,512]{1,0:T(8,128)}, f32[32,512]{1,0:T(8,128)S(1)}, u32[]{:S(2)}, u32[]{:S(2)}) collective-permute-start(f32[32,512]{1,0:T(8,128)} %get-tuple-element.64), channel_id=1, source_target_pairs={{0,2},{1,3},{2,0},{3,1},{4,6},{5,7},{6,4},{7,5},{8,10},{9,11},{10,... | collective-permute-start | bytes 196616 | tf_op jit(solution)/shard_map/ppermute | solution.py:400
  10.0 4.2 %collective-permute-start.3 = (f32[32,512]{1,0:T(8,128)}, f32[32,512]{1,0:T(8,128)S(1)}, u32[]{:S(2)}, u32[]{:S(2)}) collective-permute-start(f32[32,512]{1,0:T(8,128)} %get-tuple-element.65), channel_id=1, source_target_pairs={{0,3},{1,0},{2,1},{3,2},{4,7},{5,4},{6,5},{7,6},{8,11},{9,8},{10,9... | collective-permute-start | bytes 196616 | tf_op jit(solution)/shard_map/ppermute | solution.py:400
  11.1 1.2 %copy-start = (bf16[2064,256]{1,0:T(8,128)(2,1)S(1)}, bf16[2064,256]{1,0:T(8,128)(2,1)}, u32[]{:S(2)}) copy-start(bf16[2064,256]{1,0:T(8,128)(2,1)} %get-tuple-element.53.refs_0_) | copy-start | bytes 3170308
  12.8 1.4 %copy-start.3 = (f32[32,512]{1,0:T(8,128)S(1)}, f32[32,512]{1,0:T(8,128)}, u32[]{:S(2)}) copy-start(f32[32,512]{1,0:T(8,128)} %get-tuple-element.62.refs_0_) | copy-start | bytes 196612
  12.8 3.9 %copy-start.1 = (bf16[2064,256]{1,0:T(8,128)(2,1)S(1)}, bf16[2064,256]{1,0:T(8,128)(2,1)}, u32[]{:S(2)}) copy-start(bf16[2064,256]{1,0:T(8,128)(2,1)} %get-tuple-element.53.refs_0_) | copy-start | bytes 3170308
  14.2 2.5 %collective-permute-start.4 = (f32[16,512]{1,0:T(8,128)S(1)}, f32[16,512]{1,0:T(8,128)S(1)}, u32[]{:S(2)}, u32[]{:S(2)}) collective-permute-start(f32[16,512]{1,0:T(8,128)S(1)} %get-tuple-element.68), channel_id=1, source_target_pairs={{0,4},{4,0},{8,12},{12,8},{16,20},{20,16},{24,28},{28,24},{32,36},... | collective-permute-start | bytes 98312 | tf_op jit(solution)/shard_map/ppermute | solution.py:390
  17.4 4.1 %collective-permute-start.6 = (bf16[384,128]{1,0:T(8,128)(2,1)S(1)}, bf16[384,128]{1,0:T(8,128)(2,1)S(1)}, u32[]{:S(2)}, u32[]{:S(2)}) collective-permute-start(bf16[384,128]{1,0:T(8,128)(2,1)S(1)} %get-tuple-element.72), channel_id=1, source_target_pairs={{0,8},{4,12},{8,0},{12,4},{16,24},{20,28},{24,16},{28,20},{32,40},... | collective-permute-start | bytes 294920 | tf_op jit(solution)/shard_map/ppermute | solution.py:393
  18.5 7.1 %collective-permute-start.7 = (bf16[384,128]{1,0:T(8,128)(2,1)S(1)}, bf16[384,128]{1,0:T(8,128)(2,1)S(1)}, u32[]{:S(2)}, u32[]{:S(2)}) collective-permute-start(bf16[384,128]{1,0:T(8,128)(2,1)S(1)} %get-tuple-element.73), channel_id=1, source_target_pairs={{0,16},{4,20},{8,24},{12,28},{16,0},{20,4},{24,8},{28,12},{32,48},... | collective-permute-start | bytes 294920 | tf_op jit(solution)/shard_map/ppermute | solution.py:393
  20.9 7.3 %collective-permute-start.8 = (bf16[384,128]{1,0:T(8,128)(2,1)S(1)}, bf16[384,128]{1,0:T(8,128)(2,1)S(1)}, u32[]{:S(2)}, u32[]{:S(2)}) collective-permute-start(bf16[384,128]{1,0:T(8,128)(2,1)S(1)} %get-tuple-element.74), channel_id=1, source_target_pairs={{0,24},{4,28},{8,16},{12,20},{16,8},{20,12},{24,0},{28,4},{32,56},... | collective-permute-start | bytes 294920 | tf_op jit(solution)/shard_map/ppermute | solution.py:393
  41.5 3.9 %collective-permute-start.9 = (bf16[128,128]{1,0:T(8,128)(2,1)S(1)}, bf16[128,128]{1,0:T(8,128)(2,1)S(1)}, u32[]{:S(2)}, u32[]{:S(2)}) collective-permute-start(bf16[128,128]{1,0:T(8,128)(2,1)S(1)} %shard_map.108.refs_0_), channel_id=1, source_target_pairs={{0,8},{4,12},{8,0},{12,4},{16,24},{20,28},{24,16},{28,20},{32,40},... | collective-permute-start | bytes 98312 | tf_op jit(solution)/shard_map/ppermute | solution.py:393
  41.6 4.4 %collective-permute-start.10 = (bf16[128,128]{1,0:T(8,128)(2,1)S(1)}, bf16[128,128]{1,0:T(8,128)(2,1)S(1)}, u32[]{:S(2)}, u32[]{:S(2)}) collective-permute-start(bf16[128,128]{1,0:T(8,128)(2,1)S(1)} %shard_map.108.refs_0_), channel_id=1, source_target_pairs={{0,16},{4,20},{8,24},{12,28},{16,0},{20,4},{24,8},{28,12},{32,48},... | collective-permute-start | bytes 98312 | tf_op jit(solution)/shard_map/ppermute | solution.py:393
  43.2 4.0 %collective-permute-start.11 = (bf16[128,128]{1,0:T(8,128)(2,1)S(1)}, bf16[128,128]{1,0:T(8,128)(2,1)S(1)}, u32[]{:S(2)}, u32[]{:S(2)}) collective-permute-start(bf16[128,128]{1,0:T(8,128)(2,1)S(1)} %shard_map.108.refs_0_), channel_id=1, source_target_pairs={{0,24},{4,28},{8,16},{12,20},{16,8},{20,12},{24,0},{28,4},{32,56},... | collective-permute-start | bytes 98312 | tf_op jit(solution)/shard_map/ppermute | solution.py:393
  47.9 10.2 %collective-permute-start.13 = (bf16[32,512]{1,0:T(8,128)(2,1)S(1)}, bf16[32,512]{1,0:T(8,128)(2,1)S(1)}, u32[]{:S(2)}, u32[]{:S(2)}) collective-permute-start(bf16[32,512]{1,0:T(8,128)(2,1)S(1)} %get-tuple-element.89.refs_10_.refs_2_), channel_id=1, source_target_pairs={{0,1},{1,2},{2,3},{3,0},{4,5},{5,6},{6,7},{7,4},{8,9},{9,10},{10,1... | collective-permute-start | bytes 98312 | tf_op jit(solution)/shard_map/ppermute | solution.py:400
  48.3 9.8 %collective-permute-start.14 = (bf16[32,512]{1,0:T(8,128)(2,1)S(1)}, bf16[32,512]{1,0:T(8,128)(2,1)S(1)}, u32[]{:S(2)}, u32[]{:S(2)}) collective-permute-start(bf16[32,512]{1,0:T(8,128)(2,1)S(1)} %get-tuple-element.89.refs_10_.refs_2_), channel_id=1, source_target_pairs={{0,2},{1,3},{2,0},{3,1},{4,6},{5,7},{6,4},{7,5},{8,10},{9,11},{10,... | collective-permute-start | bytes 98312 | tf_op jit(solution)/shard_map/ppermute | solution.py:400
  51.4 6.7 %collective-permute-start.15 = (bf16[32,512]{1,0:T(8,128)(2,1)S(1)}, bf16[32,512]{1,0:T(8,128)(2,1)S(1)}, u32[]{:S(2)}, u32[]{:S(2)}) collective-permute-start(bf16[32,512]{1,0:T(8,128)(2,1)S(1)} %get-tuple-element.89.refs_10_.refs_2_), channel_id=1, source_target_pairs={{0,3},{1,0},{2,1},{3,2},{4,7},{5,4},{6,5},{7,6},{8,11},{9,8},{10,9... | collective-permute-start | bytes 98312 | tf_op jit(solution)/shard_map/ppermute | solution.py:400
  52.6 33.2 %collective-permute-start.12 = (bf16[1536,256]{1,0:T(8,128)(2,1)S(1)}, bf16[1536,256]{1,0:T(8,128)(2,1)S(1)}, u32[]{:S(2)}, u32[]{:S(2)}) collective-permute-start(bf16[1536,256]{1,0:T(8,128)(2,1)S(1)} %get-tuple-element.92), channel_id=1, source_target_pairs={{0,4},{4,0},{8,12},{12,8},{16,20},{20,16},{24,28},{28,24},{32,36},... | collective-permute-start | bytes 2359304 | tf_op jit(solution)/shard_map/ppermute | solution.py:390
  58.6 4.1 %collective-permute-start.16 = (bf16[128,128]{1,0:T(8,128)(2,1)S(1)}, bf16[128,128]{1,0:T(8,128)(2,1)S(1)}, u32[]{:S(2)}, u32[]{:S(2)}) collective-permute-start(bf16[128,128]{1,0:T(8,128)(2,1)S(1)} %get-tuple-element.95), channel_id=1, source_target_pairs={{0,8},{4,12},{8,16},{12,20},{16,24},{20,28},{24,0},{28,4},{32,40},... | collective-permute-start | bytes 98312 | tf_op jit(solution)/shard_map/ppermute | solution.py:397
  58.7 5.2 %collective-permute-start.17 = (bf16[128,128]{1,0:T(8,128)(2,1)S(1)}, bf16[128,128]{1,0:T(8,128)(2,1)S(1)}, u32[]{:S(2)}, u32[]{:S(2)}) collective-permute-start(bf16[128,128]{1,0:T(8,128)(2,1)S(1)} %get-tuple-element.96), channel_id=1, source_target_pairs={{0,16},{4,20},{8,24},{12,28},{16,0},{20,4},{24,8},{28,12},{32,48},... | collective-permute-start | bytes 98312 | tf_op jit(solution)/shard_map/ppermute | solution.py:397
  62.3 3.1 %collective-permute-start.18 = (bf16[128,128]{1,0:T(8,128)(2,1)S(1)}, bf16[128,128]{1,0:T(8,128)(2,1)S(1)}, u32[]{:S(2)}, u32[]{:S(2)}) collective-permute-start(bf16[128,128]{1,0:T(8,128)(2,1)S(1)} %get-tuple-element.97), channel_id=1, source_target_pairs={{0,24},{4,28},{8,0},{12,4},{16,8},{20,12},{24,16},{28,20},{32,56},... | collective-permute-start | bytes 98312 | tf_op jit(solution)/shard_map/ppermute | solution.py:397
  76.5 5.9 %collective-permute-start.19 = (bf16[128,128]{1,0:T(8,128)(2,1)S(1)}, bf16[128,128]{1,0:T(8,128)(2,1)S(1)}, u32[]{:S(2)}, u32[]{:S(2)}) collective-permute-start(bf16[128,128]{1,0:T(8,128)(2,1)S(1)} %shard_map.115.refs_2_.refs_0_), channel_id=1, source_target_pairs={{0,4},{4,0},{8,12},{12,8},{16,20},{20,16},{24,28},{28,24},{32,36},... | collective-permute-start | bytes 98312 | tf_op jit(solution)/shard_map/ppermute | solution.py:390
  82.4 5.2 %collective-permute-start.20 = (bf16[256,128]{1,0:T(8,128)(2,1)S(1)}, bf16[256,128]{1,0:T(8,128)(2,1)S(1)}, u32[]{:S(2)}, u32[]{:S(2)}) collective-permute-start(bf16[256,128]{1,0:T(8,128)(2,1)S(1)} %shard_map.117.refs_0_), channel_id=1, source_target_pairs={{0,8},{4,12},{8,16},{12,20},{16,24},{20,28},{24,0},{28,4},{32,40},... | collective-permute-start | bytes 196616 | tf_op jit(solution)/shard_map/ppermute | solution.py:397
  82.5 5.7 %collective-permute-start.21 = (bf16[256,128]{1,0:T(8,128)(2,1)S(1)}, bf16[256,128]{1,0:T(8,128)(2,1)S(1)}, u32[]{:S(2)}, u32[]{:S(2)}) collective-permute-start(bf16[256,128]{1,0:T(8,128)(2,1)S(1)} %shard_map.117.refs_0_), channel_id=1, source_target_pairs={{0,16},{4,20},{8,24},{12,28},{16,0},{20,4},{24,8},{28,12},{32,48},... | collective-permute-start | bytes 196616 | tf_op jit(solution)/shard_map/ppermute | solution.py:397
  84.6 4.1 %collective-permute-start.22 = (bf16[256,128]{1,0:T(8,128)(2,1)S(1)}, bf16[256,128]{1,0:T(8,128)(2,1)S(1)}, u32[]{:S(2)}, u32[]{:S(2)}) collective-permute-start(bf16[256,128]{1,0:T(8,128)(2,1)S(1)} %shard_map.117.refs_0_), channel_id=1, source_target_pairs={{0,24},{4,28},{8,0},{12,4},{16,8},{20,12},{24,16},{28,20},{32,56},... | collective-permute-start | bytes 196616 | tf_op jit(solution)/shard_map/ppermute | solution.py:397

commit v9 on v8

--- a/solution.py
+++ b/solution.py
@@ -31,7 +31,7 @@
 
 def call(
     body, out_shape, args, in_specs=None, out_specs=None, grid=(), scratch=(), cost=(10**7, 10**6), after=(),
-    limit=VMEM_LIMIT,
+    limit=VMEM_LIMIT, aliases=None,
 ):
     whole = pl.BlockSpec(memory_space=pltpu.VMEM)
     many = isinstance(out_shape, (tuple, list))
@@ -47,6 +47,7 @@
         out_shape=out_shape,
         grid=grid,
         in_specs=in_specs,
+        input_output_aliases=aliases or {},
         out_specs=out_specs or ([whole] * len(out_shape) if many else whole),
         scratch_shapes=list(scratch),
         compiler_params=pltpu.CompilerParams(vmem_limit_bytes=limit),
@@ -194,25 +195,31 @@
     place = (lax.axis_index("seq") // 2) % 4
     own_slice_ref[0:64, :] = scr[aligned(place, 64), :]
     own_slice_ref[64:128, :] = scr[pl.ds(pl.multiple_of(768 + 64 * place, 64), 64), :]
-    for mask, out in ((1, m1_ref), (2, m2_ref), (3, m3_ref)):
-        later = (place >> (mask >> 1)) & 1
-        start = later * (256 if mask == 1 else 512)
+    for step, out in ((1, m1_ref), (2, m2_ref), (3, m3_ref)):
+        peer = lax.rem(place + step, 4)
+        gradient = jnp.where((place ^ peer) == 1, 256, 512)
+        start = jnp.where(peer < place, gradient, 0)
         out[0:256, :] = scr[pl.ds(pl.multiple_of(start, 256), 256), :].astype(BF16)
-        peer = 64 * (place ^ mask)
         for part in range(2):
-            rows = scr[pl.ds(pl.multiple_of(768 * part + peer, 64), 64), :]
+            rows = scr[pl.ds(pl.multiple_of(768 * part + 64 * peer, 64), 64), :]
             out[256 + 64 * part : 320 + 64 * part, :] = rows.astype(BF16)
 
 
 def along_x_body(own_ref, m1_ref, m2_ref, m3_ref, spread_ref, states_ref, later_ref):
     place = (lax.axis_index("seq") // 2) % 4
     got = [m1_ref[...].astype(F32), m2_ref[...].astype(F32), m3_ref[...].astype(F32)]
-    level5, level6 = got[0][:256], got[1][:256] + got[2][:256]
-    upper5 = (place & 1).astype(F32)
-    upper6 = (place >> 1).astype(F32)
-    states_ref[0:256, :] = (level5 * upper5).astype(BF16)
-    states_ref[256:512, :] = (level6 * upper6).astype(BF16)
-    later_ref[...] = level5 * (1.0 - upper5) + level6 * (1.0 - upper6)
+    states = [jnp.zeros((256, DIM), F32)] * 2
+    later = jnp.zeros((256, DIM), F32)
+    for step in range(1, 4):
+        source = lax.rem(place + 4 - step, 4)
+        part = got[step - 1][:256]
+        earlier = (source < place).astype(F32)
+        level5 = ((place ^ source) == 1).astype(F32)
+        states = [states[0] + part * (earlier * level5), states[1] + part * (earlier * (1.0 - level5))]
+        later = later + part * (1.0 - earlier)
+    states_ref[0:256, :] = states[0].astype(BF16)
+    states_ref[256:512, :] = states[1].astype(BF16)
+    later_ref[...] = later
     total = own_ref[...] + got[0][256:] + (got[1][256:] + got[2][256:])
     here = lax.axis_index("seq") // 8
     for group in range(8):
@@ -233,8 +240,8 @@
 def far_body(own_ref, r1, r2, r3, states_ref, near_ref, mine_ref, later_ref):
     place = (lax.axis_index("seq") // 2) % 4
     mine_ref[0:512, :] = states_ref[...]
-    for mask, ref in enumerate((own_ref, r1, r2, r3)):
-        peer = 64 * (place ^ mask)
+    for step, ref in enumerate((own_ref, r1, r2, r3)):
+        peer = 64 * lax.rem(place + 4 - step, 4)
         mine_ref[pl.ds(pl.multiple_of(512 + peer, 64), 64), :] = ref[0:64, :]
         rows = pl.ds(pl.multiple_of(peer, 64), 64)
         later_ref[rows, :] = near_ref[rows, :] + ref[64:128, :].astype(F32)
@@ -339,7 +346,7 @@
     o_ref[...] = (total * scale).astype(BF16)
 
 
-def both_body(mine_ref, other_ref, o_ref):
+def both_body(mine_ref, other_ref, held_ref, o_ref, passed_ref):
     core = lax.axis_index("seq") & 1
     o_ref[aligned(core, DIM), :] = mine_ref[...]
     o_ref[aligned(1 - core, DIM), :] = other_ref[...]
@@ -389,9 +396,6 @@
     def sibling(value):
         return lax.ppermute(value, "seq", swap)
 
-    def swap_x(value, mask):
-        return lax.ppermute(value, "seq", [(d, d ^ (2 * mask)) for d in range(seq_count)])
-
     def rotate_x(value, step):
         pairs = [(d, d // 8 * 8 + (d + 2 * step) % 8) for d in range(seq_count)]
         return lax.ppermute(value, "seq", pairs)
@@ -442,12 +446,12 @@
     )
     spread, close_states, close_later = call(
         along_x_body, [shape((8, 64, DIM), BF16), shape((512, DIM), BF16), half],
-        (own_slice, *(swap_x(messages[mask - 1], mask) for mask in (1, 2, 3))),
+        (own_slice, *(rotate_x(messages[step - 1], step) for step in (1, 2, 3))),
     )
     got = call(along_z_body, eighth, (lax.all_to_all(spread, "seq", 0, 0, axis_index_groups=columns),))
     mine, later = call(
         far_body, [shape((768, DIM), BF16), half],
-        (got, *(swap_x(got, mask) for mask in (1, 2, 3)), close_states, close_later),
+        (got, *(rotate_x(got, step) for step in (1, 2, 3)), close_states, close_later),
     )
     tok256 = shape((256, TOK), F32)
     grad_logits, cross_own, cross_sib = call(
@@ -463,7 +467,6 @@
         )
 
     out_sib, token = tail(1, sib, kt_sib, state_own, allow_sib, gates_sib, cross_sib, sc_sib, pr_sib, (grad_logits,))
-    out_recv = sibling(out_sib)
     out_own, token = tail(0, own, kt_own, state_sib, allow_own, gates_own, cross_own, sc_own, pr_own, (token,))
     quarter = shape((DIM, DIM), BF16)
     sums = call(
@@ -477,11 +480,15 @@
     scale = 1.0 / math.sqrt(TOK * seq_count)
     mine_sum = call(functools.partial(sum_z_body, scale), quarter, (got4,))
     other_sum = sibling(mine_sum)
+    both, out_sib = call(
+        both_body, [shape((256, DIM), BF16), shape((3 * TOK, 256), BF16)], (mine_sum, other_sum, out_sib),
+        in_specs=[whole, whole, hbm], out_specs=[whole, hbm], aliases={2: 1},
+    )
+    out_recv = sibling(out_sib)
     *grads, token = call(
         place_body, [shape((TOK, 512), BF16)] * 3 + [shape((8, DIM), F32)], (out_own, out_recv),
-        out_specs=[hbm] * 3 + [whole], scratch=[pltpu.SemaphoreType.DMA((6,))], after=(mine_sum,),
-    )
-    both = call(both_body, shape((256, DIM), BF16), (mine_sum, other_sum))
+        out_specs=[hbm] * 3 + [whole], scratch=[pltpu.SemaphoreType.DMA((6,))], after=(both,),
+    )
     got5 = [both] + [rotate_x(both, step) for step in range(1, 4)]
     grad_weight = call(
         join_body, shape((1024, DIM), F32), tuple(got5),

time: 90 us -> 88.3 us (0.981)
  waiting for transfers between devices: 15.2 us -> 12.2 us
  starting transfers between devices: 36.3 us -> 37.5 us
    ppermute x6 -> x0, waiting for transfers between devices: 8.54 us -> none  [swap_x(): lax.ppermute(value, 'seq', [(d, d ^ 2 * mask) for d in range(seq_count)])]
    ppermute x6 -> x12, starting transfers between devices: 6.96 us -> 15.5 us  [rotate_x(): return lax.ppermute(value, 'seq', pairs)]
    ppermute x6 -> x0, starting transfers between devices: 7.88 us -> none  [swap_x(): lax.ppermute(value, 'seq', [(d, d ^ 2 * mask) for d in range(seq_count)])]
    ppermute x6 -> x12, waiting for transfers between devices: 4.77 us -> 9.72 us  [rotate_x(): return lax.ppermute(value, 'seq', pairs)]
where the time goes in v9:
time: 88.3 us; the launch traced here: 88.1 us
  starting transfers between devices  37.5 us (42%)
  blocking collectives  24.3 us (28%)
  waiting for transfers between devices  12.2 us (14%)
  Pallas kernels  11.9 us (13%)
  local copies, waits for them, and re-layouts  1.24 us (1%)
  between operations  0.97 us (1%)
    ppermute x12, starting transfers between devices, rotate_x(): return lax.ppermute(value, 'seq', pairs)  15.5 us
    ppermute x5, starting transfers between devices, sibling(): return lax.ppermute(value, 'seq', swap)  14.9 us
    all_to_all x1, blocking collectives, shards(): lax.all_to_all(spread, 'seq', 0, 0, axis_index_groups=columns)  13.2 us
    pallas_call x17, Pallas kernels, call(): pl.pallas_call(kernel, out_shape=out_shape, grid=grid, in_specs=in_specs,...  11.9 us
    all_to_all x1, blocking collectives, shards(): got4 = lax.all_to_all(spread, 'seq', 0, 0, axis_index_groups=columns)  11.1 us
    ppermute x12, waiting for transfers between devices, rotate_x(): return lax.ppermute(value, 'seq', pairs)  9.72 us
    ppermute x6, starting transfers between devices, rotate(): return lax.ppermute(value, 'head', [(h, (h + step) % 4) for h in range(4)])  7.05 us
  transfers between devices with their start and end apart: 23, of which 14 were waited for; matrix products, arithmetic and copies ran while one was open for 0% of the time, Pallas kernels for 6%

profile of v9, /device:TPU:1, one launch (start us, length us, event | category | flops | bytes accessed | tf_op | source)
XLA Modules:
  0.0 88.1 jit_solution(4794299067966320944)
XLA Ops:
  0.6 3.7 %shard_map.102 = (f32[32,512]{1,0:T(8,128)}, f32[32,512]{1,0:T(8,128)}, f32[32,512]{1,0:T(8,128)}, f32[32,512]{1,0:T(8,128)}, bf16[2064,256]{1,0:T(8,128)(2,1)}, /*index=5*/bf16[2064,256]{1,0:T(8,128)(2,1)}) custom-call(bf16[512,1024]{1,0:T(8,128)(2,1)} %refs_0_.3, bf16[1024,128]{1,0:T(8,128)(2,1)} %refs_1_.1, bf16[512,512]{1,0:T(8,128)(2,1)} %refs_2_.1, ...), custom_call_target="tpu_custom_call" | custom-call | flops 10000000 | bytes 1000000 | tf_op jit(solution)/shard_map/pallas_call | solution.py:45
  4.4 3.3 %collective-permute-start = (bf16[2064,256]{1,0:T(8,128)(2,1)}, bf16[2064,256]{1,0:T(8,128)(2,1)S(1)}, u32[]{:S(2)}, u32[]{:S(2)}) collective-permute-start(bf16[2064,256]{1,0:T(8,128)(2,1)} %get-tuple-element.56), channel_id=1, source_target_pairs={{0,4},{4,0},{8,12},{12,8},{16,20},{20,16},{24,28},{28,24},{32,36},... | collective-permute-start | bytes 3170312 | tf_op jit(solution)/shard_map/ppermute | solution.py:397
  7.7 0.1 collective-permute-start.5
  7.8 2.2 %collective-permute-start.2 = (f32[32,512]{1,0:T(8,128)}, f32[32,512]{1,0:T(8,128)S(1)}, u32[]{:S(2)}, u32[]{:S(2)}) collective-permute-start(f32[32,512]{1,0:T(8,128)} %get-tuple-element.66), channel_id=1, source_target_pairs={{0,2},{1,3},{2,0},{3,1},{4,6},{5,7},{6,4},{7,5},{8,10},{9,11},{10,... | collective-permute-start | bytes 196616 | tf_op jit(solution)/shard_map/ppermute | solution.py:404
  10.0 1.1 %collective-permute-start.3 = (f32[32,512]{1,0:T(8,128)}, f32[32,512]{1,0:T(8,128)S(1)}, u32[]{:S(2)}, u32[]{:S(2)}) collective-permute-start(f32[32,512]{1,0:T(8,128)} %get-tuple-element.67), channel_id=1, source_target_pairs={{0,3},{1,0},{2,1},{3,2},{4,7},{5,4},{6,5},{7,6},{8,11},{9,8},{10,9... | collective-permute-start | bytes 196616 | tf_op jit(solution)/shard_map/ppermute | solution.py:404
  11.1 1.2 %copy-done = bf16[2064,256]{1,0:T(8,128)(2,1)S(1)} copy-done((bf16[2064,256]{1,0:T(8,128)(2,1)S(1)}, bf16[2064,256]{1,0:T(8,128)(2,1)}, u32[]{:S(2)}) %copy-start) | copy-done | bytes 1056792
  12.3 0.5 shard_map.103
  12.8 1.2 %shard_map.104 = (f32[16,512]{1,0:T(8,128)S(1)}, f32[16,512]{1,0:T(8,128)S(1)}, f32[1536,256]{1,0:T(8,128)S(1)}, f32[1536,256]{1,0:T(8,128)S(1)}, f32[1536,256]{1,0:T(8,128)S(1)}, /*index=5*/f32[1536,256]{1,0:T(8,128)S(1)}) custom-call(bf16[2064,256]{1,0:T(8,128)(2,1)S(1)} %copy-done, bf16[2064,256]{1,0:T(8,128)(2,1)S(1)} %collective-permute-done.refs_1_.refs_0_, ...), custom_call_target="tpu_custom_call" | custom-call | flops 10000000 | bytes 1000000 | tf_op jit(solution)/shard_map/pallas_call | solution.py:45
  14.0 0.1 collective-permute-done.3.refs_3_
  14.2 1.6 %collective-permute-start.4 = (f32[16,512]{1,0:T(8,128)S(1)}, f32[16,512]{1,0:T(8,128)S(1)}, u32[]{:S(2)}, u32[]{:S(2)}) collective-permute-start(f32[16,512]{1,0:T(8,128)S(1)} %get-tuple-element.70), channel_id=1, source_target_pairs={{0,4},{4,0},{8,12},{12,8},{16,20},{20,16},{24,28},{28,24},{32,36},... | collective-permute-start | bytes 98312 | tf_op jit(solution)/shard_map/ppermute | solution.py:397
  15.8 0.9 collective-permute-done.4.refs_9_
  16.7 0.8 shard_map.106
  17.5 1.0 %collective-permute-start.6 = (bf16[384,128]{1,0:T(8,128)(2,1)S(1)}, bf16[384,128]{1,0:T(8,128)(2,1)S(1)}, u32[]{:S(2)}, u32[]{:S(2)}) collective-permute-start(bf16[384,128]{1,0:T(8,128)(2,1)S(1)} %get-tuple-element.74), channel_id=1, source_target_pairs={{0,8},{4,12},{8,16},{12,20},{16,24},{20,28},{24,0},{28,4},{32,40},... | collective-permute-start | bytes 294920 | tf_op jit(solution)/shard_map/ppermute | solution.py:401
  18.5 2.5 %collective-permute-start.7 = (bf16[384,128]{1,0:T(8,128)(2,1)S(1)}, bf16[384,128]{1,0:T(8,128)(2,1)S(1)}, u32[]{:S(2)}, u32[]{:S(2)}) collective-permute-start(bf16[384,128]{1,0:T(8,128)(2,1)S(1)} %get-tuple-element.75), channel_id=1, source_target_pairs={{0,16},{4,20},{8,24},{12,28},{16,0},{20,4},{24,8},{28,12},{32,48},... | collective-permute-start | bytes 294920 | tf_op jit(solution)/shard_map/ppermute | solution.py:401
  20.9 1.2 %collective-permute-start.8 = (bf16[384,128]{1,0:T(8,128)(2,1)S(1)}, bf16[384,128]{1,0:T(8,128)(2,1)S(1)}, u32[]{:S(2)}, u32[]{:S(2)}) collective-permute-start(bf16[384,128]{1,0:T(8,128)(2,1)S(1)} %get-tuple-element.76), channel_id=1, source_target_pairs={{0,24},{4,28},{8,0},{12,4},{16,8},{20,12},{24,16},{28,20},{32,56},... | collective-permute-start | bytes 294920 | tf_op jit(solution)/shard_map/ppermute | solution.py:401
  22.1 0.7 collective-permute-done.6.refs_1_
  22.8 2.8 %collective-permute-done.7.refs_2_ = bf16[384,128]{1,0:T(8,128)(2,1)S(1)} collective-permute-done((bf16[384,128]{1,0:T(8,128)(2,1)S(1)}, bf16[384,128]{1,0:T(8,128)(2,1)S(1)}, u32[]{:S(2)}, u32[]{:S(2)}) %collective-permute-start.7) | collective-permute-done | bytes 98336 | tf_op jit(solution)/shard_map/ppermute | solution.py:401
  25.6 0.1 shard_map.107
  25.7 13.2 %all_to_all.10.refs_0_ = bf16[8,64,128]{2,1,0:T(8,128)(2,1)S(1)} all-to-all(bf16[8,64,128]{2,1,0:T(8,128)(2,1)S(1)} %get-tuple-element.77), channel_id=1, replica_groups={{224,192,160,128,96,64,32,0},{228,196,164,132,100,68,36,4},{232,200,168..., dimensions={0} | all-to-all | bytes 262144 | tf_op jit(solution)/shard_map/all_to_all | solution.py:451
  39.0 0.5 collective-permute-start.9
  39.5 2.1 %collective-permute-start.10 = (bf16[128,128]{1,0:T(8,128)(2,1)S(1)}, bf16[128,128]{1,0:T(8,128)(2,1)S(1)}, u32[]{:S(2)}, u32[]{:S(2)}) collective-permute-start(bf16[128,128]{1,0:T(8,128)(2,1)S(1)} %shard_map.108.refs_0_), channel_id=1, source_target_pairs={{0,16},{4,20},{8,24},{12,28},{16,0},{20,4},{24,8},{28,12},{32,48},... | collective-permute-start | bytes 98312 | tf_op jit(solution)/shard_map/ppermute | solution.py:401
  41.6 1.2 %collective-permute-start.11 = (bf16[128,128]{1,0:T(8,128)(2,1)S(1)}, bf16[128,128]{1,0:T(8,128)(2,1)S(1)}, u32[]{:S(2)}, u32[]{:S(2)}) collective-permute-start(bf16[128,128]{1,0:T(8,128)(2,1)S(1)} %shard_map.108.refs_0_), channel_id=1, source_target_pairs={{0,24},{4,28},{8,0},{12,4},{16,8},{20,12},{24,16},{28,20},{32,56},... | collective-permute-start | bytes 98312 | tf_op jit(solution)/shard_map/ppermute | solution.py:401
  42.9 0.2 collective-permute-done.9.refs_1_
  43.1 0.7 collective-permute-done.10.refs_2_
  43.8 0.6 collective-permute-done.11.refs_3_
  44.4 0.7 shard_map.110
  45.1 0.6 collective-permute-start.12
  45.7 3.2 %collective-permute-start.13 = (bf16[32,512]{1,0:T(8,128)(2,1)S(1)}, bf16[32,512]{1,0:T(8,128)(2,1)S(1)}, u32[]{:S(2)}, u32[]{:S(2)}) collective-permute-start(bf16[32,512]{1,0:T(8,128)(2,1)S(1)} %get-tuple-element.91.refs_10_.refs_2_), channel_id=1, source_target_pairs={{0,2},{1,3},{2,0},{3,1},{4,6},{5,7},{6,4},{7,5},{8,10},{9,11},{10,... | collective-permute-start | bytes 98312 | tf_op jit(solution)/shard_map/ppermute | solution.py:404
  48.9 0.1 collective-permute-start.14
  48.9 1.1 %shard_map.111 = (bf16[1536,256]{1,0:T(8,128)(2,1)S(1)}, f32[8,128]{1,0:T(8,128)S(1)}) custom-call(bf16[2064,256]{1,0:T(8,128)(2,1)S(1)} %collective-permute-done.refs_1_.refs_0_, bf16[256,512]{1,0:T(8,128)(2,1)S(1)} %get-tuple-element.87.refs_1_, f32[256,128]{1,0:T(8,128)S(1)} %get-tuple-element.63.refs_4_.refs_6_.refs_2_, ...), custom_call_target="tpu_custom_call" | custom-call | flops 4000000000 | bytes 16000000 | tf_op jit(solution)/shard_map/pallas_call | solution.py:45
  50.0 1.0 %shard_map.112 = (bf16[1536,256]{1,0:T(8,128)(2,1)S(1)}, f32[8,128]{1,0:T(8,128)S(1)}) custom-call(bf16[2064,256]{1,0:T(8,128)(2,1)S(1)} %copy-done.1, bf16[256,512]{1,0:T(8,128)(2,1)S(1)} %get-tuple-element.57.refs_1_, f32[256,128]{1,0:T(8,128)S(1)} %get-tuple-element.58.refs_5_.refs_7_.refs_2_, f32[256,128]{1,0:T(8,128)S(1)} %get-tuple-element.71.refs_3_, ...), custom_call_target="tpu_custom_call" | custom-call | flops 4000000000 | bytes 16000000 | tf_op jit(solution)/shard_map/pallas_call | solution.py:45
  51.0 0.6 collective-permute-done.14.refs_5_
  51.6 0.5 shard_map.113
  52.2 0.8 collective-permute-start.15
  53.0 2.9 %collective-permute-start.16 = (bf16[128,128]{1,0:T(8,128)(2,1)S(1)}, bf16[128,128]{1,0:T(8,128)(2,1)S(1)}, u32[]{:S(2)}, u32[]{:S(2)}) collective-permute-start(bf16[128,128]{1,0:T(8,128)(2,1)S(1)} %get-tuple-element.97), channel_id=1, source_target_pairs={{0,16},{4,20},{8,24},{12,28},{16,0},{20,4},{24,8},{28,12},{32,48},... | collective-permute-start | bytes 98312 | tf_op jit(solution)/shard_map/ppermute | solution.py:401
  55.9 0.6 collective-permute-done.15.refs_1_
  56.5 1.0 %collective-permute-done.16.refs_2_ = bf16[128,128]{1,0:T(8,128)(2,1)S(1)} collective-permute-done((bf16[128,128]{1,0:T(8,128)(2,1)S(1)}, bf16[128,128]{1,0:T(8,128)(2,1)S(1)}, u32[]{:S(2)}, u32[]{:S(2)}) %collective-permute-start.16) | collective-permute-done | bytes 32800 | tf_op jit(solution)/shard_map/ppermute | solution.py:401
  57.5 1.1 %collective-permute-done.17.refs_3_ = bf16[128,128]{1,0:T(8,128)(2,1)S(1)} collective-permute-done((bf16[128,128]{1,0:T(8,128)(2,1)S(1)}, bf16[128,128]{1,0:T(8,128)(2,1)S(1)}, u32[]{:S(2)}, u32[]{:S(2)}) %collective-permute-start.17) | collective-permute-done | bytes 32800 | tf_op jit(solution)/shard_map/ppermute | solution.py:401
  58.7 11.1 %all_to_all.11.refs_0_ = bf16[8,128,128]{2,1,0:T(8,128)(2,1)S(1)} all-to-all(bf16[8,128,128]{2,1,0:T(8,128)(2,1)S(1)} %shard_map.114), channel_id=1, replica_groups={{224,192,160,128,96,64,32,0},{228,196,164,132,100,68,36,4},{232,200,168..., dimensions={0} | all-to-all | bytes 524288 | tf_op jit(solution)/shard_map/all_to_all | solution.py:479
  69.9 9.4 %collective-permute-start.18 = (bf16[128,128]{1,0:T(8,128)(2,1)S(1)}, bf16[128,128]{1,0:T(8,128)(2,1)S(1)}, u32[]{:S(2)}, u32[]{:S(2)}) collective-permute-start(bf16[128,128]{1,0:T(8,128)(2,1)S(1)} %shard_map.115.refs_0_), channel_id=1, source_target_pairs={{0,4},{4,0},{8,12},{12,8},{16,20},{20,16},{24,28},{28,24},{32,36},... | collective-permute-start | bytes 98312 | tf_op jit(solution)/shard_map/ppermute | solution.py:397
  79.3 0.9 collective-permute-done.18.refs_1_
  80.2 0.4 collective-permute-start.19
  80.6 2.1 %collective-permute-start.21 = (bf16[256,128]{1,0:T(8,128)(2,1)S(1)}, bf16[256,128]{1,0:T(8,128)(2,1)S(1)}, u32[]{:S(2)}, u32[]{:S(2)}) collective-permute-start(bf16[256,128]{1,0:T(8,128)(2,1)S(1)} %get-tuple-element.101.refs_2_.refs_0_), channel_id=1, source_target_pairs={{0,16},{4,20},{8,24},{12,28},{16,0},{20,4},{24,8},{28,12},{32,48},... | collective-permute-start | bytes 196616 | tf_op jit(solution)/shard_map/ppermute | solution.py:401
  82.7 1.2 %collective-permute-start.22 = (bf16[256,128]{1,0:T(8,128)(2,1)S(1)}, bf16[256,128]{1,0:T(8,128)(2,1)S(1)}, u32[]{:S(2)}, u32[]{:S(2)}) collective-permute-start(bf16[256,128]{1,0:T(8,128)(2,1)S(1)} %get-tuple-element.101.refs_2_.refs_0_), channel_id=1, source_target_pairs={{0,24},{4,28},{8,0},{12,4},{16,8},{20,12},{24,16},{28,20},{32,56},... | collective-permute-start | bytes 196616 | tf_op jit(solution)/shard_map/ppermute | solution.py:401
  83.9 1.2 %shard_map.117 = (bf16[512,512]{1,0:T(8,128)(2,1)}, bf16[512,512]{1,0:T(8,128)(2,1)}, bf16[512,512]{1,0:T(8,128)(2,1)}, f32[8,128]{1,0:T(8,128)S(1)}) custom-call(bf16[1536,256]{1,0:T(8,128)(2,1)S(1)} %get-tuple-element.93.refs_0_, bf16[1536,256]{1,0:T(8,128)(2,1)S(1)} %collective-permute-done.19.refs_1_, bf16[256,128]{1,0:T(8,128)(2,1)S(1)} %get-tuple-element.101.refs_2_.refs_0_), custom_call_target="tpu_custom_call" | custom-call | flops 10000000 | bytes 1000000 | tf_op jit(solution)/shard_map/pallas_call | solution.py:45
  85.1 1.8 %collective-permute-done.20.refs_1_ = bf16[256,128]{1,0:T(8,128)(2,1)S(1)} collective-permute-done((bf16[256,128]{1,0:T(8,128)(2,1)S(1)}, bf16[256,128]{1,0:T(8,128)(2,1)S(1)}, u32[]{:S(2)}, u32[]{:S(2)}) %collective-permute-start.20) | collective-permute-done | bytes 65568 | tf_op jit(solution)/shard_map/ppermute | solution.py:401
  86.9 0.1 collective-permute-done.22.refs_3_
  87.0 0.9 %shard_map.118 = f32[1024,128]{1,0:T(8,128)} custom-call(bf16[256,128]{1,0:T(8,128)(2,1)S(1)} %get-tuple-element.101.refs_2_.refs_0_, bf16[256,128]{1,0:T(8,128)(2,1)S(1)} %collective-permute-done.20.refs_1_, bf16[256,128]{1,0:T(8,128)(2,1)S(1)} %collective-permute-done.21.refs_2_, bf16[256,128]{1,0:T(8,128)(2,1)S(1)} %collective-permute-done.22.refs_3_, ...), custom_call_target="tpu_custom_call" | custom-call | flops 10000000 | bytes 1000000 | tf_op jit(solution)/shard_map/pallas_call | solution.py:45
  (25 shorter events, 0.2 us)
Async XLA Ops:
  0.6 7.1 %copy-start.2 = (bf16[512,1024]{1,0:T(8,128)(2,1)S(1)}, bf16[512,1024]{1,0:T(8,128)(2,1)}, u32[]{:S(2)}) copy-start(bf16[512,1024]{1,0:T(8,128)(2,1)} %refs_0_.3) | copy-start | bytes 3145732
  4.4 6.7 %collective-permute-start = (bf16[2064,256]{1,0:T(8,128)(2,1)}, bf16[2064,256]{1,0:T(8,128)(2,1)S(1)}, u32[]{:S(2)}, u32[]{:S(2)}) collective-permute-start(bf16[2064,256]{1,0:T(8,128)(2,1)} %get-tuple-element.56), channel_id=1, source_target_pairs={{0,4},{4,0},{8,12},{12,8},{16,20},{20,16},{24,28},{28,24},{32,36},... | collective-permute-start | bytes 3170312 | tf_op jit(solution)/shard_map/ppermute | solution.py:397
  7.7 8.1 %collective-permute-start.5 = (bf16[512,1024]{1,0:T(8,128)(2,1)S(1)}, bf16[512,1024]{1,0:T(8,128)(2,1)S(1)}, u32[]{:S(2)}, u32[]{:S(2)}) collective-permute-start(bf16[512,1024]{1,0:T(8,128)(2,1)S(1)} %copy-done.2), channel_id=1, source_target_pairs={{0,4},{4,0},{8,12},{12,8},{16,20},{20,16},{24,28},{28,24},{32,36},... | collective-permute-start | bytes 3145736 | tf_op jit(solution)/shard_map/ppermute | solution.py:397
  7.8 6.2 %collective-permute-start.1 = (f32[32,512]{1,0:T(8,128)}, f32[32,512]{1,0:T(8,128)S(1)}, u32[]{:S(2)}, u32[]{:S(2)}) collective-permute-start(f32[32,512]{1,0:T(8,128)} %get-tuple-element.65), channel_id=1, source_target_pairs={{0,1},{1,2},{2,3},{3,0},{4,5},{5,6},{6,7},{7,4},{8,9},{9,10},{10,1... | collective-permute-start | bytes 196616 | tf_op jit(solution)/shard_map/ppermute | solution.py:404
  7.8 6.2 %collective-permute-start.2 = (f32[32,512]{1,0:T(8,128)}, f32[32,512]{1,0:T(8,128)S(1)}, u32[]{:S(2)}, u32[]{:S(2)}) collective-permute-start(f32[32,512]{1,0:T(8,128)} %get-tuple-element.66), channel_id=1, source_target_pairs={{0,2},{1,3},{2,0},{3,1},{4,6},{5,7},{6,4},{7,5},{8,10},{9,11},{10,... | collective-permute-start | bytes 196616 | tf_op jit(solution)/shard_map/ppermute | solution.py:404
  10.0 4.2 %collective-permute-start.3 = (f32[32,512]{1,0:T(8,128)}, f32[32,512]{1,0:T(8,128)S(1)}, u32[]{:S(2)}, u32[]{:S(2)}) collective-permute-start(f32[32,512]{1,0:T(8,128)} %get-tuple-element.67), channel_id=1, source_target_pairs={{0,3},{1,0},{2,1},{3,2},{4,7},{5,4},{6,5},{7,6},{8,11},{9,8},{10,9... | collective-permute-start | bytes 196616 | tf_op jit(solution)/shard_map/ppermute | solution.py:404
  11.1 1.2 %copy-start = (bf16[2064,256]{1,0:T(8,128)(2,1)S(1)}, bf16[2064,256]{1,0:T(8,128)(2,1)}, u32[]{:S(2)}) copy-start(bf16[2064,256]{1,0:T(8,128)(2,1)} %get-tuple-element.55.refs_0_) | copy-start | bytes 3170308
  12.8 1.4 %copy-start.3 = (f32[32,512]{1,0:T(8,128)S(1)}, f32[32,512]{1,0:T(8,128)}, u32[]{:S(2)}) copy-start(f32[32,512]{1,0:T(8,128)} %get-tuple-element.64.refs_0_) | copy-start | bytes 196612
  12.8 3.9 %copy-start.1 = (bf16[2064,256]{1,0:T(8,128)(2,1)S(1)}, bf16[2064,256]{1,0:T(8,128)(2,1)}, u32[]{:S(2)}) copy-start(bf16[2064,256]{1,0:T(8,128)(2,1)} %get-tuple-element.55.refs_0_) | copy-start | bytes 3170308
  14.2 2.5 %collective-permute-start.4 = (f32[16,512]{1,0:T(8,128)S(1)}, f32[16,512]{1,0:T(8,128)S(1)}, u32[]{:S(2)}, u32[]{:S(2)}) collective-permute-start(f32[16,512]{1,0:T(8,128)S(1)} %get-tuple-element.70), channel_id=1, source_target_pairs={{0,4},{4,0},{8,12},{12,8},{16,20},{20,16},{24,28},{28,24},{32,36},... | collective-permute-start | bytes 98312 | tf_op jit(solution)/shard_map/ppermute | solution.py:397
  17.5 5.3 %collective-permute-start.6 = (bf16[384,128]{1,0:T(8,128)(2,1)S(1)}, bf16[384,128]{1,0:T(8,128)(2,1)S(1)}, u32[]{:S(2)}, u32[]{:S(2)}) collective-permute-start(bf16[384,128]{1,0:T(8,128)(2,1)S(1)} %get-tuple-element.74), channel_id=1, source_target_pairs={{0,8},{4,12},{8,16},{12,20},{16,24},{20,28},{24,0},{28,4},{32,40},... | collective-permute-start | bytes 294920 | tf_op jit(solution)/shard_map/ppermute | solution.py:401
  18.5 7.1 %collective-permute-start.7 = (bf16[384,128]{1,0:T(8,128)(2,1)S(1)}, bf16[384,128]{1,0:T(8,128)(2,1)S(1)}, u32[]{:S(2)}, u32[]{:S(2)}) collective-permute-start(bf16[384,128]{1,0:T(8,128)(2,1)S(1)} %get-tuple-element.75), channel_id=1, source_target_pairs={{0,16},{4,20},{8,24},{12,28},{16,0},{20,4},{24,8},{28,12},{32,48},... | collective-permute-start | bytes 294920 | tf_op jit(solution)/shard_map/ppermute | solution.py:401
  20.9 4.7 %collective-permute-start.8 = (bf16[384,128]{1,0:T(8,128)(2,1)S(1)}, bf16[384,128]{1,0:T(8,128)(2,1)S(1)}, u32[]{:S(2)}, u32[]{:S(2)}) collective-permute-start(bf16[384,128]{1,0:T(8,128)(2,1)S(1)} %get-tuple-element.76), channel_id=1, source_target_pairs={{0,24},{4,28},{8,0},{12,4},{16,8},{20,12},{24,16},{28,20},{32,56},... | collective-permute-start | bytes 294920 | tf_op jit(solution)/shard_map/ppermute | solution.py:401
  39.0 4.1 %collective-permute-start.9 = (bf16[128,128]{1,0:T(8,128)(2,1)S(1)}, bf16[128,128]{1,0:T(8,128)(2,1)S(1)}, u32[]{:S(2)}, u32[]{:S(2)}) collective-permute-start(bf16[128,128]{1,0:T(8,128)(2,1)S(1)} %shard_map.108.refs_0_), channel_id=1, source_target_pairs={{0,8},{4,12},{8,16},{12,20},{16,24},{20,28},{24,0},{28,4},{32,40},... | collective-permute-start | bytes 98312 | tf_op jit(solution)/shard_map/ppermute | solution.py:401
  39.5 4.3 %collective-permute-start.10 = (bf16[128,128]{1,0:T(8,128)(2,1)S(1)}, bf16[128,128]{1,0:T(8,128)(2,1)S(1)}, u32[]{:S(2)}, u32[]{:S(2)}) collective-permute-start(bf16[128,128]{1,0:T(8,128)(2,1)S(1)} %shard_map.108.refs_0_), channel_id=1, source_target_pairs={{0,16},{4,20},{8,24},{12,28},{16,0},{20,4},{24,8},{28,12},{32,48},... | collective-permute-start | bytes 98312 | tf_op jit(solution)/shard_map/ppermute | solution.py:401
  41.6 2.8 %collective-permute-start.11 = (bf16[128,128]{1,0:T(8,128)(2,1)S(1)}, bf16[128,128]{1,0:T(8,128)(2,1)S(1)}, u32[]{:S(2)}, u32[]{:S(2)}) collective-permute-start(bf16[128,128]{1,0:T(8,128)(2,1)S(1)} %shard_map.108.refs_0_), channel_id=1, source_target_pairs={{0,24},{4,28},{8,0},{12,4},{16,8},{20,12},{24,16},{28,20},{32,56},... | collective-permute-start | bytes 98312 | tf_op jit(solution)/shard_map/ppermute | solution.py:401
  45.1 5.9 %collective-permute-start.12 = (bf16[32,512]{1,0:T(8,128)(2,1)S(1)}, bf16[32,512]{1,0:T(8,128)(2,1)S(1)}, u32[]{:S(2)}, u32[]{:S(2)}) collective-permute-start(bf16[32,512]{1,0:T(8,128)(2,1)S(1)} %get-tuple-element.91.refs_10_.refs_2_), channel_id=1, source_target_pairs={{0,1},{1,2},{2,3},{3,0},{4,5},{5,6},{6,7},{7,4},{8,9},{9,10},{10,1... | collective-permute-start | bytes 98312 | tf_op jit(solution)/shard_map/ppermute | solution.py:404
  45.7 5.3 %collective-permute-start.13 = (bf16[32,512]{1,0:T(8,128)(2,1)S(1)}, bf16[32,512]{1,0:T(8,128)(2,1)S(1)}, u32[]{:S(2)}, u32[]{:S(2)}) collective-permute-start(bf16[32,512]{1,0:T(8,128)(2,1)S(1)} %get-tuple-element.91.refs_10_.refs_2_), channel_id=1, source_target_pairs={{0,2},{1,3},{2,0},{3,1},{4,6},{5,7},{6,4},{7,5},{8,10},{9,11},{10,... | collective-permute-start | bytes 98312 | tf_op jit(solution)/shard_map/ppermute | solution.py:404
  48.9 2.8 %collective-permute-start.14 = (bf16[32,512]{1,0:T(8,128)(2,1)S(1)}, bf16[32,512]{1,0:T(8,128)(2,1)S(1)}, u32[]{:S(2)}, u32[]{:S(2)}) collective-permute-start(bf16[32,512]{1,0:T(8,128)(2,1)S(1)} %get-tuple-element.91.refs_10_.refs_2_), channel_id=1, source_target_pairs={{0,3},{1,0},{2,1},{3,2},{4,7},{5,4},{6,5},{7,6},{8,11},{9,8},{10,9... | collective-permute-start | bytes 98312 | tf_op jit(solution)/shard_map/ppermute | solution.py:404
  52.2 4.3 %collective-permute-start.15 = (bf16[128,128]{1,0:T(8,128)(2,1)S(1)}, bf16[128,128]{1,0:T(8,128)(2,1)S(1)}, u32[]{:S(2)}, u32[]{:S(2)}) collective-permute-start(bf16[128,128]{1,0:T(8,128)(2,1)S(1)} %get-tuple-element.96), channel_id=1, source_target_pairs={{0,8},{4,12},{8,16},{12,20},{16,24},{20,28},{24,0},{28,4},{32,40},... | collective-permute-start | bytes 98312 | tf_op jit(solution)/shard_map/ppermute | solution.py:401
  53.0 4.6 %collective-permute-start.16 = (bf16[128,128]{1,0:T(8,128)(2,1)S(1)}, bf16[128,128]{1,0:T(8,128)(2,1)S(1)}, u32[]{:S(2)}, u32[]{:S(2)}) collective-permute-start(bf16[128,128]{1,0:T(8,128)(2,1)S(1)} %get-tuple-element.97), channel_id=1, source_target_pairs={{0,16},{4,20},{8,24},{12,28},{16,0},{20,4},{24,8},{28,12},{32,48},... | collective-permute-start | bytes 98312 | tf_op jit(solution)/shard_map/ppermute | solution.py:401
  55.9 2.8 %collective-permute-start.17 = (bf16[128,128]{1,0:T(8,128)(2,1)S(1)}, bf16[128,128]{1,0:T(8,128)(2,1)S(1)}, u32[]{:S(2)}, u32[]{:S(2)}) collective-permute-start(bf16[128,128]{1,0:T(8,128)(2,1)S(1)} %get-tuple-element.98), channel_id=1, source_target_pairs={{0,24},{4,28},{8,0},{12,4},{16,8},{20,12},{24,16},{28,20},{32,56},... | collective-permute-start | bytes 98312 | tf_op jit(solution)/shard_map/ppermute | solution.py:401
  69.9 10.3 %collective-permute-start.18 = (bf16[128,128]{1,0:T(8,128)(2,1)S(1)}, bf16[128,128]{1,0:T(8,128)(2,1)S(1)}, u32[]{:S(2)}, u32[]{:S(2)}) collective-permute-start(bf16[128,128]{1,0:T(8,128)(2,1)S(1)} %shard_map.115.refs_0_), channel_id=1, source_target_pairs={{0,4},{4,0},{8,12},{12,8},{16,20},{20,16},{24,28},{28,24},{32,36},... | collective-permute-start | bytes 98312 | tf_op jit(solution)/shard_map/ppermute | solution.py:397
  80.2 3.7 %collective-permute-start.19 = (bf16[1536,256]{1,0:T(8,128)(2,1)S(1)}, bf16[1536,256]{1,0:T(8,128)(2,1)S(1)}, u32[]{:S(2)}, u32[]{:S(2)}) collective-permute-start(bf16[1536,256]{1,0:T(8,128)(2,1)S(1)} %get-tuple-element.100), channel_id=1, source_target_pairs={{0,4},{4,0},{8,12},{12,8},{16,20},{20,16},{24,28},{28,24},{32,36},... | collective-permute-start | bytes 2359304 | tf_op jit(solution)/shard_map/ppermute | solution.py:397
  80.6 6.3 %collective-permute-start.20 = (bf16[256,128]{1,0:T(8,128)(2,1)S(1)}, bf16[256,128]{1,0:T(8,128)(2,1)S(1)}, u32[]{:S(2)}, u32[]{:S(2)}) collective-permute-start(bf16[256,128]{1,0:T(8,128)(2,1)S(1)} %get-tuple-element.101.refs_2_.refs_0_), channel_id=1, source_target_pairs={{0,8},{4,12},{8,16},{12,20},{16,24},{20,28},{24,0},{28,4},{32,40},... | collective-permute-start | bytes 196616 | tf_op jit(solution)/shard_map/ppermute | solution.py:401
  80.6 6.3 %collective-permute-start.21 = (bf16[256,128]{1,0:T(8,128)(2,1)S(1)}, bf16[256,128]{1,0:T(8,128)(2,1)S(1)}, u32[]{:S(2)}, u32[]{:S(2)}) collective-permute-start(bf16[256,128]{1,0:T(8,128)(2,1)S(1)} %get-tuple-element.101.refs_2_.refs_0_), channel_id=1, source_target_pairs={{0,16},{4,20},{8,24},{12,28},{16,0},{20,4},{24,8},{28,12},{32,48},... | collective-permute-start | bytes 196616 | tf_op jit(solution)/shard_map/ppermute | solution.py:401
  82.7 4.3 %collective-permute-start.22 = (bf16[256,128]{1,0:T(8,128)(2,1)S(1)}, bf16[256,128]{1,0:T(8,128)(2,1)S(1)}, u32[]{:S(2)}, u32[]{:S(2)}) collective-permute-start(bf16[256,128]{1,0:T(8,128)(2,1)S(1)} %get-tuple-element.101.refs_2_.refs_0_), channel_id=1, source_target_pairs={{0,24},{4,28},{8,0},{12,4},{16,8},{20,12},{24,16},{28,20},{32,56},... | collective-permute-start | bytes 196616 | tf_op jit(solution)/shard_map/ppermute | solution.py:401

commit v10 on v9

--- a/solution.py
+++ b/solution.py
@@ -14,6 +14,7 @@
 DIM = 128
 SPAN = 64
 LEVELS = 8
+ORDER = [5, 4, 6, 3, 2, 7, 0, 1]
 INV = 1.0 / DIM
 VMEM_LIMIT = 24 * 1024 * 1024
 VMEM_ALL = 60 * 1024 * 1024
@@ -223,7 +224,7 @@
     total = own_ref[...] + got[0][256:] + (got[1][256:] + got[2][256:])
     here = lax.axis_index("seq") // 8
     for group in range(8):
-        spread_ref[7 - group] = jnp.where(group > here, total[:64], total[64:]).astype(BF16)
+        spread_ref[ORDER.index(group)] = jnp.where(group > here, total[:64], total[64:]).astype(BF16)
 
 
 def along_z_body(r_ref, o_ref):
@@ -231,7 +232,7 @@
     before = jnp.zeros((64, DIM), F32)
     after = jnp.zeros((64, DIM), F32)
     for group in range(8):
-        part = r_ref[7 - group].astype(F32)
+        part = r_ref[ORDER.index(group)].astype(F32)
         before = before + part * (here > group).astype(F32)
         after = after + part * (here < group).astype(F32)
     o_ref[...] = jnp.concatenate([before, after], axis=0).astype(BF16)
@@ -390,7 +391,7 @@
 
 def shards(layer_input, gate_weight, queries, key_vectors, value_vectors, grad_output, reach_level):
     seq_count = lax.axis_size("seq")
-    columns = [[8 * z + place for z in reversed(range(8))] for place in range(8)]
+    columns = [[8 * z + place for z in ORDER] for place in range(8)]
     swap = [(d, d ^ 1) for d in range(seq_count)]
 
     def sibling(value):

time: 88.3 us -> 87.2 us (0.988)
  blocking collectives: 24.3 us -> 23.2 us
    all_to_all x1, blocking collectives: 13.2 us -> 12 us  [shards(): lax.all_to_all(spread, 'seq', 0, 0, axis_index_groups=columns)]
where the time goes in v10:
time: 87.2 us; the launch traced here: 87 us
  starting transfers between devices  37.5 us (43%)
  blocking collectives  23.2 us (27%)
  waiting for transfers between devices  12.2 us (14%)
  Pallas kernels  11.9 us (14%)
  local copies, waits for them, and re-layouts  1.24 us (1%)
  between operations  0.97 us (1%)
    ppermute x12, starting transfers between devices, rotate_x(): return lax.ppermute(value, 'seq', pairs)  15.9 us
    ppermute x5, starting transfers between devices, sibling(): return lax.ppermute(value, 'seq', swap)  14.5 us
    all_to_all x1, blocking collectives, shards(): lax.all_to_all(spread, 'seq', 0, 0, axis_index_groups=columns)  12 us
    pallas_call x17, Pallas kernels, call(): pl.pallas_call(kernel, out_shape=out_shape, grid=grid, in_specs=in_specs,...  11.9 us
    all_to_all x1, blocking collectives, shards(): got4 = lax.all_to_all(spread, 'seq', 0, 0, axis_index_groups=columns)  11.2 us
    ppermute x12, waiting for transfers between devices, rotate_x(): return lax.ppermute(value, 'seq', pairs)  9.72 us
    ppermute x6, starting transfers between devices, rotate(): return lax.ppermute(value, 'head', [(h, (h + step) % 4) for h in range(4)])  7.05 us
  transfers between devices with their start and end apart: 23, of which 14 were waited for; matrix products, arithmetic and copies ran while one was open for 0% of the time, Pallas kernels for 6%

profile of v10, /device:TPU:1, one launch (start us, length us, event | category | flops | bytes accessed | tf_op | source)
XLA Modules:
  0.0 87.0 jit_solution(5316222217208117187)
XLA Ops:
  0.6 3.7 %shard_map.102 = (f32[32,512]{1,0:T(8,128)}, f32[32,512]{1,0:T(8,128)}, f32[32,512]{1,0:T(8,128)}, f32[32,512]{1,0:T(8,128)}, bf16[2064,256]{1,0:T(8,128)(2,1)}, /*index=5*/bf16[2064,256]{1,0:T(8,128)(2,1)}) custom-call(bf16[512,1024]{1,0:T(8,128)(2,1)} %refs_0_.3, bf16[1024,128]{1,0:T(8,128)(2,1)} %refs_1_.1, bf16[512,512]{1,0:T(8,128)(2,1)} %refs_2_.1, ...), custom_call_target="tpu_custom_call" | custom-call | flops 10000000 | bytes 1000000 | tf_op jit(solution)/shard_map/pallas_call | solution.py:46
  4.4 3.3 %collective-permute-start = (bf16[2064,256]{1,0:T(8,128)(2,1)}, bf16[2064,256]{1,0:T(8,128)(2,1)S(1)}, u32[]{:S(2)}, u32[]{:S(2)}) collective-permute-start(bf16[2064,256]{1,0:T(8,128)(2,1)} %get-tuple-element.56), channel_id=1, source_target_pairs={{0,4},{4,0},{8,12},{12,8},{16,20},{20,16},{24,28},{28,24},{32,36},... | collective-permute-start | bytes 3170312 | tf_op jit(solution)/shard_map/ppermute | solution.py:398
  7.7 0.1 collective-permute-start.5
  7.8 2.2 %collective-permute-start.2 = (f32[32,512]{1,0:T(8,128)}, f32[32,512]{1,0:T(8,128)S(1)}, u32[]{:S(2)}, u32[]{:S(2)}) collective-permute-start(f32[32,512]{1,0:T(8,128)} %get-tuple-element.66), channel_id=1, source_target_pairs={{0,2},{1,3},{2,0},{3,1},{4,6},{5,7},{6,4},{7,5},{8,10},{9,11},{10,... | collective-permute-start | bytes 196616 | tf_op jit(solution)/shard_map/ppermute | solution.py:405
  10.0 1.1 %collective-permute-start.3 = (f32[32,512]{1,0:T(8,128)}, f32[32,512]{1,0:T(8,128)S(1)}, u32[]{:S(2)}, u32[]{:S(2)}) collective-permute-start(f32[32,512]{1,0:T(8,128)} %get-tuple-element.67), channel_id=1, source_target_pairs={{0,3},{1,0},{2,1},{3,2},{4,7},{5,4},{6,5},{7,6},{8,11},{9,8},{10,9... | collective-permute-start | bytes 196616 | tf_op jit(solution)/shard_map/ppermute | solution.py:405
  11.1 1.2 %copy-done = bf16[2064,256]{1,0:T(8,128)(2,1)S(1)} copy-done((bf16[2064,256]{1,0:T(8,128)(2,1)S(1)}, bf16[2064,256]{1,0:T(8,128)(2,1)}, u32[]{:S(2)}) %copy-start) | copy-done | bytes 1056792
  12.3 0.5 shard_map.103
  12.8 1.2 %shard_map.104 = (f32[16,512]{1,0:T(8,128)S(1)}, f32[16,512]{1,0:T(8,128)S(1)}, f32[1536,256]{1,0:T(8,128)S(1)}, f32[1536,256]{1,0:T(8,128)S(1)}, f32[1536,256]{1,0:T(8,128)S(1)}, /*index=5*/f32[1536,256]{1,0:T(8,128)S(1)}) custom-call(bf16[2064,256]{1,0:T(8,128)(2,1)S(1)} %copy-done, bf16[2064,256]{1,0:T(8,128)(2,1)S(1)} %collective-permute-done.refs_1_.refs_0_, ...), custom_call_target="tpu_custom_call" | custom-call | flops 10000000 | bytes 1000000 | tf_op jit(solution)/shard_map/pallas_call | solution.py:46
  14.0 0.1 collective-permute-done.3.refs_3_
  14.2 1.6 %collective-permute-start.4 = (f32[16,512]{1,0:T(8,128)S(1)}, f32[16,512]{1,0:T(8,128)S(1)}, u32[]{:S(2)}, u32[]{:S(2)}) collective-permute-start(f32[16,512]{1,0:T(8,128)S(1)} %get-tuple-element.70), channel_id=1, source_target_pairs={{0,4},{4,0},{8,12},{12,8},{16,20},{20,16},{24,28},{28,24},{32,36},... | collective-permute-start | bytes 98312 | tf_op jit(solution)/shard_map/ppermute | solution.py:398
  15.8 0.9 collective-permute-done.4.refs_9_
  16.7 0.8 shard_map.106
  17.5 1.0 %collective-permute-start.6 = (bf16[384,128]{1,0:T(8,128)(2,1)S(1)}, bf16[384,128]{1,0:T(8,128)(2,1)S(1)}, u32[]{:S(2)}, u32[]{:S(2)}) collective-permute-start(bf16[384,128]{1,0:T(8,128)(2,1)S(1)} %get-tuple-element.74), channel_id=1, source_target_pairs={{0,8},{4,12},{8,16},{12,20},{16,24},{20,28},{24,0},{28,4},{32,40},... | collective-permute-start | bytes 294920 | tf_op jit(solution)/shard_map/ppermute | solution.py:402
  18.5 2.5 %collective-permute-start.7 = (bf16[384,128]{1,0:T(8,128)(2,1)S(1)}, bf16[384,128]{1,0:T(8,128)(2,1)S(1)}, u32[]{:S(2)}, u32[]{:S(2)}) collective-permute-start(bf16[384,128]{1,0:T(8,128)(2,1)S(1)} %get-tuple-element.75), channel_id=1, source_target_pairs={{0,16},{4,20},{8,24},{12,28},{16,0},{20,4},{24,8},{28,12},{32,48},... | collective-permute-start | bytes 294920 | tf_op jit(solution)/shard_map/ppermute | solution.py:402
  20.9 1.2 %collective-permute-start.8 = (bf16[384,128]{1,0:T(8,128)(2,1)S(1)}, bf16[384,128]{1,0:T(8,128)(2,1)S(1)}, u32[]{:S(2)}, u32[]{:S(2)}) collective-permute-start(bf16[384,128]{1,0:T(8,128)(2,1)S(1)} %get-tuple-element.76), channel_id=1, source_target_pairs={{0,24},{4,28},{8,0},{12,4},{16,8},{20,12},{24,16},{28,20},{32,56},... | collective-permute-start | bytes 294920 | tf_op jit(solution)/shard_map/ppermute | solution.py:402
  22.1 0.7 collective-permute-done.6.refs_1_
  22.8 2.8 %collective-permute-done.7.refs_2_ = bf16[384,128]{1,0:T(8,128)(2,1)S(1)} collective-permute-done((bf16[384,128]{1,0:T(8,128)(2,1)S(1)}, bf16[384,128]{1,0:T(8,128)(2,1)S(1)}, u32[]{:S(2)}, u32[]{:S(2)}) %collective-permute-start.7) | collective-permute-done | bytes 98336 | tf_op jit(solution)/shard_map/ppermute | solution.py:402
  25.6 0.1 shard_map.107
  25.7 12.0 %all_to_all.10.refs_0_ = bf16[8,64,128]{2,1,0:T(8,128)(2,1)S(1)} all-to-all(bf16[8,64,128]{2,1,0:T(8,128)(2,1)S(1)} %get-tuple-element.77), channel_id=1, replica_groups={{160,128,192,96,64,224,0,32},{164,132,196,100,68,228,4,36},{168,136,200..., dimensions={0} | all-to-all | bytes 262144 | tf_op jit(solution)/shard_map/all_to_all | solution.py:452
  37.8 0.6 collective-permute-start.9
  38.4 2.1 %collective-permute-start.10 = (bf16[128,128]{1,0:T(8,128)(2,1)S(1)}, bf16[128,128]{1,0:T(8,128)(2,1)S(1)}, u32[]{:S(2)}, u32[]{:S(2)}) collective-permute-start(bf16[128,128]{1,0:T(8,128)(2,1)S(1)} %shard_map.108.refs_0_), channel_id=1, source_target_pairs={{0,16},{4,20},{8,24},{12,28},{16,0},{20,4},{24,8},{28,12},{32,48},... | collective-permute-start | bytes 98312 | tf_op jit(solution)/shard_map/ppermute | solution.py:402
  40.5 1.2 %collective-permute-start.11 = (bf16[128,128]{1,0:T(8,128)(2,1)S(1)}, bf16[128,128]{1,0:T(8,128)(2,1)S(1)}, u32[]{:S(2)}, u32[]{:S(2)}) collective-permute-start(bf16[128,128]{1,0:T(8,128)(2,1)S(1)} %shard_map.108.refs_0_), channel_id=1, source_target_pairs={{0,24},{4,28},{8,0},{12,4},{16,8},{20,12},{24,16},{28,20},{32,56},... | collective-permute-start | bytes 98312 | tf_op jit(solution)/shard_map/ppermute | solution.py:402
  41.8 0.1 collective-permute-done.9.refs_1_
  41.9 0.8 collective-permute-done.10.refs_2_
  42.7 0.6 collective-permute-done.11.refs_3_
  43.4 0.7 shard_map.110
  44.1 0.6 collective-permute-start.12
  44.6 3.2 %collective-permute-start.13 = (bf16[32,512]{1,0:T(8,128)(2,1)S(1)}, bf16[32,512]{1,0:T(8,128)(2,1)S(1)}, u32[]{:S(2)}, u32[]{:S(2)}) collective-permute-start(bf16[32,512]{1,0:T(8,128)(2,1)S(1)} %get-tuple-element.91.refs_10_.refs_2_), channel_id=1, source_target_pairs={{0,2},{1,3},{2,0},{3,1},{4,6},{5,7},{6,4},{7,5},{8,10},{9,11},{10,... | collective-permute-start | bytes 98312 | tf_op jit(solution)/shard_map/ppermute | solution.py:405
  47.8 0.1 collective-permute-start.14
  47.9 1.1 %shard_map.111 = (bf16[1536,256]{1,0:T(8,128)(2,1)S(1)}, f32[8,128]{1,0:T(8,128)S(1)}) custom-call(bf16[2064,256]{1,0:T(8,128)(2,1)S(1)} %collective-permute-done.refs_1_.refs_0_, bf16[256,512]{1,0:T(8,128)(2,1)S(1)} %get-tuple-element.87.refs_1_, f32[256,128]{1,0:T(8,128)S(1)} %get-tuple-element.63.refs_4_.refs_6_.refs_2_, ...), custom_call_target="tpu_custom_call" | custom-call | flops 4000000000 | bytes 16000000 | tf_op jit(solution)/shard_map/pallas_call | solution.py:46
  48.9 1.0 %shard_map.112 = (bf16[1536,256]{1,0:T(8,128)(2,1)S(1)}, f32[8,128]{1,0:T(8,128)S(1)}) custom-call(bf16[2064,256]{1,0:T(8,128)(2,1)S(1)} %copy-done.1, bf16[256,512]{1,0:T(8,128)(2,1)S(1)} %get-tuple-element.57.refs_1_, f32[256,128]{1,0:T(8,128)S(1)} %get-tuple-element.58.refs_5_.refs_7_.refs_2_, f32[256,128]{1,0:T(8,128)S(1)} %get-tuple-element.71.refs_3_, ...), custom_call_target="tpu_custom_call" | custom-call | flops 4000000000 | bytes 16000000 | tf_op jit(solution)/shard_map/pallas_call | solution.py:46
  49.9 0.6 collective-permute-done.14.refs_5_
  50.5 0.5 shard_map.113
  51.1 1.3 %collective-permute-start.15 = (bf16[128,128]{1,0:T(8,128)(2,1)S(1)}, bf16[128,128]{1,0:T(8,128)(2,1)S(1)}, u32[]{:S(2)}, u32[]{:S(2)}) collective-permute-start(bf16[128,128]{1,0:T(8,128)(2,1)S(1)} %get-tuple-element.96), channel_id=1, source_target_pairs={{0,8},{4,12},{8,16},{12,20},{16,24},{20,28},{24,0},{28,4},{32,40},... | collective-permute-start | bytes 98312 | tf_op jit(solution)/shard_map/ppermute | solution.py:402
  52.4 2.7 %collective-permute-start.16 = (bf16[128,128]{1,0:T(8,128)(2,1)S(1)}, bf16[128,128]{1,0:T(8,128)(2,1)S(1)}, u32[]{:S(2)}, u32[]{:S(2)}) collective-permute-start(bf16[128,128]{1,0:T(8,128)(2,1)S(1)} %get-tuple-element.97), channel_id=1, source_target_pairs={{0,16},{4,20},{8,24},{12,28},{16,0},{20,4},{24,8},{28,12},{32,48},... | collective-permute-start | bytes 98312 | tf_op jit(solution)/shard_map/ppermute | solution.py:402
  55.1 0.1 collective-permute-done.15.refs_1_
  55.2 1.5 %collective-permute-done.16.refs_2_ = bf16[128,128]{1,0:T(8,128)(2,1)S(1)} collective-permute-done((bf16[128,128]{1,0:T(8,128)(2,1)S(1)}, bf16[128,128]{1,0:T(8,128)(2,1)S(1)}, u32[]{:S(2)}, u32[]{:S(2)}) %collective-permute-start.16) | collective-permute-done | bytes 32800 | tf_op jit(solution)/shard_map/ppermute | solution.py:402
  56.7 1.1 %collective-permute-done.17.refs_3_ = bf16[128,128]{1,0:T(8,128)(2,1)S(1)} collective-permute-done((bf16[128,128]{1,0:T(8,128)(2,1)S(1)}, bf16[128,128]{1,0:T(8,128)(2,1)S(1)}, u32[]{:S(2)}, u32[]{:S(2)}) %collective-permute-start.17) | collective-permute-done | bytes 32800 | tf_op jit(solution)/shard_map/ppermute | solution.py:402
  57.9 11.2 %all_to_all.11.refs_0_ = bf16[8,128,128]{2,1,0:T(8,128)(2,1)S(1)} all-to-all(bf16[8,128,128]{2,1,0:T(8,128)(2,1)S(1)} %shard_map.114), channel_id=1, replica_groups={{160,128,192,96,64,224,0,32},{164,132,196,100,68,228,4,36},{168,136,200..., dimensions={0} | all-to-all | bytes 524288 | tf_op jit(solution)/shard_map/all_to_all | solution.py:480
  69.1 9.0 %collective-permute-start.18 = (bf16[128,128]{1,0:T(8,128)(2,1)S(1)}, bf16[128,128]{1,0:T(8,128)(2,1)S(1)}, u32[]{:S(2)}, u32[]{:S(2)}) collective-permute-start(bf16[128,128]{1,0:T(8,128)(2,1)S(1)} %shard_map.115.refs_0_), channel_id=1, source_target_pairs={{0,4},{4,0},{8,12},{12,8},{16,20},{20,16},{24,28},{28,24},{32,36},... | collective-permute-start | bytes 98312 | tf_op jit(solution)/shard_map/ppermute | solution.py:398
  78.2 0.9 collective-permute-done.18.refs_1_
  79.0 0.4 collective-permute-start.19
  79.5 2.1 %collective-permute-start.21 = (bf16[256,128]{1,0:T(8,128)(2,1)S(1)}, bf16[256,128]{1,0:T(8,128)(2,1)S(1)}, u32[]{:S(2)}, u32[]{:S(2)}) collective-permute-start(bf16[256,128]{1,0:T(8,128)(2,1)S(1)} %get-tuple-element.101.refs_2_.refs_0_), channel_id=1, source_target_pairs={{0,16},{4,20},{8,24},{12,28},{16,0},{20,4},{24,8},{28,12},{32,48},... | collective-permute-start | bytes 196616 | tf_op jit(solution)/shard_map/ppermute | solution.py:402
  81.6 1.2 %collective-permute-start.22 = (bf16[256,128]{1,0:T(8,128)(2,1)S(1)}, bf16[256,128]{1,0:T(8,128)(2,1)S(1)}, u32[]{:S(2)}, u32[]{:S(2)}) collective-permute-start(bf16[256,128]{1,0:T(8,128)(2,1)S(1)} %get-tuple-element.101.refs_2_.refs_0_), channel_id=1, source_target_pairs={{0,24},{4,28},{8,0},{12,4},{16,8},{20,12},{24,16},{28,20},{32,56},... | collective-permute-start | bytes 196616 | tf_op jit(solution)/shard_map/ppermute | solution.py:402
  82.8 1.2 %shard_map.117 = (bf16[512,512]{1,0:T(8,128)(2,1)}, bf16[512,512]{1,0:T(8,128)(2,1)}, bf16[512,512]{1,0:T(8,128)(2,1)}, f32[8,128]{1,0:T(8,128)S(1)}) custom-call(bf16[1536,256]{1,0:T(8,128)(2,1)S(1)} %get-tuple-element.93.refs_0_, bf16[1536,256]{1,0:T(8,128)(2,1)S(1)} %collective-permute-done.19.refs_1_, bf16[256,128]{1,0:T(8,128)(2,1)S(1)} %get-tuple-element.101.refs_2_.refs_0_), custom_call_target="tpu_custom_call" | custom-call | flops 10000000 | bytes 1000000 | tf_op jit(solution)/shard_map/pallas_call | solution.py:46
  84.0 1.8 %collective-permute-done.20.refs_1_ = bf16[256,128]{1,0:T(8,128)(2,1)S(1)} collective-permute-done((bf16[256,128]{1,0:T(8,128)(2,1)S(1)}, bf16[256,128]{1,0:T(8,128)(2,1)S(1)}, u32[]{:S(2)}, u32[]{:S(2)}) %collective-permute-start.20) | collective-permute-done | bytes 65568 | tf_op jit(solution)/shard_map/ppermute | solution.py:402
  85.8 0.1 collective-permute-done.22.refs_3_
  85.9 0.9 %shard_map.118 = f32[1024,128]{1,0:T(8,128)} custom-call(bf16[256,128]{1,0:T(8,128)(2,1)S(1)} %get-tuple-element.101.refs_2_.refs_0_, bf16[256,128]{1,0:T(8,128)(2,1)S(1)} %collective-permute-done.20.refs_1_, bf16[256,128]{1,0:T(8,128)(2,1)S(1)} %collective-permute-done.21.refs_2_, bf16[256,128]{1,0:T(8,128)(2,1)S(1)} %collective-permute-done.22.refs_3_, ...), custom_call_target="tpu_custom_call" | custom-call | flops 10000000 | bytes 1000000 | tf_op jit(solution)/shard_map/pallas_call | solution.py:46
  (25 shorter events, 0.2 us)
Async XLA Ops:
  0.6 7.1 %copy-start.2 = (bf16[512,1024]{1,0:T(8,128)(2,1)S(1)}, bf16[512,1024]{1,0:T(8,128)(2,1)}, u32[]{:S(2)}) copy-start(bf16[512,1024]{1,0:T(8,128)(2,1)} %refs_0_.3) | copy-start | bytes 3145732
  4.4 6.7 %collective-permute-start = (bf16[2064,256]{1,0:T(8,128)(2,1)}, bf16[2064,256]{1,0:T(8,128)(2,1)S(1)}, u32[]{:S(2)}, u32[]{:S(2)}) collective-permute-start(bf16[2064,256]{1,0:T(8,128)(2,1)} %get-tuple-element.56), channel_id=1, source_target_pairs={{0,4},{4,0},{8,12},{12,8},{16,20},{20,16},{24,28},{28,24},{32,36},... | collective-permute-start | bytes 3170312 | tf_op jit(solution)/shard_map/ppermute | solution.py:398
  7.7 8.1 %collective-permute-start.5 = (bf16[512,1024]{1,0:T(8,128)(2,1)S(1)}, bf16[512,1024]{1,0:T(8,128)(2,1)S(1)}, u32[]{:S(2)}, u32[]{:S(2)}) collective-permute-start(bf16[512,1024]{1,0:T(8,128)(2,1)S(1)} %copy-done.2), channel_id=1, source_target_pairs={{0,4},{4,0},{8,12},{12,8},{16,20},{20,16},{24,28},{28,24},{32,36},... | collective-permute-start | bytes 3145736 | tf_op jit(solution)/shard_map/ppermute | solution.py:398
  7.8 6.2 %collective-permute-start.1 = (f32[32,512]{1,0:T(8,128)}, f32[32,512]{1,0:T(8,128)S(1)}, u32[]{:S(2)}, u32[]{:S(2)}) collective-permute-start(f32[32,512]{1,0:T(8,128)} %get-tuple-element.65), channel_id=1, source_target_pairs={{0,1},{1,2},{2,3},{3,0},{4,5},{5,6},{6,7},{7,4},{8,9},{9,10},{10,1... | collective-permute-start | bytes 196616 | tf_op jit(solution)/shard_map/ppermute | solution.py:405
  7.8 6.2 %collective-permute-start.2 = (f32[32,512]{1,0:T(8,128)}, f32[32,512]{1,0:T(8,128)S(1)}, u32[]{:S(2)}, u32[]{:S(2)}) collective-permute-start(f32[32,512]{1,0:T(8,128)} %get-tuple-element.66), channel_id=1, source_target_pairs={{0,2},{1,3},{2,0},{3,1},{4,6},{5,7},{6,4},{7,5},{8,10},{9,11},{10,... | collective-permute-start | bytes 196616 | tf_op jit(solution)/shard_map/ppermute | solution.py:405
  10.0 4.2 %collective-permute-start.3 = (f32[32,512]{1,0:T(8,128)}, f32[32,512]{1,0:T(8,128)S(1)}, u32[]{:S(2)}, u32[]{:S(2)}) collective-permute-start(f32[32,512]{1,0:T(8,128)} %get-tuple-element.67), channel_id=1, source_target_pairs={{0,3},{1,0},{2,1},{3,2},{4,7},{5,4},{6,5},{7,6},{8,11},{9,8},{10,9... | collective-permute-start | bytes 196616 | tf_op jit(solution)/shard_map/ppermute | solution.py:405
  11.1 1.2 %copy-start = (bf16[2064,256]{1,0:T(8,128)(2,1)S(1)}, bf16[2064,256]{1,0:T(8,128)(2,1)}, u32[]{:S(2)}) copy-start(bf16[2064,256]{1,0:T(8,128)(2,1)} %get-tuple-element.55.refs_0_) | copy-start | bytes 3170308
  12.8 1.4 %copy-start.3 = (f32[32,512]{1,0:T(8,128)S(1)}, f32[32,512]{1,0:T(8,128)}, u32[]{:S(2)}) copy-start(f32[32,512]{1,0:T(8,128)} %get-tuple-element.64.refs_0_) | copy-start | bytes 196612
  12.8 3.9 %copy-start.1 = (bf16[2064,256]{1,0:T(8,128)(2,1)S(1)}, bf16[2064,256]{1,0:T(8,128)(2,1)}, u32[]{:S(2)}) copy-start(bf16[2064,256]{1,0:T(8,128)(2,1)} %get-tuple-element.55.refs_0_) | copy-start | bytes 3170308
  14.2 2.5 %collective-permute-start.4 = (f32[16,512]{1,0:T(8,128)S(1)}, f32[16,512]{1,0:T(8,128)S(1)}, u32[]{:S(2)}, u32[]{:S(2)}) collective-permute-start(f32[16,512]{1,0:T(8,128)S(1)} %get-tuple-element.70), channel_id=1, source_target_pairs={{0,4},{4,0},{8,12},{12,8},{16,20},{20,16},{24,28},{28,24},{32,36},... | collective-permute-start | bytes 98312 | tf_op jit(solution)/shard_map/ppermute | solution.py:398
  17.5 5.3 %collective-permute-start.6 = (bf16[384,128]{1,0:T(8,128)(2,1)S(1)}, bf16[384,128]{1,0:T(8,128)(2,1)S(1)}, u32[]{:S(2)}, u32[]{:S(2)}) collective-permute-start(bf16[384,128]{1,0:T(8,128)(2,1)S(1)} %get-tuple-element.74), channel_id=1, source_target_pairs={{0,8},{4,12},{8,16},{12,20},{16,24},{20,28},{24,0},{28,4},{32,40},... | collective-permute-start | bytes 294920 | tf_op jit(solution)/shard_map/ppermute | solution.py:402
  18.5 7.1 %collective-permute-start.7 = (bf16[384,128]{1,0:T(8,128)(2,1)S(1)}, bf16[384,128]{1,0:T(8,128)(2,1)S(1)}, u32[]{:S(2)}, u32[]{:S(2)}) collective-permute-start(bf16[384,128]{1,0:T(8,128)(2,1)S(1)} %get-tuple-element.75), channel_id=1, source_target_pairs={{0,16},{4,20},{8,24},{12,28},{16,0},{20,4},{24,8},{28,12},{32,48},... | collective-permute-start | bytes 294920 | tf_op jit(solution)/shard_map/ppermute | solution.py:402
  20.9 4.7 %collective-permute-start.8 = (bf16[384,128]{1,0:T(8,128)(2,1)S(1)}, bf16[384,128]{1,0:T(8,128)(2,1)S(1)}, u32[]{:S(2)}, u32[]{:S(2)}) collective-permute-start(bf16[384,128]{1,0:T(8,128)(2,1)S(1)} %get-tuple-element.76), channel_id=1, source_target_pairs={{0,24},{4,28},{8,0},{12,4},{16,8},{20,12},{24,16},{28,20},{32,56},... | collective-permute-start | bytes 294920 | tf_op jit(solution)/shard_map/ppermute | solution.py:402
  37.8 4.1 %collective-permute-start.9 = (bf16[128,128]{1,0:T(8,128)(2,1)S(1)}, bf16[128,128]{1,0:T(8,128)(2,1)S(1)}, u32[]{:S(2)}, u32[]{:S(2)}) collective-permute-start(bf16[128,128]{1,0:T(8,128)(2,1)S(1)} %shard_map.108.refs_0_), channel_id=1, source_target_pairs={{0,8},{4,12},{8,16},{12,20},{16,24},{20,28},{24,0},{28,4},{32,40},... | collective-permute-start | bytes 98312 | tf_op jit(solution)/shard_map/ppermute | solution.py:402
  38.4 4.3 %collective-permute-start.10 = (bf16[128,128]{1,0:T(8,128)(2,1)S(1)}, bf16[128,128]{1,0:T(8,128)(2,1)S(1)}, u32[]{:S(2)}, u32[]{:S(2)}) collective-permute-start(bf16[128,128]{1,0:T(8,128)(2,1)S(1)} %shard_map.108.refs_0_), channel_id=1, source_target_pairs={{0,16},{4,20},{8,24},{12,28},{16,0},{20,4},{24,8},{28,12},{32,48},... | collective-permute-start | bytes 98312 | tf_op jit(solution)/shard_map/ppermute | solution.py:402
  40.5 2.8 %collective-permute-start.11 = (bf16[128,128]{1,0:T(8,128)(2,1)S(1)}, bf16[128,128]{1,0:T(8,128)(2,1)S(1)}, u32[]{:S(2)}, u32[]{:S(2)}) collective-permute-start(bf16[128,128]{1,0:T(8,128)(2,1)S(1)} %shard_map.108.refs_0_), channel_id=1, source_target_pairs={{0,24},{4,28},{8,0},{12,4},{16,8},{20,12},{24,16},{28,20},{32,56},... | collective-permute-start | bytes 98312 | tf_op jit(solution)/shard_map/ppermute | solution.py:402
  44.1 5.8 %collective-permute-start.12 = (bf16[32,512]{1,0:T(8,128)(2,1)S(1)}, bf16[32,512]{1,0:T(8,128)(2,1)S(1)}, u32[]{:S(2)}, u32[]{:S(2)}) collective-permute-start(bf16[32,512]{1,0:T(8,128)(2,1)S(1)} %get-tuple-element.91.refs_10_.refs_2_), channel_id=1, source_target_pairs={{0,1},{1,2},{2,3},{3,0},{4,5},{5,6},{6,7},{7,4},{8,9},{9,10},{10,1... | collective-permute-start | bytes 98312 | tf_op jit(solution)/shard_map/ppermute | solution.py:405
  44.6 5.3 %collective-permute-start.13 = (bf16[32,512]{1,0:T(8,128)(2,1)S(1)}, bf16[32,512]{1,0:T(8,128)(2,1)S(1)}, u32[]{:S(2)}, u32[]{:S(2)}) collective-permute-start(bf16[32,512]{1,0:T(8,128)(2,1)S(1)} %get-tuple-element.91.refs_10_.refs_2_), channel_id=1, source_target_pairs={{0,2},{1,3},{2,0},{3,1},{4,6},{5,7},{6,4},{7,5},{8,10},{9,11},{10,... | collective-permute-start | bytes 98312 | tf_op jit(solution)/shard_map/ppermute | solution.py:405
  47.8 2.8 %collective-permute-start.14 = (bf16[32,512]{1,0:T(8,128)(2,1)S(1)}, bf16[32,512]{1,0:T(8,128)(2,1)S(1)}, u32[]{:S(2)}, u32[]{:S(2)}) collective-permute-start(bf16[32,512]{1,0:T(8,128)(2,1)S(1)} %get-tuple-element.91.refs_10_.refs_2_), channel_id=1, source_target_pairs={{0,3},{1,0},{2,1},{3,2},{4,7},{5,4},{6,5},{7,6},{8,11},{9,8},{10,9... | collective-permute-start | bytes 98312 | tf_op jit(solution)/shard_map/ppermute | solution.py:405
  51.1 4.1 %collective-permute-start.15 = (bf16[128,128]{1,0:T(8,128)(2,1)S(1)}, bf16[128,128]{1,0:T(8,128)(2,1)S(1)}, u32[]{:S(2)}, u32[]{:S(2)}) collective-permute-start(bf16[128,128]{1,0:T(8,128)(2,1)S(1)} %get-tuple-element.96), channel_id=1, source_target_pairs={{0,8},{4,12},{8,16},{12,20},{16,24},{20,28},{24,0},{28,4},{32,40},... | collective-permute-start | bytes 98312 | tf_op jit(solution)/shard_map/ppermute | solution.py:402
  52.4 4.3 %collective-permute-start.16 = (bf16[128,128]{1,0:T(8,128)(2,1)S(1)}, bf16[128,128]{1,0:T(8,128)(2,1)S(1)}, u32[]{:S(2)}, u32[]{:S(2)}) collective-permute-start(bf16[128,128]{1,0:T(8,128)(2,1)S(1)} %get-tuple-element.97), channel_id=1, source_target_pairs={{0,16},{4,20},{8,24},{12,28},{16,0},{20,4},{24,8},{28,12},{32,48},... | collective-permute-start | bytes 98312 | tf_op jit(solution)/shard_map/ppermute | solution.py:402
  55.1 2.8 %collective-permute-start.17 = (bf16[128,128]{1,0:T(8,128)(2,1)S(1)}, bf16[128,128]{1,0:T(8,128)(2,1)S(1)}, u32[]{:S(2)}, u32[]{:S(2)}) collective-permute-start(bf16[128,128]{1,0:T(8,128)(2,1)S(1)} %get-tuple-element.98), channel_id=1, source_target_pairs={{0,24},{4,28},{8,0},{12,4},{16,8},{20,12},{24,16},{28,20},{32,56},... | collective-permute-start | bytes 98312 | tf_op jit(solution)/shard_map/ppermute | solution.py:402
  69.1 9.9 %collective-permute-start.18 = (bf16[128,128]{1,0:T(8,128)(2,1)S(1)}, bf16[128,128]{1,0:T(8,128)(2,1)S(1)}, u32[]{:S(2)}, u32[]{:S(2)}) collective-permute-start(bf16[128,128]{1,0:T(8,128)(2,1)S(1)} %shard_map.115.refs_0_), channel_id=1, source_target_pairs={{0,4},{4,0},{8,12},{12,8},{16,20},{20,16},{24,28},{28,24},{32,36},... | collective-permute-start | bytes 98312 | tf_op jit(solution)/shard_map/ppermute | solution.py:398
  79.0 3.7 %collective-permute-start.19 = (bf16[1536,256]{1,0:T(8,128)(2,1)S(1)}, bf16[1536,256]{1,0:T(8,128)(2,1)S(1)}, u32[]{:S(2)}, u32[]{:S(2)}) collective-permute-start(bf16[1536,256]{1,0:T(8,128)(2,1)S(1)} %get-tuple-element.100), channel_id=1, source_target_pairs={{0,4},{4,0},{8,12},{12,8},{16,20},{20,16},{24,28},{28,24},{32,36},... | collective-permute-start | bytes 2359304 | tf_op jit(solution)/shard_map/ppermute | solution.py:398
  79.5 6.3 %collective-permute-start.20 = (bf16[256,128]{1,0:T(8,128)(2,1)S(1)}, bf16[256,128]{1,0:T(8,128)(2,1)S(1)}, u32[]{:S(2)}, u32[]{:S(2)}) collective-permute-start(bf16[256,128]{1,0:T(8,128)(2,1)S(1)} %get-tuple-element.101.refs_2_.refs_0_), channel_id=1, source_target_pairs={{0,8},{4,12},{8,16},{12,20},{16,24},{20,28},{24,0},{28,4},{32,40},... | collective-permute-start | bytes 196616 | tf_op jit(solution)/shard_map/ppermute | solution.py:402
  79.5 6.3 %collective-permute-start.21 = (bf16[256,128]{1,0:T(8,128)(2,1)S(1)}, bf16[256,128]{1,0:T(8,128)(2,1)S(1)}, u32[]{:S(2)}, u32[]{:S(2)}) collective-permute-start(bf16[256,128]{1,0:T(8,128)(2,1)S(1)} %get-tuple-element.101.refs_2_.refs_0_), channel_id=1, source_target_pairs={{0,16},{4,20},{8,24},{12,28},{16,0},{20,4},{24,8},{28,12},{32,48},... | collective-permute-start | bytes 196616 | tf_op jit(solution)/shard_map/ppermute | solution.py:402
  81.6 4.3 %collective-permute-start.22 = (bf16[256,128]{1,0:T(8,128)(2,1)S(1)}, bf16[256,128]{1,0:T(8,128)(2,1)S(1)}, u32[]{:S(2)}, u32[]{:S(2)}) collective-permute-start(bf16[256,128]{1,0:T(8,128)(2,1)S(1)} %get-tuple-element.101.refs_2_.refs_0_), channel_id=1, source_target_pairs={{0,24},{4,28},{8,0},{12,4},{16,8},{20,12},{24,16},{28,20},{32,56},... | collective-permute-start | bytes 196616 | tf_op jit(solution)/shard_map/ppermute | solution.py:402

commit v11 on v10

--- a/solution.py
+++ b/solution.py
@@ -340,17 +340,16 @@
         o_ref[place] = total
 
 
-def sum_z_body(scale, r_ref, o_ref):
+def sum_z_body(scale, r_ref, held_ref, o_ref, passed_ref):
     total = r_ref[0].astype(F32)
     for place in range(1, 8):
         total = total + r_ref[place].astype(F32)
     o_ref[...] = (total * scale).astype(BF16)
 
 
-def both_body(mine_ref, other_ref, held_ref, o_ref, passed_ref):
-    core = lax.axis_index("seq") & 1
-    o_ref[aligned(core, DIM), :] = mine_ref[...]
-    o_ref[aligned(1 - core, DIM), :] = other_ref[...]
+def pack_body(r0, r1, r2, r3, o_ref):
+    for step, ref in enumerate((r0, r1, r2, r3)):
+        o_ref[DIM * step : DIM * (step + 1), :] = ref[...]
 
 
 def place_body(own_ref, recv_ref, dq_hbm, dk_hbm, dv_hbm, token_ref, sems):
@@ -367,17 +366,16 @@
         copy.wait()
 
 
-def join_body(r0, r1, r2, r3, w_hbm, w_ref, sems):
+def join_body(mine_ref, other_ref, w_hbm, w_ref, sems):
     place = (lax.axis_index("seq") // 2) % 4
+    core = lax.axis_index("seq") & 1
+    mine, other = mine_ref[...].astype(F32), other_ref[...].astype(F32)
+    halves = [jnp.where(core == 0, mine, other), jnp.where(core == 0, other, mine)]
     copies = []
-    for step, ref in enumerate((r0, r1, r2, r3)):
-        data = ref[...].astype(F32)
+    for step in range(4):
         for block in range(2):
-            parts = [
-                data[DIM * half + 64 * block + 16 * group : DIM * half + 64 * block + 16 * group + 16]
-                for group in range(4)
-                for half in range(2)
-            ]
+            row = DIM * step + 64 * block
+            parts = [half[row + 16 * group : row + 16 * group + 16] for group in range(4) for half in halves]
             at = 2 * step + block
             w_ref[DIM * at : DIM * (at + 1), :] = jnp.concatenate(parts, axis=0).T
         rows = aligned(lax.rem(place + 4 - step, 4), 256)
@@ -479,22 +477,20 @@
     spread = call(sum_x_body, shape((8, DIM, DIM), BF16), tuple(got3))
     got4 = lax.all_to_all(spread, "seq", 0, 0, axis_index_groups=columns)
     scale = 1.0 / math.sqrt(TOK * seq_count)
-    mine_sum = call(functools.partial(sum_z_body, scale), quarter, (got4,))
-    other_sum = sibling(mine_sum)
-    both, out_sib = call(
-        both_body, [shape((256, DIM), BF16), shape((3 * TOK, 256), BF16)], (mine_sum, other_sum, out_sib),
-        in_specs=[whole, whole, hbm], out_specs=[whole, hbm], aliases={2: 1},
+    mine_sum, out_sib = call(
+        functools.partial(sum_z_body, scale), [quarter, shape((3 * TOK, 256), BF16)], (got4, out_sib),
+        in_specs=[whole, hbm], out_specs=[whole, hbm], aliases={1: 1},
     )
     out_recv = sibling(out_sib)
+    got5 = [mine_sum] + [rotate_x(mine_sum, step) for step in range(1, 4)]
     *grads, token = call(
         place_body, [shape((TOK, 512), BF16)] * 3 + [shape((8, DIM), F32)], (out_own, out_recv),
-        out_specs=[hbm] * 3 + [whole], scratch=[pltpu.SemaphoreType.DMA((6,))], after=(both,),
-    )
-    got5 = [both] + [rotate_x(both, step) for step in range(1, 4)]
+        out_specs=[hbm] * 3 + [whole], scratch=[pltpu.SemaphoreType.DMA((6,))], after=(mine_sum,),
+    )
+    w_half = call(pack_body, shape((512, DIM), BF16), tuple(got5), after=(token,))
     grad_weight = call(
-        join_body, shape((1024, DIM), F32), tuple(got5),
+        join_body, shape((1024, DIM), F32), (w_half, sibling(w_half)),
         out_specs=hbm,
-        after=(token,),
         scratch=[pltpu.VMEM((1024, DIM), F32), pltpu.SemaphoreType.DMA((4,))],
     )
     return (*grads, grad_weight)

time: 87.2 us -> 87.2 us (level)
  starting transfers between devices: 37.5 us -> 38.6 us
  waiting for transfers between devices: 12.2 us -> 11.1 us
    ppermute x12, waiting for transfers between devices: 9.72 us -> 8.48 us  [rotate_x(): return lax.ppermute(value, 'seq', pairs)]
    ppermute x5, starting transfers between devices: 14.5 us -> 15.7 us  [sibling(): return lax.ppermute(value, 'seq', swap)]
  transfers between devices with their start and end apart: 23 -> 23, of which waited for: 14 -> 13; matrix products, arithmetic and copies ran while one was open for 0% -> 0% of each run, Pallas kernels for 6% -> 6%
where the time goes in v11:
time: 87.2 us; the launch traced here: 87 us
  starting transfers between devices  38.6 us (44%)
  blocking collectives  23.2 us (27%)
  Pallas kernels  11.9 us (14%)
  waiting for transfers between devices  11.1 us (13%)
  local copies, waits for them, and re-layouts  1.24 us (1%)
  between operations  0.99 us (1%)
    ppermute x12, starting transfers between devices, rotate_x(): return lax.ppermute(value, 'seq', pairs)  15.9 us
    ppermute x5, starting transfers between devices, sibling(): return lax.ppermute(value, 'seq', swap)  15.7 us
    all_to_all x1, blocking collectives, shards(): lax.all_to_all(spread, 'seq', 0, 0, axis_index_groups=columns)  12 us
    pallas_call x17, Pallas kernels, call(): pl.pallas_call(kernel, out_shape=out_shape, grid=grid, in_specs=in_specs,...  11.9 us
    all_to_all x1, blocking collectives, shards(): got4 = lax.all_to_all(spread, 'seq', 0, 0, axis_index_groups=columns)  11.2 us
    ppermute x12, waiting for transfers between devices, rotate_x(): return lax.ppermute(value, 'seq', pairs)  8.48 us
    ppermute x6, starting transfers between devices, rotate(): return lax.ppermute(value, 'head', [(h, (h + step) % 4) for h in range(4)])  7.05 us
    ppermute x5, waiting for transfers between devices, sibling(): return lax.ppermute(value, 'seq', swap)  1.85 us
  transfers between devices with their start and end apart: 23, of which 13 were waited for; matrix products, arithmetic and copies ran while one was open for 0% of the time, Pallas kernels for 6%

profile of v11, /device:TPU:1, one launch (start us, length us, event | category | flops | bytes accessed | tf_op | source)
XLA Modules:
  0.0 87.0 jit_solution(3214571653016248923)
XLA Ops:
  0.6 3.7 %shard_map.102 = (f32[32,512]{1,0:T(8,128)}, f32[32,512]{1,0:T(8,128)}, f32[32,512]{1,0:T(8,128)}, f32[32,512]{1,0:T(8,128)}, bf16[2064,256]{1,0:T(8,128)(2,1)}, /*index=5*/bf16[2064,256]{1,0:T(8,128)(2,1)}) custom-call(bf16[512,1024]{1,0:T(8,128)(2,1)} %refs_0_.3, bf16[1024,128]{1,0:T(8,128)(2,1)} %refs_1_.1, bf16[512,512]{1,0:T(8,128)(2,1)} %refs_2_.1, ...), custom_call_target="tpu_custom_call" | custom-call | flops 10000000 | bytes 1000000 | tf_op jit(solution)/shard_map/pallas_call | solution.py:46
  4.4 3.3 %collective-permute-start = (bf16[2064,256]{1,0:T(8,128)(2,1)}, bf16[2064,256]{1,0:T(8,128)(2,1)S(1)}, u32[]{:S(2)}, u32[]{:S(2)}) collective-permute-start(bf16[2064,256]{1,0:T(8,128)(2,1)} %get-tuple-element.56), channel_id=1, source_target_pairs={{0,4},{4,0},{8,12},{12,8},{16,20},{20,16},{24,28},{28,24},{32,36},... | collective-permute-start | bytes 3170312 | tf_op jit(solution)/shard_map/ppermute | solution.py:396
  7.7 0.1 collective-permute-start.5
  7.8 2.2 %collective-permute-start.2 = (f32[32,512]{1,0:T(8,128)}, f32[32,512]{1,0:T(8,128)S(1)}, u32[]{:S(2)}, u32[]{:S(2)}) collective-permute-start(f32[32,512]{1,0:T(8,128)} %get-tuple-element.66), channel_id=1, source_target_pairs={{0,2},{1,3},{2,0},{3,1},{4,6},{5,7},{6,4},{7,5},{8,10},{9,11},{10,... | collective-permute-start | bytes 196616 | tf_op jit(solution)/shard_map/ppermute | solution.py:403
  10.0 1.1 %collective-permute-start.3 = (f32[32,512]{1,0:T(8,128)}, f32[32,512]{1,0:T(8,128)S(1)}, u32[]{:S(2)}, u32[]{:S(2)}) collective-permute-start(f32[32,512]{1,0:T(8,128)} %get-tuple-element.67), channel_id=1, source_target_pairs={{0,3},{1,0},{2,1},{3,2},{4,7},{5,4},{6,5},{7,6},{8,11},{9,8},{10,9... | collective-permute-start | bytes 196616 | tf_op jit(solution)/shard_map/ppermute | solution.py:403
  11.1 1.2 %copy-done = bf16[2064,256]{1,0:T(8,128)(2,1)S(1)} copy-done((bf16[2064,256]{1,0:T(8,128)(2,1)S(1)}, bf16[2064,256]{1,0:T(8,128)(2,1)}, u32[]{:S(2)}) %copy-start) | copy-done | bytes 1056792
  12.3 0.5 shard_map.103
  12.8 1.2 %shard_map.104 = (f32[16,512]{1,0:T(8,128)S(1)}, f32[16,512]{1,0:T(8,128)S(1)}, f32[1536,256]{1,0:T(8,128)S(1)}, f32[1536,256]{1,0:T(8,128)S(1)}, f32[1536,256]{1,0:T(8,128)S(1)}, /*index=5*/f32[1536,256]{1,0:T(8,128)S(1)}) custom-call(bf16[2064,256]{1,0:T(8,128)(2,1)S(1)} %copy-done, bf16[2064,256]{1,0:T(8,128)(2,1)S(1)} %collective-permute-done.refs_1_.refs_0_, ...), custom_call_target="tpu_custom_call" | custom-call | flops 10000000 | bytes 1000000 | tf_op jit(solution)/shard_map/pallas_call | solution.py:46
  14.0 0.1 collective-permute-done.3.refs_3_
  14.2 1.6 %collective-permute-start.4 = (f32[16,512]{1,0:T(8,128)S(1)}, f32[16,512]{1,0:T(8,128)S(1)}, u32[]{:S(2)}, u32[]{:S(2)}) collective-permute-start(f32[16,512]{1,0:T(8,128)S(1)} %get-tuple-element.70), channel_id=1, source_target_pairs={{0,4},{4,0},{8,12},{12,8},{16,20},{20,16},{24,28},{28,24},{32,36},... | collective-permute-start | bytes 98312 | tf_op jit(solution)/shard_map/ppermute | solution.py:396
  15.8 0.9 collective-permute-done.4.refs_9_
  16.7 0.8 shard_map.106
  17.5 1.0 %collective-permute-start.6 = (bf16[384,128]{1,0:T(8,128)(2,1)S(1)}, bf16[384,128]{1,0:T(8,128)(2,1)S(1)}, u32[]{:S(2)}, u32[]{:S(2)}) collective-permute-start(bf16[384,128]{1,0:T(8,128)(2,1)S(1)} %get-tuple-element.74), channel_id=1, source_target_pairs={{0,8},{4,12},{8,16},{12,20},{16,24},{20,28},{24,0},{28,4},{32,40},... | collective-permute-start | bytes 294920 | tf_op jit(solution)/shard_map/ppermute | solution.py:400
  18.5 2.5 %collective-permute-start.7 = (bf16[384,128]{1,0:T(8,128)(2,1)S(1)}, bf16[384,128]{1,0:T(8,128)(2,1)S(1)}, u32[]{:S(2)}, u32[]{:S(2)}) collective-permute-start(bf16[384,128]{1,0:T(8,128)(2,1)S(1)} %get-tuple-element.75), channel_id=1, source_target_pairs={{0,16},{4,20},{8,24},{12,28},{16,0},{20,4},{24,8},{28,12},{32,48},... | collective-permute-start | bytes 294920 | tf_op jit(solution)/shard_map/ppermute | solution.py:400
  20.9 1.2 %collective-permute-start.8 = (bf16[384,128]{1,0:T(8,128)(2,1)S(1)}, bf16[384,128]{1,0:T(8,128)(2,1)S(1)}, u32[]{:S(2)}, u32[]{:S(2)}) collective-permute-start(bf16[384,128]{1,0:T(8,128)(2,1)S(1)} %get-tuple-element.76), channel_id=1, source_target_pairs={{0,24},{4,28},{8,0},{12,4},{16,8},{20,12},{24,16},{28,20},{32,56},... | collective-permute-start | bytes 294920 | tf_op jit(solution)/shard_map/ppermute | solution.py:400
  22.1 0.7 collective-permute-done.6.refs_1_
  22.8 2.8 %collective-permute-done.7.refs_2_ = bf16[384,128]{1,0:T(8,128)(2,1)S(1)} collective-permute-done((bf16[384,128]{1,0:T(8,128)(2,1)S(1)}, bf16[384,128]{1,0:T(8,128)(2,1)S(1)}, u32[]{:S(2)}, u32[]{:S(2)}) %collective-permute-start.7) | collective-permute-done | bytes 98336 | tf_op jit(solution)/shard_map/ppermute | solution.py:400
  25.6 0.1 shard_map.107
  25.7 12.0 %all_to_all.10.refs_0_ = bf16[8,64,128]{2,1,0:T(8,128)(2,1)S(1)} all-to-all(bf16[8,64,128]{2,1,0:T(8,128)(2,1)S(1)} %get-tuple-element.77), channel_id=1, replica_groups={{160,128,192,96,64,224,0,32},{164,132,196,100,68,228,4,36},{168,136,200..., dimensions={0} | all-to-all | bytes 262144 | tf_op jit(solution)/shard_map/all_to_all | solution.py:450
  37.8 0.1 shard_map.108.refs_0_
  37.8 0.6 collective-permute-start.9
  38.4 2.1 %collective-permute-start.10 = (bf16[128,128]{1,0:T(8,128)(2,1)S(1)}, bf16[128,128]{1,0:T(8,128)(2,1)S(1)}, u32[]{:S(2)}, u32[]{:S(2)}) collective-permute-start(bf16[128,128]{1,0:T(8,128)(2,1)S(1)} %shard_map.108.refs_0_), channel_id=1, source_target_pairs={{0,16},{4,20},{8,24},{12,28},{16,0},{20,4},{24,8},{28,12},{32,48},... | collective-permute-start | bytes 98312 | tf_op jit(solution)/shard_map/ppermute | solution.py:400
  40.5 1.2 %collective-permute-start.11 = (bf16[128,128]{1,0:T(8,128)(2,1)S(1)}, bf16[128,128]{1,0:T(8,128)(2,1)S(1)}, u32[]{:S(2)}, u32[]{:S(2)}) collective-permute-start(bf16[128,128]{1,0:T(8,128)(2,1)S(1)} %shard_map.108.refs_0_), channel_id=1, source_target_pairs={{0,24},{4,28},{8,0},{12,4},{16,8},{20,12},{24,16},{28,20},{32,56},... | collective-permute-start | bytes 98312 | tf_op jit(solution)/shard_map/ppermute | solution.py:400
  41.8 0.1 collective-permute-done.9.refs_1_
  41.9 0.8 collective-permute-done.10.refs_2_
  42.7 0.6 collective-permute-done.11.refs_3_
  43.4 0.7 shard_map.110
  44.1 0.6 collective-permute-start.12
  44.6 3.2 %collective-permute-start.13 = (bf16[32,512]{1,0:T(8,128)(2,1)S(1)}, bf16[32,512]{1,0:T(8,128)(2,1)S(1)}, u32[]{:S(2)}, u32[]{:S(2)}) collective-permute-start(bf16[32,512]{1,0:T(8,128)(2,1)S(1)} %get-tuple-element.91.refs_10_.refs_2_), channel_id=1, source_target_pairs={{0,2},{1,3},{2,0},{3,1},{4,6},{5,7},{6,4},{7,5},{8,10},{9,11},{10,... | collective-permute-start | bytes 98312 | tf_op jit(solution)/shard_map/ppermute | solution.py:403
  47.8 0.1 collective-permute-start.14
  47.9 1.1 %shard_map.111 = (bf16[1536,256]{1,0:T(8,128)(2,1)S(1)}, f32[8,128]{1,0:T(8,128)S(1)}) custom-call(bf16[2064,256]{1,0:T(8,128)(2,1)S(1)} %collective-permute-done.refs_1_.refs_0_, bf16[256,512]{1,0:T(8,128)(2,1)S(1)} %get-tuple-element.87.refs_1_, f32[256,128]{1,0:T(8,128)S(1)} %get-tuple-element.63.refs_4_.refs_6_.refs_2_, ...), custom_call_target="tpu_custom_call" | custom-call | flops 4000000000 | bytes 16000000 | tf_op jit(solution)/shard_map/pallas_call | solution.py:46
  48.9 1.0 %shard_map.112 = (bf16[1536,256]{1,0:T(8,128)(2,1)S(1)}, f32[8,128]{1,0:T(8,128)S(1)}) custom-call(bf16[2064,256]{1,0:T(8,128)(2,1)S(1)} %copy-done.1, bf16[256,512]{1,0:T(8,128)(2,1)S(1)} %get-tuple-element.57.refs_1_, f32[256,128]{1,0:T(8,128)S(1)} %get-tuple-element.58.refs_5_.refs_7_.refs_2_, f32[256,128]{1,0:T(8,128)S(1)} %get-tuple-element.71.refs_3_, ...), custom_call_target="tpu_custom_call" | custom-call | flops 4000000000 | bytes 16000000 | tf_op jit(solution)/shard_map/pallas_call | solution.py:46
  49.9 0.6 collective-permute-done.14.refs_5_
  50.5 0.5 shard_map.113
  51.1 1.3 %collective-permute-start.15 = (bf16[128,128]{1,0:T(8,128)(2,1)S(1)}, bf16[128,128]{1,0:T(8,128)(2,1)S(1)}, u32[]{:S(2)}, u32[]{:S(2)}) collective-permute-start(bf16[128,128]{1,0:T(8,128)(2,1)S(1)} %get-tuple-element.96), channel_id=1, source_target_pairs={{0,8},{4,12},{8,16},{12,20},{16,24},{20,28},{24,0},{28,4},{32,40},... | collective-permute-start | bytes 98312 | tf_op jit(solution)/shard_map/ppermute | solution.py:400
  52.4 2.7 %collective-permute-start.16 = (bf16[128,128]{1,0:T(8,128)(2,1)S(1)}, bf16[128,128]{1,0:T(8,128)(2,1)S(1)}, u32[]{:S(2)}, u32[]{:S(2)}) collective-permute-start(bf16[128,128]{1,0:T(8,128)(2,1)S(1)} %get-tuple-element.97), channel_id=1, source_target_pairs={{0,16},{4,20},{8,24},{12,28},{16,0},{20,4},{24,8},{28,12},{32,48},... | collective-permute-start | bytes 98312 | tf_op jit(solution)/shard_map/ppermute | solution.py:400
  55.1 0.1 collective-permute-done.15.refs_1_
  55.2 1.5 %collective-permute-done.16.refs_2_ = bf16[128,128]{1,0:T(8,128)(2,1)S(1)} collective-permute-done((bf16[128,128]{1,0:T(8,128)(2,1)S(1)}, bf16[128,128]{1,0:T(8,128)(2,1)S(1)}, u32[]{:S(2)}, u32[]{:S(2)}) %collective-permute-start.16) | collective-permute-done | bytes 32800 | tf_op jit(solution)/shard_map/ppermute | solution.py:400
  56.7 1.1 %collective-permute-done.17.refs_3_ = bf16[128,128]{1,0:T(8,128)(2,1)S(1)} collective-permute-done((bf16[128,128]{1,0:T(8,128)(2,1)S(1)}, bf16[128,128]{1,0:T(8,128)(2,1)S(1)}, u32[]{:S(2)}, u32[]{:S(2)}) %collective-permute-start.17) | collective-permute-done | bytes 32800 | tf_op jit(solution)/shard_map/ppermute | solution.py:400
  57.9 11.2 %all_to_all.11.refs_0_ = bf16[8,128,128]{2,1,0:T(8,128)(2,1)S(1)} all-to-all(bf16[8,128,128]{2,1,0:T(8,128)(2,1)S(1)} %shard_map.114), channel_id=1, replica_groups={{160,128,192,96,64,224,0,32},{164,132,196,100,68,228,4,36},{168,136,200..., dimensions={0} | all-to-all | bytes 524288 | tf_op jit(solution)/shard_map/all_to_all | solution.py:478
  69.1 9.0 %collective-permute-start.18 = (bf16[1536,256]{1,0:T(8,128)(2,1)S(1)}, bf16[1536,256]{1,0:T(8,128)(2,1)S(1)}, u32[]{:S(2)}, u32[]{:S(2)}) collective-permute-start(bf16[1536,256]{1,0:T(8,128)(2,1)S(1)} %get-tuple-element.100), channel_id=1, source_target_pairs={{0,4},{4,0},{8,12},{12,8},{16,20},{20,16},{24,28},{28,24},{32,36},... | collective-permute-start | bytes 2359304 | tf_op jit(solution)/shard_map/ppermute | solution.py:396
  78.2 2.1 %collective-permute-start.20 = (bf16[128,128]{1,0:T(8,128)(2,1)S(1)}, bf16[128,128]{1,0:T(8,128)(2,1)S(1)}, u32[]{:S(2)}, u32[]{:S(2)}) collective-permute-start(bf16[128,128]{1,0:T(8,128)(2,1)S(1)} %get-tuple-element.101.refs_2_.refs_0_), channel_id=1, source_target_pairs={{0,16},{4,20},{8,24},{12,28},{16,0},{20,4},{24,8},{28,12},{32,48},... | collective-permute-start | bytes 98312 | tf_op jit(solution)/shard_map/ppermute | solution.py:400
  80.3 1.2 %collective-permute-start.21 = (bf16[128,128]{1,0:T(8,128)(2,1)S(1)}, bf16[128,128]{1,0:T(8,128)(2,1)S(1)}, u32[]{:S(2)}, u32[]{:S(2)}) collective-permute-start(bf16[128,128]{1,0:T(8,128)(2,1)S(1)} %get-tuple-element.101.refs_2_.refs_0_), channel_id=1, source_target_pairs={{0,24},{4,28},{8,0},{12,4},{16,8},{20,12},{24,16},{28,20},{32,56},... | collective-permute-start | bytes 98312 | tf_op jit(solution)/shard_map/ppermute | solution.py:400
  81.5 1.2 %shard_map.116 = (bf16[512,512]{1,0:T(8,128)(2,1)}, bf16[512,512]{1,0:T(8,128)(2,1)}, bf16[512,512]{1,0:T(8,128)(2,1)}, f32[8,128]{1,0:T(8,128)S(1)}) custom-call(bf16[1536,256]{1,0:T(8,128)(2,1)S(1)} %get-tuple-element.93.refs_0_, bf16[1536,256]{1,0:T(8,128)(2,1)S(1)} %collective-permute-done.18.refs_1_, bf16[128,128]{1,0:T(8,128)(2,1)S(1)} %get-tuple-element.101.refs_2_.refs_0_), custom_call_target="tpu_custom_call" | custom-call | flops 10000000 | bytes 1000000 | tf_op jit(solution)/shard_map/pallas_call | solution.py:46
  82.7 0.7 collective-permute-done.21.refs_3_
  83.4 1.6 %collective-permute-start.22 = (bf16[512,128]{1,0:T(8,128)(2,1)S(1)}, bf16[512,128]{1,0:T(8,128)(2,1)S(1)}, u32[]{:S(2)}, u32[]{:S(2)}) collective-permute-start(bf16[512,128]{1,0:T(8,128)(2,1)S(1)} %shard_map.117.refs_0_), channel_id=1, source_target_pairs={{0,4},{4,0},{8,12},{12,8},{16,20},{20,16},{24,28},{28,24},{32,36},... | collective-permute-start | bytes 393224 | tf_op jit(solution)/shard_map/ppermute | solution.py:396
  84.9 1.0 %collective-permute-done.22.refs_1_ = bf16[512,128]{1,0:T(8,128)(2,1)S(1)} collective-permute-done((bf16[512,128]{1,0:T(8,128)(2,1)S(1)}, bf16[512,128]{1,0:T(8,128)(2,1)S(1)}, u32[]{:S(2)}, u32[]{:S(2)}) %collective-permute-start.22) | collective-permute-done | bytes 131104 | tf_op jit(solution)/shard_map/ppermute | solution.py:396
  85.9 1.0 %shard_map.118 = f32[1024,128]{1,0:T(8,128)} custom-call(bf16[512,128]{1,0:T(8,128)(2,1)S(1)} %shard_map.117.refs_0_, bf16[512,128]{1,0:T(8,128)(2,1)S(1)} %collective-permute-done.22.refs_1_), custom_call_target="tpu_custom_call" | custom-call | flops 10000000 | bytes 1000000 | tf_op jit(solution)/shard_map/pallas_call | solution.py:46
  (25 shorter events, 0.2 us)
Async XLA Ops:
  0.6 7.1 %copy-start.2 = (bf16[512,1024]{1,0:T(8,128)(2,1)S(1)}, bf16[512,1024]{1,0:T(8,128)(2,1)}, u32[]{:S(2)}) copy-start(bf16[512,1024]{1,0:T(8,128)(2,1)} %refs_0_.3) | copy-start | bytes 3145732
  4.4 6.7 %collective-permute-start = (bf16[2064,256]{1,0:T(8,128)(2,1)}, bf16[2064,256]{1,0:T(8,128)(2,1)S(1)}, u32[]{:S(2)}, u32[]{:S(2)}) collective-permute-start(bf16[2064,256]{1,0:T(8,128)(2,1)} %get-tuple-element.56), channel_id=1, source_target_pairs={{0,4},{4,0},{8,12},{12,8},{16,20},{20,16},{24,28},{28,24},{32,36},... | collective-permute-start | bytes 3170312 | tf_op jit(solution)/shard_map/ppermute | solution.py:396
  7.7 8.1 %collective-permute-start.5 = (bf16[512,1024]{1,0:T(8,128)(2,1)S(1)}, bf16[512,1024]{1,0:T(8,128)(2,1)S(1)}, u32[]{:S(2)}, u32[]{:S(2)}) collective-permute-start(bf16[512,1024]{1,0:T(8,128)(2,1)S(1)} %copy-done.2), channel_id=1, source_target_pairs={{0,4},{4,0},{8,12},{12,8},{16,20},{20,16},{24,28},{28,24},{32,36},... | collective-permute-start | bytes 3145736 | tf_op jit(solution)/shard_map/ppermute | solution.py:396
  7.8 6.2 %collective-permute-start.1 = (f32[32,512]{1,0:T(8,128)}, f32[32,512]{1,0:T(8,128)S(1)}, u32[]{:S(2)}, u32[]{:S(2)}) collective-permute-start(f32[32,512]{1,0:T(8,128)} %get-tuple-element.65), channel_id=1, source_target_pairs={{0,1},{1,2},{2,3},{3,0},{4,5},{5,6},{6,7},{7,4},{8,9},{9,10},{10,1... | collective-permute-start | bytes 196616 | tf_op jit(solution)/shard_map/ppermute | solution.py:403
  7.8 6.2 %collective-permute-start.2 = (f32[32,512]{1,0:T(8,128)}, f32[32,512]{1,0:T(8,128)S(1)}, u32[]{:S(2)}, u32[]{:S(2)}) collective-permute-start(f32[32,512]{1,0:T(8,128)} %get-tuple-element.66), channel_id=1, source_target_pairs={{0,2},{1,3},{2,0},{3,1},{4,6},{5,7},{6,4},{7,5},{8,10},{9,11},{10,... | collective-permute-start | bytes 196616 | tf_op jit(solution)/shard_map/ppermute | solution.py:403
  10.0 4.2 %collective-permute-start.3 = (f32[32,512]{1,0:T(8,128)}, f32[32,512]{1,0:T(8,128)S(1)}, u32[]{:S(2)}, u32[]{:S(2)}) collective-permute-start(f32[32,512]{1,0:T(8,128)} %get-tuple-element.67), channel_id=1, source_target_pairs={{0,3},{1,0},{2,1},{3,2},{4,7},{5,4},{6,5},{7,6},{8,11},{9,8},{10,9... | collective-permute-start | bytes 196616 | tf_op jit(solution)/shard_map/ppermute | solution.py:403
  11.1 1.2 %copy-start = (bf16[2064,256]{1,0:T(8,128)(2,1)S(1)}, bf16[2064,256]{1,0:T(8,128)(2,1)}, u32[]{:S(2)}) copy-start(bf16[2064,256]{1,0:T(8,128)(2,1)} %get-tuple-element.55.refs_0_) | copy-start | bytes 3170308
  12.8 1.4 %copy-start.3 = (f32[32,512]{1,0:T(8,128)S(1)}, f32[32,512]{1,0:T(8,128)}, u32[]{:S(2)}) copy-start(f32[32,512]{1,0:T(8,128)} %get-tuple-element.64.refs_0_) | copy-start | bytes 196612
  12.8 3.9 %copy-start.1 = (bf16[2064,256]{1,0:T(8,128)(2,1)S(1)}, bf16[2064,256]{1,0:T(8,128)(2,1)}, u32[]{:S(2)}) copy-start(bf16[2064,256]{1,0:T(8,128)(2,1)} %get-tuple-element.55.refs_0_) | copy-start | bytes 3170308
  14.2 2.5 %collective-permute-start.4 = (f32[16,512]{1,0:T(8,128)S(1)}, f32[16,512]{1,0:T(8,128)S(1)}, u32[]{:S(2)}, u32[]{:S(2)}) collective-permute-start(f32[16,512]{1,0:T(8,128)S(1)} %get-tuple-element.70), channel_id=1, source_target_pairs={{0,4},{4,0},{8,12},{12,8},{16,20},{20,16},{24,28},{28,24},{32,36},... | collective-permute-start | bytes 98312 | tf_op jit(solution)/shard_map/ppermute | solution.py:396
  17.5 5.3 %collective-permute-start.6 = (bf16[384,128]{1,0:T(8,128)(2,1)S(1)}, bf16[384,128]{1,0:T(8,128)(2,1)S(1)}, u32[]{:S(2)}, u32[]{:S(2)}) collective-permute-start(bf16[384,128]{1,0:T(8,128)(2,1)S(1)} %get-tuple-element.74), channel_id=1, source_target_pairs={{0,8},{4,12},{8,16},{12,20},{16,24},{20,28},{24,0},{28,4},{32,40},... | collective-permute-start | bytes 294920 | tf_op jit(solution)/shard_map/ppermute | solution.py:400
  18.5 7.1 %collective-permute-start.7 = (bf16[384,128]{1,0:T(8,128)(2,1)S(1)}, bf16[384,128]{1,0:T(8,128)(2,1)S(1)}, u32[]{:S(2)}, u32[]{:S(2)}) collective-permute-start(bf16[384,128]{1,0:T(8,128)(2,1)S(1)} %get-tuple-element.75), channel_id=1, source_target_pairs={{0,16},{4,20},{8,24},{12,28},{16,0},{20,4},{24,8},{28,12},{32,48},... | collective-permute-start | bytes 294920 | tf_op jit(solution)/shard_map/ppermute | solution.py:400
  20.9 4.7 %collective-permute-start.8 = (bf16[384,128]{1,0:T(8,128)(2,1)S(1)}, bf16[384,128]{1,0:T(8,128)(2,1)S(1)}, u32[]{:S(2)}, u32[]{:S(2)}) collective-permute-start(bf16[384,128]{1,0:T(8,128)(2,1)S(1)} %get-tuple-element.76), channel_id=1, source_target_pairs={{0,24},{4,28},{8,0},{12,4},{16,8},{20,12},{24,16},{28,20},{32,56},... | collective-permute-start | bytes 294920 | tf_op jit(solution)/shard_map/ppermute | solution.py:400
  37.8 4.1 %collective-permute-start.9 = (bf16[128,128]{1,0:T(8,128)(2,1)S(1)}, bf16[128,128]{1,0:T(8,128)(2,1)S(1)}, u32[]{:S(2)}, u32[]{:S(2)}) collective-permute-start(bf16[128,128]{1,0:T(8,128)(2,1)S(1)} %shard_map.108.refs_0_), channel_id=1, source_target_pairs={{0,8},{4,12},{8,16},{12,20},{16,24},{20,28},{24,0},{28,4},{32,40},... | collective-permute-start | bytes 98312 | tf_op jit(solution)/shard_map/ppermute | solution.py:400
  38.4 4.3 %collective-permute-start.10 = (bf16[128,128]{1,0:T(8,128)(2,1)S(1)}, bf16[128,128]{1,0:T(8,128)(2,1)S(1)}, u32[]{:S(2)}, u32[]{:S(2)}) collective-permute-start(bf16[128,128]{1,0:T(8,128)(2,1)S(1)} %shard_map.108.refs_0_), channel_id=1, source_target_pairs={{0,16},{4,20},{8,24},{12,28},{16,0},{20,4},{24,8},{28,12},{32,48},... | collective-permute-start | bytes 98312 | tf_op jit(solution)/shard_map/ppermute | solution.py:400
  40.5 2.8 %collective-permute-start.11 = (bf16[128,128]{1,0:T(8,128)(2,1)S(1)}, bf16[128,128]{1,0:T(8,128)(2,1)S(1)}, u32[]{:S(2)}, u32[]{:S(2)}) collective-permute-start(bf16[128,128]{1,0:T(8,128)(2,1)S(1)} %shard_map.108.refs_0_), channel_id=1, source_target_pairs={{0,24},{4,28},{8,0},{12,4},{16,8},{20,12},{24,16},{28,20},{32,56},... | collective-permute-start | bytes 98312 | tf_op jit(solution)/shard_map/ppermute | solution.py:400
  44.1 5.8 %collective-permute-start.12 = (bf16[32,512]{1,0:T(8,128)(2,1)S(1)}, bf16[32,512]{1,0:T(8,128)(2,1)S(1)}, u32[]{:S(2)}, u32[]{:S(2)}) collective-permute-start(bf16[32,512]{1,0:T(8,128)(2,1)S(1)} %get-tuple-element.91.refs_10_.refs_2_), channel_id=1, source_target_pairs={{0,1},{1,2},{2,3},{3,0},{4,5},{5,6},{6,7},{7,4},{8,9},{9,10},{10,1... | collective-permute-start | bytes 98312 | tf_op jit(solution)/shard_map/ppermute | solution.py:403
  44.6 5.3 %collective-permute-start.13 = (bf16[32,512]{1,0:T(8,128)(2,1)S(1)}, bf16[32,512]{1,0:T(8,128)(2,1)S(1)}, u32[]{:S(2)}, u32[]{:S(2)}) collective-permute-start(bf16[32,512]{1,0:T(8,128)(2,1)S(1)} %get-tuple-element.91.refs_10_.refs_2_), channel_id=1, source_target_pairs={{0,2},{1,3},{2,0},{3,1},{4,6},{5,7},{6,4},{7,5},{8,10},{9,11},{10,... | collective-permute-start | bytes 98312 | tf_op jit(solution)/shard_map/ppermute | solution.py:403
  47.8 2.8 %collective-permute-start.14 = (bf16[32,512]{1,0:T(8,128)(2,1)S(1)}, bf16[32,512]{1,0:T(8,128)(2,1)S(1)}, u32[]{:S(2)}, u32[]{:S(2)}) collective-permute-start(bf16[32,512]{1,0:T(8,128)(2,1)S(1)} %get-tuple-element.91.refs_10_.refs_2_), channel_id=1, source_target_pairs={{0,3},{1,0},{2,1},{3,2},{4,7},{5,4},{6,5},{7,6},{8,11},{9,8},{10,9... | collective-permute-start | bytes 98312 | tf_op jit(solution)/shard_map/ppermute | solution.py:403
  51.1 4.1 %collective-permute-start.15 = (bf16[128,128]{1,0:T(8,128)(2,1)S(1)}, bf16[128,128]{1,0:T(8,128)(2,1)S(1)}, u32[]{:S(2)}, u32[]{:S(2)}) collective-permute-start(bf16[128,128]{1,0:T(8,128)(2,1)S(1)} %get-tuple-element.96), channel_id=1, source_target_pairs={{0,8},{4,12},{8,16},{12,20},{16,24},{20,28},{24,0},{28,4},{32,40},... | collective-permute-start | bytes 98312 | tf_op jit(solution)/shard_map/ppermute | solution.py:400
  52.4 4.3 %collective-permute-start.16 = (bf16[128,128]{1,0:T(8,128)(2,1)S(1)}, bf16[128,128]{1,0:T(8,128)(2,1)S(1)}, u32[]{:S(2)}, u32[]{:S(2)}) collective-permute-start(bf16[128,128]{1,0:T(8,128)(2,1)S(1)} %get-tuple-element.97), channel_id=1, source_target_pairs={{0,16},{4,20},{8,24},{12,28},{16,0},{20,4},{24,8},{28,12},{32,48},... | collective-permute-start | bytes 98312 | tf_op jit(solution)/shard_map/ppermute | solution.py:400
  55.1 2.8 %collective-permute-start.17 = (bf16[128,128]{1,0:T(8,128)(2,1)S(1)}, bf16[128,128]{1,0:T(8,128)(2,1)S(1)}, u32[]{:S(2)}, u32[]{:S(2)}) collective-permute-start(bf16[128,128]{1,0:T(8,128)(2,1)S(1)} %get-tuple-element.98), channel_id=1, source_target_pairs={{0,24},{4,28},{8,0},{12,4},{16,8},{20,12},{24,16},{28,20},{32,56},... | collective-permute-start | bytes 98312 | tf_op jit(solution)/shard_map/ppermute | solution.py:400
  69.1 12.3 %collective-permute-start.18 = (bf16[1536,256]{1,0:T(8,128)(2,1)S(1)}, bf16[1536,256]{1,0:T(8,128)(2,1)S(1)}, u32[]{:S(2)}, u32[]{:S(2)}) collective-permute-start(bf16[1536,256]{1,0:T(8,128)(2,1)S(1)} %get-tuple-element.100), channel_id=1, source_target_pairs={{0,4},{4,0},{8,12},{12,8},{16,20},{20,16},{24,28},{28,24},{32,36},... | collective-permute-start | bytes 2359304 | tf_op jit(solution)/shard_map/ppermute | solution.py:396
  78.2 4.5 %collective-permute-start.19 = (bf16[128,128]{1,0:T(8,128)(2,1)S(1)}, bf16[128,128]{1,0:T(8,128)(2,1)S(1)}, u32[]{:S(2)}, u32[]{:S(2)}) collective-permute-start(bf16[128,128]{1,0:T(8,128)(2,1)S(1)} %get-tuple-element.101.refs_2_.refs_0_), channel_id=1, source_target_pairs={{0,8},{4,12},{8,16},{12,20},{16,24},{20,28},{24,0},{28,4},{32,40},... | collective-permute-start | bytes 98312 | tf_op jit(solution)/shard_map/ppermute | solution.py:400
  78.2 4.5 %collective-permute-start.20 = (bf16[128,128]{1,0:T(8,128)(2,1)S(1)}, bf16[128,128]{1,0:T(8,128)(2,1)S(1)}, u32[]{:S(2)}, u32[]{:S(2)}) collective-permute-start(bf16[128,128]{1,0:T(8,128)(2,1)S(1)} %get-tuple-element.101.refs_2_.refs_0_), channel_id=1, source_target_pairs={{0,16},{4,20},{8,24},{12,28},{16,0},{20,4},{24,8},{28,12},{32,48},... | collective-permute-start | bytes 98312 | tf_op jit(solution)/shard_map/ppermute | solution.py:400
  80.3 3.1 %collective-permute-start.21 = (bf16[128,128]{1,0:T(8,128)(2,1)S(1)}, bf16[128,128]{1,0:T(8,128)(2,1)S(1)}, u32[]{:S(2)}, u32[]{:S(2)}) collective-permute-start(bf16[128,128]{1,0:T(8,128)(2,1)S(1)} %get-tuple-element.101.refs_2_.refs_0_), channel_id=1, source_target_pairs={{0,24},{4,28},{8,0},{12,4},{16,8},{20,12},{24,16},{28,20},{32,56},... | collective-permute-start | bytes 98312 | tf_op jit(solution)/shard_map/ppermute | solution.py:400
  83.4 2.5 %collective-permute-start.22 = (bf16[512,128]{1,0:T(8,128)(2,1)S(1)}, bf16[512,128]{1,0:T(8,128)(2,1)S(1)}, u32[]{:S(2)}, u32[]{:S(2)}) collective-permute-start(bf16[512,128]{1,0:T(8,128)(2,1)S(1)} %shard_map.117.refs_0_), channel_id=1, source_target_pairs={{0,4},{4,0},{8,12},{12,8},{16,20},{20,16},{24,28},{28,24},{32,36},... | collective-permute-start | bytes 393224 | tf_op jit(solution)/shard_map/ppermute | solution.py:396
